TPU v7x, 32 devices: a whole 2x2x4 slice. The times are simulated.
32 devices in a mesh: wide: 8 (over y, x, core), narrow: 4 (over z).
Axes of the slice: x: 2, y: 2, z: 4, core: 2. Of those that a mesh axis runs over, the one named last changes fastest.
Arguments:
- fractions: float32 [3, 16384], P(None, ('wide', 'narrow')), may hold values from 0 to 1
- cell_lengths: float32 [3], replicated, may hold values from 18 to 30
- features: bfloat16 [16384, 128], P(('wide', 'narrow')), may hold values from -6 to 6
- atom_counts: int32 [32], P(('wide', 'narrow')), may hold values from 384 to 512, as said below
- send_index: int32 [128, 384], P(('wide', 'narrow')), may hold values from 0 to 511, as said below
- senders: int32 [16, 16384], P(None, ('wide', 'narrow')), may hold values from 0 to 2047, as said below
- radial: float32 [16, 16384], P(None, ('wide', 'narrow')), may hold values from -1.5 to 1.5
- self_weight: bfloat16 [2, 128, 128], replicated, may hold values from -0.5 to 0.5
- message_weight: bfloat16 [2, 128, 128], replicated, may hold values from -0.5 to 0.5
- charge_weight: bfloat16 [128, 4], replicated, may hold values from -0.5 to 0.5
- wave_numbers: int32 [3, 8192], replicated, may hold values from -8 to 8, as said below
Outputs:
- forces: float32 [3, 16384], P(None, ('wide', 'narrow'))
- born_charges: float32 [3, 16384], P(None, ('wide', 'narrow'))
- energy: float32 [], replicated
Inputs may be any that keep to these rules, and one draw needn't show every extreme that they name: `atom_counts`: every value lies between 384 and 512; some device holds exactly 512; slots at or above a device's count are padding. `send_index`: every entry of device d's four blocks is below atom_counts[d]. `senders`: for an atom slot of device d an entry is either a live local atom (below atom_counts[d]) or 512 + b * 384 + g, ghost row g of received block b. `wave_numbers`: the first component is 1 to 8, the others -8 to 8.
All inputs are finite; a program needn't handle non-finite values.
Results may differ from a plain program's by a relative error of at most 0.014.
Values sent between devices are 32-bit elements; how exact they have to be, the bound alone decides.
No kernel may reach another device: no remote copies, remote signals or barrier semaphores. Data moves between devices by JAX's collectives and lax.ppermute only.
A program may use at most 192 MiB of HBM per device.

v0:
```python
import math

import jax
import jax.numpy as jnp
from jax import lax
from jax.sharding import PartitionSpec as P

smearing = 0.5
two_pi = 2.0 * math.pi
highest = lax.Precision.HIGHEST


def padded(block, sides, width):
    for axis, dim in sides:
        count = lax.axis_size(axis)
        forward = [(i, i + 1) for i in range(count - 1)]
        forward.append((count - 1, 0))
        backward = [(target, source) for source, target in forward]
        low = lax.ppermute(
            lax.slice_in_dim(block, block.shape[dim] - width, None, axis=dim), axis, forward
        )
        high = lax.ppermute(lax.slice_in_dim(block, 0, width, axis=dim), axis, backward)
        block = jnp.concatenate([low, block, high], axis=dim)
    return block


def phase_angles(fractions, numbers):
    return two_pi * (
        fractions[0][:, None] * numbers[0][None, :]
        + fractions[1][:, None] * numbers[1][None, :]
        + fractions[2][:, None] * numbers[2][None, :]
    )


def wave_weights(cell_lengths, numbers):
    wave = two_pi * numbers / cell_lengths[:, None]
    squared = jnp.sum(wave * wave, axis=0)
    return jnp.exp(-0.5 * smearing * smearing * squared) / squared


def split_blocks(numbers, block_width):
    count_blocks = numbers.shape[1] // block_width
    return numbers.reshape(3, count_blocks, block_width).transpose(1, 0, 2)


def phase_tables(fractions, number_blocks):

    def one_block(numbers_block):
        angles = phase_angles(fractions, numbers_block)
        return (jnp.cos(angles), jnp.sin(angles))

    return lax.map(one_block, number_blocks)


def factor_blocks(charges, cos_tables, sin_tables):
    charge_rows = charges.astype(jnp.bfloat16)
    real_part = jnp.einsum(
        "ca,nak->nck",
        charge_rows,
        cos_tables.astype(jnp.bfloat16),
        preferred_element_type=jnp.float32,
    )
    imag_part = jnp.einsum(
        "ca,nak->nck",
        charge_rows,
        sin_tables.astype(jnp.bfloat16),
        preferred_element_type=jnp.float32,
    )
    return jnp.stack([real_part, imag_part], axis=1)


def gradient_blocks(charges, number_blocks, factors, weights, cos_tables, sin_tables):
    dims = (((0,), (0,)), ((), ()))

    def add_block(running, inputs):
        numbers_block, factor_block, weight_block, cosine, sine_part = inputs
        with_real = lax.dot_general(
            charges,
            weight_block * factor_block[0],
            dims,
            precision=highest,
            preferred_element_type=jnp.float32,
        )
        with_imag = lax.dot_general(
            charges,
            weight_block * factor_block[1],
            dims,
            precision=highest,
            preferred_element_type=jnp.float32,
        )
        joined = (with_imag * cosine - with_real * sine_part).astype(jnp.bfloat16)
        term = lax.dot_general(
            numbers_block.astype(jnp.bfloat16),
            joined,
            (((1,), (1,)), ((), ())),
            preferred_element_type=jnp.float32,
        )
        return (running + term, None)

    start_value = jnp.zeros((3, charges.shape[1]), jnp.float32)
    gradient, _ = lax.scan(
        add_block, start_value, (number_blocks, factors, weights, cos_tables, sin_tables)
    )
    return gradient


def block_energy(factors, weights, energy_scale):
    return (
        0.5
        * energy_scale
        * jnp.sum(
            weights[:, None, :] * (factors[:, 0] * factors[:, 0] + factors[:, 1] * factors[:, 1])
        )
    )


def edge_matrix(senders, radial, ext_rows):
    ext_ids = jnp.arange(ext_rows, dtype=jnp.int32)
    matrix = jnp.zeros((senders.shape[1], ext_rows), jnp.float32)
    for slot in range(senders.shape[0]):
        matrix = matrix + jnp.where(
            senders[slot][:, None] == ext_ids[None, :], radial[slot][:, None], 0.0
        )
    return matrix


def per_device(
    fractions,
    cell_lengths,
    features,
    atom_counts,
    send_index,
    senders,
    radial,
    self_weight,
    message_weight,
    charge_weight,
    wave_numbers,
):
    atom_dev = features.shape[0]
    ghost_rows = send_index.shape[1]
    slot_ids = jnp.arange(atom_dev, dtype=jnp.int32)
    alive_mask = slot_ids < atom_counts[0]
    weight_matrix = edge_matrix(senders, radial, atom_dev + 4 * ghost_rows)
    hidden = features
    for layer_index in range(self_weight.shape[0]):
        message = jnp.dot(hidden, message_weight[layer_index], preferred_element_type=jnp.float32)
        picked = jnp.take(message, send_index, axis=0)
        wide_rim = padded(picked[0:2], (("wide", 0),), 1)
        narrow_rim = padded(picked[2:4], (("narrow", 0),), 1)
        extended = jnp.concatenate(
            [message, wide_rim[0], wide_rim[3], narrow_rim[0], narrow_rim[3]], axis=0
        )
        combined = jnp.dot(
            weight_matrix, extended, precision=highest, preferred_element_type=jnp.float32
        )
        self_term = jnp.dot(hidden, self_weight[layer_index], preferred_element_type=jnp.float32)
        hidden = (hidden.astype(jnp.float32) + jax.nn.silu(self_term + combined)).astype(
            jnp.bfloat16
        )
    charges = lax.dot_general(
        charge_weight, hidden, (((0,), (1,)), ((), ())), preferred_element_type=jnp.float32
    )
    charges = jnp.where(alive_mask[None, :], charges, 0.0)
    numbers = wave_numbers.astype(jnp.float32)
    total_atoms = atom_dev * lax.axis_size("wide") * lax.axis_size("narrow")
    energy_scale = 4.0 / math.sqrt(total_atoms * numbers.shape[1])
    frac_slab, charge_slab = (
        lax.all_gather(fractions, "narrow", axis=1, tiled=True),
        lax.all_gather(charges, "narrow", axis=1, tiled=True),
    )
    share_width = numbers.shape[1] // lax.axis_size("narrow")
    own_numbers = lax.dynamic_slice_in_dim(
        numbers, lax.axis_index("narrow") * share_width, share_width, 1
    )
    number_blocks = split_blocks(own_numbers, min(share_width, 1024))
    cos_tables, sin_tables = phase_tables(frac_slab, number_blocks)
    factors = factor_blocks(charge_slab, cos_tables, sin_tables)
    factors = lax.psum(factors, "wide")
    weights = jax.vmap(lambda numbers_block: wave_weights(cell_lengths, numbers_block))(
        number_blocks
    )
    energy = lax.psum(block_energy(factors, weights, energy_scale), "narrow")
    slab_gradient = gradient_blocks(
        charge_slab, number_blocks, factors, weights, cos_tables, sin_tables
    )
    gradient = lax.psum_scatter(slab_gradient, "narrow", scatter_dimension=1, tiled=True)
    forces = jnp.where(
        alive_mask[None, :], -(two_pi * energy_scale / cell_lengths[:, None]) * gradient, 0.0
    )
    charge_total = jnp.sum(charges, axis=0)
    born_charges = jnp.where(
        alive_mask[None, :], charge_total[None, :] * jnp.cos(two_pi * fractions), 0.0
    )
    return (forces, born_charges, energy)


def solution(mesh):
    return jax.shard_map(
        per_device,
        mesh=mesh,
        in_specs=(
            P(None, ("wide", "narrow")),
            P(),
            P(("wide", "narrow"), None),
            P(("wide", "narrow")),
            P(("wide", "narrow"), None),
            P(None, ("wide", "narrow")),
            P(None, ("wide", "narrow")),
            P(),
            P(),
            P(),
            P(),
        ),
        out_specs=(P(None, ("wide", "narrow")), P(None, ("wide", "narrow")), P()),
        check_vma=False,
    )
```

profile of v0, /device:TPU:0, one launch (start us, length us, event | category | flops | bytes accessed | tf_op | source)
XLA Modules:
  0.0 313.0 jit_solution(9824375336096345678)
XLA Ops:
  8.6 1.1 constant_dynamic-update-slice_fusion
  9.8 2.6 gather_fusion
  13.2 2.9 collective-permute-start.1
  16.2 2.3 collective-permute-start.2
  18.4 2.0 collective-permute-start.3
  21.4 14.6 %all_gather.6 = f32[3,2048]{1,0:T(4,128)S(1)} all-gather(f32[3,512]{1,0:T(4,128)S(1)} %copy-done.4), channel_id=1, replica_groups=mesh['wide'=8,'narrow'=4] {'narrow'}, dimensions={1}, use_global_device_ids=true | all-gather | bytes 30720 | tf_op jit(solution)/shard_map/all_gather | solution.py:169
  36.7 69.6 %while.23 = (s32[]{:T(128)}, f32[2,2048,1024]{2,1,0:T(8,128)}, f32[2,2048,1024]{2,1,0:T(8,128)}, f32[3,2048]{1,0:T(4,128)S(1)}, f32[2,3,1024]{2,1,0:T(4,128)S(1)}, /*index=5*/s32[]{:T(128)}, s32[]{:T(128)}, s32[]{}, s32[]{}) while((s32[]{:T(128)}, f32[2,2048,1024]{2,1,0:T(8,128)}, f32[2,2048,1024]{2,1,0:T(8,128)}, f32[3,2048]{1,0:T(4,128)S(1)}, ...), condition=%wide.region_1.2_spmd, body=%wide.region_0.1_spmd.sunk | while | flops 12582916 | bytes 16888448 | solution.py:52
  36.8 34.8 %sine_dynamic-update-slice_fusion.2 = (f32[2,2048,1024]{2,1,0:T(8,128)}, f32[2,2048,1024]{2,1,0:T(8,128)}) fusion(f32[2,2048,1024]{2,1,0:T(8,128)} %get-tuple-element.309, s32[]{:T(128)} %get-tuple-element.307, f32[1024]{0:T(1024)S(1)} %bitcast.187, f32[2048]{0:T(1024)S(1)} %bitcast.182, f32[1024]{0:T(1024)S(1)} %bitcast.186, f32[2048]{0:T(1024)S(1)} %bitcast.183, ...), kind=kLoop, calls=%fused_computation.2.clone.1 | loop fusion | flops 12582912 | bytes 16814592 | tf_op jit(solution)/shard_map/while/body/jit(dynamic_update_index_in_dim)/dynamic_update_slice | solution.py:52
  71.7 34.7 %sine_dynamic-update-slice_fusion.2 = (f32[2,2048,1024]{2,1,0:T(8,128)}, f32[2,2048,1024]{2,1,0:T(8,128)}) fusion(f32[2,2048,1024]{2,1,0:T(8,128)} %get-tuple-element.309, s32[]{:T(128)} %get-tuple-element.307, f32[1024]{0:T(1024)S(1)} %bitcast.187, f32[2048]{0:T(1024)S(1)} %bitcast.182, f32[1024]{0:T(1024)S(1)} %bitcast.186, f32[2048]{0:T(1024)S(1)} %bitcast.183, ...), kind=kLoop, calls=%fused_computation.2.clone.1 | loop fusion | flops 12582912 | bytes 16814592 | tf_op jit(solution)/shard_map/while/body/jit(dynamic_update_index_in_dim)/dynamic_update_slice | solution.py:52
  106.7 15.5 %convolution_add_fusion.2 = f32[512,128]{1,0:T(8,128)S(1)} fusion(f32[512,128]{1,0:T(8,128)S(1)} %fusion.36, f32[2048,128]{1,0:T(8,128)S(1)} %bitcast_dynamic-update-slice_fusion.4, f32[512]{0:T(512)S(1)} %bitcast.250, s32[512]{0:T(512)S(1)} %bitcast.218, f32[512]{0:T(512)S(1)} %bitcast.252, s32[512]{0:T(512)S(1)} %bitcast.220, f32[512]{0:T(512)S(1)} %bitcast.224, ...), kind=kOutput, calls=%fused_computation.47 | convolution fusion | flops 1659961344 | bytes 1638400 | tf_op jit(solution)/shard_map/dot_general | solution.py:154
  122.9 2.6 gather_fusion.1
  125.9 2.6 collective-permute-start.5
  128.5 3.8 %collective-permute-start.7 = (f32[1,384,128]{2,1,0:T(8,128)S(1)}, f32[1,384,128]{2,1,0:T(8,128)S(1)}, u32[]{:S(2)}, u32[]{:S(2)}) collective-permute-start(f32[1,384,128]{2,1,0:T(8,128)S(1)} %get-tuple-element.154), channel_id=1, source_target_pairs={{1,0},{2,1},{3,2},{0,3},{5,4},{6,5},{7,6},{4,7},{9,8},{10,9},{11,1... | collective-permute-start | bytes 589832 | tf_op jit(solution)/shard_map/ppermute | solution.py:22
  133.2 5.0 %collective-permute-done.6 = f32[1,384,128]{2,1,0:T(8,128)S(1)} collective-permute-done((f32[1,384,128]{2,1,0:T(8,128)S(1)}, f32[1,384,128]{2,1,0:T(8,128)S(1)}, u32[]{:S(2)}, u32[]{:S(2)}) %collective-permute-start.6) | collective-permute-done | bytes 196640 | tf_op jit(solution)/shard_map/ppermute | solution.py:19
  138.6 15.7 %add_convert_fusion = bf16[512,128]{1,0:T(8,128)(2,1)S(1)} fusion(f32[512,128]{1,0:T(8,128)S(1)} %fusion.23, f32[2048,128]{1,0:T(8,128)S(1)} %bitcast_dynamic-update-slice_fusion, f32[512,128]{1,0:T(8,128)S(1)} %copy-done.9, bf16[512,128]{1,0:T(8,128)(2,1)S(1)} %copy-done.1, f32[512]{0:T(512)S(1)} %bitcast.251, s32[512]{0:T(512)S(1)} %bitcast.219, ...), kind=kOutput, calls=%fused_computation.53 | convolution fusion | flops 1660878848 | bytes 1900544 | tf_op jit(solution)/shard_map/dot_general | solution.py:154
  154.5 13.3 %all_gather.7 = f32[4,2048]{1,0:T(4,128)S(1)} all-gather(f32[4,512]{1,0:T(4,128)S(1)} %bitcast.189), channel_id=1, replica_groups=mesh['wide'=8,'narrow'=4] {'narrow'}, dimensions={1}, use_global_device_ids=true | all-gather | bytes 40960 | tf_op jit(solution)/shard_map/all_gather | solution.py:170
  167.9 1.2 fusion.16
  169.1 7.0 %fusion.19 = f32[2,1,4,1024]{3,2,0,1:T(4,128)S(1)} fusion(f32[2,2048,1024]{2,1,0:T(8,128)} %get-tuple-element.332, f32[4,2048]{1,0:T(4,128)S(1)} %all_gather.7), kind=kOutput, calls=%fused_computation.49 | convolution fusion | flops 37756928 | bytes 16842752 | tf_op jit(solution)/shard_map/ca,nak->nck/dot_general | solution.py:63
  176.8 51.2 %all-reduce.2.cloned.1.call-done = f32[2,2,4,1024]{3,2,0,1:T(4,128)} async-done(((f32[2,2,4,1024]{3,2,0,1:T(4,128)}), f32[2,2,4,1024]{3,2,0,1:T(4,128)}) %all-reduce.2.cloned.1.call-update) | async-done | bytes 65552 | tf_op jit(solution)/shard_map/psum | solution.py:179
  228.0 48.1 %while.24 = (s32[]{:T(128)}, f32[3,2048]{1,0:T(4,128)S(1)}, bf16[2,3,1024]{2,1,0:T(4,128)(2,1)S(1)}, f32[2,1024]{1,0:T(2,128)S(1)}, f32[2,2,4,1024]{3,2,0,1:T(4,...) while((s32[]{:T(128)}, f32[3,2048]{1,0:T(4,128)S(1)}, ...), condition=%wide.region_5.7_spmd.clone, body=%wide.region_4.6_spmd.clone.sunk | while | flops 222318592 | bytes 42188924 | solution.py:101
  228.8 6.8 %fusion.80 = f32[1024,2048]{0,1:T(8,128)S(1)} fusion(f32[4,2048]{1,0:T(4,128)S(1)} %get-tuple-element.350, f32[1,2,4,1024]{3,2,1,0:T(4,128)S(1)} %dynamic-slice_bitcast_fusion.2, f32[1024]{0:T(1024)S(1)} %bitcast.177), kind=kOutput, calls=%fused_computation.18.clone.1 | convolution fusion | flops 100667392 | bytes 8441856 | tf_op jit(solution)/shard_map/while/body/eval_jaxpr/dot_general | solution.py:84
  235.6 13.1 %fusion.81 = bf16[2048,1024]{1,0:T(8,128)(2,1)} fusion(f32[1024,2048]{0,1:T(8,128)S(1)} %fusion.80, f32[2,2048,1024]{2,1,0:T(8,128)} %get-tuple-element.352, s32[]{:T(128)} %get-tuple-element.335, f32[2,2048,1024]{2,1,0:T(8,128)} %get-tuple-element.351, f32[4,2048]{1,0:T(4,128)S(1)} %get-tuple-element.350, ...), kind=kOutput, calls=%fused_computation.10.clone.1 | convolution fusion | flops 109056000 | bytes 29413380 | tf_op jit(solution)/shard_map/while/body/eval_jaxpr/dot_general | solution.py:77
  248.7 3.4 %convolution_add_fusion.4 = f32[3,2048]{1,0:T(4,128)S(1)} fusion(bf16[2048,1024]{1,0:T(8,128)(2,1)} %fusion.81, f32[3,2048]{1,0:T(4,128)S(1)} %get-tuple-element.336, pred[]{:T(512)S(6)} %compare.3, bf16[2,3,1024]{2,1,0:T(4,128)(2,1)S(1)} %get-tuple-element.347, s32[]{:T(128)} %get-tuple-element.335), kind=kOutput, calls=%fused_computation.12.clone.1 | convolution fusion | flops 12595200 | bytes 4259845 | tf_op jit(solution)/shard_map/while/body/eval_jaxpr/dot_general | solution.py:92
  252.1 0.8 dynamic-slice_bitcast_fusion.2
  252.9 6.8 %fusion.80 = f32[1024,2048]{0,1:T(8,128)S(1)} fusion(f32[4,2048]{1,0:T(4,128)S(1)} %get-tuple-element.350, f32[1,2,4,1024]{3,2,1,0:T(4,128)S(1)} %dynamic-slice_bitcast_fusion.2, f32[1024]{0:T(1024)S(1)} %bitcast.177), kind=kOutput, calls=%fused_computation.18.clone.1 | convolution fusion | flops 100667392 | bytes 8441856 | tf_op jit(solution)/shard_map/while/body/eval_jaxpr/dot_general | solution.py:84
  259.7 13.1 %fusion.81 = bf16[2048,1024]{1,0:T(8,128)(2,1)} fusion(f32[1024,2048]{0,1:T(8,128)S(1)} %fusion.80, f32[2,2048,1024]{2,1,0:T(8,128)} %get-tuple-element.352, s32[]{:T(128)} %get-tuple-element.335, f32[2,2048,1024]{2,1,0:T(8,128)} %get-tuple-element.351, f32[4,2048]{1,0:T(4,128)S(1)} %get-tuple-element.350, ...), kind=kOutput, calls=%fused_computation.10.clone.1 | convolution fusion | flops 109056000 | bytes 29413380 | tf_op jit(solution)/shard_map/while/body/eval_jaxpr/dot_general | solution.py:77
  272.8 3.4 %convolution_add_fusion.4 = f32[3,2048]{1,0:T(4,128)S(1)} fusion(bf16[2048,1024]{1,0:T(8,128)(2,1)} %fusion.81, f32[3,2048]{1,0:T(4,128)S(1)} %get-tuple-element.336, pred[]{:T(512)S(6)} %compare.3, bf16[2,3,1024]{2,1,0:T(4,128)(2,1)S(1)} %get-tuple-element.347, s32[]{:T(128)} %get-tuple-element.335), kind=kOutput, calls=%fused_computation.12.clone.1 | convolution fusion | flops 12595200 | bytes 4259845 | tf_op jit(solution)/shard_map/while/body/eval_jaxpr/dot_general | solution.py:92
  276.2 1.4 copy.16
  277.6 1.4 fusion.31
  279.7 12.5 %psum.15 = f32[]{:T(128)} all-reduce(f32[]{:T(128)S(6)} %mul_shard_map.3), channel_id=1, replica_groups=mesh['wide'=8,'narrow'=4] {'narrow'}, use_global_device_ids=true, to_apply=%region_9.11 | all-reduce | flops 1 | bytes 8 | tf_op jit(solution)/shard_map/psum | solution.py:183
  292.2 12.2 %reduce-scatter.4.cloned.1.call-done = f32[512,3]{1,0:T(8,128)} async-done(((f32[2048,3]{1,0:T(8,128)}), f32[512,3]{1,0:T(8,128)}) %reduce-scatter.4.cloned.1.call-update) | async-done | bytes 6160
  304.4 1.1 copy.17
  (83 shorter events, 8.2 us)
Async XLA Ops:
  7.2 147.2 %copy-start = (bf16[128,4]{0,1:T(4,128)(2,1)S(1)}, bf16[128,4]{0,1:T(4,128)(2,1)}, u32[]{:S(2)}) copy-start(bf16[128,4]{0,1:T(4,128)(2,1)} %param.26) | copy-start | bytes 3076
  7.2 220.9 %all-reduce.2.cloned.1.call-start = ((), (), s32[]{:S(2)}) async-start(), calls=%async_computation.1 | async-start | bytes 131072 | tf_op jit(solution)/shard_map/psum | solution.py:179
  9.7 10.7 %copy-start.2 = (s32[16,512]{1,0:T(8,128)S(1)}, s32[16,512]{1,0:T(8,128)}, u32[]{:S(2)}) copy-start(s32[16,512]{1,0:T(8,128)} %param.22) | copy-start | bytes 98308
  9.7 10.8 %copy-start.1 = (bf16[512,128]{1,0:T(8,128)(2,1)S(1)}, bf16[512,128]{1,0:T(8,128)(2,1)}, u32[]{:S(2)}) copy-start(bf16[512,128]{1,0:T(8,128)(2,1)} %param.19) | copy-start | bytes 393220
  9.8 10.8 %copy-start.5 = (bf16[2,128,128]{2,1,0:T(8,128)(2,1)S(1)}, bf16[2,128,128]{2,1,0:T(8,128)(2,1)}, u32[]{:S(2)}) copy-start(bf16[2,128,128]{2,1,0:T(8,128)(2,1)} %param.24) | copy-start | bytes 196612
  9.8 11.6 %copy-start.4 = (f32[3,512]{1,0:T(4,128)S(1)}, f32[3,512]{1,0:T(4,128)}, u32[]{:S(2)}) copy-start(f32[3,512]{1,0:T(4,128)} %param.17) | copy-start | bytes 18436
  12.7 93.8 %collective-permute-start = (f32[1,384,128]{2,1,0:T(8,128)S(1)}, f32[1,384,128]{2,1,0:T(8,128)S(1)}, u32[]{:S(2)}, u32[]{:S(2)}) collective-permute-start(f32[1,384,128]{2,1,0:T(8,128)S(1)} %get-tuple-element.161), channel_id=1, source_target_pairs={{0,4},{4,8},{8,12},{12,16},{16,20},{20,24},{24,28},{28,0},{1,5},{5... | collective-permute-start | bytes 589832 | tf_op jit(solution)/shard_map/ppermute | solution.py:19
  13.2 93.3 %collective-permute-start.1 = (f32[1,384,128]{2,1,0:T(8,128)S(1)}, f32[1,384,128]{2,1,0:T(8,128)S(1)}, u32[]{:S(2)}, u32[]{:S(2)}) collective-permute-start(f32[1,384,128]{2,1,0:T(8,128)S(1)} %get-tuple-element.160), channel_id=1, source_target_pairs={{4,0},{8,4},{12,8},{16,12},{20,16},{24,20},{28,24},{0,28},{5,1},{9... | collective-permute-start | bytes 589832 | tf_op jit(solution)/shard_map/ppermute | solution.py:22
  16.2 90.4 %collective-permute-start.2 = (f32[1,384,128]{2,1,0:T(8,128)S(1)}, f32[1,384,128]{2,1,0:T(8,128)S(1)}, u32[]{:S(2)}, u32[]{:S(2)}) collective-permute-start(f32[1,384,128]{2,1,0:T(8,128)S(1)} %get-tuple-element.159), channel_id=1, source_target_pairs={{0,1},{1,2},{2,3},{3,0},{4,5},{5,6},{6,7},{7,4},{8,9},{9,10},{10,1... | collective-permute-start | bytes 589832 | tf_op jit(solution)/shard_map/ppermute | solution.py:19
  18.4 88.2 %collective-permute-start.3 = (f32[1,384,128]{2,1,0:T(8,128)S(1)}, f32[1,384,128]{2,1,0:T(8,128)S(1)}, u32[]{:S(2)}, u32[]{:S(2)}) collective-permute-start(f32[1,384,128]{2,1,0:T(8,128)S(1)} %get-tuple-element.158), channel_id=1, source_target_pairs={{1,0},{2,1},{3,2},{0,3},{5,4},{6,5},{7,6},{4,7},{9,8},{10,9},{11,1... | collective-permute-start | bytes 589832 | tf_op jit(solution)/shard_map/ppermute | solution.py:22
  36.7 69.6 %copy-start.7 = (f32[3]{0:T(128)S(1)}, f32[3]{0:T(128)}, u32[]{:S(2)}) copy-start(f32[3]{0:T(128)} %param.18) | copy-start | bytes 40
  36.7 69.8 %copy-start.3 = (f32[16,512]{1,0:T(8,128)S(1)}, f32[16,512]{1,0:T(8,128)}, u32[]{:S(2)}) copy-start(f32[16,512]{1,0:T(8,128)} %param.23) | copy-start | bytes 98308
  106.6 15.5 %copy-start.6 = (bf16[2,128,128]{2,1,0:T(8,128)(2,1)S(1)}, bf16[2,128,128]{2,1,0:T(8,128)(2,1)}, u32[]{:S(2)}) copy-start(bf16[2,128,128]{2,1,0:T(8,128)(2,1)} %param.25) | copy-start | bytes 196612
  122.2 0.7 copy-start.8
  122.9 9.5 %copy-start.9 = (f32[512,128]{1,0:T(8,128)S(1)}, f32[512,128]{1,0:T(8,128)}, u32[]{:S(2)}) copy-start(f32[512,128]{1,0:T(8,128)} %copy-done.8) | copy-start | bytes 786436
  125.8 7.3 %collective-permute-start.4 = (f32[1,384,128]{2,1,0:T(8,128)S(1)}, f32[1,384,128]{2,1,0:T(8,128)S(1)}, u32[]{:S(2)}, u32[]{:S(2)}) collective-permute-start(f32[1,384,128]{2,1,0:T(8,128)S(1)} %get-tuple-element.157), channel_id=1, source_target_pairs={{0,4},{4,8},{8,12},{12,16},{16,20},{20,24},{24,28},{28,0},{1,5},{5... | collective-permute-start | bytes 589832 | tf_op jit(solution)/shard_map/ppermute | solution.py:19
  125.9 7.3 %collective-permute-start.5 = (f32[1,384,128]{2,1,0:T(8,128)S(1)}, f32[1,384,128]{2,1,0:T(8,128)S(1)}, u32[]{:S(2)}, u32[]{:S(2)}) collective-permute-start(f32[1,384,128]{2,1,0:T(8,128)S(1)} %get-tuple-element.156), channel_id=1, source_target_pairs={{4,0},{8,4},{12,8},{16,12},{20,16},{24,20},{28,24},{0,28},{5,1},{9... | collective-permute-start | bytes 589832 | tf_op jit(solution)/shard_map/ppermute | solution.py:22
  128.5 9.6 %collective-permute-start.6 = (f32[1,384,128]{2,1,0:T(8,128)S(1)}, f32[1,384,128]{2,1,0:T(8,128)S(1)}, u32[]{:S(2)}, u32[]{:S(2)}) collective-permute-start(f32[1,384,128]{2,1,0:T(8,128)S(1)} %get-tuple-element.155), channel_id=1, source_target_pairs={{0,1},{1,2},{2,3},{3,0},{4,5},{5,6},{6,7},{7,4},{8,9},{9,10},{10,1... | collective-permute-start | bytes 589832 | tf_op jit(solution)/shard_map/ppermute | solution.py:19
  128.5 10.0 %collective-permute-start.7 = (f32[1,384,128]{2,1,0:T(8,128)S(1)}, f32[1,384,128]{2,1,0:T(8,128)S(1)}, u32[]{:S(2)}, u32[]{:S(2)}) collective-permute-start(f32[1,384,128]{2,1,0:T(8,128)S(1)} %get-tuple-element.154), channel_id=1, source_target_pairs={{1,0},{2,1},{3,2},{0,3},{5,4},{6,5},{7,6},{4,7},{9,8},{10,9},{11,1... | collective-permute-start | bytes 589832 | tf_op jit(solution)/shard_map/ppermute | solution.py:22
  138.5 29.3 %slice-start = ((s8[16777216]{0:T(1024)(128)(4,1)}), s8[4194304]{0:T(1024)(128)(4,1)S(1)}, s32[]{:S(2)}) async-start(s8[16777216]{0:T(1024)(128)(4,1)} %bitcast.174), calls=%async_computation.3 | async-start | bytes 8388608
  138.6 29.3 %slice-start.1 = ((s8[16777216]{0:T(1024)(128)(4,1)}), s8[4194304]{0:T(1024)(128)(4,1)S(1)}, s32[]{:S(2)}) async-start(s8[16777216]{0:T(1024)(128)(4,1)} %bitcast.174), calls=%async_computation.4 | async-start | bytes 8388608
  138.6 29.3 %slice-start.2 = ((s8[16777216]{0:T(1024)(128)(4,1)}), s8[4194304]{0:T(1024)(128)(4,1)S(1)}, s32[]{:S(2)}) async-start(s8[16777216]{0:T(1024)(128)(4,1)} %bitcast.174), calls=%async_computation.5 | async-start | bytes 8388608
  138.6 29.3 %slice-start.3 = ((s8[16777216]{0:T(1024)(128)(4,1)}), s8[4194304]{0:T(1024)(128)(4,1)S(1)}, s32[]{:S(2)}) async-start(s8[16777216]{0:T(1024)(128)(4,1)} %bitcast.174), calls=%async_computation.6 | async-start | bytes 8388608
  176.7 127.7 %reduce-scatter.4.cloned.1.call-start = ((), (), s32[]{:S(2)}) async-start(), calls=%async_computation.2 | async-start | bytes 1310720
Sparse Core Ops, SparseCore 0:
  176.8 51.1 all-reduce.1
  277.7 26.6 reduce-scatter.3
where the time goes:
time: 314 us; the launch traced here: 313 us
  matrix products  87.8 us (28%)
  other arithmetic  75.1 us (24%)
  waiting for transfers between devices  69.4 us (22%)
  blocking collectives  40.4 us (13%)
  between operations  15.8 us (5%)
  starting transfers between devices  14.3 us (5%)
  local copies, waits for them, and re-layouts  10.1 us (3%)
    dynamic_update_slice x2, other arithmetic, phase_tables(): return lax.map(one_block, number_blocks)  69.5 us
    psum x1, waiting for transfers between devices, per_device(): factors = lax.psum(factors, 'wide')  51.2 us
    dot_general x2, matrix products, per_device(): jnp.dot(weight_matrix, extended, precision=highest, preferred_element_typ...  31.2 us
    dot_general x2, matrix products, add_block(): lax.dot_general(charges, weight_block * factor_block[0], dims, precision=...  26.2 us
    all_gather x1, blocking collectives, per_device(): lax.all_gather(fractions, 'narrow', axis=1, tiled=True)  14.6 us
    dot_general x2, matrix products, add_block(): lax.dot_general(charges, weight_block * factor_block[1], dims, precision=...  13.6 us
    all_gather x1, blocking collectives, per_device(): lax.all_gather(charges, 'narrow', axis=1, tiled=True)  13.3 us
    psum x1, blocking collectives, per_device(): energy = lax.psum(block_energy(factors, weights, energy_scale), 'narrow')  12.5 us
  transfers between devices with their start and end apart: 10, of which 5 were waited for; matrix products, arithmetic and copies ran while one was open for 23% of the time, Pallas kernels for 0%

commit v1 on v0

v1 whole, which is shorter than its diff:
```python
import functools
import math

import jax
import jax.numpy as jnp
from jax import lax
from jax.experimental import pallas as pl
from jax.experimental.pallas import tpu as pltpu
from jax.sharding import PartitionSpec as P

smearing = 0.5
two_pi = 2.0 * math.pi
kmax = 8
grid_rows = (2 * kmax + 1) * kmax
f32 = jnp.float32
bf16 = jnp.bfloat16
highest = lax.Precision.HIGHEST
params = pltpu.CompilerParams(vmem_limit_bytes=48 * 1024 * 1024)


def dot_nn(a, b):
    return lax.dot_general(a, b, (((1,), (0,)), ((), ())), preferred_element_type=f32)


def dot_tn(a, b):
    return lax.dot_general(a, b, (((0,), (0,)), ((), ())), preferred_element_type=f32)


def dot_nt(a, b, precision=None):
    return lax.dot_general(
        a, b, (((1,), (1,)), ((), ())), precision=precision, preferred_element_type=f32
    )


def pick_columns(hidden, index_ref, block):
    atoms = hidden.shape[1]
    ghosts = index_ref.shape[1]
    row_ids = lax.broadcasted_iota(jnp.int32, (atoms, ghosts), 0)
    one_hot = jnp.where(row_ids == index_ref[block : block + 1, :], 1.0, 0.0).astype(bf16)
    return dot_nn(hidden, one_hot)


def first_kernel(features_ref, index_ref, hidden_ref, *picked_refs):
    hidden = jnp.transpose(features_ref[...].astype(f32)).astype(bf16)
    hidden_ref[...] = hidden
    for block in (2, 3, 0, 1):
        picked_refs[block][...] = pick_columns(hidden, index_ref, block)


def edge_kernel(senders_ref, radial_ref, edges_ref):
    slots, atoms = senders_ref.shape
    rows = 128
    lanes = 128
    row_ids = lax.broadcasted_iota(jnp.int32, (rows, lanes), 0).astype(f32).astype(bf16)

    def one_tile(tile, carry):
        first = pl.multiple_of(tile * rows, rows)
        for part in range(atoms // lanes):
            window = pl.ds(part * lanes, lanes)
            local = jnp.clip(senders_ref[:, window] - first, -1, rows)
            local = local.astype(f32).astype(bf16)
            weight = radial_ref[:, window].astype(bf16)
            total = jnp.zeros((rows, lanes), bf16)
            for slot in range(slots):
                total = total + jnp.where(
                    row_ids == local[slot : slot + 1, :],
                    weight[slot : slot + 1, :],
                    jnp.zeros((), bf16),
                )
            edges_ref[pl.ds(first, rows), window] = total
        return carry

    lax.fori_loop(0, edges_ref.shape[0] // rows, one_tile, 0)


def interact(hidden, ghost_refs, edges_ref, self_ref, message_ref):
    atoms = hidden.shape[1]
    ghosts = ghost_refs[0].shape[1]
    gathered = dot_nn(hidden, edges_ref[0:atoms, :])
    for block, ghost_ref in enumerate(ghost_refs):
        start = atoms + block * ghosts
        gathered = gathered + dot_nn(
            ghost_ref[...].astype(bf16), edges_ref[start : start + ghosts, :]
        )
    high = gathered.astype(bf16)
    low = (gathered - high.astype(f32)).astype(bf16)
    message = message_ref[...]
    total = dot_tn(self_ref[...], hidden) + dot_tn(message, high) + dot_tn(message, low)
    return (hidden.astype(f32) + total * (1.0 / (1.0 + jnp.exp(-total)))).astype(bf16)


def layer_kernel(
    hidden_ref, g0, g1, g2, g3, edges_ref, self_ref, message_ref, index_ref, out_ref, *picked_refs
):
    hidden = interact(hidden_ref[...], (g0, g1, g2, g3), edges_ref, self_ref, message_ref)
    out_ref[...] = hidden
    for block in (2, 3, 0, 1):
        picked_refs[block][...] = pick_columns(hidden, index_ref, block)


def last_kernel(
    hidden_ref,
    g0,
    g1,
    g2,
    g3,
    edges_ref,
    self_ref,
    message_ref,
    readout_ref,
    count_ref,
    real_ref,
    imag_ref,
    third_ref,
    sums_ref,
    charges_ref,
    lattice_ref,
):
    hidden = interact(hidden_ref[...], (g0, g1, g2, g3), edges_ref, self_ref, message_ref)
    atoms = hidden.shape[1]
    slot_ids = lax.broadcasted_iota(jnp.int32, (8, atoms), 1)
    charges = jnp.where(slot_ids < count_ref[0], dot_tn(readout_ref[...], hidden), 0.0)
    charges_ref[...] = charges
    cosine = third_ref[0:8, :]
    sine = third_ref[8:16, :]
    for c in range(4):
        lattice_ref[8 * c : 8 * c + 8, :] = charges[c : c + 1, :] * cosine
        lattice_ref[32 + 8 * c : 40 + 8 * c, :] = charges[c : c + 1, :] * sine
    with_cos = lattice_ref[0:32, :].astype(bf16)
    with_sin = lattice_ref[32:64, :].astype(bf16)
    none = jnp.zeros((64, atoms), bf16)
    real = real_ref[...]
    imag = imag_ref[...]
    sums_ref[0:grid_rows, :] = dot_nt(real, jnp.concatenate([with_cos, with_sin, none])) + dot_nt(
        imag, jnp.concatenate([none, with_sin, with_cos])
    )
    flat = charges.astype(bf16)
    flat_real = dot_nt(flat, real)
    flat_imag = dot_nt(flat, imag)
    sums_ref[grid_rows : grid_rows + 4, :] = flat_real[0:4, 0:128]
    sums_ref[grid_rows + 4 : grid_rows + 8, :] = flat_imag[0:4, 0:128]
    sums_ref[grid_rows + 8 : grid_rows + 16, :] = jnp.zeros((8, 128), f32)
    sums_ref[grid_rows + 8 : grid_rows + 12, 0:8] = flat_real[0:4, 128:grid_rows]
    sums_ref[grid_rows + 12 : grid_rows + 16, 0:8] = flat_imag[0:4, 128:grid_rows]


def wave_weight(m0, m1, m2, cell_ref):
    w0 = two_pi * m0 / cell_ref[0]
    w1 = two_pi * m1 / cell_ref[1]
    w2 = two_pi * m2 / cell_ref[2]
    squared = w0 * w0 + w1 * w1 + w2 * w2
    return jnp.exp(-0.5 * smearing * smearing * squared) / squared


def table_kernel(
    fractions_ref, cell_ref, numbers_ref, real_ref, imag_ref, third_ref, factor_ref, flat_ref, acc, acc0
):
    atoms = fractions_ref.shape[1]
    orders = lax.broadcasted_iota(jnp.int32, (8, atoms), 0).astype(f32) + 1.0
    cosines, sines = [], []
    for axis in range(3):
        turns = orders * fractions_ref[axis : axis + 1, :]
        angle = two_pi * (turns - jnp.round(turns))
        cosines.append(jnp.cos(angle))
        sines.append(jnp.sin(angle))
    third_ref[0:8, :] = cosines[2]
    third_ref[8:16, :] = sines[2]
    for axis in range(3):
        third_ref[16 + axis : 17 + axis, :] = cosines[axis][0:1, :]
    c0, s0 = cosines[0], sines[0]
    for m in range(-kmax, kmax + 1):
        window = pl.ds((m + kmax) * kmax, kmax)
        if m == 0:
            re, im = c0, s0
        else:
            row = abs(m) - 1
            c1 = cosines[1][row : row + 1, :]
            s1 = sines[1][row : row + 1, :]
            if m < 0:
                s1 = -s1
            re, im = c0 * c1 - s0 * s1, s0 * c1 + c0 * s1
        real_ref[window, :] = re.astype(bf16)
        imag_ref[window, :] = im.astype(bf16)

    acc[...] = jnp.zeros_like(acc)
    acc0[...] = jnp.zeros_like(acc0)
    width = math.gcd(numbers_ref.shape[1], 1024)
    plane_ids = lax.broadcasted_iota(jnp.int32, (grid_rows, width), 0)
    third_ids = lax.broadcasted_iota(jnp.int32, (32, width), 0)
    third_ids = jnp.where(third_ids < 8, third_ids + 1, jnp.where(third_ids < 16, 7 - third_ids, 0))
    zero_row = lax.broadcasted_iota(jnp.int32, (32, width), 0) <= 16

    def count(step, carry):
        window = pl.ds(pl.multiple_of(step * width, width), width)
        numbers = numbers_ref[:, window]
        plane = (numbers[1:2, :] + kmax) * kmax + numbers[0:1, :] - 1
        in_plane = jnp.where(plane_ids == plane, 1.0, 0.0).astype(bf16)
        in_third = jnp.where((third_ids == numbers[2:3, :]) & zero_row, 1.0, 0.0).astype(bf16)
        acc[...] += dot_nt(in_plane, in_third)
        acc0[...] += dot_nt(in_third[16:32, :], in_plane)
        return carry

    lax.fori_loop(0, numbers_ref.shape[1] // width, count, 0)

    lane = lax.broadcasted_iota(jnp.int32, (grid_rows, 128), 1)
    row = lax.broadcasted_iota(jnp.int32, (grid_rows, 128), 0)
    m0 = (row % 8 + 1).astype(f32)
    m1 = (row // 8 - kmax).astype(f32)
    m2 = (lane % 8 + 1).astype(f32)
    weight = wave_weight(m0, m1, m2, cell_ref)
    from_ids = lax.broadcasted_iota(jnp.int32, (32, 128), 0)
    lane_ids = lax.broadcasted_iota(jnp.int32, (32, 128), 1) % 8
    expand_up = jnp.where(from_ids == lane_ids, 1.0, 0.0)
    expand_down = jnp.where(from_ids == lane_ids + 8, 1.0, 0.0)
    counts = acc[...]
    up = weight * jnp.dot(counts, expand_up, precision=highest, preferred_element_type=f32)
    down = weight * jnp.dot(counts, expand_down, precision=highest, preferred_element_type=f32)
    block = lane // 32
    first, second, third = block == 0, block == 1, block == 2
    factor_ref[0] = jnp.where(first, up, jnp.where(second, down, jnp.where(third, -up, -down)))
    factor_ref[1] = jnp.where(first, down, jnp.where(second, -up, jnp.where(third, -down, up)))
    factor_ref[2] = m2 * jnp.where(first, up, jnp.where(second, -down, jnp.where(third, -up, down)))
    factor_ref[3] = m2 * jnp.where(first, -down, jnp.where(second, -up, jnp.where(third, down, up)))
    lane0 = lax.broadcasted_iota(jnp.int32, (8, grid_rows), 1)
    n0 = (lane0 % 8 + 1).astype(f32)
    n1 = (lane0 // 8 - kmax).astype(f32)
    flat_ref[...] = wave_weight(n0, n1, 0.0 * n0, cell_ref) * acc0[0:1, :]


def force_kernel(
    scale,
    sums_ref,
    charges_ref,
    lattice_ref,
    real_ref,
    imag_ref,
    third_ref,
    factor_ref,
    flat_ref,
    cell_ref,
    count_ref,
    forces_ref,
    born_ref,
    energy_ref,
    flat_sums,
):
    atoms = real_ref.shape[1]
    sums = sums_ref[0:grid_rows, :]
    swapped = pltpu.roll(sums, 64, 1)
    plus = pltpu.roll(sums + swapped, 32, 1)
    minus = pltpu.roll(sums - swapped, 32, 1)
    f0 = factor_ref[0]
    f1 = factor_ref[1]
    even = f0 * plus + f1 * minus
    odd = factor_ref[2] * plus + factor_ref[3] * minus
    row = lax.broadcasted_iota(jnp.int32, (grid_rows, 128), 0)
    m0 = (row % 8 + 1).astype(f32)
    m1 = (row // 8 - kmax).astype(f32)
    flat_sums[:, 0:128] = sums_ref[grid_rows : grid_rows + 8, :]
    flat_sums[:, 128:grid_rows] = sums_ref[grid_rows + 8 : grid_rows + 16, 0:8]
    flat_re = flat_sums[0:4, :]
    flat_im = flat_sums[4:8, :]
    flat_weight = flat_ref[0:4, :]
    part = jnp.sum(jnp.abs(f0) * plus * plus + jnp.abs(f1) * minus * minus, axis=0, keepdims=True)
    flat_part = jnp.sum(
        flat_weight * (flat_re * flat_re + flat_im * flat_im), axis=0, keepdims=True
    )
    energy_ref[...] = (0.5 * scale) * (
        0.5 * jnp.sum(part, axis=1, keepdims=True) + jnp.sum(flat_part, axis=1, keepdims=True)
    )

    lane0 = lax.broadcasted_iota(jnp.int32, (4, grid_rows), 1)
    n0 = (lane0 % 8 + 1).astype(f32)
    n1 = (lane0 // 8 - kmax).astype(f32)
    up = flat_weight * flat_im
    down = -flat_weight * flat_re
    flat_up = jnp.concatenate([up * n0, up * n1], axis=0).astype(bf16)
    flat_down = jnp.concatenate([down * n0, down * n1], axis=0).astype(bf16)
    real = real_ref[...]
    imag = imag_ref[...]
    tables = [jnp.transpose(t) for t in (even * m0, even * m1, odd)]
    with_real = jnp.concatenate([t[0:64] for t in tables], axis=0).astype(bf16)
    with_imag = jnp.concatenate([t[64:128] for t in tables], axis=0).astype(bf16)
    from_real = dot_nn(with_real, real)
    from_imag = dot_nn(with_imag, imag)
    flat = dot_nn(flat_up, real) + dot_nn(flat_down, imag)
    with_cos = lattice_ref[0:32, :]
    with_sin = lattice_ref[32:64, :]
    charges = charges_ref[...]
    alive = lax.broadcasted_iota(jnp.int32, (1, atoms), 1) < count_ref[0]
    total = jnp.sum(charges[0:4], axis=0, keepdims=True)
    for axis in range(3):
        base = 64 * axis
        terms = with_cos * (from_real[base : base + 32] + from_imag[base + 32 : base + 64])
        terms = terms + with_sin * (from_real[base + 32 : base + 64] + from_imag[base : base + 32])
        gradient = jnp.sum(terms, axis=0, keepdims=True)
        if axis < 2:
            gradient = gradient + jnp.sum(
                charges[0:4] * flat[4 * axis : 4 * axis + 4], axis=0, keepdims=True
            )
        forces_ref[axis : axis + 1, :] = jnp.where(
            alive, -(two_pi * scale / cell_ref[axis]) * gradient, 0.0
        )
        born_ref[axis : axis + 1, :] = jnp.where(
            alive, total * third_ref[16 + axis : 17 + axis, :], 0.0
        )


def call(kernel, outs, *args, smem=(), scratch=(), cost=None):
    specs = [
        pl.BlockSpec(memory_space=pltpu.SMEM if i in smem else pltpu.VMEM)
        for i in range(len(args))
    ]
    return pl.pallas_call(
        kernel,
        out_shape=[jax.ShapeDtypeStruct(shape, dtype) for shape, dtype in outs],
        in_specs=specs,
        out_specs=[pl.BlockSpec(memory_space=pltpu.VMEM)] * len(outs),
        scratch_shapes=list(scratch),
        compiler_params=params,
        cost_estimate=cost,
    )(*args)


def shifted(block, axis, step):
    count = lax.axis_size(axis)
    return lax.ppermute(block, axis, [(i, (i + step) % count) for i in range(count)])


def exchange(picked):
    lower_narrow = shifted(picked[3], "narrow", 1)
    upper_narrow = shifted(picked[2], "narrow", -1)
    lower_wide = shifted(picked[1], "wide", 1)
    upper_wide = shifted(picked[0], "wide", -1)
    return lower_wide, upper_wide, lower_narrow, upper_narrow


def summed(block):
    for axis in ("wide", "narrow"):
        count = lax.axis_size(axis)
        step = 1
        while step < count:
            block = block + lax.ppermute(block, axis, [(i, i ^ step) for i in range(count)])
            step *= 2
    return block


def per_device(
    fractions,
    cell_lengths,
    features,
    atom_counts,
    send_index,
    senders,
    radial,
    self_weight,
    message_weight,
    charge_weight,
    wave_numbers,
):
    atoms, width = features.shape
    ghosts = send_index.shape[1]
    rows = atoms + 4 * ghosts
    total_atoms = atoms * lax.axis_size("wide") * lax.axis_size("narrow")
    scale = 4.0 / math.sqrt(total_atoms * wave_numbers.shape[1])
    picked_outs = [((width, ghosts), f32)] * 4
    hidden_out = [((width, atoms), bf16)]
    readout = jnp.pad(charge_weight, ((0, 0), (0, 8 - charge_weight.shape[1])))

    hidden, *picked = call(first_kernel, hidden_out + picked_outs, features, send_index)
    received = exchange(picked)
    (edges,) = call(
        edge_kernel,
        [((rows, atoms), bf16)],
        senders,
        radial,
        cost=pl.CostEstimate(flops=10**9, bytes_accessed=20 * 2**20, transcendentals=0),
    )
    layers = self_weight.shape[0]
    for layer in range(layers - 1):
        hidden, *picked = call(
            layer_kernel,
            hidden_out + picked_outs,
            hidden,
            *received,
            edges,
            self_weight[layer],
            message_weight[layer],
            send_index,
        )
        received = exchange(picked)
    real, imag, third, factor, flat = call(
        table_kernel,
        [
            ((grid_rows, atoms), bf16),
            ((grid_rows, atoms), bf16),
            ((24, atoms), f32),
            ((4, grid_rows, 128), f32),
            ((8, grid_rows), f32),
        ],
        fractions,
        cell_lengths,
        wave_numbers,
        smem=(1,),
        scratch=[pltpu.VMEM((grid_rows, 32), f32), pltpu.VMEM((16, grid_rows), f32)],
        cost=pl.CostEstimate(flops=10**9, bytes_accessed=20 * 2**20, transcendentals=0),
    )
    sums, charges, lattice = call(
        last_kernel,
        [((grid_rows + 16, 128), f32), ((8, atoms), f32), ((64, atoms), f32)],
        hidden,
        *received,
        edges,
        self_weight[layers - 1],
        message_weight[layers - 1],
        readout,
        atom_counts,
        real,
        imag,
        third,
        smem=(9,),
    )
    sums = summed(sums)
    forces, born_charges, energy = call(
        functools.partial(force_kernel, scale),
        [((3, atoms), f32), ((3, atoms), f32), ((1, 1), f32)],
        sums,
        charges,
        lattice,
        real,
        imag,
        third,
        factor,
        flat,
        cell_lengths,
        atom_counts,
        smem=(8, 9),
        scratch=[pltpu.VMEM((8, grid_rows), f32)],
    )
    return (forces, born_charges, energy[0, 0])


def solution(mesh):
    return jax.shard_map(
        per_device,
        mesh=mesh,
        in_specs=(
            P(None, ("wide", "narrow")),
            P(),
            P(("wide", "narrow"), None),
            P(("wide", "narrow")),
            P(("wide", "narrow"), None),
            P(None, ("wide", "narrow")),
            P(None, ("wide", "narrow")),
            P(),
            P(),
            P(),
            P(),
        ),
        out_specs=(P(None, ("wide", "narrow")), P(None, ("wide", "narrow")), P()),
        check_vma=False,
    )
```

time: 314 us -> 57.7 us (0.18)
  matrix products: 87.8 us -> 0 us
  other arithmetic: 75.1 us -> 0.06 us
  waiting for transfers between devices: 69.4 us -> 19.9 us
  blocking collectives: 40.4 us -> 0 us
  between operations: 15.8 us -> 1.46 us
  Pallas kernels: 0 us -> 12.7 us
  local copies, waits for them, and re-layouts: 10.1 us -> 4.19 us
  starting transfers between devices: 14.3 us -> 19.1 us
    dot_general x15 -> x0, matrix products: 87.8 us -> none  [the longest x2 31.2 us: per_device(): jnp.dot(weight_matrix, extended, precision=highest, preferred_element_typ...]
    dynamic_update_slice x2 -> x0, other arithmetic: 69.5 us -> none  [phase_tables(): return lax.map(one_block, number_blocks)]
    psum x1 -> x0, waiting for transfers between devices: 51.2 us -> none  [per_device(): factors = lax.psum(factors, 'wide')]
    all_gather x2 -> x0, blocking collectives: 27.9 us -> none  [the longest x1 14.6 us: per_device(): lax.all_gather(fractions, 'narrow', axis=1, tiled=True)]
    ppermute x8 -> x13, waiting for transfers between devices: 5.92 us -> 19.9 us  [the longest x5 16 us: summed(): lax.ppermute(block, axis, [(i, i ^ step) for i in range(count)])]
    pallas_call x0 -> x6, Pallas kernels: none -> 12.7 us  [call(): pl.pallas_call(kernel, out_shape=[jax.ShapeDtypeStruct(shape, dtype) for...]
    psum x1 -> x0, blocking collectives: 12.5 us -> none  [per_device(): energy = lax.psum(block_energy(factors, weights, energy_scale), 'narrow')]
    unnamed x3 -> x0, waiting for transfers between devices: 12.3 us -> none
  transfers between devices with their start and end apart: 10 -> 13, of which waited for: 5 -> 9; matrix products, arithmetic and copies ran while one was open for 23% -> 0% of each run, Pallas kernels for 0% -> 13%
where the time goes in v1:
time: 57.7 us; the launch traced here: 57.4 us
  waiting for transfers between devices  19.9 us (34%)
  starting transfers between devices  19.1 us (33%)
  Pallas kernels  12.7 us (22%)
  local copies, waits for them, and re-layouts  4.19 us (7%)
  between operations  1.46 us (3%)
    ppermute x5, waiting for transfers between devices, summed(): lax.ppermute(block, axis, [(i, i ^ step) for i in range(count)])  16 us
    ppermute x8, starting transfers between devices, shifted(): lax.ppermute(block, axis, [(i, (i + step) % count) for i in range(count)])  14.2 us
    pallas_call x6, Pallas kernels, call(): pl.pallas_call(kernel, out_shape=[jax.ShapeDtypeStruct(shape, dtype) for...  12.7 us
    ppermute x5, starting transfers between devices, summed(): lax.ppermute(block, axis, [(i, i ^ step) for i in range(count)])  4.88 us
    unnamed x21, local copies, waits for them, and re-layouts  4.16 us
    ppermute x8, waiting for transfers between devices, shifted(): lax.ppermute(block, axis, [(i, (i + step) % count) for i in range(count)])  3.82 us
  transfers between devices with their start and end apart: 13, of which 9 were waited for; matrix products, arithmetic and copies ran while one was open for 0% of the time, Pallas kernels for 13%

profile of v1, /device:TPU:0, one launch (start us, length us, event | category | flops | bytes accessed | tf_op | source)
XLA Modules:
  0.0 57.4 jit_solution(812955083317995136)
XLA Ops:
  0.6 0.9 %copy-done = bf16[512,128]{1,0:T(8,128)(2,1)S(1)} copy-done((bf16[512,128]{1,0:T(8,128)(2,1)S(1)}, bf16[512,128]{1,0:T(8,128)(2,1)}, u32[]{:S(2)}) %copy-start) | copy-done | bytes 131096
  1.5 0.7 %copy-done.1 = s32[4,384]{1,0:T(4,128)S(1)} copy-done((s32[4,384]{1,0:T(4,128)S(1)}, s32[4,384]{1,0:T(4,128)}, u32[]{:S(2)}) %copy-start.1) | copy-done | bytes 6168
  2.2 0.5 shard_map.130
  2.7 0.5 collective-permute-start
  3.2 2.9 %collective-permute-start.1 = (f32[128,384]{1,0:T(8,128)S(1)}, f32[128,384]{1,0:T(8,128)S(1)}, u32[]{:S(2)}, u32[]{:S(2)}) collective-permute-start(f32[128,384]{1,0:T(8,128)S(1)} %get-tuple-element.26), channel_id=1, source_target_pairs={{0,28},{4,0},{8,4},{12,8},{16,12},{20,16},{24,20},{28,24},{1,29},{... | collective-permute-start | bytes 589832 | tf_op jit(solution)/shard_map/ppermute | solution.py:327
  6.2 2.3 %collective-permute-start.2 = (f32[128,384]{1,0:T(8,128)S(1)}, f32[128,384]{1,0:T(8,128)S(1)}, u32[]{:S(2)}, u32[]{:S(2)}) collective-permute-start(f32[128,384]{1,0:T(8,128)S(1)} %get-tuple-element.27), channel_id=1, source_target_pairs={{0,1},{1,2},{2,3},{3,0},{4,5},{5,6},{6,7},{7,4},{8,9},{9,10},{10,1... | collective-permute-start | bytes 589832 | tf_op jit(solution)/shard_map/ppermute | solution.py:327
  8.5 2.0 %collective-permute-start.3 = (f32[128,384]{1,0:T(8,128)S(1)}, f32[128,384]{1,0:T(8,128)S(1)}, u32[]{:S(2)}, u32[]{:S(2)}) collective-permute-start(f32[128,384]{1,0:T(8,128)S(1)} %get-tuple-element.28), channel_id=1, source_target_pairs={{0,3},{1,0},{2,1},{3,2},{4,7},{5,4},{6,5},{7,6},{8,11},{9,8},{10,9... | collective-permute-start | bytes 589832 | tf_op jit(solution)/shard_map/ppermute | solution.py:327
  10.5 0.8 %copy-done.4 = s32[16,512]{1,0:T(8,128)S(1)} copy-done((s32[16,512]{1,0:T(8,128)S(1)}, s32[16,512]{1,0:T(8,128)}, u32[]{:S(2)}) %copy-start.4) | copy-done | bytes 32792
  11.3 0.8 %copy-done.5 = f32[16,512]{1,0:T(8,128)S(1)} copy-done((f32[16,512]{1,0:T(8,128)S(1)}, f32[16,512]{1,0:T(8,128)}, u32[]{:S(2)}) %copy-start.5) | copy-done | bytes 32792
  12.0 4.0 %shard_map.131.edges_ref = bf16[2048,512]{1,0:T(8,128)(2,1)S(1)} custom-call(s32[16,512]{1,0:T(8,128)S(1)} %copy-done.4, f32[16,512]{1,0:T(8,128)S(1)} %copy-done.5), custom_call_target="tpu_custom_call" | custom-call | flops 1000000000 | bytes 20971520 | tf_op jit(solution)/shard_map/pallas_call | solution.py:314
  16.1 0.3 collective-permute-done.2.g2
  16.4 1.8 %collective-permute-done.3.g3 = f32[128,384]{1,0:T(8,128)S(1)} collective-permute-done((f32[128,384]{1,0:T(8,128)S(1)}, f32[128,384]{1,0:T(8,128)S(1)}, u32[]{:S(2)}, u32[]{:S(2)}) %collective-permute-start.3) | collective-permute-done | bytes 196640 | tf_op jit(solution)/shard_map/ppermute | solution.py:327
  18.2 1.9 %shard_map.132 = (bf16[128,512]{1,0:T(8,128)(2,1)S(1)}, f32[128,384]{1,0:T(8,128)}, f32[128,384]{1,0:T(8,128)}, f32[128,384]{1,0:T(8,128)S(1)}, f32[128,384]{1,0:T(8,128)S(1)}) custom-call(bf16[128,512]{1,0:T(8,128)(2,1)S(1)} %get-tuple-element.24.hidden_ref, f32[128,384]{1,0:T(8,128)S(1)} %collective-permute-done.g0, ...), custom_call_target="tpu_custom_call" | custom-call | tf_op jit(solution)/shard_map/pallas_call | solution.py:314
  20.1 2.6 %collective-permute-start.5 = (f32[128,384]{1,0:T(8,128)}, f32[128,384]{1,0:T(8,128)S(1)}, u32[]{:S(2)}, u32[]{:S(2)}) collective-permute-start(f32[128,384]{1,0:T(8,128)} %get-tuple-element.31), channel_id=1, source_target_pairs={{0,28},{4,0},{8,4},{12,8},{16,12},{20,16},{24,20},{28,24},{1,29},{... | collective-permute-start | bytes 589832 | tf_op jit(solution)/shard_map/ppermute | solution.py:327
  22.7 1.1 %collective-permute-start.6 = (f32[128,384]{1,0:T(8,128)S(1)}, f32[128,384]{1,0:T(8,128)S(1)}, u32[]{:S(2)}, u32[]{:S(2)}) collective-permute-start(f32[128,384]{1,0:T(8,128)S(1)} %get-tuple-element.32), channel_id=1, source_target_pairs={{0,1},{1,2},{2,3},{3,0},{4,5},{5,6},{6,7},{7,4},{8,9},{9,10},{10,1... | collective-permute-start | bytes 589832 | tf_op jit(solution)/shard_map/ppermute | solution.py:327
  23.8 2.7 %collective-permute-start.7 = (f32[128,384]{1,0:T(8,128)S(1)}, f32[128,384]{1,0:T(8,128)S(1)}, u32[]{:S(2)}, u32[]{:S(2)}) collective-permute-start(f32[128,384]{1,0:T(8,128)S(1)} %get-tuple-element.33), channel_id=1, source_target_pairs={{0,3},{1,0},{2,1},{3,2},{4,7},{5,4},{6,5},{7,6},{8,11},{9,8},{10,9... | collective-permute-start | bytes 589832 | tf_op jit(solution)/shard_map/ppermute | solution.py:327
  27.2 0.1 copy.14
  27.4 0.9 %copy-done.3 = s32[3,8192]{1,0:T(4,128)S(1)} copy-done((s32[3,8192]{1,0:T(4,128)S(1)}, s32[3,8192]{1,0:T(4,128)}, u32[]{:S(2)}) %copy-start.3) | copy-done | bytes 98328
  28.3 3.5 %shard_map.133 = (bf16[136,512]{1,0:T(8,128)(2,1)S(1)}, bf16[136,512]{1,0:T(8,128)(2,1)S(1)}, f32[24,512]{1,0:T(8,128)S(1)}, f32[4,136,128]{2,1,0:T(8,128)S(1)}, f32[8,136]{1,0:T(8,128)S(1)}) custom-call(f32[3,512]{1,0:T(4,128)S(1)} %copy-done.6, f32[3]{0:T(128)S(1)} %copy-done.2, s32[3,8192]{1,0:T(4,128)S(1)} %copy-done.3), custom_call_target="tpu_custom_call" | custom-call | flops 1000000000 | bytes 20971520 | tf_op jit(solution)/shard_map/pallas_call | solution.py:314
  31.8 0.5 collective-permute-done.6.g2
  32.3 1.2 %collective-permute-done.7.g3 = f32[128,384]{1,0:T(8,128)S(1)} collective-permute-done((f32[128,384]{1,0:T(8,128)S(1)}, f32[128,384]{1,0:T(8,128)S(1)}, u32[]{:S(2)}, u32[]{:S(2)}) %collective-permute-start.7) | collective-permute-done | bytes 196640 | tf_op jit(solution)/shard_map/ppermute | solution.py:327
  33.5 1.1 %shard_map.134 = (f32[152,128]{1,0:T(8,128)S(1)}, f32[8,512]{1,0:T(8,128)S(1)}, f32[64,512]{1,0:T(8,128)S(1)}) custom-call(bf16[128,512]{1,0:T(8,128)(2,1)S(1)} %get-tuple-element.29.hidden_ref, f32[128,384]{1,0:T(8,128)S(1)} %collective-permute-done.4.g0, f32[128,384]{1,0:T(8,128)S(1)} %collective-permute-done.5.g1, ...), custom_call_target="tpu_custom_call" | custom-call | tf_op jit(solution)/shard_map/pallas_call | solution.py:314
  34.8 1.3 %collective-permute-done.8 = f32[152,128]{1,0:T(8,128)S(1)} collective-permute-done((f32[152,128]{1,0:T(8,128)S(1)}, f32[152,128]{1,0:T(8,128)S(1)}, u32[]{:S(2)}, u32[]{:S(2)}) %collective-permute-start.8) | collective-permute-done | bytes 77856 | tf_op jit(solution)/shard_map/ppermute | solution.py:343
  36.0 1.5 %collective-permute-start.9 = (f32[152,128]{1,0:T(8,128)S(1)}, f32[152,128]{1,0:T(8,128)S(1)}, u32[]{:S(2)}, u32[]{:S(2)}) collective-permute-start(f32[152,128]{1,0:T(8,128)S(1)} %add.17), channel_id=1, source_target_pairs={{0,8},{4,12},{8,0},{12,4},{16,24},{20,28},{24,16},{28,20},{1,9},{5... | collective-permute-start | bytes 233480 | tf_op jit(solution)/shard_map/ppermute | solution.py:343
  37.6 2.9 %collective-permute-done.9 = f32[152,128]{1,0:T(8,128)S(1)} collective-permute-done((f32[152,128]{1,0:T(8,128)S(1)}, f32[152,128]{1,0:T(8,128)S(1)}, u32[]{:S(2)}, u32[]{:S(2)}) %collective-permute-start.9) | collective-permute-done | bytes 77856 | tf_op jit(solution)/shard_map/ppermute | solution.py:343
  40.5 0.6 collective-permute-start.10
  41.1 3.9 %collective-permute-done.10 = f32[152,128]{1,0:T(8,128)S(1)} collective-permute-done((f32[152,128]{1,0:T(8,128)S(1)}, f32[152,128]{1,0:T(8,128)S(1)}, u32[]{:S(2)}, u32[]{:S(2)}) %collective-permute-start.10) | collective-permute-done | bytes 77856 | tf_op jit(solution)/shard_map/ppermute | solution.py:343
  45.0 0.8 %collective-permute-start.11 = (f32[152,128]{1,0:T(8,128)S(1)}, f32[152,128]{1,0:T(8,128)S(1)}, u32[]{:S(2)}, u32[]{:S(2)}) collective-permute-start(f32[152,128]{1,0:T(8,128)S(1)} %add.19), channel_id=1, source_target_pairs={{0,1},{1,0},{2,3},{3,2},{4,5},{5,4},{6,7},{7,6},{8,9},{9,8},{10,11... | collective-permute-start | bytes 233480 | tf_op jit(solution)/shard_map/ppermute | solution.py:343
  45.8 3.7 %collective-permute-done.11 = f32[152,128]{1,0:T(8,128)S(1)} collective-permute-done((f32[152,128]{1,0:T(8,128)S(1)}, f32[152,128]{1,0:T(8,128)S(1)}, u32[]{:S(2)}, u32[]{:S(2)}) %collective-permute-start.11) | collective-permute-done | bytes 77856 | tf_op jit(solution)/shard_map/ppermute | solution.py:343
  49.5 1.9 %collective-permute-start.12 = (f32[152,128]{1,0:T(8,128)S(1)}, f32[152,128]{1,0:T(8,128)S(1)}, u32[]{:S(2)}, u32[]{:S(2)}) collective-permute-start(f32[152,128]{1,0:T(8,128)S(1)} %add.20), channel_id=1, source_target_pairs={{0,2},{1,3},{2,0},{3,1},{4,6},{5,7},{6,4},{7,5},{8,10},{9,11},{10,... | collective-permute-start | bytes 233480 | tf_op jit(solution)/shard_map/ppermute | solution.py:343
  51.4 4.3 %collective-permute-done.12 = f32[152,128]{1,0:T(8,128)S(1)} collective-permute-done((f32[152,128]{1,0:T(8,128)S(1)}, f32[152,128]{1,0:T(8,128)S(1)}, u32[]{:S(2)}, u32[]{:S(2)}) %collective-permute-start.12) | collective-permute-done | bytes 77856 | tf_op jit(solution)/shard_map/ppermute | solution.py:343
  55.7 1.7 %shard_map.135 = (f32[3,512]{1,0:T(4,128)}, f32[3,512]{1,0:T(4,128)}, f32[1,1]{1,0:T(1,128)}) custom-call(f32[152,128]{1,0:T(8,128)S(1)} %add.21.sums_ref, f32[8,512]{1,0:T(8,128)S(1)} %get-tuple-element.38.charges_ref, f32[64,512]{1,0:T(8,128)S(1)} %get-tuple-element.39.lattice_ref, bf16[136,512]{1,0:T(8,128)(2,1)S(1)} %get-tuple-element.34.real_ref, ...), custom_call_target="tpu_custom_call" | custom-call | tf_op jit(solution)/shard_map/pallas_call | solution.py:314
  (28 shorter events, 0.2 us)
Async XLA Ops:
  0.6 0.9 %copy-start = (bf16[512,128]{1,0:T(8,128)(2,1)S(1)}, bf16[512,128]{1,0:T(8,128)(2,1)}, u32[]{:S(2)}) copy-start(bf16[512,128]{1,0:T(8,128)(2,1)} %features_ref.1) | copy-start | bytes 393220
  1.5 0.7 %copy-start.1 = (s32[4,384]{1,0:T(4,128)S(1)}, s32[4,384]{1,0:T(4,128)}, u32[]{:S(2)}) copy-start(s32[4,384]{1,0:T(4,128)} %index_ref.3) | copy-start | bytes 18436
  2.2 13.8 %copy-start.7 = (bf16[2,128,128]{2,1,0:T(8,128)(2,1)S(1)}, bf16[2,128,128]{2,1,0:T(8,128)(2,1)}, u32[]{:S(2)}) copy-start(bf16[2,128,128]{2,1,0:T(8,128)(2,1)} %param.19) | copy-start | bytes 196612
  2.2 13.8 %copy-start.8 = (bf16[2,128,128]{2,1,0:T(8,128)(2,1)S(1)}, bf16[2,128,128]{2,1,0:T(8,128)(2,1)}, u32[]{:S(2)}) copy-start(bf16[2,128,128]{2,1,0:T(8,128)(2,1)} %param.18) | copy-start | bytes 196612
  2.7 13.3 %collective-permute-start = (f32[128,384]{1,0:T(8,128)S(1)}, f32[128,384]{1,0:T(8,128)S(1)}, u32[]{:S(2)}, u32[]{:S(2)}) collective-permute-start(f32[128,384]{1,0:T(8,128)S(1)} %get-tuple-element.25), channel_id=1, source_target_pairs={{0,4},{4,8},{8,12},{12,16},{16,20},{20,24},{24,28},{28,0},{1,5},{5... | collective-permute-start | bytes 589832 | tf_op jit(solution)/shard_map/ppermute | solution.py:327
  3.2 12.8 %collective-permute-start.1 = (f32[128,384]{1,0:T(8,128)S(1)}, f32[128,384]{1,0:T(8,128)S(1)}, u32[]{:S(2)}, u32[]{:S(2)}) collective-permute-start(f32[128,384]{1,0:T(8,128)S(1)} %get-tuple-element.26), channel_id=1, source_target_pairs={{0,28},{4,0},{8,4},{12,8},{16,12},{20,16},{24,20},{28,24},{1,29},{... | collective-permute-start | bytes 589832 | tf_op jit(solution)/shard_map/ppermute | solution.py:327
  6.2 10.2 %collective-permute-start.2 = (f32[128,384]{1,0:T(8,128)S(1)}, f32[128,384]{1,0:T(8,128)S(1)}, u32[]{:S(2)}, u32[]{:S(2)}) collective-permute-start(f32[128,384]{1,0:T(8,128)S(1)} %get-tuple-element.27), channel_id=1, source_target_pairs={{0,1},{1,2},{2,3},{3,0},{4,5},{5,6},{6,7},{7,4},{8,9},{9,10},{10,1... | collective-permute-start | bytes 589832 | tf_op jit(solution)/shard_map/ppermute | solution.py:327
  8.5 9.7 %collective-permute-start.3 = (f32[128,384]{1,0:T(8,128)S(1)}, f32[128,384]{1,0:T(8,128)S(1)}, u32[]{:S(2)}, u32[]{:S(2)}) collective-permute-start(f32[128,384]{1,0:T(8,128)S(1)} %get-tuple-element.28), channel_id=1, source_target_pairs={{0,3},{1,0},{2,1},{3,2},{4,7},{5,4},{6,5},{7,6},{8,11},{9,8},{10,9... | collective-permute-start | bytes 589832 | tf_op jit(solution)/shard_map/ppermute | solution.py:327
  10.5 0.8 %copy-start.4 = (s32[16,512]{1,0:T(8,128)S(1)}, s32[16,512]{1,0:T(8,128)}, u32[]{:S(2)}) copy-start(s32[16,512]{1,0:T(8,128)} %senders_ref.1) | copy-start | bytes 98308
  11.3 0.8 %copy-start.5 = (f32[16,512]{1,0:T(8,128)S(1)}, f32[16,512]{1,0:T(8,128)}, u32[]{:S(2)}) copy-start(f32[16,512]{1,0:T(8,128)} %radial_ref.1) | copy-start | bytes 98308
  16.0 11.2 %copy-start.9 = (bf16[128,4]{0,1:T(4,128)(2,1)S(1)}, bf16[128,4]{0,1:T(4,128)(2,1)}, u32[]{:S(2)}) copy-start(bf16[128,4]{0,1:T(4,128)(2,1)} %param.20) | copy-start | bytes 3076
  16.0 11.3 %copy-start.2 = (f32[3]{0:T(128)S(1)}, f32[3]{0:T(128)}, u32[]{:S(2)}) copy-start(f32[3]{0:T(128)} %cell_ref.3) | copy-start | bytes 40
  16.1 11.3 %copy-start.6 = (f32[3,512]{1,0:T(4,128)S(1)}, f32[3,512]{1,0:T(4,128)}, u32[]{:S(2)}) copy-start(f32[3,512]{1,0:T(4,128)} %fractions_ref.1) | copy-start | bytes 18436
  20.1 11.7 %collective-permute-start.4 = (f32[128,384]{1,0:T(8,128)}, f32[128,384]{1,0:T(8,128)S(1)}, u32[]{:S(2)}, u32[]{:S(2)}) collective-permute-start(f32[128,384]{1,0:T(8,128)} %get-tuple-element.30), channel_id=1, source_target_pairs={{0,4},{4,8},{8,12},{12,16},{16,20},{20,24},{24,28},{28,0},{1,5},{5... | collective-permute-start | bytes 589832 | tf_op jit(solution)/shard_map/ppermute | solution.py:327
  20.1 11.7 %collective-permute-start.5 = (f32[128,384]{1,0:T(8,128)}, f32[128,384]{1,0:T(8,128)S(1)}, u32[]{:S(2)}, u32[]{:S(2)}) collective-permute-start(f32[128,384]{1,0:T(8,128)} %get-tuple-element.31), channel_id=1, source_target_pairs={{0,28},{4,0},{8,4},{12,8},{16,12},{20,16},{24,20},{28,24},{1,29},{... | collective-permute-start | bytes 589832 | tf_op jit(solution)/shard_map/ppermute | solution.py:327
  22.7 9.6 %collective-permute-start.6 = (f32[128,384]{1,0:T(8,128)S(1)}, f32[128,384]{1,0:T(8,128)S(1)}, u32[]{:S(2)}, u32[]{:S(2)}) collective-permute-start(f32[128,384]{1,0:T(8,128)S(1)} %get-tuple-element.32), channel_id=1, source_target_pairs={{0,1},{1,2},{2,3},{3,0},{4,5},{5,6},{6,7},{7,4},{8,9},{9,10},{10,1... | collective-permute-start | bytes 589832 | tf_op jit(solution)/shard_map/ppermute | solution.py:327
  23.8 9.7 %collective-permute-start.7 = (f32[128,384]{1,0:T(8,128)S(1)}, f32[128,384]{1,0:T(8,128)S(1)}, u32[]{:S(2)}, u32[]{:S(2)}) collective-permute-start(f32[128,384]{1,0:T(8,128)S(1)} %get-tuple-element.33), channel_id=1, source_target_pairs={{0,3},{1,0},{2,1},{3,2},{4,7},{5,4},{6,5},{7,6},{8,11},{9,8},{10,9... | collective-permute-start | bytes 589832 | tf_op jit(solution)/shard_map/ppermute | solution.py:327
  27.4 0.9 %copy-start.3 = (s32[3,8192]{1,0:T(4,128)S(1)}, s32[3,8192]{1,0:T(4,128)}, u32[]{:S(2)}) copy-start(s32[3,8192]{1,0:T(4,128)} %numbers_ref.1) | copy-start | bytes 294916
  34.7 1.3 %collective-permute-start.8 = (f32[152,128]{1,0:T(8,128)S(1)}, f32[152,128]{1,0:T(8,128)S(1)}, u32[]{:S(2)}, u32[]{:S(2)}) collective-permute-start(f32[152,128]{1,0:T(8,128)S(1)} %get-tuple-element.37), channel_id=1, source_target_pairs={{0,4},{4,0},{8,12},{12,8},{16,20},{20,16},{24,28},{28,24},{1,5},{5... | collective-permute-start | bytes 233480 | tf_op jit(solution)/shard_map/ppermute | solution.py:343
  36.0 4.5 %collective-permute-start.9 = (f32[152,128]{1,0:T(8,128)S(1)}, f32[152,128]{1,0:T(8,128)S(1)}, u32[]{:S(2)}, u32[]{:S(2)}) collective-permute-start(f32[152,128]{1,0:T(8,128)S(1)} %add.17), channel_id=1, source_target_pairs={{0,8},{4,12},{8,0},{12,4},{16,24},{20,28},{24,16},{28,20},{1,9},{5... | collective-permute-start | bytes 233480 | tf_op jit(solution)/shard_map/ppermute | solution.py:343
  40.5 4.5 %collective-permute-start.10 = (f32[152,128]{1,0:T(8,128)S(1)}, f32[152,128]{1,0:T(8,128)S(1)}, u32[]{:S(2)}, u32[]{:S(2)}) collective-permute-start(f32[152,128]{1,0:T(8,128)S(1)} %add.18), channel_id=1, source_target_pairs={{0,16},{4,20},{8,24},{12,28},{16,0},{20,4},{24,8},{28,12},{1,17},{... | collective-permute-start | bytes 233480 | tf_op jit(solution)/shard_map/ppermute | solution.py:343
  45.0 4.5 %collective-permute-start.11 = (f32[152,128]{1,0:T(8,128)S(1)}, f32[152,128]{1,0:T(8,128)S(1)}, u32[]{:S(2)}, u32[]{:S(2)}) collective-permute-start(f32[152,128]{1,0:T(8,128)S(1)} %add.19), channel_id=1, source_target_pairs={{0,1},{1,0},{2,3},{3,2},{4,5},{5,4},{6,7},{7,6},{8,9},{9,8},{10,11... | collective-permute-start | bytes 233480 | tf_op jit(solution)/shard_map/ppermute | solution.py:343
  49.5 6.2 %collective-permute-start.12 = (f32[152,128]{1,0:T(8,128)S(1)}, f32[152,128]{1,0:T(8,128)S(1)}, u32[]{:S(2)}, u32[]{:S(2)}) collective-permute-start(f32[152,128]{1,0:T(8,128)S(1)} %add.20), channel_id=1, source_target_pairs={{0,2},{1,3},{2,0},{3,1},{4,6},{5,7},{6,4},{7,5},{8,10},{9,11},{10,... | collective-permute-start | bytes 233480 | tf_op jit(solution)/shard_map/ppermute | solution.py:343

commit v2 on v1

--- a/solution.py
+++ b/solution.py
@@ -12,6 +12,7 @@
 two_pi = 2.0 * math.pi
 kmax = 8
 grid_rows = (2 * kmax + 1) * kmax
+half_rows = 80
 f32 = jnp.float32
 bf16 = jnp.bfloat16
 highest = lax.Precision.HIGHEST
@@ -32,22 +33,25 @@
     )
 
 
-def pick_columns(hidden, index_ref, block):
-    atoms = hidden.shape[1]
-    ghosts = index_ref.shape[1]
-    row_ids = lax.broadcasted_iota(jnp.int32, (atoms, ghosts), 0)
-    one_hot = jnp.where(row_ids == index_ref[block : block + 1, :], 1.0, 0.0).astype(bf16)
-    return dot_nn(hidden, one_hot)
-
-
-def first_kernel(features_ref, index_ref, hidden_ref, *picked_refs):
+def pick_matrix(index_ref, block, atoms):
+    row_ids = lax.broadcasted_iota(jnp.int32, (atoms, index_ref.shape[1]), 0)
+    return jnp.where(row_ids == index_ref[block : block + 1, :], 1.0, 0.0).astype(bf16)
+
+
+def first_kernel(features_ref, index_ref, hidden_ref, p2, p3):
     hidden = jnp.transpose(features_ref[...].astype(f32)).astype(bf16)
     hidden_ref[...] = hidden
-    for block in (2, 3, 0, 1):
-        picked_refs[block][...] = pick_columns(hidden, index_ref, block)
-
-
-def edge_kernel(senders_ref, radial_ref, edges_ref):
+    for block, picked_ref in ((2, p2), (3, p3)):
+        picked_ref[...] = dot_nn(hidden, pick_matrix(index_ref, block, hidden.shape[1]))
+
+
+def wide_kernel(hidden_ref, index_ref, p0, p1):
+    hidden = hidden_ref[...]
+    for block, picked_ref in ((0, p0), (1, p1)):
+        picked_ref[...] = dot_nn(hidden, pick_matrix(index_ref, block, hidden.shape[1]))
+
+
+def edge_tiles(senders_ref, radial_ref, edges_ref, skip_from, skip):
     slots, atoms = senders_ref.shape
     rows = 128
     lanes = 128
@@ -55,9 +59,10 @@
 
     def one_tile(tile, carry):
         first = pl.multiple_of(tile * rows, rows)
+        sender = jnp.where(first >= skip_from, first + skip, first)
         for part in range(atoms // lanes):
             window = pl.ds(part * lanes, lanes)
-            local = jnp.clip(senders_ref[:, window] - first, -1, rows)
+            local = jnp.clip(senders_ref[:, window] - sender, -1, rows)
             local = local.astype(f32).astype(bf16)
             weight = radial_ref[:, window].astype(bf16)
             total = jnp.zeros((rows, lanes), bf16)
@@ -73,50 +78,80 @@
     lax.fori_loop(0, edges_ref.shape[0] // rows, one_tile, 0)
 
 
-def interact(hidden, ghost_refs, edges_ref, self_ref, message_ref):
+def far_edge_kernel(senders_ref, radial_ref, index_ref, hidden_ref, edges_ref, pick_ref, p0, p1):
+    for block in (2, 3):
+        pick_ref[block - 2] = pick_matrix(index_ref, block, senders_ref.shape[1])
+    wide_kernel(hidden_ref, index_ref, p0, p1)
+    edge_tiles(senders_ref, radial_ref, edges_ref, 0, senders_ref.shape[1])
+
+
+def near_edge_kernel(senders_ref, radial_ref, edges_ref):
+    atoms = senders_ref.shape[1]
+    edge_tiles(senders_ref, radial_ref, edges_ref, atoms, edges_ref.shape[0] - atoms)
+
+
+def near_kernel(layer, hidden_ref, g2, g3, edges_ref, self_ref, own_ref, gathered_ref):
+    hidden = hidden_ref[...]
     atoms = hidden.shape[1]
-    ghosts = ghost_refs[0].shape[1]
+    ghosts = g2.shape[1]
+    own_ref[...] = dot_tn(self_ref[layer], hidden)
     gathered = dot_nn(hidden, edges_ref[0:atoms, :])
-    for block, ghost_ref in enumerate(ghost_refs):
-        start = atoms + block * ghosts
-        gathered = gathered + dot_nn(
-            ghost_ref[...].astype(bf16), edges_ref[start : start + ghosts, :]
-        )
+    gathered = gathered + dot_nn(g2[...].astype(bf16), edges_ref[atoms : atoms + ghosts, :])
+    gathered_ref[...] = gathered + dot_nn(
+        g3[...].astype(bf16), edges_ref[atoms + ghosts : atoms + 2 * ghosts, :]
+    )
+
+
+def interact(layer, hidden_ref, own_ref, gathered_ref, g0, g1, edges_ref, message_ref):
+    hidden = hidden_ref[...]
+    ghosts = g0.shape[1]
+    gathered = gathered_ref[...]
+    gathered = gathered + dot_nn(g0[...].astype(bf16), edges_ref[0:ghosts, :])
+    gathered = gathered + dot_nn(g1[...].astype(bf16), edges_ref[ghosts : 2 * ghosts, :])
     high = gathered.astype(bf16)
     low = (gathered - high.astype(f32)).astype(bf16)
-    message = message_ref[...]
-    total = dot_tn(self_ref[...], hidden) + dot_tn(message, high) + dot_tn(message, low)
+    message = message_ref[layer]
+    total = own_ref[...] + dot_tn(message, high) + dot_tn(message, low)
     return (hidden.astype(f32) + total * (1.0 / (1.0 + jnp.exp(-total)))).astype(bf16)
 
 
 def layer_kernel(
-    hidden_ref, g0, g1, g2, g3, edges_ref, self_ref, message_ref, index_ref, out_ref, *picked_refs
+    layer, hidden_ref, own_ref, gathered_ref, g0, g1, edges_ref, message_ref, pick_ref, out_ref, p2, p3
 ):
-    hidden = interact(hidden_ref[...], (g0, g1, g2, g3), edges_ref, self_ref, message_ref)
+    hidden = interact(layer, hidden_ref, own_ref, gathered_ref, g0, g1, edges_ref, message_ref)
     out_ref[...] = hidden
-    for block in (2, 3, 0, 1):
-        picked_refs[block][...] = pick_columns(hidden, index_ref, block)
+    p2[...] = dot_nn(hidden, pick_ref[0])
+    p3[...] = dot_nn(hidden, pick_ref[1])
+
+
+def half_windows(core):
+    own = pl.ds(pl.multiple_of(core * half_rows, half_rows), half_rows)
+    other = pl.ds(pl.multiple_of((1 - core) * half_rows, half_rows), half_rows)
+    return own, other
 
 
 def last_kernel(
+    layer,
     hidden_ref,
+    own_ref,
+    gathered_ref,
     g0,
     g1,
-    g2,
-    g3,
     edges_ref,
-    self_ref,
     message_ref,
     readout_ref,
     count_ref,
+    core_ref,
     real_ref,
     imag_ref,
     third_ref,
-    sums_ref,
+    send_ref,
+    keep_ref,
     charges_ref,
     lattice_ref,
+    sums_ref,
 ):
-    hidden = interact(hidden_ref[...], (g0, g1, g2, g3), edges_ref, self_ref, message_ref)
+    hidden = interact(layer, hidden_ref, own_ref, gathered_ref, g0, g1, edges_ref, message_ref)
     atoms = hidden.shape[1]
     slot_ids = lax.broadcasted_iota(jnp.int32, (8, atoms), 1)
     charges = jnp.where(slot_ids < count_ref[0], dot_tn(readout_ref[...], hidden), 0.0)
@@ -139,9 +174,12 @@
     flat_imag = dot_nt(flat, imag)
     sums_ref[grid_rows : grid_rows + 4, :] = flat_real[0:4, 0:128]
     sums_ref[grid_rows + 4 : grid_rows + 8, :] = flat_imag[0:4, 0:128]
-    sums_ref[grid_rows + 8 : grid_rows + 16, :] = jnp.zeros((8, 128), f32)
+    sums_ref[grid_rows + 8 :, :] = jnp.zeros((sums_ref.shape[0] - grid_rows - 8, 128), f32)
     sums_ref[grid_rows + 8 : grid_rows + 12, 0:8] = flat_real[0:4, 128:grid_rows]
     sums_ref[grid_rows + 12 : grid_rows + 16, 0:8] = flat_imag[0:4, 128:grid_rows]
+    own, other = half_windows(core_ref[0])
+    keep_ref[...] = sums_ref[own, :]
+    send_ref[...] = sums_ref[other, :]
 
 
 def wave_weight(m0, m1, m2, cell_ref):
@@ -152,9 +190,8 @@
     return jnp.exp(-0.5 * smearing * smearing * squared) / squared
 
 
-def table_kernel(
-    fractions_ref, cell_ref, numbers_ref, real_ref, imag_ref, third_ref, factor_ref, flat_ref, acc, acc0
-):
+def phase_kernel(fractions_ref, hidden_ref, index_ref, real_ref, imag_ref, third_ref, p0, p1):
+    wide_kernel(hidden_ref, index_ref, p0, p1)
     atoms = fractions_ref.shape[1]
     orders = lax.broadcasted_iota(jnp.int32, (8, atoms), 0).astype(f32) + 1.0
     cosines, sines = [], []
@@ -182,6 +219,8 @@
         real_ref[window, :] = re.astype(bf16)
         imag_ref[window, :] = im.astype(bf16)
 
+
+def weight_kernel(cell_ref, numbers_ref, after_ref, factor_ref, flat_ref, acc, acc0):
     acc[...] = jnp.zeros_like(acc)
     acc0[...] = jnp.zeros_like(acc0)
     width = math.gcd(numbers_ref.shape[1], 1024)
@@ -229,7 +268,9 @@
 
 def force_kernel(
     scale,
-    sums_ref,
+    half_ref,
+    other_ref,
+    core_ref,
     charges_ref,
     lattice_ref,
     real_ref,
@@ -242,9 +283,13 @@
     forces_ref,
     born_ref,
     energy_ref,
+    sums_ref,
     flat_sums,
 ):
     atoms = real_ref.shape[1]
+    own, other = half_windows(core_ref[0])
+    sums_ref[own, :] = half_ref[...]
+    sums_ref[other, :] = other_ref[...]
     sums = sums_ref[0:grid_rows, :]
     swapped = pltpu.roll(sums, 64, 1)
     plus = pltpu.roll(sums + swapped, 32, 1)
@@ -327,22 +372,27 @@
     return lax.ppermute(block, axis, [(i, (i + step) % count) for i in range(count)])
 
 
-def exchange(picked):
-    lower_narrow = shifted(picked[3], "narrow", 1)
-    upper_narrow = shifted(picked[2], "narrow", -1)
-    lower_wide = shifted(picked[1], "wide", 1)
-    upper_wide = shifted(picked[0], "wide", -1)
-    return lower_wide, upper_wide, lower_narrow, upper_narrow
-
-
-def summed(block):
-    for axis in ("wide", "narrow"):
-        count = lax.axis_size(axis)
-        step = 1
-        while step < count:
-            block = block + lax.ppermute(block, axis, [(i, i ^ step) for i in range(count)])
+def exchange_narrow(p2, p3):
+    return shifted(p3, "narrow", 1), shifted(p2, "narrow", -1)
+
+
+def exchange_wide(p0, p1):
+    return shifted(p1, "wide", 1), shifted(p0, "wide", -1)
+
+
+def flipped(block, axis, step):
+    return lax.ppermute(block, axis, [(i, i ^ step) for i in range(lax.axis_size(axis))])
+
+
+def summed(send, keep, beside):
+    block = keep + flipped(send, "wide", 1)
+    for axis, step in (("wide", 2), ("narrow", 1)):
+        while step < lax.axis_size(axis):
+            if axis == "narrow" and 2 * step >= lax.axis_size(axis):
+                block, beside = lax.optimization_barrier((block, beside))
+            block = block + flipped(block, axis, step)
             step *= 2
-    return block
+    return block, flipped(block, "wide", 1), beside
 
 
 def per_device(
@@ -363,68 +413,100 @@
     rows = atoms + 4 * ghosts
     total_atoms = atoms * lax.axis_size("wide") * lax.axis_size("narrow")
     scale = 4.0 / math.sqrt(total_atoms * wave_numbers.shape[1])
-    picked_outs = [((width, ghosts), f32)] * 4
+    picked_outs = [((width, ghosts), f32)] * 2
     hidden_out = [((width, atoms), bf16)]
+    sum_out = [((width, atoms), f32)]
+    busy = pl.CostEstimate(flops=10**9, bytes_accessed=20 * 2**20, transcendentals=0)
     readout = jnp.pad(charge_weight, ((0, 0), (0, 8 - charge_weight.shape[1])))
-
-    hidden, *picked = call(first_kernel, hidden_out + picked_outs, features, send_index)
-    received = exchange(picked)
-    (edges,) = call(
-        edge_kernel,
-        [((rows, atoms), bf16)],
+    core = jnp.reshape(lax.axis_index("wide") % 2, (1,)).astype(jnp.int32)
+
+    hidden, p2, p3 = call(
+        first_kernel,
+        hidden_out + picked_outs,
+        features,
+        send_index,
+        cost=busy,
+    )
+    g2, g3 = exchange_narrow(p2, p3)
+    far_edges, picks, p0, p1 = call(
+        far_edge_kernel,
+        [((2 * ghosts, atoms), bf16), ((2, atoms, ghosts), bf16)] + picked_outs,
         senders,
         radial,
-        cost=pl.CostEstimate(flops=10**9, bytes_accessed=20 * 2**20, transcendentals=0),
+        send_index,
+        hidden,
+        cost=busy,
+    )
+    g0, g1 = exchange_wide(p0, p1)
+    (near_edges,) = call(
+        near_edge_kernel, [((rows - 2 * ghosts, atoms), bf16)], senders, radial, cost=busy
     )
     layers = self_weight.shape[0]
-    for layer in range(layers - 1):
-        hidden, *picked = call(
-            layer_kernel,
+    for layer in range(layers):
+        own, gathered = call(
+            functools.partial(near_kernel, layer), sum_out * 2, hidden, g2, g3, near_edges, self_weight
+        )
+        if layer == layers - 1:
+            break
+        hidden, p2, p3 = call(
+            functools.partial(layer_kernel, layer),
             hidden_out + picked_outs,
             hidden,
-            *received,
-            edges,
-            self_weight[layer],
-            message_weight[layer],
+            own,
+            gathered,
+            g0,
+            g1,
+            far_edges,
+            message_weight,
+            picks,
+        )
+        g2, g3 = exchange_narrow(p2, p3)
+        real, imag, third, p0, p1 = call(
+            phase_kernel,
+            [((grid_rows, atoms), bf16), ((grid_rows, atoms), bf16), ((24, atoms), f32)]
+            + picked_outs,
+            fractions,
+            hidden,
             send_index,
+            cost=busy,
         )
-        received = exchange(picked)
-    real, imag, third, factor, flat = call(
-        table_kernel,
-        [
-            ((grid_rows, atoms), bf16),
-            ((grid_rows, atoms), bf16),
-            ((24, atoms), f32),
-            ((4, grid_rows, 128), f32),
-            ((8, grid_rows), f32),
-        ],
-        fractions,
-        cell_lengths,
-        wave_numbers,
-        smem=(1,),
-        scratch=[pltpu.VMEM((grid_rows, 32), f32), pltpu.VMEM((16, grid_rows), f32)],
-        cost=pl.CostEstimate(flops=10**9, bytes_accessed=20 * 2**20, transcendentals=0),
-    )
-    sums, charges, lattice = call(
-        last_kernel,
-        [((grid_rows + 16, 128), f32), ((8, atoms), f32), ((64, atoms), f32)],
+        g0, g1 = exchange_wide(p0, p1)
+    send, keep, charges, lattice = call(
+        functools.partial(last_kernel, layers - 1),
+        [((half_rows, 128), f32)] * 2 + [((8, atoms), f32), ((64, atoms), f32)],
         hidden,
-        *received,
-        edges,
-        self_weight[layers - 1],
-        message_weight[layers - 1],
+        own,
+        gathered,
+        g0,
+        g1,
+        far_edges,
+        message_weight,
         readout,
         atom_counts,
+        core,
         real,
         imag,
         third,
-        smem=(9,),
-    )
-    sums = summed(sums)
+        smem=(8, 9),
+        scratch=[pltpu.VMEM((2 * half_rows, 128), f32)],
+    )
+    factor, flat = call(
+        weight_kernel,
+        [((4, grid_rows, 128), f32), ((8, grid_rows), f32)],
+        cell_lengths,
+        wave_numbers,
+        send,
+        smem=(0,),
+        scratch=[pltpu.VMEM((grid_rows, 32), f32), pltpu.VMEM((16, grid_rows), f32)],
+        cost=busy,
+    )
+    half, other, (factor, flat) = summed(send, keep, (factor, flat))
     forces, born_charges, energy = call(
         functools.partial(force_kernel, scale),
         [((3, atoms), f32), ((3, atoms), f32), ((1, 1), f32)],
-        sums,
+        half,
+        other,
+        core,
         charges,
         lattice,
         real,
@@ -434,8 +516,8 @@
         flat,
         cell_lengths,
         atom_counts,
-        smem=(8, 9),
-        scratch=[pltpu.VMEM((8, grid_rows), f32)],
+        smem=(2, 10, 11),
+        scratch=[pltpu.VMEM((2 * half_rows, 128), f32), pltpu.VMEM((8, grid_rows), f32)],
     )
     return (forces, born_charges, energy[0, 0])
 

time: 57.7 us -> 53.9 us (0.934)
  waiting for transfers between devices: 19.9 us -> 16.3 us
  local copies, waits for them, and re-layouts: 4.19 us -> 1.78 us
  Pallas kernels: 12.7 us -> 14.1 us
  starting transfers between devices: 19.1 us -> 20 us
    ppermute x5 -> x6, waiting for transfers between devices: 16 us -> 11 us  [flipped(): lax.ppermute(block, axis, [(i, i ^ step) for i in range(lax.axis_size(axi...]
    unnamed x21, local copies, waits for them, and re-layouts: 4.16 us -> 1.77 us
    pallas_call x6 -> x10, Pallas kernels: 12.7 us -> 14.1 us  [call(): pl.pallas_call(kernel, out_shape=[jax.ShapeDtypeStruct(shape, dtype) for...]
    ppermute x8, waiting for transfers between devices: 3.82 us -> 5.22 us  [shifted(): lax.ppermute(block, axis, [(i, (i + step) % count) for i in range(count)])]
    ppermute x5 -> x6, starting transfers between devices: 4.88 us -> 5.72 us  [flipped(): lax.ppermute(block, axis, [(i, i ^ step) for i in range(lax.axis_size(axi...]
  transfers between devices with their start and end apart: 13 -> 14, of which waited for: 9 -> 9; matrix products, arithmetic and copies ran while one was open for 0% -> 0% of each run, Pallas kernels for 13% -> 18%
where the time goes in v2:
time: 53.9 us; the launch traced here: 53.7 us
  starting transfers between devices  20 us (37%)
  waiting for transfers between devices  16.3 us (30%)
  Pallas kernels  14.1 us (26%)
  local copies, waits for them, and re-layouts  1.78 us (3%)
  between operations  1.47 us (3%)
    ppermute x8, starting transfers between devices, shifted(): lax.ppermute(block, axis, [(i, (i + step) % count) for i in range(count)])  14.3 us
    pallas_call x10, Pallas kernels, call(): pl.pallas_call(kernel, out_shape=[jax.ShapeDtypeStruct(shape, dtype) for...  14.1 us
    ppermute x6, waiting for transfers between devices, flipped(): lax.ppermute(block, axis, [(i, i ^ step) for i in range(lax.axis_size(axi...  11 us
    ppermute x6, starting transfers between devices, flipped(): lax.ppermute(block, axis, [(i, i ^ step) for i in range(lax.axis_size(axi...  5.72 us
    ppermute x8, waiting for transfers between devices, shifted(): lax.ppermute(block, axis, [(i, (i + step) % count) for i in range(count)])  5.22 us
    unnamed x21, local copies, waits for them, and re-layouts  1.77 us
  transfers between devices with their start and end apart: 14, of which 9 were waited for; matrix products, arithmetic and copies ran while one was open for 0% of the time, Pallas kernels for 18%

profile of v2, /device:TPU:0, one launch (start us, length us, event | category | flops | bytes accessed | tf_op | source)
XLA Modules:
  0.0 53.7 jit_solution(18398975775501390345)
XLA Ops:
  0.6 0.9 %copy-done.3 = bf16[512,128]{1,0:T(8,128)(2,1)S(1)} copy-done((bf16[512,128]{1,0:T(8,128)(2,1)S(1)}, bf16[512,128]{1,0:T(8,128)(2,1)}, u32[]{:S(2)}) %copy-start.3) | copy-done | bytes 131096
  1.5 0.7 %copy-done.8 = s32[4,384]{1,0:T(4,128)S(1)} copy-done((s32[4,384]{1,0:T(4,128)S(1)}, s32[4,384]{1,0:T(4,128)}, u32[]{:S(2)}) %copy-start.8) | copy-done | bytes 6168
  2.2 0.4 shard_map.130
  2.6 3.1 %collective-permute-start = (f32[128,384]{1,0:T(8,128)S(1)}, f32[128,384]{1,0:T(8,128)S(1)}, u32[]{:S(2)}, u32[]{:S(2)}) collective-permute-start(f32[128,384]{1,0:T(8,128)S(1)} %get-tuple-element.35), channel_id=1, source_target_pairs={{0,1},{1,2},{2,3},{3,0},{4,5},{5,6},{6,7},{7,4},{8,9},{9,10},{10,1... | collective-permute-start | bytes 589832 | tf_op jit(solution)/shard_map/ppermute | solution.py:372
  5.7 2.1 %collective-permute-start.1 = (f32[128,384]{1,0:T(8,128)S(1)}, f32[128,384]{1,0:T(8,128)S(1)}, u32[]{:S(2)}, u32[]{:S(2)}) collective-permute-start(f32[128,384]{1,0:T(8,128)S(1)} %get-tuple-element.36), channel_id=1, source_target_pairs={{0,3},{1,0},{2,1},{3,2},{4,7},{5,4},{6,5},{7,6},{8,11},{9,8},{10,9... | collective-permute-start | bytes 589832 | tf_op jit(solution)/shard_map/ppermute | solution.py:372
  7.8 1.9 %shard_map.133 = (bf16[768,512]{1,0:T(8,128)(2,1)S(1)}, bf16[2,512,384]{2,1,0:T(8,128)(2,1)S(1)}, f32[128,384]{1,0:T(8,128)S(1)}, f32[128,384]{1,0:T(8,128)S(1)}) custom-call(s32[16,512]{1,0:T(8,128)S(1)} %copy-done.5, f32[16,512]{1,0:T(8,128)S(1)} %copy-done.6, s32[4,384]{1,0:T(4,128)S(1)} %copy-done.8, bf16[128,512]{1,0:T(8,128)(2,1)S(1)} %get-tuple-element.34.hidden_ref), custom_call_target="tpu_custom_call" | custom-call | flops 1000000000 | bytes 20971520 | tf_op jit(solution)/shard_map/pallas_call | solution.py:359
  9.8 2.6 %collective-permute-start.3 = (f32[128,384]{1,0:T(8,128)S(1)}, f32[128,384]{1,0:T(8,128)S(1)}, u32[]{:S(2)}, u32[]{:S(2)}) collective-permute-start(f32[128,384]{1,0:T(8,128)S(1)} %get-tuple-element.40), channel_id=1, source_target_pairs={{0,28},{4,0},{8,4},{12,8},{16,12},{20,16},{24,20},{28,24},{1,29},{... | collective-permute-start | bytes 589832 | tf_op jit(solution)/shard_map/ppermute | solution.py:372
  12.4 2.5 %shard_map.131.edges_ref = bf16[1280,512]{1,0:T(8,128)(2,1)S(1)} custom-call(s32[16,512]{1,0:T(8,128)S(1)} %copy-done.5, f32[16,512]{1,0:T(8,128)S(1)} %copy-done.6), custom_call_target="tpu_custom_call" | custom-call | flops 1000000000 | bytes 20971520 | tf_op jit(solution)/shard_map/pallas_call | solution.py:359
  14.9 1.3 %collective-permute-done.1.g3 = f32[128,384]{1,0:T(8,128)S(1)} collective-permute-done((f32[128,384]{1,0:T(8,128)S(1)}, f32[128,384]{1,0:T(8,128)S(1)}, u32[]{:S(2)}, u32[]{:S(2)}) %collective-permute-start.1) | collective-permute-done | bytes 196640 | tf_op jit(solution)/shard_map/ppermute | solution.py:372
  16.3 0.4 shard_map.132
  16.7 1.5 %shard_map.134 = (bf16[128,512]{1,0:T(8,128)(2,1)S(1)}, f32[128,384]{1,0:T(8,128)}, f32[128,384]{1,0:T(8,128)}) custom-call(bf16[128,512]{1,0:T(8,128)(2,1)S(1)} %get-tuple-element.34.hidden_ref, f32[128,512]{1,0:T(8,128)S(1)} %get-tuple-element.37.own_ref, f32[128,512]{1,0:T(8,128)S(1)} %get-tuple-element.38.gathered_ref, ...), custom_call_target="tpu_custom_call" | custom-call | tf_op jit(solution)/shard_map/pallas_call | solution.py:359
  18.2 1.1 %collective-permute-start.4 = (f32[128,384]{1,0:T(8,128)}, f32[128,384]{1,0:T(8,128)S(1)}, u32[]{:S(2)}, u32[]{:S(2)}) collective-permute-start(f32[128,384]{1,0:T(8,128)} %get-tuple-element.44), channel_id=1, source_target_pairs={{0,1},{1,2},{2,3},{3,0},{4,5},{5,6},{6,7},{7,4},{8,9},{9,10},{10,1... | collective-permute-start | bytes 589832 | tf_op jit(solution)/shard_map/ppermute | solution.py:372
  19.4 2.7 %collective-permute-start.5 = (f32[128,384]{1,0:T(8,128)}, f32[128,384]{1,0:T(8,128)S(1)}, u32[]{:S(2)}, u32[]{:S(2)}) collective-permute-start(f32[128,384]{1,0:T(8,128)} %get-tuple-element.45), channel_id=1, source_target_pairs={{0,3},{1,0},{2,1},{3,2},{4,7},{5,4},{6,5},{7,6},{8,11},{9,8},{10,9... | collective-permute-start | bytes 589832 | tf_op jit(solution)/shard_map/ppermute | solution.py:372
  22.1 1.2 %shard_map.136 = (bf16[136,512]{1,0:T(8,128)(2,1)S(1)}, bf16[136,512]{1,0:T(8,128)(2,1)S(1)}, f32[24,512]{1,0:T(8,128)S(1)}, f32[128,384]{1,0:T(8,128)}, f32[128,384]{1,0:T(8,128)}) custom-call(f32[3,512]{1,0:T(4,128)S(1)} %copy-done.7, bf16[128,512]{1,0:T(8,128)(2,1)S(1)} %get-tuple-element.43.hidden_ref, s32[4,384]{1,0:T(4,128)S(1)} %copy-done.8), custom_call_target="tpu_custom_call" | custom-call | flops 1000000000 | bytes 20971520 | tf_op jit(solution)/shard_map/pallas_call | solution.py:359
  23.3 0.6 %collective-permute-start.6 = (f32[128,384]{1,0:T(8,128)}, f32[128,384]{1,0:T(8,128)S(1)}, u32[]{:S(2)}, u32[]{:S(2)}) collective-permute-start(f32[128,384]{1,0:T(8,128)} %get-tuple-element.48), channel_id=1, source_target_pairs={{0,4},{4,8},{8,12},{12,16},{16,20},{20,24},{24,28},{28,0},{1,5},{5... | collective-permute-start | bytes 589832 | tf_op jit(solution)/shard_map/ppermute | solution.py:372
  23.9 2.0 %collective-permute-start.7 = (f32[128,384]{1,0:T(8,128)}, f32[128,384]{1,0:T(8,128)S(1)}, u32[]{:S(2)}, u32[]{:S(2)}) collective-permute-start(f32[128,384]{1,0:T(8,128)} %get-tuple-element.49), channel_id=1, source_target_pairs={{0,28},{4,0},{8,4},{12,8},{16,12},{20,16},{24,20},{28,24},{1,29},{... | collective-permute-start | bytes 589832 | tf_op jit(solution)/shard_map/ppermute | solution.py:372
  26.8 1.2 %collective-permute-done.4.g2 = f32[128,384]{1,0:T(8,128)S(1)} collective-permute-done((f32[128,384]{1,0:T(8,128)}, f32[128,384]{1,0:T(8,128)S(1)}, u32[]{:S(2)}, u32[]{:S(2)}) %collective-permute-start.4) | collective-permute-done | bytes 196640 | tf_op jit(solution)/shard_map/ppermute | solution.py:372
  28.0 2.7 %collective-permute-done.5.g3 = f32[128,384]{1,0:T(8,128)S(1)} collective-permute-done((f32[128,384]{1,0:T(8,128)}, f32[128,384]{1,0:T(8,128)S(1)}, u32[]{:S(2)}, u32[]{:S(2)}) %collective-permute-start.5) | collective-permute-done | bytes 196640 | tf_op jit(solution)/shard_map/ppermute | solution.py:372
  30.6 0.4 shard_map.135
  31.1 0.9 %shard_map.137 = (f32[80,128]{1,0:T(8,128)S(1)}, f32[80,128]{1,0:T(8,128)S(1)}, f32[8,512]{1,0:T(8,128)S(1)}, f32[64,512]{1,0:T(8,128)S(1)}) custom-call(bf16[128,512]{1,0:T(8,128)(2,1)S(1)} %get-tuple-element.43.hidden_ref, f32[128,512]{1,0:T(8,128)S(1)} %get-tuple-element.46.own_ref, f32[128,512]{1,0:T(8,128)S(1)} %get-tuple-element.47.gathered_ref, ...), custom_call_target="tpu_custom_call" | custom-call | tf_op jit(solution)/shard_map/pallas_call | solution.py:359
  32.0 1.0 %collective-permute-start.8 = (f32[80,128]{1,0:T(8,128)S(1)}, f32[80,128]{1,0:T(8,128)S(1)}, u32[]{:S(2)}, u32[]{:S(2)}) collective-permute-start(f32[80,128]{1,0:T(8,128)S(1)} %get-tuple-element.54.after_ref), channel_id=1, source_target_pairs={{0,4},{4,0},{8,12},{12,8},{16,20},{20,16},{24,28},{28,24},{1,5},{5... | collective-permute-start | bytes 122888 | tf_op jit(solution)/shard_map/ppermute | solution.py:384
  33.0 0.9 %collective-permute-done.8 = f32[80,128]{1,0:T(8,128)S(1)} collective-permute-done((f32[80,128]{1,0:T(8,128)S(1)}, f32[80,128]{1,0:T(8,128)S(1)}, u32[]{:S(2)}, u32[]{:S(2)}) %collective-permute-start.8) | collective-permute-done | bytes 40992 | tf_op jit(solution)/shard_map/ppermute | solution.py:384
  33.9 1.1 %collective-permute-start.9 = (f32[80,128]{1,0:T(8,128)S(1)}, f32[80,128]{1,0:T(8,128)S(1)}, u32[]{:S(2)}, u32[]{:S(2)}) collective-permute-start(f32[80,128]{1,0:T(8,128)S(1)} %add.22), channel_id=1, source_target_pairs={{0,8},{4,12},{8,0},{12,4},{16,24},{20,28},{24,16},{28,20},{1,9},{5... | collective-permute-start | bytes 122888 | tf_op jit(solution)/shard_map/ppermute | solution.py:384
  35.0 2.9 %collective-permute-done.9 = f32[80,128]{1,0:T(8,128)S(1)} collective-permute-done((f32[80,128]{1,0:T(8,128)S(1)}, f32[80,128]{1,0:T(8,128)S(1)}, u32[]{:S(2)}, u32[]{:S(2)}) %collective-permute-start.9) | collective-permute-done | bytes 40992 | tf_op jit(solution)/shard_map/ppermute | solution.py:384
  37.9 1.6 %collective-permute-start.10 = (f32[80,128]{1,0:T(8,128)S(1)}, f32[80,128]{1,0:T(8,128)S(1)}, u32[]{:S(2)}, u32[]{:S(2)}) collective-permute-start(f32[80,128]{1,0:T(8,128)S(1)} %add.23), channel_id=1, source_target_pairs={{0,16},{4,20},{8,24},{12,28},{16,0},{20,4},{24,8},{28,12},{1,17},{... | collective-permute-start | bytes 122888 | tf_op jit(solution)/shard_map/ppermute | solution.py:384
  39.5 2.4 %collective-permute-done.10 = f32[80,128]{1,0:T(8,128)S(1)} collective-permute-done((f32[80,128]{1,0:T(8,128)S(1)}, f32[80,128]{1,0:T(8,128)S(1)}, u32[]{:S(2)}, u32[]{:S(2)}) %collective-permute-start.10) | collective-permute-done | bytes 40992 | tf_op jit(solution)/shard_map/ppermute | solution.py:384
  41.9 0.5 collective-permute-start.11
  42.4 3.2 %shard_map.138 = (f32[4,136,128]{2,1,0:T(8,128)S(1)}, f32[8,136]{1,0:T(8,128)S(1)}) custom-call(f32[3]{0:T(128)S(1)} %copy-done.2, s32[3,8192]{1,0:T(4,128)S(1)} %copy-done.4, f32[80,128]{1,0:T(8,128)S(1)} %get-tuple-element.54.after_ref), custom_call_target="tpu_custom_call" | custom-call | flops 1000000000 | bytes 20971520 | tf_op jit(solution)/shard_map/pallas_call | solution.py:359
  45.9 1.5 %collective-permute-start.12 = (f32[80,128]{1,0:T(8,128)S(1)}, f32[80,128]{1,0:T(8,128)S(1)}, u32[]{:S(2)}, u32[]{:S(2)}) collective-permute-start(f32[80,128]{1,0:T(8,128)S(1)} %add.25), channel_id=1, source_target_pairs={{0,2},{1,3},{2,0},{3,1},{4,6},{5,7},{6,4},{7,5},{8,10},{9,11},{10,... | collective-permute-start | bytes 122888 | tf_op jit(solution)/shard_map/ppermute | solution.py:384
  47.4 3.4 %collective-permute-done.12 = f32[80,128]{1,0:T(8,128)S(1)} collective-permute-done((f32[80,128]{1,0:T(8,128)S(1)}, f32[80,128]{1,0:T(8,128)S(1)}, u32[]{:S(2)}, u32[]{:S(2)}) %collective-permute-start.12) | collective-permute-done | bytes 40992 | tf_op jit(solution)/shard_map/ppermute | solution.py:384
  50.8 1.2 %collective-permute-done.13.other_ref = f32[80,128]{1,0:T(8,128)S(1)} collective-permute-done((f32[80,128]{1,0:T(8,128)S(1)}, f32[80,128]{1,0:T(8,128)S(1)}, u32[]{:S(2)}, u32[]{:S(2)}) %collective-permute-start.13) | collective-permute-done | bytes 40992 | tf_op jit(solution)/shard_map/ppermute | solution.py:384
  52.0 1.7 %shard_map.139 = (f32[3,512]{1,0:T(4,128)}, f32[3,512]{1,0:T(4,128)}, f32[1,1]{1,0:T(1,128)}) custom-call(f32[80,128]{1,0:T(8,128)S(1)} %add.26.half_ref, f32[80,128]{1,0:T(8,128)S(1)} %collective-permute-done.13.other_ref, s32[1]{0:T(128)} %bitcast.core_ref, f32[8,512]{1,0:T(8,128)S(1)} %get-tuple-element.58.charges_ref, ...), custom_call_target="tpu_custom_call" | custom-call | tf_op jit(solution)/shard_map/pallas_call | solution.py:359
  (33 shorter events, 0.6 us)
Async XLA Ops:
  0.6 0.9 %copy-start.3 = (bf16[512,128]{1,0:T(8,128)(2,1)S(1)}, bf16[512,128]{1,0:T(8,128)(2,1)}, u32[]{:S(2)}) copy-start(bf16[512,128]{1,0:T(8,128)(2,1)} %features_ref.1) | copy-start | bytes 393220
  1.5 0.7 %copy-start.8 = (s32[4,384]{1,0:T(4,128)S(1)}, s32[4,384]{1,0:T(4,128)}, u32[]{:S(2)}) copy-start(s32[4,384]{1,0:T(4,128)} %index_ref.5) | copy-start | bytes 18436
  2.2 5.6 %copy-start.5 = (s32[16,512]{1,0:T(8,128)S(1)}, s32[16,512]{1,0:T(8,128)}, u32[]{:S(2)}) copy-start(s32[16,512]{1,0:T(8,128)} %senders_ref.3) | copy-start | bytes 98308
  2.2 5.6 %copy-start.6 = (f32[16,512]{1,0:T(8,128)S(1)}, f32[16,512]{1,0:T(8,128)}, u32[]{:S(2)}) copy-start(f32[16,512]{1,0:T(8,128)} %radial_ref.3) | copy-start | bytes 98308
  2.6 12.3 %collective-permute-start = (f32[128,384]{1,0:T(8,128)S(1)}, f32[128,384]{1,0:T(8,128)S(1)}, u32[]{:S(2)}, u32[]{:S(2)}) collective-permute-start(f32[128,384]{1,0:T(8,128)S(1)} %get-tuple-element.35), channel_id=1, source_target_pairs={{0,1},{1,2},{2,3},{3,0},{4,5},{5,6},{6,7},{7,4},{8,9},{9,10},{10,1... | collective-permute-start | bytes 589832 | tf_op jit(solution)/shard_map/ppermute | solution.py:372
  5.7 10.6 %collective-permute-start.1 = (f32[128,384]{1,0:T(8,128)S(1)}, f32[128,384]{1,0:T(8,128)S(1)}, u32[]{:S(2)}, u32[]{:S(2)}) collective-permute-start(f32[128,384]{1,0:T(8,128)S(1)} %get-tuple-element.36), channel_id=1, source_target_pairs={{0,3},{1,0},{2,1},{3,2},{4,7},{5,4},{6,5},{7,6},{8,11},{9,8},{10,9... | collective-permute-start | bytes 589832 | tf_op jit(solution)/shard_map/ppermute | solution.py:372
  9.7 7.0 %collective-permute-start.2 = (f32[128,384]{1,0:T(8,128)S(1)}, f32[128,384]{1,0:T(8,128)S(1)}, u32[]{:S(2)}, u32[]{:S(2)}) collective-permute-start(f32[128,384]{1,0:T(8,128)S(1)} %get-tuple-element.39), channel_id=1, source_target_pairs={{0,4},{4,8},{8,12},{12,16},{16,20},{20,24},{24,28},{28,0},{1,5},{5... | collective-permute-start | bytes 589832 | tf_op jit(solution)/shard_map/ppermute | solution.py:372
  9.8 6.5 %copy-start.1 = (bf16[2,128,128]{2,1,0:T(8,128)(2,1)S(1)}, bf16[2,128,128]{2,1,0:T(8,128)(2,1)}, u32[]{:S(2)}) copy-start(bf16[2,128,128]{2,1,0:T(8,128)(2,1)} %self_ref.3) | copy-start | bytes 196612
  9.8 6.9 %collective-permute-start.3 = (f32[128,384]{1,0:T(8,128)S(1)}, f32[128,384]{1,0:T(8,128)S(1)}, u32[]{:S(2)}, u32[]{:S(2)}) collective-permute-start(f32[128,384]{1,0:T(8,128)S(1)} %get-tuple-element.40), channel_id=1, source_target_pairs={{0,28},{4,0},{8,4},{12,8},{16,12},{20,16},{24,20},{28,24},{1,29},{... | collective-permute-start | bytes 589832 | tf_op jit(solution)/shard_map/ppermute | solution.py:372
  14.9 1.8 %copy-start = (bf16[2,128,128]{2,1,0:T(8,128)(2,1)S(1)}, bf16[2,128,128]{2,1,0:T(8,128)(2,1)}, u32[]{:S(2)}) copy-start(bf16[2,128,128]{2,1,0:T(8,128)(2,1)} %message_ref.3) | copy-start | bytes 196612
  16.7 5.3 %copy-start.7 = (f32[3,512]{1,0:T(4,128)S(1)}, f32[3,512]{1,0:T(4,128)}, u32[]{:S(2)}) copy-start(f32[3,512]{1,0:T(4,128)} %fractions_ref.1) | copy-start | bytes 18436
  18.2 9.7 %collective-permute-start.4 = (f32[128,384]{1,0:T(8,128)}, f32[128,384]{1,0:T(8,128)S(1)}, u32[]{:S(2)}, u32[]{:S(2)}) collective-permute-start(f32[128,384]{1,0:T(8,128)} %get-tuple-element.44), channel_id=1, source_target_pairs={{0,1},{1,2},{2,3},{3,0},{4,5},{5,6},{6,7},{7,4},{8,9},{9,10},{10,1... | collective-permute-start | bytes 589832 | tf_op jit(solution)/shard_map/ppermute | solution.py:372
  19.4 11.3 %collective-permute-start.5 = (f32[128,384]{1,0:T(8,128)}, f32[128,384]{1,0:T(8,128)S(1)}, u32[]{:S(2)}, u32[]{:S(2)}) collective-permute-start(f32[128,384]{1,0:T(8,128)} %get-tuple-element.45), channel_id=1, source_target_pairs={{0,3},{1,0},{2,1},{3,2},{4,7},{5,4},{6,5},{7,6},{8,11},{9,8},{10,9... | collective-permute-start | bytes 589832 | tf_op jit(solution)/shard_map/ppermute | solution.py:372
  22.1 4.6 %copy-start.9 = (bf16[128,4]{0,1:T(4,128)(2,1)S(1)}, bf16[128,4]{0,1:T(4,128)(2,1)}, u32[]{:S(2)}) copy-start(bf16[128,4]{0,1:T(4,128)(2,1)} %param.20) | copy-start | bytes 3076
  23.3 7.8 %collective-permute-start.6 = (f32[128,384]{1,0:T(8,128)}, f32[128,384]{1,0:T(8,128)S(1)}, u32[]{:S(2)}, u32[]{:S(2)}) collective-permute-start(f32[128,384]{1,0:T(8,128)} %get-tuple-element.48), channel_id=1, source_target_pairs={{0,4},{4,8},{8,12},{12,16},{16,20},{20,24},{24,28},{28,0},{1,5},{5... | collective-permute-start | bytes 589832 | tf_op jit(solution)/shard_map/ppermute | solution.py:372
  23.9 7.2 %collective-permute-start.7 = (f32[128,384]{1,0:T(8,128)}, f32[128,384]{1,0:T(8,128)S(1)}, u32[]{:S(2)}, u32[]{:S(2)}) collective-permute-start(f32[128,384]{1,0:T(8,128)} %get-tuple-element.49), channel_id=1, source_target_pairs={{0,28},{4,0},{8,4},{12,8},{16,12},{20,16},{24,20},{28,24},{1,29},{... | collective-permute-start | bytes 589832 | tf_op jit(solution)/shard_map/ppermute | solution.py:372
  31.1 11.3 %copy-start.2 = (f32[3]{0:T(128)S(1)}, f32[3]{0:T(128)}, u32[]{:S(2)}) copy-start(f32[3]{0:T(128)} %cell_ref.3) | copy-start | bytes 40
  31.1 11.3 %copy-start.4 = (s32[3,8192]{1,0:T(4,128)S(1)}, s32[3,8192]{1,0:T(4,128)}, u32[]{:S(2)}) copy-start(s32[3,8192]{1,0:T(4,128)} %numbers_ref.1) | copy-start | bytes 294916
  32.0 1.8 %collective-permute-start.8 = (f32[80,128]{1,0:T(8,128)S(1)}, f32[80,128]{1,0:T(8,128)S(1)}, u32[]{:S(2)}, u32[]{:S(2)}) collective-permute-start(f32[80,128]{1,0:T(8,128)S(1)} %get-tuple-element.54.after_ref), channel_id=1, source_target_pairs={{0,4},{4,0},{8,12},{12,8},{16,20},{20,16},{24,28},{28,24},{1,5},{5... | collective-permute-start | bytes 122888 | tf_op jit(solution)/shard_map/ppermute | solution.py:384
  33.9 4.0 %collective-permute-start.9 = (f32[80,128]{1,0:T(8,128)S(1)}, f32[80,128]{1,0:T(8,128)S(1)}, u32[]{:S(2)}, u32[]{:S(2)}) collective-permute-start(f32[80,128]{1,0:T(8,128)S(1)} %add.22), channel_id=1, source_target_pairs={{0,8},{4,12},{8,0},{12,4},{16,24},{20,28},{24,16},{28,20},{1,9},{5... | collective-permute-start | bytes 122888 | tf_op jit(solution)/shard_map/ppermute | solution.py:384
  37.9 4.0 %collective-permute-start.10 = (f32[80,128]{1,0:T(8,128)S(1)}, f32[80,128]{1,0:T(8,128)S(1)}, u32[]{:S(2)}, u32[]{:S(2)}) collective-permute-start(f32[80,128]{1,0:T(8,128)S(1)} %add.23), channel_id=1, source_target_pairs={{0,16},{4,20},{8,24},{12,28},{16,0},{20,4},{24,8},{28,12},{1,17},{... | collective-permute-start | bytes 122888 | tf_op jit(solution)/shard_map/ppermute | solution.py:384
  41.9 4.0 %collective-permute-start.11 = (f32[80,128]{1,0:T(8,128)S(1)}, f32[80,128]{1,0:T(8,128)S(1)}, u32[]{:S(2)}, u32[]{:S(2)}) collective-permute-start(f32[80,128]{1,0:T(8,128)S(1)} %add.24), channel_id=1, source_target_pairs={{0,1},{1,0},{2,3},{3,2},{4,5},{5,4},{6,7},{7,6},{8,9},{9,8},{10,11... | collective-permute-start | bytes 122888 | tf_op jit(solution)/shard_map/ppermute | solution.py:384
  45.9 4.9 %collective-permute-start.12 = (f32[80,128]{1,0:T(8,128)S(1)}, f32[80,128]{1,0:T(8,128)S(1)}, u32[]{:S(2)}, u32[]{:S(2)}) collective-permute-start(f32[80,128]{1,0:T(8,128)S(1)} %add.25), channel_id=1, source_target_pairs={{0,2},{1,3},{2,0},{3,1},{4,6},{5,7},{6,4},{7,5},{8,10},{9,11},{10,... | collective-permute-start | bytes 122888 | tf_op jit(solution)/shard_map/ppermute | solution.py:384
  50.8 1.2 %collective-permute-start.13 = (f32[80,128]{1,0:T(8,128)S(1)}, f32[80,128]{1,0:T(8,128)S(1)}, u32[]{:S(2)}, u32[]{:S(2)}) collective-permute-start(f32[80,128]{1,0:T(8,128)S(1)} %add.26.half_ref), channel_id=1, source_target_pairs={{0,4},{4,0},{8,12},{12,8},{16,20},{20,16},{24,28},{28,24},{1,5},{5... | collective-permute-start | bytes 122888 | tf_op jit(solution)/shard_map/ppermute | solution.py:384

commit v3 on v2

v3 whole, which is shorter than its diff:
```python
import functools
import math

import jax
import jax.numpy as jnp
from jax import lax
from jax.experimental import pallas as pl
from jax.experimental.pallas import tpu as pltpu
from jax.sharding import PartitionSpec as P

smearing = 0.5
two_pi = 2.0 * math.pi
kmax = 8
grid_rows = (2 * kmax + 1) * kmax
half_rows = 80
f32 = jnp.float32
bf16 = jnp.bfloat16
params = pltpu.CompilerParams(vmem_limit_bytes=48 * 1024 * 1024)


def dot_nn(a, b):
    return lax.dot_general(a, b, (((1,), (0,)), ((), ())), preferred_element_type=f32)


def dot_nt(a, b):
    return lax.dot_general(a, b, (((1,), (1,)), ((), ())), preferred_element_type=f32)


def pick_matrix(index_ref, block, atoms):
    row_ids = lax.broadcasted_iota(jnp.int32, (atoms, index_ref.shape[1]), 0)
    return jnp.where(row_ids == index_ref[block : block + 1, :], 1.0, 0.0).astype(bf16)


def first_kernel(features_ref, index_ref, hidden_ref, p2, p3):
    hidden = jnp.transpose(features_ref[...].astype(f32)).astype(bf16)
    hidden_ref[...] = hidden
    for block, picked_ref in ((2, p2), (3, p3)):
        picked_ref[...] = dot_nn(hidden, pick_matrix(index_ref, block, hidden.shape[1]))


def wide_kernel(hidden_ref, index_ref, p0, p1):
    hidden = hidden_ref[...]
    for block, picked_ref in ((0, p0), (1, p1)):
        picked_ref[...] = dot_nn(hidden, pick_matrix(index_ref, block, hidden.shape[1]))


def edge_tiles(senders_ref, radial_ref, edges_ref, skip_from, skip):
    slots, atoms = senders_ref.shape
    rows = 128
    lanes = 128
    row_ids = lax.broadcasted_iota(jnp.int32, (rows, lanes), 0).astype(f32).astype(bf16)

    def one_tile(tile, carry):
        first = pl.multiple_of(tile * rows, rows)
        sender = jnp.where(first >= skip_from, first + skip, first)
        for part in range(atoms // lanes):
            window = pl.ds(part * lanes, lanes)
            local = jnp.clip(senders_ref[:, window] - sender, -1, rows)
            local = local.astype(f32).astype(bf16)
            weight = radial_ref[:, window].astype(bf16)
            total = jnp.zeros((rows, lanes), bf16)
            for slot in range(slots):
                total = total + jnp.where(
                    row_ids == local[slot : slot + 1, :],
                    weight[slot : slot + 1, :],
                    jnp.zeros((), bf16),
                )
            edges_ref[pl.ds(first, rows), window] = total
        return carry

    lax.fori_loop(0, edges_ref.shape[0] // rows, one_tile, 0)


def far_edge_kernel(senders_ref, radial_ref, index_ref, hidden_ref, edges_ref, pick_ref, p0, p1):
    ghosts = index_ref.shape[1]
    for block in (2, 3):
        window = pl.ds((block - 2) * ghosts, ghosts)
        pick_ref[:, window] = pick_matrix(index_ref, block, senders_ref.shape[1])
    wide_kernel(hidden_ref, index_ref, p0, p1)
    edge_tiles(senders_ref, radial_ref, edges_ref, 0, senders_ref.shape[1])


def near_edge_kernel(
    senders_ref, radial_ref, self_ref, message_ref, edges_ref, self_rows_ref, message_rows_ref
):
    atoms = senders_ref.shape[1]
    edge_tiles(senders_ref, radial_ref, edges_ref, atoms, edges_ref.shape[0] - atoms)
    for layer in range(self_ref.shape[0]):
        self_rows_ref[layer] = jnp.transpose(self_ref[layer].astype(f32)).astype(bf16)
        message = jnp.transpose(message_ref[layer].astype(f32)).astype(bf16)
        message_rows_ref[layer] = jnp.concatenate([message, message], axis=1)


def near_kernel(layer, hidden_ref, g2, g3, edges_ref, self_rows_ref, own_ref, gathered_ref):
    hidden = hidden_ref[...]
    own_ref[...] = dot_nn(self_rows_ref[layer], hidden)
    known = jnp.concatenate([hidden, g2[...].astype(bf16), g3[...].astype(bf16)], axis=1)
    gathered_ref[...] = dot_nn(known, edges_ref[...])


def interact(layer, hidden_ref, own_ref, gathered_ref, g0, g1, edges_ref, message_rows_ref):
    received = jnp.concatenate([g0[...].astype(bf16), g1[...].astype(bf16)], axis=1)
    gathered = gathered_ref[...] + dot_nn(received, edges_ref[...])
    high = gathered.astype(bf16)
    low = (gathered - high.astype(f32)).astype(bf16)
    total = own_ref[...] + dot_nn(message_rows_ref[layer], jnp.concatenate([high, low], axis=0))
    gate = 0.5 * total * (1.0 + jnp.tanh(0.5 * total))
    return (hidden_ref[...].astype(f32) + gate).astype(bf16)


def layer_kernel(
    layer, hidden_ref, own_ref, gathered_ref, g0, g1, edges_ref, message_rows_ref, pick_ref, out_ref, p2, p3
):
    hidden = interact(layer, hidden_ref, own_ref, gathered_ref, g0, g1, edges_ref, message_rows_ref)
    out_ref[...] = hidden
    picked = dot_nn(hidden, pick_ref[...])
    ghosts = p2.shape[1]
    p2[...] = picked[:, 0:ghosts]
    p3[...] = picked[:, ghosts:]


def last_kernel(
    layer,
    hidden_ref,
    own_ref,
    gathered_ref,
    g0,
    g1,
    edges_ref,
    message_rows_ref,
    readout_ref,
    count_ref,
    phase_ref,
    third_ref,
    send_ref,
    keep_ref,
    lattice_ref,
):
    hidden = interact(layer, hidden_ref, own_ref, gathered_ref, g0, g1, edges_ref, message_rows_ref)
    atoms = hidden.shape[1]
    slot_ids = lax.broadcasted_iota(jnp.int32, (8, atoms), 1)
    readout = readout_ref[...].astype(f32)
    readout = jnp.concatenate([readout, jnp.zeros_like(readout)], axis=0).astype(bf16)
    charges = jnp.where(slot_ids < count_ref[...], dot_nn(readout, hidden), 0.0)
    cosine = third_ref[0:8, :]
    sine = third_ref[8:16, :]
    rows = [charges[c : c + 1, :] * cosine for c in range(4)]
    rows = rows + [charges[c : c + 1, :] * sine for c in range(4)]
    lattice = jnp.concatenate(rows + [charges], axis=0)
    lattice_ref[...] = lattice
    lattice = lattice.astype(bf16)
    core = lax.rem(lax.axis_index("wide"), 2)
    for out_ref, part in ((keep_ref, core), (send_ref, 1 - core)):
        phases = phase_ref[part]
        out_ref[0:72, :] = dot_nt(lattice, phases[0:128, :])
        out_ref[72:80, 0:72] = dot_nt(phases[128:grid_rows, :], lattice)
        out_ref[72:80, 72:128] = jnp.zeros((8, 56), f32)


def wave_weight(m0, m1, m2, cell_ref):
    w0 = two_pi * m0 / cell_ref[0]
    w1 = two_pi * m1 / cell_ref[1]
    w2 = two_pi * m2 / cell_ref[2]
    squared = w0 * w0 + w1 * w1 + w2 * w2
    return jnp.exp(-0.5 * smearing * smearing * squared) / squared


def phase_kernel(fractions_ref, hidden_ref, index_ref, phase_ref, third_ref, p0, p1):
    wide_kernel(hidden_ref, index_ref, p0, p1)
    atoms = fractions_ref.shape[1]
    orders = lax.broadcasted_iota(jnp.int32, (8, atoms), 0).astype(f32) + 1.0
    cosines, sines = [], []
    for axis in range(3):
        turns = orders * fractions_ref[axis : axis + 1, :]
        angle = two_pi * (turns - jnp.round(turns))
        cosines.append(jnp.cos(angle))
        sines.append(jnp.sin(angle))
    third_ref[0:8, :] = cosines[2]
    third_ref[8:16, :] = sines[2]
    for axis in range(3):
        third_ref[16 + axis : 17 + axis, :] = cosines[axis][0:1, :]
    c0, s0 = cosines[0], sines[0]
    for m in range(-kmax, kmax + 1):
        window = pl.ds((m + kmax) * kmax, kmax)
        if m == 0:
            re, im = c0, s0
        else:
            row = abs(m) - 1
            c1 = cosines[1][row : row + 1, :]
            s1 = sines[1][row : row + 1, :]
            if m < 0:
                s1 = -s1
            re, im = c0 * c1 - s0 * s1, s0 * c1 + c0 * s1
        phase_ref[0, window, :] = re.astype(bf16)
        phase_ref[1, window, :] = im.astype(bf16)


def weight_kernel(cell_ref, numbers_ref, lattice_ref, third_ref, weight_ref, born_ref, acc):
    total = jnp.sum(lattice_ref[64:68, :], axis=0, keepdims=True)
    born_ref[...] = total * third_ref[16:19, :]
    acc[...] = jnp.zeros_like(acc)
    width = math.gcd(numbers_ref.shape[1], 1024)
    plane_ids = lax.broadcasted_iota(jnp.int32, (grid_rows, width), 0)
    third_ids = lax.broadcasted_iota(jnp.int32, (32, width), 0)
    third_ids = jnp.where(
        third_ids < 8, third_ids + 1, jnp.where(third_ids < 16, 7 - third_ids, (third_ids - 16) * 64)
    )

    def count(step, carry):
        window = pl.ds(pl.multiple_of(step * width, width), width)
        numbers = numbers_ref[:, window]
        plane = (numbers[1:2, :] + kmax) * kmax + numbers[0:1, :] - 1
        in_plane = jnp.where(plane_ids == plane, 1.0, 0.0).astype(bf16)
        in_third = jnp.where(third_ids == numbers[2:3, :], 1.0, 0.0).astype(bf16)
        acc[...] += dot_nt(in_third, in_plane)
        return carry

    lax.fori_loop(0, numbers_ref.shape[1] // width, count, 0)
    lane = lax.broadcasted_iota(jnp.int32, (8, grid_rows), 1)
    m0 = (lane % 8 + 1).astype(f32)
    m1 = (lane // 8 - kmax).astype(f32)
    m2 = lax.broadcasted_iota(jnp.int32, (8, grid_rows), 0).astype(f32) + 1.0
    weight = wave_weight(m0, m1, m2, cell_ref)
    up = weight * acc[0:8, :]
    down = weight * acc[8:16, :]
    flat = wave_weight(m0, m1, 0.0 * m0, cell_ref) * acc[16:17, :]
    for c in range(4):
        weight_ref[8 * c : 8 * c + 8, :] = up
        weight_ref[32 + 8 * c : 40 + 8 * c, :] = down
    weight_ref[64:72, :] = flat


def force_kernel(
    scale,
    half_ref,
    other_ref,
    lattice_ref,
    phase_ref,
    weight_ref,
    cell_ref,
    count_ref,
    forces_ref,
    energy_ref,
    sums_ref,
):
    atoms = lattice_ref.shape[1]
    core = lax.rem(lax.axis_index("wide"), 2)
    for part_ref, part in ((half_ref, core), (other_ref, 1 - core)):
        sums_ref[part, :, 0:128] = part_ref[0:72, :]
        sums_ref[part, :, 128:grid_rows] = jnp.transpose(part_ref[72:80, :])[0:72, :]
    real = sums_ref[0]
    imag = sums_ref[1]
    real_cos, real_sin, real_flat = real[0:32], real[32:64], real[64:72]
    imag_cos, imag_sin, imag_flat = imag[0:32], imag[32:64], imag[64:72]
    weight_up = weight_ref[0:32, :]
    weight_down = weight_ref[32:64, :]
    weight_flat = weight_ref[64:72, :]
    up_re, up_im = real_cos - imag_sin, imag_cos + real_sin
    down_re, down_im = real_cos + imag_sin, imag_cos - real_sin
    up_im_w, up_re_w = weight_up * up_im, weight_up * up_re
    down_im_w, down_re_w = weight_down * down_im, weight_down * down_re
    flat_im_w, flat_re_w = weight_flat * imag_flat, weight_flat * real_flat
    power = up_im_w * up_im + up_re_w * up_re + down_im_w * down_im + down_re_w * down_re
    flat_power = flat_im_w * imag_flat + flat_re_w * real_flat
    power = jnp.sum(power, axis=0, keepdims=True) + jnp.sum(flat_power, axis=0, keepdims=True)
    energy_ref[...] = (0.5 * scale) * jnp.sum(power, axis=1, keepdims=True)

    im_sum, im_diff = up_im_w + down_im_w, up_im_w - down_im_w
    re_sum, re_diff = up_re_w + down_re_w, down_re_w - up_re_w
    even_real = jnp.concatenate([im_sum, re_diff, flat_im_w], axis=0)
    even_imag = jnp.concatenate([-re_sum, -im_diff, -flat_re_w], axis=0)
    m2 = (lax.broadcasted_iota(jnp.int32, (32, grid_rows), 0) % 8 + 1).astype(f32)
    odd_real = jnp.concatenate([m2 * im_diff, -m2 * re_sum], axis=0)
    odd_imag = jnp.concatenate([m2 * re_diff, -m2 * im_sum], axis=0)
    lane = lax.broadcasted_iota(jnp.int32, (72, grid_rows), 1)
    m0 = (lane % 8 + 1).astype(f32)
    m1 = (lane // 8 - kmax).astype(f32)
    with_real = jnp.concatenate([even_real * m0, even_real * m1, odd_real], axis=0).astype(bf16)
    with_imag = jnp.concatenate([even_imag * m0, even_imag * m1, odd_imag], axis=0).astype(bf16)
    back = dot_nn(with_real, phase_ref[0]) + dot_nn(with_imag, phase_ref[1])
    lattice = lattice_ref[...]
    alive = lax.broadcasted_iota(jnp.int32, (1, atoms), 1) < count_ref[...]
    for axis in range(3):
        rows = 64 if axis == 2 else 72
        terms = lattice[0:rows] * back[72 * axis : 72 * axis + rows]
        gradient = jnp.sum(terms, axis=0, keepdims=True)
        forces_ref[axis : axis + 1, :] = jnp.where(
            alive, -(two_pi * scale / cell_ref[axis]) * gradient, 0.0
        )


def call(kernel, outs, *args, smem=(), scratch=(), cost=None):
    specs = [
        pl.BlockSpec(memory_space=pltpu.SMEM if i in smem else pltpu.VMEM)
        for i in range(len(args))
    ]
    return pl.pallas_call(
        kernel,
        out_shape=[jax.ShapeDtypeStruct(shape, dtype) for shape, dtype in outs],
        in_specs=specs,
        out_specs=[pl.BlockSpec(memory_space=pltpu.VMEM)] * len(outs),
        scratch_shapes=list(scratch),
        compiler_params=params,
        cost_estimate=cost,
    )(*args)


def shifted(block, axis, step):
    count = lax.axis_size(axis)
    return lax.ppermute(block, axis, [(i, (i + step) % count) for i in range(count)])


def exchange_narrow(p2, p3):
    return shifted(p3, "narrow", 1), shifted(p2, "narrow", -1)


def exchange_wide(p0, p1):
    return shifted(p1, "wide", 1), shifted(p0, "wide", -1)


def flipped(block, axis, step):
    return lax.ppermute(block, axis, [(i, i ^ step) for i in range(lax.axis_size(axis))])


def summed(send, keep, beside):
    block = keep + flipped(send, "wide", 1)
    for axis, step in (("wide", 2), ("narrow", 1)):
        while step < lax.axis_size(axis):
            if axis == "narrow" and 2 * step >= lax.axis_size(axis):
                block, beside = lax.optimization_barrier((block, beside))
            block = block + flipped(block, axis, step)
            step *= 2
    return block, flipped(block, "wide", 1), beside


def per_device(
    fractions,
    cell_lengths,
    features,
    atom_counts,
    send_index,
    senders,
    radial,
    self_weight,
    message_weight,
    charge_weight,
    wave_numbers,
):
    atoms, width = features.shape
    ghosts = send_index.shape[1]
    rows = atoms + 4 * ghosts
    total_atoms = atoms * lax.axis_size("wide") * lax.axis_size("narrow")
    scale = 4.0 / math.sqrt(total_atoms * wave_numbers.shape[1])
    picked_outs = [((width, ghosts), f32)] * 2
    hidden_out = [((width, atoms), bf16)]
    sum_out = [((width, atoms), f32)]
    busy = pl.CostEstimate(flops=10**9, bytes_accessed=20 * 2**20, transcendentals=0)
    readout = charge_weight.T
    counts = atom_counts.reshape(1, 1)

    hidden, p2, p3 = call(
        first_kernel,
        hidden_out + picked_outs,
        features,
        send_index,
        cost=busy,
    )
    g2, g3 = exchange_narrow(p2, p3)
    far_edges, picks, p0, p1 = call(
        far_edge_kernel,
        [((2 * ghosts, atoms), bf16), ((atoms, 2 * ghosts), bf16)] + picked_outs,
        senders,
        radial,
        send_index,
        hidden,
        cost=busy,
    )
    g0, g1 = exchange_wide(p0, p1)
    layers = self_weight.shape[0]
    near_edges, self_rows, message_rows = call(
        near_edge_kernel,
        [
            ((rows - 2 * ghosts, atoms), bf16),
            ((layers, width, width), bf16),
            ((layers, width, 2 * width), bf16),
        ],
        senders,
        radial,
        self_weight,
        message_weight,
        cost=busy,
    )
    for layer in range(layers):
        own, gathered = call(
            functools.partial(near_kernel, layer), sum_out * 2, hidden, g2, g3, near_edges, self_rows
        )
        if layer == layers - 1:
            break
        hidden, p2, p3 = call(
            functools.partial(layer_kernel, layer),
            hidden_out + picked_outs,
            hidden,
            own,
            gathered,
            g0,
            g1,
            far_edges,
            message_rows,
            picks,
            cost=busy,
        )
        g2, g3 = exchange_narrow(p2, p3)
        phases, third, p0, p1 = call(
            phase_kernel,
            [((2, grid_rows, atoms), bf16), ((24, atoms), f32)] + picked_outs,
            fractions,
            hidden,
            send_index,
            cost=busy,
        )
        g0, g1 = exchange_wide(p0, p1)
    send, keep, lattice = call(
        functools.partial(last_kernel, layers - 1),
        [((half_rows, 128), f32)] * 2 + [((72, atoms), f32)],
        hidden,
        own,
        gathered,
        g0,
        g1,
        far_edges,
        message_rows,
        readout,
        counts,
        phases,
        third,
    )
    weights, born_charges = call(
        weight_kernel,
        [((72, grid_rows), f32), ((3, atoms), f32)],
        cell_lengths,
        wave_numbers,
        lattice,
        third,
        smem=(0,),
        scratch=[pltpu.VMEM((32, grid_rows), f32)],
        cost=busy,
    )
    half, other, weights = summed(send, keep, weights)
    forces, energy = call(
        functools.partial(force_kernel, scale),
        [((3, atoms), f32), ((1, 1), f32)],
        half,
        other,
        lattice,
        phases,
        weights,
        cell_lengths,
        counts,
        smem=(5,),
        scratch=[pltpu.VMEM((2, 72, grid_rows), f32)],
    )
    return (forces, born_charges, energy[0, 0])


def solution(mesh):
    return jax.shard_map(
        per_device,
        mesh=mesh,
        in_specs=(
            P(None, ("wide", "narrow")),
            P(),
            P(("wide", "narrow"), None),
            P(("wide", "narrow")),
            P(("wide", "narrow"), None),
            P(None, ("wide", "narrow")),
            P(None, ("wide", "narrow")),
            P(),
            P(),
            P(),
            P(),
        ),
        out_specs=(P(None, ("wide", "narrow")), P(None, ("wide", "narrow")), P()),
        check_vma=False,
    )
```

time: 53.9 us -> 52.2 us (0.968)
  Pallas kernels: 14.1 us -> 11.9 us
  starting transfers between devices: 20 us -> 20.7 us
    pallas_call x10, Pallas kernels: 14.1 us -> 11.9 us  [call(): pl.pallas_call(kernel, out_shape=[jax.ShapeDtypeStruct(shape, dtype) for...]
    ppermute x6, waiting for transfers between devices: 11 us -> 10.4 us  [flipped(): lax.ppermute(block, axis, [(i, i ^ step) for i in range(lax.axis_size(axi...]
    ppermute x8, waiting for transfers between devices: 5.22 us -> 5.84 us  [shifted(): lax.ppermute(block, axis, [(i, (i + step) % count) for i in range(count)])]
    ppermute x6, starting transfers between devices: 5.72 us -> 6.28 us  [flipped(): lax.ppermute(block, axis, [(i, i ^ step) for i in range(lax.axis_size(axi...]
    unnamed x21 -> x20, local copies, waits for them, and re-layouts: 1.77 us -> 1.63 us
  transfers between devices with their start and end apart: 14 -> 14, of which waited for: 9 -> 9; matrix products, arithmetic and copies ran while one was open for 0% -> 0% of each run, Pallas kernels for 18% -> 16%
where the time goes in v3:
time: 52.2 us; the launch traced here: 52 us
  starting transfers between devices  20.7 us (40%)
  waiting for transfers between devices  16.3 us (31%)
  Pallas kernels  11.9 us (23%)
  local copies, waits for them, and re-layouts  1.63 us (3%)
  between operations  1.47 us (3%)
    ppermute x8, starting transfers between devices, shifted(): lax.ppermute(block, axis, [(i, (i + step) % count) for i in range(count)])  14.4 us
    pallas_call x10, Pallas kernels, call(): pl.pallas_call(kernel, out_shape=[jax.ShapeDtypeStruct(shape, dtype) for...  11.9 us
    ppermute x6, waiting for transfers between devices, flipped(): lax.ppermute(block, axis, [(i, i ^ step) for i in range(lax.axis_size(axi...  10.4 us
    ppermute x6, starting transfers between devices, flipped(): lax.ppermute(block, axis, [(i, i ^ step) for i in range(lax.axis_size(axi...  6.28 us
    ppermute x8, waiting for transfers between devices, shifted(): lax.ppermute(block, axis, [(i, (i + step) % count) for i in range(count)])  5.84 us
    unnamed x20, local copies, waits for them, and re-layouts  1.63 us
  transfers between devices with their start and end apart: 14, of which 9 were waited for; matrix products, arithmetic and copies ran while one was open for 0% of the time, Pallas kernels for 16%

profile of v3, /device:TPU:0, one launch (start us, length us, event | category | flops | bytes accessed | tf_op | source)
XLA Modules:
  0.0 52.0 jit_solution(2623086083798163636)
XLA Ops:
  0.6 0.9 %copy-done.2 = bf16[512,128]{1,0:T(8,128)(2,1)S(1)} copy-done((bf16[512,128]{1,0:T(8,128)(2,1)S(1)}, bf16[512,128]{1,0:T(8,128)(2,1)}, u32[]{:S(2)}) %copy-start.2) | copy-done | bytes 131096
  1.5 0.7 %copy-done.9 = s32[4,384]{1,0:T(4,128)S(1)} copy-done((s32[4,384]{1,0:T(4,128)S(1)}, s32[4,384]{1,0:T(4,128)}, u32[]{:S(2)}) %copy-start.9) | copy-done | bytes 6168
  2.2 0.4 shard_map.130
  2.6 3.1 %collective-permute-start = (f32[128,384]{1,0:T(8,128)S(1)}, f32[128,384]{1,0:T(8,128)S(1)}, u32[]{:S(2)}, u32[]{:S(2)}) collective-permute-start(f32[128,384]{1,0:T(8,128)S(1)} %get-tuple-element.34), channel_id=1, source_target_pairs={{0,1},{1,2},{2,3},{3,0},{4,5},{5,6},{6,7},{7,4},{8,9},{9,10},{10,1... | collective-permute-start | bytes 589832 | tf_op jit(solution)/shard_map/ppermute | solution.py:310
  5.7 2.1 %collective-permute-start.1 = (f32[128,384]{1,0:T(8,128)S(1)}, f32[128,384]{1,0:T(8,128)S(1)}, u32[]{:S(2)}, u32[]{:S(2)}) collective-permute-start(f32[128,384]{1,0:T(8,128)S(1)} %get-tuple-element.35), channel_id=1, source_target_pairs={{0,3},{1,0},{2,1},{3,2},{4,7},{5,4},{6,5},{7,6},{8,11},{9,8},{10,9... | collective-permute-start | bytes 589832 | tf_op jit(solution)/shard_map/ppermute | solution.py:310
  7.8 1.9 %shard_map.133 = (bf16[768,512]{1,0:T(8,128)(2,1)S(1)}, bf16[512,768]{1,0:T(8,128)(2,1)S(1)}, f32[128,384]{1,0:T(8,128)S(1)}, f32[128,384]{1,0:T(8,128)S(1)}) custom-call(s32[16,512]{1,0:T(8,128)S(1)} %copy-done.6, f32[16,512]{1,0:T(8,128)S(1)} %copy-done.7, s32[4,384]{1,0:T(4,128)S(1)} %copy-done.9, bf16[128,512]{1,0:T(8,128)(2,1)S(1)} %get-tuple-element.33.hidden_ref), custom_call_target="tpu_custom_call" | custom-call | flops 1000000000 | bytes 20971520 | tf_op jit(solution)/shard_map/pallas_call | solution.py:297
  9.8 2.6 %collective-permute-start.3 = (f32[128,384]{1,0:T(8,128)S(1)}, f32[128,384]{1,0:T(8,128)S(1)}, u32[]{:S(2)}, u32[]{:S(2)}) collective-permute-start(f32[128,384]{1,0:T(8,128)S(1)} %get-tuple-element.41), channel_id=1, source_target_pairs={{0,28},{4,0},{8,4},{12,8},{16,12},{20,16},{24,20},{28,24},{1,29},{... | collective-permute-start | bytes 589832 | tf_op jit(solution)/shard_map/ppermute | solution.py:310
  12.4 2.6 %shard_map.131 = (bf16[1280,512]{1,0:T(8,128)(2,1)S(1)}, bf16[2,128,128]{2,1,0:T(8,128)(2,1)S(1)}, bf16[2,128,256]{2,1,0:T(8,128)(2,1)S(1)}) custom-call(s32[16,512]{1,0:T(8,128)S(1)} %copy-done.6, f32[16,512]{1,0:T(8,128)S(1)} %copy-done.7, bf16[2,128,128]{2,1,0:T(8,128)(2,1)S(1)} %copy-done.4, bf16[2,128,128]{2,1,0:T(8,128)(2,1)S(1)} %copy-done.5), custom_call_target="tpu_custom_call" | custom-call | flops 1000000000 | bytes 20971520 | tf_op jit(solution)/shard_map/pallas_call | solution.py:297
  15.0 1.2 %collective-permute-done.1.g3 = f32[128,384]{1,0:T(8,128)S(1)} collective-permute-done((f32[128,384]{1,0:T(8,128)S(1)}, f32[128,384]{1,0:T(8,128)S(1)}, u32[]{:S(2)}, u32[]{:S(2)}) %collective-permute-start.1) | collective-permute-done | bytes 196640 | tf_op jit(solution)/shard_map/ppermute | solution.py:310
  16.3 0.3 shard_map.132
  16.7 0.7 %shard_map.134 = (bf16[128,512]{1,0:T(8,128)(2,1)S(1)}, f32[128,384]{1,0:T(8,128)S(1)}, f32[128,384]{1,0:T(8,128)S(1)}) custom-call(bf16[128,512]{1,0:T(8,128)(2,1)S(1)} %get-tuple-element.33.hidden_ref, f32[128,512]{1,0:T(8,128)S(1)} %get-tuple-element.38.own_ref, f32[128,512]{1,0:T(8,128)S(1)} %get-tuple-element.39.gathered_ref, ...), custom_call_target="tpu_custom_call" | custom-call | flops 1000000000 | bytes 20971520 | tf_op jit(solution)/shard_map/pallas_call | solution.py:297
  17.3 1.2 %collective-permute-start.4 = (f32[128,384]{1,0:T(8,128)S(1)}, f32[128,384]{1,0:T(8,128)S(1)}, u32[]{:S(2)}, u32[]{:S(2)}) collective-permute-start(f32[128,384]{1,0:T(8,128)S(1)} %get-tuple-element.46), channel_id=1, source_target_pairs={{0,1},{1,2},{2,3},{3,0},{4,5},{5,6},{6,7},{7,4},{8,9},{9,10},{10,1... | collective-permute-start | bytes 589832 | tf_op jit(solution)/shard_map/ppermute | solution.py:310
  18.5 2.7 %collective-permute-start.5 = (f32[128,384]{1,0:T(8,128)S(1)}, f32[128,384]{1,0:T(8,128)S(1)}, u32[]{:S(2)}, u32[]{:S(2)}) collective-permute-start(f32[128,384]{1,0:T(8,128)S(1)} %get-tuple-element.47), channel_id=1, source_target_pairs={{0,3},{1,0},{2,1},{3,2},{4,7},{5,4},{6,5},{7,6},{8,11},{9,8},{10,9... | collective-permute-start | bytes 589832 | tf_op jit(solution)/shard_map/ppermute | solution.py:310
  21.2 0.5 %shard_map.136 = (bf16[2,136,512]{2,1,0:T(8,128)(2,1)S(1)}, f32[24,512]{1,0:T(8,128)S(1)}, f32[128,384]{1,0:T(8,128)S(1)}, f32[128,384]{1,0:T(8,128)S(1)}) custom-call(f32[3,512]{1,0:T(4,128)S(1)} %copy-done.8, bf16[128,512]{1,0:T(8,128)(2,1)S(1)} %get-tuple-element.45.hidden_ref, s32[4,384]{1,0:T(4,128)S(1)} %copy-done.9), custom_call_target="tpu_custom_call" | custom-call | flops 1000000000 | bytes 20971520 | tf_op jit(solution)/shard_map/pallas_call | solution.py:297
  21.8 0.7 %collective-permute-start.6 = (f32[128,384]{1,0:T(8,128)S(1)}, f32[128,384]{1,0:T(8,128)S(1)}, u32[]{:S(2)}, u32[]{:S(2)}) collective-permute-start(f32[128,384]{1,0:T(8,128)S(1)} %get-tuple-element.50), channel_id=1, source_target_pairs={{0,4},{4,8},{8,12},{12,16},{16,20},{20,24},{24,28},{28,0},{1,5},{5... | collective-permute-start | bytes 589832 | tf_op jit(solution)/shard_map/ppermute | solution.py:310
  22.5 2.0 %collective-permute-start.7 = (f32[128,384]{1,0:T(8,128)S(1)}, f32[128,384]{1,0:T(8,128)S(1)}, u32[]{:S(2)}, u32[]{:S(2)}) collective-permute-start(f32[128,384]{1,0:T(8,128)S(1)} %get-tuple-element.51), channel_id=1, source_target_pairs={{0,28},{4,0},{8,4},{12,8},{16,12},{20,16},{24,20},{28,24},{1,29},{... | collective-permute-start | bytes 589832 | tf_op jit(solution)/shard_map/ppermute | solution.py:310
  25.1 1.7 %collective-permute-done.4.g2 = f32[128,384]{1,0:T(8,128)S(1)} collective-permute-done((f32[128,384]{1,0:T(8,128)S(1)}, f32[128,384]{1,0:T(8,128)S(1)}, u32[]{:S(2)}, u32[]{:S(2)}) %collective-permute-start.4) | collective-permute-done | bytes 196640 | tf_op jit(solution)/shard_map/ppermute | solution.py:310
  26.9 2.9 %collective-permute-done.5.g3 = f32[128,384]{1,0:T(8,128)S(1)} collective-permute-done((f32[128,384]{1,0:T(8,128)S(1)}, f32[128,384]{1,0:T(8,128)S(1)}, u32[]{:S(2)}, u32[]{:S(2)}) %collective-permute-start.5) | collective-permute-done | bytes 196640 | tf_op jit(solution)/shard_map/ppermute | solution.py:310
  29.7 0.3 shard_map.135
  30.1 0.9 %shard_map.137 = (f32[80,128]{1,0:T(8,128)S(1)}, f32[80,128]{1,0:T(8,128)S(1)}, f32[72,512]{1,0:T(8,128)S(1)}) custom-call(bf16[128,512]{1,0:T(8,128)(2,1)S(1)} %get-tuple-element.45.hidden_ref, f32[128,512]{1,0:T(8,128)S(1)} %get-tuple-element.48.own_ref, f32[128,512]{1,0:T(8,128)S(1)} %get-tuple-element.49.gathered_ref, ...), custom_call_target="tpu_custom_call" | custom-call | tf_op jit(solution)/shard_map/pallas_call | solution.py:297
  31.0 0.3 collective-permute-start.8
  31.3 1.0 %collective-permute-done.8 = f32[80,128]{1,0:T(8,128)S(1)} collective-permute-done((f32[80,128]{1,0:T(8,128)S(1)}, f32[80,128]{1,0:T(8,128)S(1)}, u32[]{:S(2)}, u32[]{:S(2)}) %collective-permute-start.8) | collective-permute-done | bytes 40992 | tf_op jit(solution)/shard_map/ppermute | solution.py:322
  32.3 1.5 %collective-permute-start.9 = (f32[80,128]{1,0:T(8,128)S(1)}, f32[80,128]{1,0:T(8,128)S(1)}, u32[]{:S(2)}, u32[]{:S(2)}) collective-permute-start(f32[80,128]{1,0:T(8,128)S(1)} %add.15), channel_id=1, source_target_pairs={{0,8},{4,12},{8,0},{12,4},{16,24},{20,28},{24,16},{28,20},{1,9},{5... | collective-permute-start | bytes 122888 | tf_op jit(solution)/shard_map/ppermute | solution.py:322
  33.8 2.5 %collective-permute-done.9 = f32[80,128]{1,0:T(8,128)S(1)} collective-permute-done((f32[80,128]{1,0:T(8,128)S(1)}, f32[80,128]{1,0:T(8,128)S(1)}, u32[]{:S(2)}, u32[]{:S(2)}) %collective-permute-start.9) | collective-permute-done | bytes 40992 | tf_op jit(solution)/shard_map/ppermute | solution.py:322
  36.3 1.7 %collective-permute-start.10 = (f32[80,128]{1,0:T(8,128)S(1)}, f32[80,128]{1,0:T(8,128)S(1)}, u32[]{:S(2)}, u32[]{:S(2)}) collective-permute-start(f32[80,128]{1,0:T(8,128)S(1)} %add.16), channel_id=1, source_target_pairs={{0,16},{4,20},{8,24},{12,28},{16,0},{20,4},{24,8},{28,12},{1,17},{... | collective-permute-start | bytes 122888 | tf_op jit(solution)/shard_map/ppermute | solution.py:322
  38.0 2.3 %collective-permute-done.10 = f32[80,128]{1,0:T(8,128)S(1)} collective-permute-done((f32[80,128]{1,0:T(8,128)S(1)}, f32[80,128]{1,0:T(8,128)S(1)}, u32[]{:S(2)}, u32[]{:S(2)}) %collective-permute-start.10) | collective-permute-done | bytes 40992 | tf_op jit(solution)/shard_map/ppermute | solution.py:322
  40.3 1.0 %collective-permute-start.11 = (f32[80,128]{1,0:T(8,128)S(1)}, f32[80,128]{1,0:T(8,128)S(1)}, u32[]{:S(2)}, u32[]{:S(2)}) collective-permute-start(f32[80,128]{1,0:T(8,128)S(1)} %add.17), channel_id=1, source_target_pairs={{0,1},{1,0},{2,3},{3,2},{4,5},{5,4},{6,7},{7,6},{8,9},{9,8},{10,11... | collective-permute-start | bytes 122888 | tf_op jit(solution)/shard_map/ppermute | solution.py:322
  41.3 2.7 %shard_map.138 = (f32[72,136]{1,0:T(8,128)S(1)}, f32[3,512]{1,0:T(4,128)}) custom-call(f32[3]{0:T(128)S(1)} %copy-done.1, s32[3,8192]{1,0:T(4,128)S(1)} %copy-done.3, f32[72,512]{1,0:T(8,128)S(1)} %get-tuple-element.56.lattice_ref, f32[24,512]{1,0:T(8,128)S(1)} %get-tuple-element.53.third_ref), custom_call_target="tpu_custom_call" | custom-call | flops 1000000000 | bytes 20971520 | tf_op jit(solution)/shard_map/pallas_call | solution.py:297
  44.3 1.8 %collective-permute-start.12 = (f32[80,128]{1,0:T(8,128)S(1)}, f32[80,128]{1,0:T(8,128)S(1)}, u32[]{:S(2)}, u32[]{:S(2)}) collective-permute-start(f32[80,128]{1,0:T(8,128)S(1)} %add.18), channel_id=1, source_target_pairs={{0,2},{1,3},{2,0},{3,1},{4,6},{5,7},{6,4},{7,5},{8,10},{9,11},{10,... | collective-permute-start | bytes 122888 | tf_op jit(solution)/shard_map/ppermute | solution.py:322
  46.1 3.1 %collective-permute-done.12 = f32[80,128]{1,0:T(8,128)S(1)} collective-permute-done((f32[80,128]{1,0:T(8,128)S(1)}, f32[80,128]{1,0:T(8,128)S(1)}, u32[]{:S(2)}, u32[]{:S(2)}) %collective-permute-start.12) | collective-permute-done | bytes 40992 | tf_op jit(solution)/shard_map/ppermute | solution.py:322
  49.3 1.2 %collective-permute-done.13.other_ref = f32[80,128]{1,0:T(8,128)S(1)} collective-permute-done((f32[80,128]{1,0:T(8,128)S(1)}, f32[80,128]{1,0:T(8,128)S(1)}, u32[]{:S(2)}, u32[]{:S(2)}) %collective-permute-start.13) | collective-permute-done | bytes 40992 | tf_op jit(solution)/shard_map/ppermute | solution.py:322
  50.5 1.5 %shard_map.139 = (f32[3,512]{1,0:T(4,128)}, f32[1,1]{1,0:T(1,128)}) custom-call(f32[80,128]{1,0:T(8,128)S(1)} %add.19.half_ref, f32[80,128]{1,0:T(8,128)S(1)} %collective-permute-done.13.other_ref, f32[72,512]{1,0:T(8,128)S(1)} %get-tuple-element.56.lattice_ref, bf16[2,136,512]{2,1,0:T(8,128)(2,1)S(1)} %get-tuple-element.52.phase_ref, ...), custom_call_target="tpu_custom_call" | custom-call | tf_op jit(solution)/shard_map/pallas_call | solution.py:297
  (31 shorter events, 0.4 us)
Async XLA Ops:
  0.6 0.9 %copy-start.2 = (bf16[512,128]{1,0:T(8,128)(2,1)S(1)}, bf16[512,128]{1,0:T(8,128)(2,1)}, u32[]{:S(2)}) copy-start(bf16[512,128]{1,0:T(8,128)(2,1)} %features_ref.1) | copy-start | bytes 393220
  1.5 0.7 %copy-start.9 = (s32[4,384]{1,0:T(4,128)S(1)}, s32[4,384]{1,0:T(4,128)}, u32[]{:S(2)}) copy-start(s32[4,384]{1,0:T(4,128)} %index_ref.5) | copy-start | bytes 18436
  2.2 5.6 %copy-start.6 = (s32[16,512]{1,0:T(8,128)S(1)}, s32[16,512]{1,0:T(8,128)}, u32[]{:S(2)}) copy-start(s32[16,512]{1,0:T(8,128)} %senders_ref.3) | copy-start | bytes 98308
  2.2 5.6 %copy-start.7 = (f32[16,512]{1,0:T(8,128)S(1)}, f32[16,512]{1,0:T(8,128)}, u32[]{:S(2)}) copy-start(f32[16,512]{1,0:T(8,128)} %radial_ref.3) | copy-start | bytes 98308
  2.6 12.4 %collective-permute-start = (f32[128,384]{1,0:T(8,128)S(1)}, f32[128,384]{1,0:T(8,128)S(1)}, u32[]{:S(2)}, u32[]{:S(2)}) collective-permute-start(f32[128,384]{1,0:T(8,128)S(1)} %get-tuple-element.34), channel_id=1, source_target_pairs={{0,1},{1,2},{2,3},{3,0},{4,5},{5,6},{6,7},{7,4},{8,9},{9,10},{10,1... | collective-permute-start | bytes 589832 | tf_op jit(solution)/shard_map/ppermute | solution.py:310
  5.7 10.6 %collective-permute-start.1 = (f32[128,384]{1,0:T(8,128)S(1)}, f32[128,384]{1,0:T(8,128)S(1)}, u32[]{:S(2)}, u32[]{:S(2)}) collective-permute-start(f32[128,384]{1,0:T(8,128)S(1)} %get-tuple-element.35), channel_id=1, source_target_pairs={{0,3},{1,0},{2,1},{3,2},{4,7},{5,4},{6,5},{7,6},{8,11},{9,8},{10,9... | collective-permute-start | bytes 589832 | tf_op jit(solution)/shard_map/ppermute | solution.py:310
  7.8 4.6 %copy-start.4 = (bf16[2,128,128]{2,1,0:T(8,128)(2,1)S(1)}, bf16[2,128,128]{2,1,0:T(8,128)(2,1)}, u32[]{:S(2)}) copy-start(bf16[2,128,128]{2,1,0:T(8,128)(2,1)} %self_ref.1) | copy-start | bytes 196612
  7.8 4.6 %copy-start.5 = (bf16[2,128,128]{2,1,0:T(8,128)(2,1)S(1)}, bf16[2,128,128]{2,1,0:T(8,128)(2,1)}, u32[]{:S(2)}) copy-start(bf16[2,128,128]{2,1,0:T(8,128)(2,1)} %message_ref.1) | copy-start | bytes 196612
  9.7 6.9 %collective-permute-start.2 = (f32[128,384]{1,0:T(8,128)S(1)}, f32[128,384]{1,0:T(8,128)S(1)}, u32[]{:S(2)}, u32[]{:S(2)}) collective-permute-start(f32[128,384]{1,0:T(8,128)S(1)} %get-tuple-element.40), channel_id=1, source_target_pairs={{0,4},{4,8},{8,12},{12,16},{16,20},{20,24},{24,28},{28,0},{1,5},{5... | collective-permute-start | bytes 589832 | tf_op jit(solution)/shard_map/ppermute | solution.py:310
  9.8 6.9 %collective-permute-start.3 = (f32[128,384]{1,0:T(8,128)S(1)}, f32[128,384]{1,0:T(8,128)S(1)}, u32[]{:S(2)}, u32[]{:S(2)}) collective-permute-start(f32[128,384]{1,0:T(8,128)S(1)} %get-tuple-element.41), channel_id=1, source_target_pairs={{0,28},{4,0},{8,4},{12,8},{16,12},{20,16},{24,20},{28,24},{1,29},{... | collective-permute-start | bytes 589832 | tf_op jit(solution)/shard_map/ppermute | solution.py:310
  16.6 4.6 %copy-start.8 = (f32[3,512]{1,0:T(4,128)S(1)}, f32[3,512]{1,0:T(4,128)}, u32[]{:S(2)}) copy-start(f32[3,512]{1,0:T(4,128)} %fractions_ref.1) | copy-start | bytes 18436
  17.3 9.5 %collective-permute-start.4 = (f32[128,384]{1,0:T(8,128)S(1)}, f32[128,384]{1,0:T(8,128)S(1)}, u32[]{:S(2)}, u32[]{:S(2)}) collective-permute-start(f32[128,384]{1,0:T(8,128)S(1)} %get-tuple-element.46), channel_id=1, source_target_pairs={{0,1},{1,2},{2,3},{3,0},{4,5},{5,6},{6,7},{7,4},{8,9},{9,10},{10,1... | collective-permute-start | bytes 589832 | tf_op jit(solution)/shard_map/ppermute | solution.py:310
  18.5 11.2 %collective-permute-start.5 = (f32[128,384]{1,0:T(8,128)S(1)}, f32[128,384]{1,0:T(8,128)S(1)}, u32[]{:S(2)}, u32[]{:S(2)}) collective-permute-start(f32[128,384]{1,0:T(8,128)S(1)} %get-tuple-element.47), channel_id=1, source_target_pairs={{0,3},{1,0},{2,1},{3,2},{4,7},{5,4},{6,5},{7,6},{8,11},{9,8},{10,9... | collective-permute-start | bytes 589832 | tf_op jit(solution)/shard_map/ppermute | solution.py:310
  21.8 8.3 %copy-start = (bf16[128,4]{0,1:T(4,128)(2,1)S(1)}, bf16[128,4]{0,1:T(4,128)(2,1)}, u32[]{:S(2)}) copy-start(bf16[128,4]{0,1:T(4,128)(2,1)} %param.20) | copy-start | bytes 3076
  21.8 8.3 %collective-permute-start.6 = (f32[128,384]{1,0:T(8,128)S(1)}, f32[128,384]{1,0:T(8,128)S(1)}, u32[]{:S(2)}, u32[]{:S(2)}) collective-permute-start(f32[128,384]{1,0:T(8,128)S(1)} %get-tuple-element.50), channel_id=1, source_target_pairs={{0,4},{4,8},{8,12},{12,16},{16,20},{20,24},{24,28},{28,0},{1,5},{5... | collective-permute-start | bytes 589832 | tf_op jit(solution)/shard_map/ppermute | solution.py:310
  22.5 7.6 %collective-permute-start.7 = (f32[128,384]{1,0:T(8,128)S(1)}, f32[128,384]{1,0:T(8,128)S(1)}, u32[]{:S(2)}, u32[]{:S(2)}) collective-permute-start(f32[128,384]{1,0:T(8,128)S(1)} %get-tuple-element.51), channel_id=1, source_target_pairs={{0,28},{4,0},{8,4},{12,8},{16,12},{20,16},{24,20},{28,24},{1,29},{... | collective-permute-start | bytes 589832 | tf_op jit(solution)/shard_map/ppermute | solution.py:310
  30.1 11.2 %copy-start.1 = (f32[3]{0:T(128)S(1)}, f32[3]{0:T(128)}, u32[]{:S(2)}) copy-start(f32[3]{0:T(128)} %cell_ref.3) | copy-start | bytes 40
  30.1 11.2 %copy-start.3 = (s32[3,8192]{1,0:T(4,128)S(1)}, s32[3,8192]{1,0:T(4,128)}, u32[]{:S(2)}) copy-start(s32[3,8192]{1,0:T(4,128)} %numbers_ref.1) | copy-start | bytes 294916
  31.0 1.3 %collective-permute-start.8 = (f32[80,128]{1,0:T(8,128)S(1)}, f32[80,128]{1,0:T(8,128)S(1)}, u32[]{:S(2)}, u32[]{:S(2)}) collective-permute-start(f32[80,128]{1,0:T(8,128)S(1)} %get-tuple-element.55), channel_id=1, source_target_pairs={{0,4},{4,0},{8,12},{12,8},{16,20},{20,16},{24,28},{28,24},{1,5},{5... | collective-permute-start | bytes 122888 | tf_op jit(solution)/shard_map/ppermute | solution.py:322
  32.3 4.0 %collective-permute-start.9 = (f32[80,128]{1,0:T(8,128)S(1)}, f32[80,128]{1,0:T(8,128)S(1)}, u32[]{:S(2)}, u32[]{:S(2)}) collective-permute-start(f32[80,128]{1,0:T(8,128)S(1)} %add.15), channel_id=1, source_target_pairs={{0,8},{4,12},{8,0},{12,4},{16,24},{20,28},{24,16},{28,20},{1,9},{5... | collective-permute-start | bytes 122888 | tf_op jit(solution)/shard_map/ppermute | solution.py:322
  36.3 4.0 %collective-permute-start.10 = (f32[80,128]{1,0:T(8,128)S(1)}, f32[80,128]{1,0:T(8,128)S(1)}, u32[]{:S(2)}, u32[]{:S(2)}) collective-permute-start(f32[80,128]{1,0:T(8,128)S(1)} %add.16), channel_id=1, source_target_pairs={{0,16},{4,20},{8,24},{12,28},{16,0},{20,4},{24,8},{28,12},{1,17},{... | collective-permute-start | bytes 122888 | tf_op jit(solution)/shard_map/ppermute | solution.py:322
  40.3 4.0 %collective-permute-start.11 = (f32[80,128]{1,0:T(8,128)S(1)}, f32[80,128]{1,0:T(8,128)S(1)}, u32[]{:S(2)}, u32[]{:S(2)}) collective-permute-start(f32[80,128]{1,0:T(8,128)S(1)} %add.17), channel_id=1, source_target_pairs={{0,1},{1,0},{2,3},{3,2},{4,5},{5,4},{6,7},{7,6},{8,9},{9,8},{10,11... | collective-permute-start | bytes 122888 | tf_op jit(solution)/shard_map/ppermute | solution.py:322
  44.3 4.9 %collective-permute-start.12 = (f32[80,128]{1,0:T(8,128)S(1)}, f32[80,128]{1,0:T(8,128)S(1)}, u32[]{:S(2)}, u32[]{:S(2)}) collective-permute-start(f32[80,128]{1,0:T(8,128)S(1)} %add.18), channel_id=1, source_target_pairs={{0,2},{1,3},{2,0},{3,1},{4,6},{5,7},{6,4},{7,5},{8,10},{9,11},{10,... | collective-permute-start | bytes 122888 | tf_op jit(solution)/shard_map/ppermute | solution.py:322
  49.2 1.2 %collective-permute-start.13 = (f32[80,128]{1,0:T(8,128)S(1)}, f32[80,128]{1,0:T(8,128)S(1)}, u32[]{:S(2)}, u32[]{:S(2)}) collective-permute-start(f32[80,128]{1,0:T(8,128)S(1)} %add.19.half_ref), channel_id=1, source_target_pairs={{0,4},{4,0},{8,12},{12,8},{16,20},{20,16},{24,28},{28,24},{1,5},{5... | collective-permute-start | bytes 122888 | tf_op jit(solution)/shard_map/ppermute | solution.py:322

commit v4 on v3

--- a/solution.py
+++ b/solution.py
@@ -26,42 +26,61 @@
     return lax.dot_general(a, b, (((1,), (1,)), ((), ())), preferred_element_type=f32)
 
 
+def parity(axis):
+    return lax.rem(lax.axis_index(axis), 2)
+
+
+def block_order(axis):
+    odd = parity(axis)
+    first = 0 if axis == "wide" else 2
+    return first + odd, first + 1 - odd
+
+
 def pick_matrix(index_ref, block, atoms):
     row_ids = lax.broadcasted_iota(jnp.int32, (atoms, index_ref.shape[1]), 0)
-    return jnp.where(row_ids == index_ref[block : block + 1, :], 1.0, 0.0).astype(bf16)
-
-
-def first_kernel(features_ref, index_ref, hidden_ref, p2, p3):
+    return jnp.where(row_ids == index_ref[pl.ds(block, 1), :], 1.0, 0.0).astype(bf16)
+
+
+def opening_kernel(opened_ref):
+    opened_ref[...] = jnp.zeros(opened_ref.shape, f32)
+
+
+def first_kernel(opened_ref, features_ref, index_ref, hidden_ref, pa, pb):
     hidden = jnp.transpose(features_ref[...].astype(f32)).astype(bf16)
     hidden_ref[...] = hidden
-    for block, picked_ref in ((2, p2), (3, p3)):
+    for block, picked_ref in zip(block_order("narrow"), (pa, pb)):
         picked_ref[...] = dot_nn(hidden, pick_matrix(index_ref, block, hidden.shape[1]))
 
 
-def wide_kernel(hidden_ref, index_ref, p0, p1):
+def wide_kernel(hidden_ref, index_ref, pa, pb):
     hidden = hidden_ref[...]
-    for block, picked_ref in ((0, p0), (1, p1)):
+    for block, picked_ref in zip(block_order("wide"), (pa, pb)):
         picked_ref[...] = dot_nn(hidden, pick_matrix(index_ref, block, hidden.shape[1]))
 
 
-def edge_tiles(senders_ref, radial_ref, edges_ref, skip_from, skip):
+def edge_tiles(senders_ref, radial_ref, edges_ref, local, axis):
     slots, atoms = senders_ref.shape
     rows = 128
     lanes = 128
     row_ids = lax.broadcasted_iota(jnp.int32, (rows, lanes), 0).astype(f32).astype(bf16)
+    ghosts = (edges_ref.shape[0] - local) // 2
+    one, two = block_order(axis)
+    skip_one = atoms + one * ghosts - local
+    skip_two = atoms + two * ghosts - local - ghosts
 
     def one_tile(tile, carry):
         first = pl.multiple_of(tile * rows, rows)
-        sender = jnp.where(first >= skip_from, first + skip, first)
+        skip = jnp.where(first < local, 0, jnp.where(first < local + ghosts, skip_one, skip_two))
+        sender = first + skip
         for part in range(atoms // lanes):
             window = pl.ds(part * lanes, lanes)
-            local = jnp.clip(senders_ref[:, window] - sender, -1, rows)
-            local = local.astype(f32).astype(bf16)
+            local_row = jnp.clip(senders_ref[:, window] - sender, -1, rows)
+            local_row = local_row.astype(f32).astype(bf16)
             weight = radial_ref[:, window].astype(bf16)
             total = jnp.zeros((rows, lanes), bf16)
             for slot in range(slots):
                 total = total + jnp.where(
-                    row_ids == local[slot : slot + 1, :],
+                    row_ids == local_row[slot : slot + 1, :],
                     weight[slot : slot + 1, :],
                     jnp.zeros((), bf16),
                 )
@@ -71,31 +90,36 @@
     lax.fori_loop(0, edges_ref.shape[0] // rows, one_tile, 0)
 
 
-def far_edge_kernel(senders_ref, radial_ref, index_ref, hidden_ref, edges_ref, pick_ref, p0, p1):
+def far_edge_kernel(senders_ref, radial_ref, index_ref, hidden_ref, edges_ref, pick_ref, pa, pb):
+    wide_kernel(hidden_ref, index_ref, pa, pb)
     ghosts = index_ref.shape[1]
-    for block in (2, 3):
-        window = pl.ds((block - 2) * ghosts, ghosts)
-        pick_ref[:, window] = pick_matrix(index_ref, block, senders_ref.shape[1])
-    wide_kernel(hidden_ref, index_ref, p0, p1)
-    edge_tiles(senders_ref, radial_ref, edges_ref, 0, senders_ref.shape[1])
+    for i, block in enumerate(block_order("narrow")):
+        pick_ref[:, i * ghosts : (i + 1) * ghosts] = pick_matrix(
+            index_ref, block, senders_ref.shape[1]
+        )
+    edge_tiles(senders_ref, radial_ref, edges_ref, 0, "wide")
 
 
 def near_edge_kernel(
     senders_ref, radial_ref, self_ref, message_ref, edges_ref, self_rows_ref, message_rows_ref
 ):
-    atoms = senders_ref.shape[1]
-    edge_tiles(senders_ref, radial_ref, edges_ref, atoms, edges_ref.shape[0] - atoms)
+    edge_tiles(senders_ref, radial_ref, edges_ref, senders_ref.shape[1], "narrow")
     for layer in range(self_ref.shape[0]):
         self_rows_ref[layer] = jnp.transpose(self_ref[layer].astype(f32)).astype(bf16)
         message = jnp.transpose(message_ref[layer].astype(f32)).astype(bf16)
         message_rows_ref[layer] = jnp.concatenate([message, message], axis=1)
 
 
-def near_kernel(layer, hidden_ref, g2, g3, edges_ref, self_rows_ref, own_ref, gathered_ref):
+def local_kernel(layer, hidden_ref, edges_ref, self_rows_ref, own_ref, gathered_ref):
     hidden = hidden_ref[...]
     own_ref[...] = dot_nn(self_rows_ref[layer], hidden)
-    known = jnp.concatenate([hidden, g2[...].astype(bf16), g3[...].astype(bf16)], axis=1)
-    gathered_ref[...] = dot_nn(known, edges_ref[...])
+    gathered_ref[...] = dot_nn(hidden, edges_ref[0 : hidden.shape[1], :])
+
+
+def near_kernel(gathered_ref, g2, g3, edges_ref, sum_ref):
+    received = jnp.concatenate([g2[...].astype(bf16), g3[...].astype(bf16)], axis=1)
+    local = edges_ref.shape[0] - received.shape[1]
+    sum_ref[...] = gathered_ref[...] + dot_nn(received, edges_ref[local:, :])
 
 
 def interact(layer, hidden_ref, own_ref, gathered_ref, g0, g1, edges_ref, message_rows_ref):
@@ -149,7 +173,7 @@
     lattice = jnp.concatenate(rows + [charges], axis=0)
     lattice_ref[...] = lattice
     lattice = lattice.astype(bf16)
-    core = lax.rem(lax.axis_index("wide"), 2)
+    core = parity("wide")
     for out_ref, part in ((keep_ref, core), (send_ref, 1 - core)):
         phases = phase_ref[part]
         out_ref[0:72, :] = dot_nt(lattice, phases[0:128, :])
@@ -195,7 +219,21 @@
         phase_ref[1, window, :] = im.astype(bf16)
 
 
-def weight_kernel(cell_ref, numbers_ref, lattice_ref, third_ref, weight_ref, born_ref, acc):
+def weight_kernel(
+    scale,
+    cell_ref,
+    numbers_ref,
+    lattice_ref,
+    third_ref,
+    count_ref,
+    weight_ref,
+    factor_ref,
+    born_ref,
+    acc,
+):
+    alive = lax.broadcasted_iota(jnp.int32, (1, lattice_ref.shape[1]), 1) < count_ref[...]
+    for axis in range(3):
+        factor_ref[axis : axis + 1, :] = jnp.where(alive, -(two_pi * scale / cell_ref[axis]), 0.0)
     total = jnp.sum(lattice_ref[64:68, :], axis=0, keepdims=True)
     born_ref[...] = total * third_ref[16:19, :]
     acc[...] = jnp.zeros_like(acc)
@@ -237,14 +275,12 @@
     lattice_ref,
     phase_ref,
     weight_ref,
-    cell_ref,
-    count_ref,
+    factor_ref,
     forces_ref,
     energy_ref,
     sums_ref,
 ):
-    atoms = lattice_ref.shape[1]
-    core = lax.rem(lax.axis_index("wide"), 2)
+    core = parity("wide")
     for part_ref, part in ((half_ref, core), (other_ref, 1 - core)):
         sums_ref[part, :, 0:128] = part_ref[0:72, :]
         sums_ref[part, :, 128:grid_rows] = jnp.transpose(part_ref[72:80, :])[0:72, :]
@@ -279,14 +315,11 @@
     with_imag = jnp.concatenate([even_imag * m0, even_imag * m1, odd_imag], axis=0).astype(bf16)
     back = dot_nn(with_real, phase_ref[0]) + dot_nn(with_imag, phase_ref[1])
     lattice = lattice_ref[...]
-    alive = lax.broadcasted_iota(jnp.int32, (1, atoms), 1) < count_ref[...]
     for axis in range(3):
         rows = 64 if axis == 2 else 72
         terms = lattice[0:rows] * back[72 * axis : 72 * axis + rows]
         gradient = jnp.sum(terms, axis=0, keepdims=True)
-        forces_ref[axis : axis + 1, :] = jnp.where(
-            alive, -(two_pi * scale / cell_ref[axis]) * gradient, 0.0
-        )
+        forces_ref[axis : axis + 1, :] = factor_ref[axis : axis + 1, :] * gradient
 
 
 def call(kernel, outs, *args, smem=(), scratch=(), cost=None):
@@ -305,17 +338,12 @@
     )(*args)
 
 
-def shifted(block, axis, step):
+def matched(first, second, axis):
     count = lax.axis_size(axis)
-    return lax.ppermute(block, axis, [(i, (i + step) % count) for i in range(count)])
-
-
-def exchange_narrow(p2, p3):
-    return shifted(p3, "narrow", 1), shifted(p2, "narrow", -1)
-
-
-def exchange_wide(p0, p1):
-    return shifted(p1, "wide", 1), shifted(p0, "wide", -1)
+    ways = (-1, 1)
+    one = lax.ppermute(first, axis, [(i, (i + ways[i % 2]) % count) for i in range(count)])
+    two = lax.ppermute(second, axis, [(i, (i - ways[i % 2]) % count) for i in range(count)])
+    return one, two
 
 
 def flipped(block, axis, step):
@@ -358,14 +386,16 @@
     readout = charge_weight.T
     counts = atom_counts.reshape(1, 1)
 
+    (opened,) = call(opening_kernel, [((8, 128), f32)], cost=busy)
     hidden, p2, p3 = call(
         first_kernel,
         hidden_out + picked_outs,
+        opened,
         features,
         send_index,
         cost=busy,
     )
-    g2, g3 = exchange_narrow(p2, p3)
+    g2, g3 = matched(p2, p3, "narrow")
     far_edges, picks, p0, p1 = call(
         far_edge_kernel,
         [((2 * ghosts, atoms), bf16), ((atoms, 2 * ghosts), bf16)] + picked_outs,
@@ -375,7 +405,7 @@
         hidden,
         cost=busy,
     )
-    g0, g1 = exchange_wide(p0, p1)
+    g0, g1 = matched(p0, p1, "wide")
     layers = self_weight.shape[0]
     near_edges, self_rows, message_rows = call(
         near_edge_kernel,
@@ -392,8 +422,9 @@
     )
     for layer in range(layers):
         own, gathered = call(
-            functools.partial(near_kernel, layer), sum_out * 2, hidden, g2, g3, near_edges, self_rows
+            functools.partial(local_kernel, layer), sum_out * 2, hidden, near_edges, self_rows, cost=busy
         )
+        (gathered,) = call(near_kernel, sum_out, gathered, g2, g3, near_edges)
         if layer == layers - 1:
             break
         hidden, p2, p3 = call(
@@ -409,7 +440,7 @@
             picks,
             cost=busy,
         )
-        g2, g3 = exchange_narrow(p2, p3)
+        g2, g3 = matched(p2, p3, "narrow")
         phases, third, p0, p1 = call(
             phase_kernel,
             [((2, grid_rows, atoms), bf16), ((24, atoms), f32)] + picked_outs,
@@ -418,7 +449,7 @@
             send_index,
             cost=busy,
         )
-        g0, g1 = exchange_wide(p0, p1)
+        g0, g1 = matched(p0, p1, "wide")
     send, keep, lattice = call(
         functools.partial(last_kernel, layers - 1),
         [((half_rows, 128), f32)] * 2 + [((72, atoms), f32)],
@@ -434,18 +465,19 @@
         phases,
         third,
     )
-    weights, born_charges = call(
-        weight_kernel,
-        [((72, grid_rows), f32), ((3, atoms), f32)],
+    weights, factor, born_charges = call(
+        functools.partial(weight_kernel, scale),
+        [((72, grid_rows), f32), ((8, atoms), f32), ((3, atoms), f32)],
         cell_lengths,
         wave_numbers,
         lattice,
         third,
+        counts,
         smem=(0,),
         scratch=[pltpu.VMEM((32, grid_rows), f32)],
         cost=busy,
     )
-    half, other, weights = summed(send, keep, weights)
+    half, other, (weights, factor) = summed(send, keep, (weights, factor))
     forces, energy = call(
         functools.partial(force_kernel, scale),
         [((3, atoms), f32), ((1, 1), f32)],
@@ -454,9 +486,7 @@
         lattice,
         phases,
         weights,
-        cell_lengths,
-        counts,
-        smem=(5,),
+        factor,
         scratch=[pltpu.VMEM((2, 72, grid_rows), f32)],
     )
     return (forces, born_charges, energy[0, 0])

time: 52.2 us -> 50.5 us (0.967)
  starting transfers between devices: 20.7 us -> 15.8 us
  waiting for transfers between devices: 16.3 us -> 20.4 us
  local copies, waits for them, and re-layouts: 1.63 us -> 0.92 us
    ppermute x8, starting transfers between devices: 14.4 us -> 9.81 us  [the longest x4 8.91 us: matched(): lax.ppermute(first, axis, [(i, (i + ways[i % 2]) % count) for i in range(...]
    ppermute x8, waiting for transfers between devices: 5.84 us -> 9.69 us  [the longest x4 5.71 us: matched(): lax.ppermute(first, axis, [(i, (i + ways[i % 2]) % count) for i in range(...]
    unnamed x20, local copies, waits for them, and re-layouts: 1.63 us -> 0.92 us
    pallas_call x10 -> x13, Pallas kernels: 11.9 us -> 11.8 us  [call(): pl.pallas_call(kernel, out_shape=[jax.ShapeDtypeStruct(shape, dtype) for...]
  transfers between devices with their start and end apart: 14 -> 14, of which waited for: 9 -> 10; matrix products, arithmetic and copies ran while one was open for 0% -> 0% of each run, Pallas kernels for 16% -> 18%
where the time goes in v4:
time: 50.5 us; the launch traced here: 50.4 us
  waiting for transfers between devices  20.4 us (40%)
  starting transfers between devices  15.8 us (31%)
  Pallas kernels  11.8 us (23%)
  between operations  1.48 us (3%)
  local copies, waits for them, and re-layouts  0.92 us (2%)
    pallas_call x13, Pallas kernels, call(): pl.pallas_call(kernel, out_shape=[jax.ShapeDtypeStruct(shape, dtype) for...  11.8 us
    ppermute x6, waiting for transfers between devices, flipped(): lax.ppermute(block, axis, [(i, i ^ step) for i in range(lax.axis_size(axi...  10.7 us
    ppermute x4, starting transfers between devices, matched(): lax.ppermute(first, axis, [(i, (i + ways[i % 2]) % count) for i in range(...  8.91 us
    ppermute x6, starting transfers between devices, flipped(): lax.ppermute(block, axis, [(i, i ^ step) for i in range(lax.axis_size(axi...  5.95 us
    ppermute x4, waiting for transfers between devices, matched(): lax.ppermute(first, axis, [(i, (i + ways[i % 2]) % count) for i in range(...  5.71 us
    ppermute x4, waiting for transfers between devices, matched(): lax.ppermute(second, axis, [(i, (i - ways[i % 2]) % count) for i in range...  3.98 us
  transfers between devices with their start and end apart: 14, of which 10 were waited for; matrix products, arithmetic and copies ran while one was open for 0% of the time, Pallas kernels for 18%

profile of v4, /device:TPU:0, one launch (start us, length us, event | category | flops | bytes accessed | tf_op | source)
XLA Modules:
  0.0 50.4 jit_solution(3556092856592774716)
XLA Ops:
  0.7 0.9 %copy-done.1 = bf16[512,128]{1,0:T(8,128)(2,1)S(1)} copy-done((bf16[512,128]{1,0:T(8,128)(2,1)S(1)}, bf16[512,128]{1,0:T(8,128)(2,1)}, u32[]{:S(2)}) %copy-start.1) | copy-done | bytes 131096
  1.5 0.4 shard_map.131
  1.9 5.1 %collective-permute-start = (f32[128,384]{1,0:T(8,128)S(1)}, f32[128,384]{1,0:T(8,128)S(1)}, u32[]{:S(2)}, u32[]{:S(2)}) collective-permute-start(f32[128,384]{1,0:T(8,128)S(1)} %get-tuple-element.40), channel_id=1, source_target_pairs={{0,3},{1,2},{2,1},{3,0},{4,7},{5,6},{6,5},{7,4},{8,11},{9,10},{10,... | collective-permute-start | bytes 589832 | tf_op jit(solution)/shard_map/ppermute | solution.py:344
  7.1 1.9 %shard_map.135 = (bf16[768,512]{1,0:T(8,128)(2,1)S(1)}, bf16[512,768]{1,0:T(8,128)(2,1)S(1)}, f32[128,384]{1,0:T(8,128)S(1)}, f32[128,384]{1,0:T(8,128)S(1)}) custom-call(s32[16,512]{1,0:T(8,128)S(1)} %copy-done.5, f32[16,512]{1,0:T(8,128)S(1)} %copy-done.6, s32[4,384]{1,0:T(4,128)S(1)} %copy-done.8, bf16[128,512]{1,0:T(8,128)(2,1)S(1)} %get-tuple-element.35.hidden_ref), custom_call_target="tpu_custom_call" | custom-call | flops 1000000000 | bytes 20971520 | tf_op jit(solution)/shard_map/pallas_call | solution.py:330
  9.0 1.7 %collective-permute-start.2 = (f32[128,384]{1,0:T(8,128)S(1)}, f32[128,384]{1,0:T(8,128)S(1)}, u32[]{:S(2)}, u32[]{:S(2)}) collective-permute-start(f32[128,384]{1,0:T(8,128)S(1)} %get-tuple-element.42), channel_id=1, source_target_pairs={{0,28},{4,8},{8,4},{12,16},{16,12},{20,24},{24,20},{28,0},{1,29},{... | collective-permute-start | bytes 589832 | tf_op jit(solution)/shard_map/ppermute | solution.py:344
  10.7 2.6 %shard_map.132 = (bf16[1280,512]{1,0:T(8,128)(2,1)S(1)}, bf16[2,128,128]{2,1,0:T(8,128)(2,1)S(1)}, bf16[2,128,256]{2,1,0:T(8,128)(2,1)S(1)}) custom-call(s32[16,512]{1,0:T(8,128)S(1)} %copy-done.5, f32[16,512]{1,0:T(8,128)S(1)} %copy-done.6, bf16[2,128,128]{2,1,0:T(8,128)(2,1)S(1)} %copy-done.3, bf16[2,128,128]{2,1,0:T(8,128)(2,1)S(1)} %copy-done.4), custom_call_target="tpu_custom_call" | custom-call | flops 1000000000 | bytes 20971520 | tf_op jit(solution)/shard_map/pallas_call | solution.py:330
  13.3 0.3 shard_map.133
  13.6 2.7 %collective-permute-done.1.g3 = f32[128,384]{1,0:T(8,128)S(1)} collective-permute-done((f32[128,384]{1,0:T(8,128)S(1)}, f32[128,384]{1,0:T(8,128)S(1)}, u32[]{:S(2)}, u32[]{:S(2)}) %collective-permute-start.1) | collective-permute-done | bytes 196640 | tf_op jit(solution)/shard_map/ppermute | solution.py:345
  16.3 0.3 shard_map.134.gathered_ref
  16.5 0.5 %collective-permute-done.2.g0 = f32[128,384]{1,0:T(8,128)S(1)} collective-permute-done((f32[128,384]{1,0:T(8,128)S(1)}, f32[128,384]{1,0:T(8,128)S(1)}, u32[]{:S(2)}, u32[]{:S(2)}) %collective-permute-start.2) | collective-permute-done | bytes 196640 | tf_op jit(solution)/shard_map/ppermute | solution.py:344
  17.1 0.7 %shard_map.136 = (bf16[128,512]{1,0:T(8,128)(2,1)S(1)}, f32[128,384]{1,0:T(8,128)S(1)}, f32[128,384]{1,0:T(8,128)S(1)}) custom-call(bf16[128,512]{1,0:T(8,128)(2,1)S(1)} %get-tuple-element.35.hidden_ref, f32[128,512]{1,0:T(8,128)S(1)} %get-tuple-element.38.own_ref, f32[128,512]{1,0:T(8,128)S(1)} %shard_map.134.gathered_ref, ...), custom_call_target="tpu_custom_call" | custom-call | flops 1000000000 | bytes 20971520 | tf_op jit(solution)/shard_map/pallas_call | solution.py:330
  17.7 1.3 %collective-permute-start.4 = (f32[128,384]{1,0:T(8,128)S(1)}, f32[128,384]{1,0:T(8,128)S(1)}, u32[]{:S(2)}, u32[]{:S(2)}) collective-permute-start(f32[128,384]{1,0:T(8,128)S(1)} %get-tuple-element.50), channel_id=1, source_target_pairs={{0,3},{1,2},{2,1},{3,0},{4,7},{5,6},{6,5},{7,4},{8,11},{9,10},{10,... | collective-permute-start | bytes 589832 | tf_op jit(solution)/shard_map/ppermute | solution.py:344
  19.1 0.8 %collective-permute-start.5 = (f32[128,384]{1,0:T(8,128)S(1)}, f32[128,384]{1,0:T(8,128)S(1)}, u32[]{:S(2)}, u32[]{:S(2)}) collective-permute-start(f32[128,384]{1,0:T(8,128)S(1)} %get-tuple-element.51), channel_id=1, source_target_pairs={{0,1},{1,0},{2,3},{3,2},{4,5},{5,4},{6,7},{7,6},{8,9},{9,8},{10,11... | collective-permute-start | bytes 589832 | tf_op jit(solution)/shard_map/ppermute | solution.py:345
  19.9 0.6 %shard_map.139 = (bf16[2,136,512]{2,1,0:T(8,128)(2,1)S(1)}, f32[24,512]{1,0:T(8,128)S(1)}, f32[128,384]{1,0:T(8,128)S(1)}, f32[128,384]{1,0:T(8,128)S(1)}) custom-call(f32[3,512]{1,0:T(4,128)S(1)} %copy-done.7, bf16[128,512]{1,0:T(8,128)(2,1)S(1)} %get-tuple-element.47.hidden_ref, s32[4,384]{1,0:T(4,128)S(1)} %copy-done.8), custom_call_target="tpu_custom_call" | custom-call | flops 1000000000 | bytes 20971520 | tf_op jit(solution)/shard_map/pallas_call | solution.py:330
  20.5 0.8 %collective-permute-start.6 = (f32[128,384]{1,0:T(8,128)S(1)}, f32[128,384]{1,0:T(8,128)S(1)}, u32[]{:S(2)}, u32[]{:S(2)}) collective-permute-start(f32[128,384]{1,0:T(8,128)S(1)} %get-tuple-element.52), channel_id=1, source_target_pairs={{0,28},{4,8},{8,4},{12,16},{16,12},{20,24},{24,20},{28,0},{1,29},{... | collective-permute-start | bytes 589832 | tf_op jit(solution)/shard_map/ppermute | solution.py:344
  22.0 0.2 shard_map.137
  22.3 5.2 %collective-permute-done.4.g2 = f32[128,384]{1,0:T(8,128)S(1)} collective-permute-done((f32[128,384]{1,0:T(8,128)S(1)}, f32[128,384]{1,0:T(8,128)S(1)}, u32[]{:S(2)}, u32[]{:S(2)}) %collective-permute-start.4) | collective-permute-done | bytes 196640 | tf_op jit(solution)/shard_map/ppermute | solution.py:344
  27.4 1.3 %collective-permute-done.5.g3 = f32[128,384]{1,0:T(8,128)S(1)} collective-permute-done((f32[128,384]{1,0:T(8,128)S(1)}, f32[128,384]{1,0:T(8,128)S(1)}, u32[]{:S(2)}, u32[]{:S(2)}) %collective-permute-start.5) | collective-permute-done | bytes 196640 | tf_op jit(solution)/shard_map/ppermute | solution.py:345
  28.7 0.3 shard_map.138.gathered_ref
  29.1 0.9 %shard_map.140 = (f32[80,128]{1,0:T(8,128)S(1)}, f32[80,128]{1,0:T(8,128)S(1)}, f32[72,512]{1,0:T(8,128)S(1)}) custom-call(bf16[128,512]{1,0:T(8,128)(2,1)S(1)} %get-tuple-element.47.hidden_ref, f32[128,512]{1,0:T(8,128)S(1)} %get-tuple-element.48.own_ref, f32[128,512]{1,0:T(8,128)S(1)} %shard_map.138.gathered_ref, ...), custom_call_target="tpu_custom_call" | custom-call | tf_op jit(solution)/shard_map/pallas_call | solution.py:330
  30.0 1.2 %collective-permute-done.8 = f32[80,128]{1,0:T(8,128)S(1)} collective-permute-done((f32[80,128]{1,0:T(8,128)S(1)}, f32[80,128]{1,0:T(8,128)S(1)}, u32[]{:S(2)}, u32[]{:S(2)}) %collective-permute-start.8) | collective-permute-done | bytes 40992 | tf_op jit(solution)/shard_map/ppermute | solution.py:350
  31.2 1.3 %collective-permute-start.9 = (f32[80,128]{1,0:T(8,128)S(1)}, f32[80,128]{1,0:T(8,128)S(1)}, u32[]{:S(2)}, u32[]{:S(2)}) collective-permute-start(f32[80,128]{1,0:T(8,128)S(1)} %add.15), channel_id=1, source_target_pairs={{0,8},{4,12},{8,0},{12,4},{16,24},{20,28},{24,16},{28,20},{1,9},{5... | collective-permute-start | bytes 122888 | tf_op jit(solution)/shard_map/ppermute | solution.py:350
  32.6 2.7 %collective-permute-done.9 = f32[80,128]{1,0:T(8,128)S(1)} collective-permute-done((f32[80,128]{1,0:T(8,128)S(1)}, f32[80,128]{1,0:T(8,128)S(1)}, u32[]{:S(2)}, u32[]{:S(2)}) %collective-permute-start.9) | collective-permute-done | bytes 40992 | tf_op jit(solution)/shard_map/ppermute | solution.py:350
  35.3 1.5 %collective-permute-start.10 = (f32[80,128]{1,0:T(8,128)S(1)}, f32[80,128]{1,0:T(8,128)S(1)}, u32[]{:S(2)}, u32[]{:S(2)}) collective-permute-start(f32[80,128]{1,0:T(8,128)S(1)} %add.16), channel_id=1, source_target_pairs={{0,16},{4,20},{8,24},{12,28},{16,0},{20,4},{24,8},{28,12},{1,17},{... | collective-permute-start | bytes 122888 | tf_op jit(solution)/shard_map/ppermute | solution.py:350
  36.7 2.5 %collective-permute-done.10 = f32[80,128]{1,0:T(8,128)S(1)} collective-permute-done((f32[80,128]{1,0:T(8,128)S(1)}, f32[80,128]{1,0:T(8,128)S(1)}, u32[]{:S(2)}, u32[]{:S(2)}) %collective-permute-start.10) | collective-permute-done | bytes 40992 | tf_op jit(solution)/shard_map/ppermute | solution.py:350
  39.3 0.9 %collective-permute-start.11 = (f32[80,128]{1,0:T(8,128)S(1)}, f32[80,128]{1,0:T(8,128)S(1)}, u32[]{:S(2)}, u32[]{:S(2)}) collective-permute-start(f32[80,128]{1,0:T(8,128)S(1)} %add.17), channel_id=1, source_target_pairs={{0,1},{1,0},{2,3},{3,2},{4,5},{5,4},{6,7},{7,6},{8,9},{9,8},{10,11... | collective-permute-start | bytes 122888 | tf_op jit(solution)/shard_map/ppermute | solution.py:350
  40.1 2.8 %shard_map.141 = (f32[72,136]{1,0:T(8,128)S(1)}, f32[8,512]{1,0:T(8,128)S(1)}, f32[3,512]{1,0:T(4,128)}) custom-call(f32[3]{0:T(128)S(1)} %copy-done.9, s32[3,8192]{1,0:T(4,128)S(1)} %copy-done.2, f32[72,512]{1,0:T(8,128)S(1)} %get-tuple-element.58.lattice_ref, f32[24,512]{1,0:T(8,128)S(1)} %get-tuple-element.55.third_ref, s32[1,1]{1,0:T(1,128)} %bitcast.4.count_ref), custom_call_target="tpu_custom_call" | custom-call | flops 1000000000 | bytes 20971520 | tf_op jit(solution)/shard_map/pallas_call | solution.py:330
  42.9 0.4 collective-permute-done.11
  43.3 2.2 %collective-permute-start.12 = (f32[80,128]{1,0:T(8,128)S(1)}, f32[80,128]{1,0:T(8,128)S(1)}, u32[]{:S(2)}, u32[]{:S(2)}) collective-permute-start(f32[80,128]{1,0:T(8,128)S(1)} %add.18), channel_id=1, source_target_pairs={{0,2},{1,3},{2,0},{3,1},{4,6},{5,7},{6,4},{7,5},{8,10},{9,11},{10,... | collective-permute-start | bytes 122888 | tf_op jit(solution)/shard_map/ppermute | solution.py:350
  45.5 2.7 %collective-permute-done.12 = f32[80,128]{1,0:T(8,128)S(1)} collective-permute-done((f32[80,128]{1,0:T(8,128)S(1)}, f32[80,128]{1,0:T(8,128)S(1)}, u32[]{:S(2)}, u32[]{:S(2)}) %collective-permute-start.12) | collective-permute-done | bytes 40992 | tf_op jit(solution)/shard_map/ppermute | solution.py:350
  48.2 1.2 %collective-permute-done.13.other_ref = f32[80,128]{1,0:T(8,128)S(1)} collective-permute-done((f32[80,128]{1,0:T(8,128)S(1)}, f32[80,128]{1,0:T(8,128)S(1)}, u32[]{:S(2)}, u32[]{:S(2)}) %collective-permute-start.13) | collective-permute-done | bytes 40992 | tf_op jit(solution)/shard_map/ppermute | solution.py:350
  49.4 1.0 %shard_map.142 = (f32[3,512]{1,0:T(4,128)}, f32[1,1]{1,0:T(1,128)}) custom-call(f32[80,128]{1,0:T(8,128)S(1)} %add.19.half_ref, f32[80,128]{1,0:T(8,128)S(1)} %collective-permute-done.13.other_ref, f32[72,512]{1,0:T(8,128)S(1)} %get-tuple-element.58.lattice_ref, bf16[2,136,512]{2,1,0:T(8,128)(2,1)S(1)} %get-tuple-element.54.phase_ref, ...), custom_call_target="tpu_custom_call" | custom-call | tf_op jit(solution)/shard_map/pallas_call | solution.py:330
  (34 shorter events, 0.2 us)
Async XLA Ops:
  0.6 0.9 %copy-start.1 = (bf16[512,128]{1,0:T(8,128)(2,1)S(1)}, bf16[512,128]{1,0:T(8,128)(2,1)}, u32[]{:S(2)}) copy-start(bf16[512,128]{1,0:T(8,128)(2,1)} %features_ref.1) | copy-start | bytes 393220
  0.6 0.9 %copy-start.8 = (s32[4,384]{1,0:T(4,128)S(1)}, s32[4,384]{1,0:T(4,128)}, u32[]{:S(2)}) copy-start(s32[4,384]{1,0:T(4,128)} %index_ref.5) | copy-start | bytes 18436
  1.5 5.5 %copy-start.5 = (s32[16,512]{1,0:T(8,128)S(1)}, s32[16,512]{1,0:T(8,128)}, u32[]{:S(2)}) copy-start(s32[16,512]{1,0:T(8,128)} %senders_ref.3) | copy-start | bytes 98308
  1.5 5.5 %copy-start.6 = (f32[16,512]{1,0:T(8,128)S(1)}, f32[16,512]{1,0:T(8,128)}, u32[]{:S(2)}) copy-start(f32[16,512]{1,0:T(8,128)} %radial_ref.3) | copy-start | bytes 98308
  1.9 11.6 %collective-permute-start = (f32[128,384]{1,0:T(8,128)S(1)}, f32[128,384]{1,0:T(8,128)S(1)}, u32[]{:S(2)}, u32[]{:S(2)}) collective-permute-start(f32[128,384]{1,0:T(8,128)S(1)} %get-tuple-element.40), channel_id=1, source_target_pairs={{0,3},{1,2},{2,1},{3,0},{4,7},{5,6},{6,5},{7,4},{8,11},{9,10},{10,... | collective-permute-start | bytes 589832 | tf_op jit(solution)/shard_map/ppermute | solution.py:344
  7.0 9.2 %collective-permute-start.1 = (f32[128,384]{1,0:T(8,128)S(1)}, f32[128,384]{1,0:T(8,128)S(1)}, u32[]{:S(2)}, u32[]{:S(2)}) collective-permute-start(f32[128,384]{1,0:T(8,128)S(1)} %get-tuple-element.41), channel_id=1, source_target_pairs={{0,1},{1,0},{2,3},{3,2},{4,5},{5,4},{6,7},{7,6},{8,9},{9,8},{10,11... | collective-permute-start | bytes 589832 | tf_op jit(solution)/shard_map/ppermute | solution.py:345
  7.1 3.6 %copy-start.3 = (bf16[2,128,128]{2,1,0:T(8,128)(2,1)S(1)}, bf16[2,128,128]{2,1,0:T(8,128)(2,1)}, u32[]{:S(2)}) copy-start(bf16[2,128,128]{2,1,0:T(8,128)(2,1)} %self_ref.1) | copy-start | bytes 196612
  7.1 3.6 %copy-start.4 = (bf16[2,128,128]{2,1,0:T(8,128)(2,1)S(1)}, bf16[2,128,128]{2,1,0:T(8,128)(2,1)}, u32[]{:S(2)}) copy-start(bf16[2,128,128]{2,1,0:T(8,128)(2,1)} %message_ref.1) | copy-start | bytes 196612
  9.0 8.1 %collective-permute-start.2 = (f32[128,384]{1,0:T(8,128)S(1)}, f32[128,384]{1,0:T(8,128)S(1)}, u32[]{:S(2)}, u32[]{:S(2)}) collective-permute-start(f32[128,384]{1,0:T(8,128)S(1)} %get-tuple-element.42), channel_id=1, source_target_pairs={{0,28},{4,8},{8,4},{12,16},{16,12},{20,24},{24,20},{28,0},{1,29},{... | collective-permute-start | bytes 589832 | tf_op jit(solution)/shard_map/ppermute | solution.py:344
  10.7 6.4 %collective-permute-start.3 = (f32[128,384]{1,0:T(8,128)S(1)}, f32[128,384]{1,0:T(8,128)S(1)}, u32[]{:S(2)}, u32[]{:S(2)}) collective-permute-start(f32[128,384]{1,0:T(8,128)S(1)} %get-tuple-element.43), channel_id=1, source_target_pairs={{0,4},{4,0},{8,12},{12,8},{16,20},{20,16},{24,28},{28,24},{1,5},{5... | collective-permute-start | bytes 589832 | tf_op jit(solution)/shard_map/ppermute | solution.py:345
  17.1 2.8 %copy-start.7 = (f32[3,512]{1,0:T(4,128)S(1)}, f32[3,512]{1,0:T(4,128)}, u32[]{:S(2)}) copy-start(f32[3,512]{1,0:T(4,128)} %fractions_ref.1) | copy-start | bytes 18436
  17.7 9.7 %collective-permute-start.4 = (f32[128,384]{1,0:T(8,128)S(1)}, f32[128,384]{1,0:T(8,128)S(1)}, u32[]{:S(2)}, u32[]{:S(2)}) collective-permute-start(f32[128,384]{1,0:T(8,128)S(1)} %get-tuple-element.50), channel_id=1, source_target_pairs={{0,3},{1,2},{2,1},{3,0},{4,7},{5,6},{6,5},{7,4},{8,11},{9,10},{10,... | collective-permute-start | bytes 589832 | tf_op jit(solution)/shard_map/ppermute | solution.py:344
  19.1 9.7 %collective-permute-start.5 = (f32[128,384]{1,0:T(8,128)S(1)}, f32[128,384]{1,0:T(8,128)S(1)}, u32[]{:S(2)}, u32[]{:S(2)}) collective-permute-start(f32[128,384]{1,0:T(8,128)S(1)} %get-tuple-element.51), channel_id=1, source_target_pairs={{0,1},{1,0},{2,3},{3,2},{4,5},{5,4},{6,7},{7,6},{8,9},{9,8},{10,11... | collective-permute-start | bytes 589832 | tf_op jit(solution)/shard_map/ppermute | solution.py:345
  20.5 8.6 %collective-permute-start.6 = (f32[128,384]{1,0:T(8,128)S(1)}, f32[128,384]{1,0:T(8,128)S(1)}, u32[]{:S(2)}, u32[]{:S(2)}) collective-permute-start(f32[128,384]{1,0:T(8,128)S(1)} %get-tuple-element.52), channel_id=1, source_target_pairs={{0,28},{4,8},{8,4},{12,16},{16,12},{20,24},{24,20},{28,0},{1,29},{... | collective-permute-start | bytes 589832 | tf_op jit(solution)/shard_map/ppermute | solution.py:344
  21.3 7.8 %collective-permute-start.7 = (f32[128,384]{1,0:T(8,128)S(1)}, f32[128,384]{1,0:T(8,128)S(1)}, u32[]{:S(2)}, u32[]{:S(2)}) collective-permute-start(f32[128,384]{1,0:T(8,128)S(1)} %get-tuple-element.53), channel_id=1, source_target_pairs={{0,4},{4,0},{8,12},{12,8},{16,20},{20,16},{24,28},{28,24},{1,5},{5... | collective-permute-start | bytes 589832 | tf_op jit(solution)/shard_map/ppermute | solution.py:345
  22.2 6.8 %copy-start = (bf16[128,4]{0,1:T(4,128)(2,1)S(1)}, bf16[128,4]{0,1:T(4,128)(2,1)}, u32[]{:S(2)}) copy-start(bf16[128,4]{0,1:T(4,128)(2,1)} %param.20) | copy-start | bytes 3076
  29.1 11.1 %copy-start.2 = (s32[3,8192]{1,0:T(4,128)S(1)}, s32[3,8192]{1,0:T(4,128)}, u32[]{:S(2)}) copy-start(s32[3,8192]{1,0:T(4,128)} %numbers_ref.1) | copy-start | bytes 294916
  29.1 11.1 %copy-start.9 = (f32[3]{0:T(128)S(1)}, f32[3]{0:T(128)}, u32[]{:S(2)}) copy-start(f32[3]{0:T(128)} %cell_ref.1) | copy-start | bytes 40
  30.0 1.3 %collective-permute-start.8 = (f32[80,128]{1,0:T(8,128)S(1)}, f32[80,128]{1,0:T(8,128)S(1)}, u32[]{:S(2)}, u32[]{:S(2)}) collective-permute-start(f32[80,128]{1,0:T(8,128)S(1)} %get-tuple-element.57), channel_id=1, source_target_pairs={{0,4},{4,0},{8,12},{12,8},{16,20},{20,16},{24,28},{28,24},{1,5},{5... | collective-permute-start | bytes 122888 | tf_op jit(solution)/shard_map/ppermute | solution.py:350
  31.2 4.0 %collective-permute-start.9 = (f32[80,128]{1,0:T(8,128)S(1)}, f32[80,128]{1,0:T(8,128)S(1)}, u32[]{:S(2)}, u32[]{:S(2)}) collective-permute-start(f32[80,128]{1,0:T(8,128)S(1)} %add.15), channel_id=1, source_target_pairs={{0,8},{4,12},{8,0},{12,4},{16,24},{20,28},{24,16},{28,20},{1,9},{5... | collective-permute-start | bytes 122888 | tf_op jit(solution)/shard_map/ppermute | solution.py:350
  35.3 4.0 %collective-permute-start.10 = (f32[80,128]{1,0:T(8,128)S(1)}, f32[80,128]{1,0:T(8,128)S(1)}, u32[]{:S(2)}, u32[]{:S(2)}) collective-permute-start(f32[80,128]{1,0:T(8,128)S(1)} %add.16), channel_id=1, source_target_pairs={{0,16},{4,20},{8,24},{12,28},{16,0},{20,4},{24,8},{28,12},{1,17},{... | collective-permute-start | bytes 122888 | tf_op jit(solution)/shard_map/ppermute | solution.py:350
  39.3 4.0 %collective-permute-start.11 = (f32[80,128]{1,0:T(8,128)S(1)}, f32[80,128]{1,0:T(8,128)S(1)}, u32[]{:S(2)}, u32[]{:S(2)}) collective-permute-start(f32[80,128]{1,0:T(8,128)S(1)} %add.17), channel_id=1, source_target_pairs={{0,1},{1,0},{2,3},{3,2},{4,5},{5,4},{6,7},{7,6},{8,9},{9,8},{10,11... | collective-permute-start | bytes 122888 | tf_op jit(solution)/shard_map/ppermute | solution.py:350
  43.3 4.9 %collective-permute-start.12 = (f32[80,128]{1,0:T(8,128)S(1)}, f32[80,128]{1,0:T(8,128)S(1)}, u32[]{:S(2)}, u32[]{:S(2)}) collective-permute-start(f32[80,128]{1,0:T(8,128)S(1)} %add.18), channel_id=1, source_target_pairs={{0,2},{1,3},{2,0},{3,1},{4,6},{5,7},{6,4},{7,5},{8,10},{9,11},{10,... | collective-permute-start | bytes 122888 | tf_op jit(solution)/shard_map/ppermute | solution.py:350
  48.2 1.2 %collective-permute-start.13 = (f32[80,128]{1,0:T(8,128)S(1)}, f32[80,128]{1,0:T(8,128)S(1)}, u32[]{:S(2)}, u32[]{:S(2)}) collective-permute-start(f32[80,128]{1,0:T(8,128)S(1)} %add.19.half_ref), channel_id=1, source_target_pairs={{0,4},{4,0},{8,12},{12,8},{16,20},{20,16},{24,28},{28,24},{1,5},{5... | collective-permute-start | bytes 122888 | tf_op jit(solution)/shard_map/ppermute | solution.py:350

commit v5 on v4

--- a/solution.py
+++ b/solution.py
@@ -143,6 +143,13 @@
     p3[...] = picked[:, ghosts:]
 
 
+def structure_part(lattice, phase_ref, part, out_ref):
+    phases = phase_ref[part]
+    out_ref[0:72, :] = dot_nt(lattice, phases[0:128, :])
+    out_ref[72:80, 0:72] = dot_nt(phases[128:grid_rows, :], lattice)
+    out_ref[72:80, 72:128] = jnp.zeros((8, 56), f32)
+
+
 def last_kernel(
     layer,
     hidden_ref,
@@ -157,7 +164,6 @@
     phase_ref,
     third_ref,
     send_ref,
-    keep_ref,
     lattice_ref,
 ):
     hidden = interact(layer, hidden_ref, own_ref, gathered_ref, g0, g1, edges_ref, message_rows_ref)
@@ -172,13 +178,11 @@
     rows = rows + [charges[c : c + 1, :] * sine for c in range(4)]
     lattice = jnp.concatenate(rows + [charges], axis=0)
     lattice_ref[...] = lattice
-    lattice = lattice.astype(bf16)
-    core = parity("wide")
-    for out_ref, part in ((keep_ref, core), (send_ref, 1 - core)):
-        phases = phase_ref[part]
-        out_ref[0:72, :] = dot_nt(lattice, phases[0:128, :])
-        out_ref[72:80, 0:72] = dot_nt(phases[128:grid_rows, :], lattice)
-        out_ref[72:80, 72:128] = jnp.zeros((8, 56), f32)
+    structure_part(lattice.astype(bf16), phase_ref, 1 - parity("wide"), send_ref)
+
+
+def keep_kernel(lattice_ref, phase_ref, keep_ref):
+    structure_part(lattice_ref[...].astype(bf16), phase_ref, parity("wide"), keep_ref)
 
 
 def wave_weight(m0, m1, m2, cell_ref):
@@ -450,9 +454,9 @@
             cost=busy,
         )
         g0, g1 = matched(p0, p1, "wide")
-    send, keep, lattice = call(
+    send, lattice = call(
         functools.partial(last_kernel, layers - 1),
-        [((half_rows, 128), f32)] * 2 + [((72, atoms), f32)],
+        [((half_rows, 128), f32), ((72, atoms), f32)],
         hidden,
         own,
         gathered,
@@ -477,6 +481,7 @@
         scratch=[pltpu.VMEM((32, grid_rows), f32)],
         cost=busy,
     )
+    (keep,) = call(keep_kernel, [((half_rows, 128), f32)], lattice, phases, cost=busy)
     half, other, (weights, factor) = summed(send, keep, (weights, factor))
     forces, energy = call(
         functools.partial(force_kernel, scale),

time: 50.5 us -> 50.4 us (level)
    pallas_call x13 -> x14, Pallas kernels: 11.8 us -> 11.9 us  [call(): pl.pallas_call(kernel, out_shape=[jax.ShapeDtypeStruct(shape, dtype) for...]
where the time goes in v5:
time: 50.4 us; the launch traced here: 50.3 us
  waiting for transfers between devices  20.2 us (40%)
  starting transfers between devices  15.7 us (31%)
  Pallas kernels  11.9 us (24%)
  between operations  1.48 us (3%)
  local copies, waits for them, and re-layouts  0.92 us (2%)
    pallas_call x14, Pallas kernels, call(): pl.pallas_call(kernel, out_shape=[jax.ShapeDtypeStruct(shape, dtype) for...  11.9 us
    ppermute x6, waiting for transfers between devices, flipped(): lax.ppermute(block, axis, [(i, i ^ step) for i in range(lax.axis_size(axi...  10.5 us
    ppermute x4, starting transfers between devices, matched(): lax.ppermute(first, axis, [(i, (i + ways[i % 2]) % count) for i in range(...  8.9 us
    ppermute x6, starting transfers between devices, flipped(): lax.ppermute(block, axis, [(i, i ^ step) for i in range(lax.axis_size(axi...  5.94 us
    ppermute x4, waiting for transfers between devices, matched(): lax.ppermute(first, axis, [(i, (i + ways[i % 2]) % count) for i in range(...  5.71 us
    ppermute x4, waiting for transfers between devices, matched(): lax.ppermute(second, axis, [(i, (i - ways[i % 2]) % count) for i in range...  3.98 us
  transfers between devices with their start and end apart: 14, of which 10 were waited for; matrix products, arithmetic and copies ran while one was open for 0% of the time, Pallas kernels for 18%

profile of v5, /device:TPU:0, one launch (start us, length us, event | category | flops | bytes accessed | tf_op | source)
XLA Modules:
  0.0 50.3 jit_solution(10409912297438076825)
XLA Ops:
  0.7 0.9 %copy-done.1 = bf16[512,128]{1,0:T(8,128)(2,1)S(1)} copy-done((bf16[512,128]{1,0:T(8,128)(2,1)S(1)}, bf16[512,128]{1,0:T(8,128)(2,1)}, u32[]{:S(2)}) %copy-start.1) | copy-done | bytes 131096
  1.5 0.4 shard_map.131
  1.9 5.1 %collective-permute-start = (f32[128,384]{1,0:T(8,128)S(1)}, f32[128,384]{1,0:T(8,128)S(1)}, u32[]{:S(2)}, u32[]{:S(2)}) collective-permute-start(f32[128,384]{1,0:T(8,128)S(1)} %get-tuple-element.39), channel_id=1, source_target_pairs={{0,3},{1,2},{2,1},{3,0},{4,7},{5,6},{6,5},{7,4},{8,11},{9,10},{10,... | collective-permute-start | bytes 589832 | tf_op jit(solution)/shard_map/ppermute | solution.py:348
  7.1 1.9 %shard_map.135 = (bf16[768,512]{1,0:T(8,128)(2,1)S(1)}, bf16[512,768]{1,0:T(8,128)(2,1)S(1)}, f32[128,384]{1,0:T(8,128)S(1)}, f32[128,384]{1,0:T(8,128)S(1)}) custom-call(s32[16,512]{1,0:T(8,128)S(1)} %copy-done.5, f32[16,512]{1,0:T(8,128)S(1)} %copy-done.6, s32[4,384]{1,0:T(4,128)S(1)} %copy-done.8, bf16[128,512]{1,0:T(8,128)(2,1)S(1)} %get-tuple-element.34.hidden_ref), custom_call_target="tpu_custom_call" | custom-call | flops 1000000000 | bytes 20971520 | tf_op jit(solution)/shard_map/pallas_call | solution.py:334
  9.0 1.7 %collective-permute-start.2 = (f32[128,384]{1,0:T(8,128)S(1)}, f32[128,384]{1,0:T(8,128)S(1)}, u32[]{:S(2)}, u32[]{:S(2)}) collective-permute-start(f32[128,384]{1,0:T(8,128)S(1)} %get-tuple-element.41), channel_id=1, source_target_pairs={{0,28},{4,8},{8,4},{12,16},{16,12},{20,24},{24,20},{28,0},{1,29},{... | collective-permute-start | bytes 589832 | tf_op jit(solution)/shard_map/ppermute | solution.py:348
  10.7 2.6 %shard_map.132 = (bf16[1280,512]{1,0:T(8,128)(2,1)S(1)}, bf16[2,128,128]{2,1,0:T(8,128)(2,1)S(1)}, bf16[2,128,256]{2,1,0:T(8,128)(2,1)S(1)}) custom-call(s32[16,512]{1,0:T(8,128)S(1)} %copy-done.5, f32[16,512]{1,0:T(8,128)S(1)} %copy-done.6, bf16[2,128,128]{2,1,0:T(8,128)(2,1)S(1)} %copy-done.3, bf16[2,128,128]{2,1,0:T(8,128)(2,1)S(1)} %copy-done.4), custom_call_target="tpu_custom_call" | custom-call | flops 1000000000 | bytes 20971520 | tf_op jit(solution)/shard_map/pallas_call | solution.py:334
  13.3 0.3 shard_map.133
  13.6 2.7 %collective-permute-done.1.g3 = f32[128,384]{1,0:T(8,128)S(1)} collective-permute-done((f32[128,384]{1,0:T(8,128)S(1)}, f32[128,384]{1,0:T(8,128)S(1)}, u32[]{:S(2)}, u32[]{:S(2)}) %collective-permute-start.1) | collective-permute-done | bytes 196640 | tf_op jit(solution)/shard_map/ppermute | solution.py:349
  16.3 0.3 shard_map.134.gathered_ref
  16.5 0.5 %collective-permute-done.2.g0 = f32[128,384]{1,0:T(8,128)S(1)} collective-permute-done((f32[128,384]{1,0:T(8,128)S(1)}, f32[128,384]{1,0:T(8,128)S(1)}, u32[]{:S(2)}, u32[]{:S(2)}) %collective-permute-start.2) | collective-permute-done | bytes 196640 | tf_op jit(solution)/shard_map/ppermute | solution.py:348
  17.1 0.7 %shard_map.136 = (bf16[128,512]{1,0:T(8,128)(2,1)S(1)}, f32[128,384]{1,0:T(8,128)S(1)}, f32[128,384]{1,0:T(8,128)S(1)}) custom-call(bf16[128,512]{1,0:T(8,128)(2,1)S(1)} %get-tuple-element.34.hidden_ref, f32[128,512]{1,0:T(8,128)S(1)} %get-tuple-element.37.own_ref, f32[128,512]{1,0:T(8,128)S(1)} %shard_map.134.gathered_ref, ...), custom_call_target="tpu_custom_call" | custom-call | flops 1000000000 | bytes 20971520 | tf_op jit(solution)/shard_map/pallas_call | solution.py:334
  17.7 1.3 %collective-permute-start.4 = (f32[128,384]{1,0:T(8,128)S(1)}, f32[128,384]{1,0:T(8,128)S(1)}, u32[]{:S(2)}, u32[]{:S(2)}) collective-permute-start(f32[128,384]{1,0:T(8,128)S(1)} %get-tuple-element.49), channel_id=1, source_target_pairs={{0,3},{1,2},{2,1},{3,0},{4,7},{5,6},{6,5},{7,4},{8,11},{9,10},{10,... | collective-permute-start | bytes 589832 | tf_op jit(solution)/shard_map/ppermute | solution.py:348
  19.0 0.8 %collective-permute-start.5 = (f32[128,384]{1,0:T(8,128)S(1)}, f32[128,384]{1,0:T(8,128)S(1)}, u32[]{:S(2)}, u32[]{:S(2)}) collective-permute-start(f32[128,384]{1,0:T(8,128)S(1)} %get-tuple-element.50), channel_id=1, source_target_pairs={{0,1},{1,0},{2,3},{3,2},{4,5},{5,4},{6,7},{7,6},{8,9},{9,8},{10,11... | collective-permute-start | bytes 589832 | tf_op jit(solution)/shard_map/ppermute | solution.py:349
  19.9 0.6 %shard_map.139 = (bf16[2,136,512]{2,1,0:T(8,128)(2,1)S(1)}, f32[24,512]{1,0:T(8,128)S(1)}, f32[128,384]{1,0:T(8,128)S(1)}, f32[128,384]{1,0:T(8,128)S(1)}) custom-call(f32[3,512]{1,0:T(4,128)S(1)} %copy-done.7, bf16[128,512]{1,0:T(8,128)(2,1)S(1)} %get-tuple-element.46.hidden_ref, s32[4,384]{1,0:T(4,128)S(1)} %copy-done.8), custom_call_target="tpu_custom_call" | custom-call | flops 1000000000 | bytes 20971520 | tf_op jit(solution)/shard_map/pallas_call | solution.py:334
  20.5 0.8 %collective-permute-start.6 = (f32[128,384]{1,0:T(8,128)S(1)}, f32[128,384]{1,0:T(8,128)S(1)}, u32[]{:S(2)}, u32[]{:S(2)}) collective-permute-start(f32[128,384]{1,0:T(8,128)S(1)} %get-tuple-element.51), channel_id=1, source_target_pairs={{0,28},{4,8},{8,4},{12,16},{16,12},{20,24},{24,20},{28,0},{1,29},{... | collective-permute-start | bytes 589832 | tf_op jit(solution)/shard_map/ppermute | solution.py:348
  22.0 0.3 shard_map.137
  22.3 5.2 %collective-permute-done.4.g2 = f32[128,384]{1,0:T(8,128)S(1)} collective-permute-done((f32[128,384]{1,0:T(8,128)S(1)}, f32[128,384]{1,0:T(8,128)S(1)}, u32[]{:S(2)}, u32[]{:S(2)}) %collective-permute-start.4) | collective-permute-done | bytes 196640 | tf_op jit(solution)/shard_map/ppermute | solution.py:348
  27.4 1.3 %collective-permute-done.5.g3 = f32[128,384]{1,0:T(8,128)S(1)} collective-permute-done((f32[128,384]{1,0:T(8,128)S(1)}, f32[128,384]{1,0:T(8,128)S(1)}, u32[]{:S(2)}, u32[]{:S(2)}) %collective-permute-start.5) | collective-permute-done | bytes 196640 | tf_op jit(solution)/shard_map/ppermute | solution.py:349
  28.7 0.3 shard_map.138.gathered_ref
  29.1 0.8 %shard_map.140 = (f32[80,128]{1,0:T(8,128)S(1)}, f32[72,512]{1,0:T(8,128)S(1)}) custom-call(bf16[128,512]{1,0:T(8,128)(2,1)S(1)} %get-tuple-element.46.hidden_ref, f32[128,512]{1,0:T(8,128)S(1)} %get-tuple-element.47.own_ref, f32[128,512]{1,0:T(8,128)S(1)} %shard_map.138.gathered_ref, f32[128,384]{1,0:T(8,128)S(1)} %collective-permute-done.6.g0, ...), custom_call_target="tpu_custom_call" | custom-call | tf_op jit(solution)/shard_map/pallas_call | solution.py:334
  30.1 1.0 %collective-permute-done.8 = f32[80,128]{1,0:T(8,128)S(1)} collective-permute-done((f32[80,128]{1,0:T(8,128)S(1)}, f32[80,128]{1,0:T(8,128)S(1)}, u32[]{:S(2)}, u32[]{:S(2)}) %collective-permute-start.8) | collective-permute-done | bytes 40992 | tf_op jit(solution)/shard_map/ppermute | solution.py:354
  31.1 1.3 %collective-permute-start.9 = (f32[80,128]{1,0:T(8,128)S(1)}, f32[80,128]{1,0:T(8,128)S(1)}, u32[]{:S(2)}, u32[]{:S(2)}) collective-permute-start(f32[80,128]{1,0:T(8,128)S(1)} %add.15), channel_id=1, source_target_pairs={{0,8},{4,12},{8,0},{12,4},{16,24},{20,28},{24,16},{28,20},{1,9},{5... | collective-permute-start | bytes 122888 | tf_op jit(solution)/shard_map/ppermute | solution.py:354
  32.4 2.7 %collective-permute-done.9 = f32[80,128]{1,0:T(8,128)S(1)} collective-permute-done((f32[80,128]{1,0:T(8,128)S(1)}, f32[80,128]{1,0:T(8,128)S(1)}, u32[]{:S(2)}, u32[]{:S(2)}) %collective-permute-start.9) | collective-permute-done | bytes 40992 | tf_op jit(solution)/shard_map/ppermute | solution.py:354
  35.1 1.5 %collective-permute-start.10 = (f32[80,128]{1,0:T(8,128)S(1)}, f32[80,128]{1,0:T(8,128)S(1)}, u32[]{:S(2)}, u32[]{:S(2)}) collective-permute-start(f32[80,128]{1,0:T(8,128)S(1)} %add.16), channel_id=1, source_target_pairs={{0,16},{4,20},{8,24},{12,28},{16,0},{20,4},{24,8},{28,12},{1,17},{... | collective-permute-start | bytes 122888 | tf_op jit(solution)/shard_map/ppermute | solution.py:354
  36.6 2.5 %collective-permute-done.10 = f32[80,128]{1,0:T(8,128)S(1)} collective-permute-done((f32[80,128]{1,0:T(8,128)S(1)}, f32[80,128]{1,0:T(8,128)S(1)}, u32[]{:S(2)}, u32[]{:S(2)}) %collective-permute-start.10) | collective-permute-done | bytes 40992 | tf_op jit(solution)/shard_map/ppermute | solution.py:354
  39.1 0.9 %collective-permute-start.11 = (f32[80,128]{1,0:T(8,128)S(1)}, f32[80,128]{1,0:T(8,128)S(1)}, u32[]{:S(2)}, u32[]{:S(2)}) collective-permute-start(f32[80,128]{1,0:T(8,128)S(1)} %add.17), channel_id=1, source_target_pairs={{0,1},{1,0},{2,3},{3,2},{4,5},{5,4},{6,7},{7,6},{8,9},{9,8},{10,11... | collective-permute-start | bytes 122888 | tf_op jit(solution)/shard_map/ppermute | solution.py:354
  40.0 2.8 %shard_map.142 = (f32[72,136]{1,0:T(8,128)S(1)}, f32[8,512]{1,0:T(8,128)S(1)}, f32[3,512]{1,0:T(4,128)}) custom-call(f32[3]{0:T(128)S(1)} %copy-done.9, s32[3,8192]{1,0:T(4,128)S(1)} %copy-done.2, f32[72,512]{1,0:T(8,128)S(1)} %get-tuple-element.55.lattice_ref, f32[24,512]{1,0:T(8,128)S(1)} %get-tuple-element.54.third_ref, s32[1,1]{1,0:T(1,128)} %bitcast.4.count_ref), custom_call_target="tpu_custom_call" | custom-call | flops 1000000000 | bytes 20971520 | tf_op jit(solution)/shard_map/pallas_call | solution.py:334
  42.8 0.4 collective-permute-done.11
  43.2 2.2 %collective-permute-start.12 = (f32[80,128]{1,0:T(8,128)S(1)}, f32[80,128]{1,0:T(8,128)S(1)}, u32[]{:S(2)}, u32[]{:S(2)}) collective-permute-start(f32[80,128]{1,0:T(8,128)S(1)} %add.18), channel_id=1, source_target_pairs={{0,2},{1,3},{2,0},{3,1},{4,6},{5,7},{6,4},{7,5},{8,10},{9,11},{10,... | collective-permute-start | bytes 122888 | tf_op jit(solution)/shard_map/ppermute | solution.py:354
  45.4 2.7 %collective-permute-done.12 = f32[80,128]{1,0:T(8,128)S(1)} collective-permute-done((f32[80,128]{1,0:T(8,128)S(1)}, f32[80,128]{1,0:T(8,128)S(1)}, u32[]{:S(2)}, u32[]{:S(2)}) %collective-permute-start.12) | collective-permute-done | bytes 40992 | tf_op jit(solution)/shard_map/ppermute | solution.py:354
  48.1 1.2 %collective-permute-done.13.other_ref = f32[80,128]{1,0:T(8,128)S(1)} collective-permute-done((f32[80,128]{1,0:T(8,128)S(1)}, f32[80,128]{1,0:T(8,128)S(1)}, u32[]{:S(2)}, u32[]{:S(2)}) %collective-permute-start.13) | collective-permute-done | bytes 40992 | tf_op jit(solution)/shard_map/ppermute | solution.py:354
  49.3 1.0 %shard_map.143 = (f32[3,512]{1,0:T(4,128)}, f32[1,1]{1,0:T(1,128)}) custom-call(f32[80,128]{1,0:T(8,128)S(1)} %add.19.half_ref, f32[80,128]{1,0:T(8,128)S(1)} %collective-permute-done.13.other_ref, f32[72,512]{1,0:T(8,128)S(1)} %get-tuple-element.55.lattice_ref, bf16[2,136,512]{2,1,0:T(8,128)(2,1)S(1)} %get-tuple-element.53.phase_ref, ...), custom_call_target="tpu_custom_call" | custom-call | tf_op jit(solution)/shard_map/pallas_call | solution.py:334
  (35 shorter events, 0.4 us)
Async XLA Ops:
  0.6 0.9 %copy-start.1 = (bf16[512,128]{1,0:T(8,128)(2,1)S(1)}, bf16[512,128]{1,0:T(8,128)(2,1)}, u32[]{:S(2)}) copy-start(bf16[512,128]{1,0:T(8,128)(2,1)} %features_ref.1) | copy-start | bytes 393220
  0.6 0.9 %copy-start.8 = (s32[4,384]{1,0:T(4,128)S(1)}, s32[4,384]{1,0:T(4,128)}, u32[]{:S(2)}) copy-start(s32[4,384]{1,0:T(4,128)} %index_ref.5) | copy-start | bytes 18436
  1.5 5.5 %copy-start.5 = (s32[16,512]{1,0:T(8,128)S(1)}, s32[16,512]{1,0:T(8,128)}, u32[]{:S(2)}) copy-start(s32[16,512]{1,0:T(8,128)} %senders_ref.3) | copy-start | bytes 98308
  1.5 5.5 %copy-start.6 = (f32[16,512]{1,0:T(8,128)S(1)}, f32[16,512]{1,0:T(8,128)}, u32[]{:S(2)}) copy-start(f32[16,512]{1,0:T(8,128)} %radial_ref.3) | copy-start | bytes 98308
  1.9 11.6 %collective-permute-start = (f32[128,384]{1,0:T(8,128)S(1)}, f32[128,384]{1,0:T(8,128)S(1)}, u32[]{:S(2)}, u32[]{:S(2)}) collective-permute-start(f32[128,384]{1,0:T(8,128)S(1)} %get-tuple-element.39), channel_id=1, source_target_pairs={{0,3},{1,2},{2,1},{3,0},{4,7},{5,6},{6,5},{7,4},{8,11},{9,10},{10,... | collective-permute-start | bytes 589832 | tf_op jit(solution)/shard_map/ppermute | solution.py:348
  7.0 9.2 %collective-permute-start.1 = (f32[128,384]{1,0:T(8,128)S(1)}, f32[128,384]{1,0:T(8,128)S(1)}, u32[]{:S(2)}, u32[]{:S(2)}) collective-permute-start(f32[128,384]{1,0:T(8,128)S(1)} %get-tuple-element.40), channel_id=1, source_target_pairs={{0,1},{1,0},{2,3},{3,2},{4,5},{5,4},{6,7},{7,6},{8,9},{9,8},{10,11... | collective-permute-start | bytes 589832 | tf_op jit(solution)/shard_map/ppermute | solution.py:349
  7.1 3.6 %copy-start.3 = (bf16[2,128,128]{2,1,0:T(8,128)(2,1)S(1)}, bf16[2,128,128]{2,1,0:T(8,128)(2,1)}, u32[]{:S(2)}) copy-start(bf16[2,128,128]{2,1,0:T(8,128)(2,1)} %self_ref.1) | copy-start | bytes 196612
  7.1 3.6 %copy-start.4 = (bf16[2,128,128]{2,1,0:T(8,128)(2,1)S(1)}, bf16[2,128,128]{2,1,0:T(8,128)(2,1)}, u32[]{:S(2)}) copy-start(bf16[2,128,128]{2,1,0:T(8,128)(2,1)} %message_ref.1) | copy-start | bytes 196612
  9.0 8.1 %collective-permute-start.2 = (f32[128,384]{1,0:T(8,128)S(1)}, f32[128,384]{1,0:T(8,128)S(1)}, u32[]{:S(2)}, u32[]{:S(2)}) collective-permute-start(f32[128,384]{1,0:T(8,128)S(1)} %get-tuple-element.41), channel_id=1, source_target_pairs={{0,28},{4,8},{8,4},{12,16},{16,12},{20,24},{24,20},{28,0},{1,29},{... | collective-permute-start | bytes 589832 | tf_op jit(solution)/shard_map/ppermute | solution.py:348
  10.7 6.4 %collective-permute-start.3 = (f32[128,384]{1,0:T(8,128)S(1)}, f32[128,384]{1,0:T(8,128)S(1)}, u32[]{:S(2)}, u32[]{:S(2)}) collective-permute-start(f32[128,384]{1,0:T(8,128)S(1)} %get-tuple-element.42), channel_id=1, source_target_pairs={{0,4},{4,0},{8,12},{12,8},{16,20},{20,16},{24,28},{28,24},{1,5},{5... | collective-permute-start | bytes 589832 | tf_op jit(solution)/shard_map/ppermute | solution.py:349
  17.1 2.8 %copy-start.7 = (f32[3,512]{1,0:T(4,128)S(1)}, f32[3,512]{1,0:T(4,128)}, u32[]{:S(2)}) copy-start(f32[3,512]{1,0:T(4,128)} %fractions_ref.1) | copy-start | bytes 18436
  17.7 9.7 %collective-permute-start.4 = (f32[128,384]{1,0:T(8,128)S(1)}, f32[128,384]{1,0:T(8,128)S(1)}, u32[]{:S(2)}, u32[]{:S(2)}) collective-permute-start(f32[128,384]{1,0:T(8,128)S(1)} %get-tuple-element.49), channel_id=1, source_target_pairs={{0,3},{1,2},{2,1},{3,0},{4,7},{5,6},{6,5},{7,4},{8,11},{9,10},{10,... | collective-permute-start | bytes 589832 | tf_op jit(solution)/shard_map/ppermute | solution.py:348
  19.0 9.7 %collective-permute-start.5 = (f32[128,384]{1,0:T(8,128)S(1)}, f32[128,384]{1,0:T(8,128)S(1)}, u32[]{:S(2)}, u32[]{:S(2)}) collective-permute-start(f32[128,384]{1,0:T(8,128)S(1)} %get-tuple-element.50), channel_id=1, source_target_pairs={{0,1},{1,0},{2,3},{3,2},{4,5},{5,4},{6,7},{7,6},{8,9},{9,8},{10,11... | collective-permute-start | bytes 589832 | tf_op jit(solution)/shard_map/ppermute | solution.py:349
  20.5 8.6 %collective-permute-start.6 = (f32[128,384]{1,0:T(8,128)S(1)}, f32[128,384]{1,0:T(8,128)S(1)}, u32[]{:S(2)}, u32[]{:S(2)}) collective-permute-start(f32[128,384]{1,0:T(8,128)S(1)} %get-tuple-element.51), channel_id=1, source_target_pairs={{0,28},{4,8},{8,4},{12,16},{16,12},{20,24},{24,20},{28,0},{1,29},{... | collective-permute-start | bytes 589832 | tf_op jit(solution)/shard_map/ppermute | solution.py:348
  21.3 7.8 %collective-permute-start.7 = (f32[128,384]{1,0:T(8,128)S(1)}, f32[128,384]{1,0:T(8,128)S(1)}, u32[]{:S(2)}, u32[]{:S(2)}) collective-permute-start(f32[128,384]{1,0:T(8,128)S(1)} %get-tuple-element.52), channel_id=1, source_target_pairs={{0,4},{4,0},{8,12},{12,8},{16,20},{20,16},{24,28},{28,24},{1,5},{5... | collective-permute-start | bytes 589832 | tf_op jit(solution)/shard_map/ppermute | solution.py:349
  22.2 6.8 %copy-start = (bf16[128,4]{0,1:T(4,128)(2,1)S(1)}, bf16[128,4]{0,1:T(4,128)(2,1)}, u32[]{:S(2)}) copy-start(bf16[128,4]{0,1:T(4,128)(2,1)} %param.20) | copy-start | bytes 3076
  29.8 1.3 %collective-permute-start.8 = (f32[80,128]{1,0:T(8,128)S(1)}, f32[80,128]{1,0:T(8,128)S(1)}, u32[]{:S(2)}, u32[]{:S(2)}) collective-permute-start(f32[80,128]{1,0:T(8,128)S(1)} %get-tuple-element.56), channel_id=1, source_target_pairs={{0,4},{4,0},{8,12},{12,8},{16,20},{20,16},{24,28},{28,24},{1,5},{5... | collective-permute-start | bytes 122888 | tf_op jit(solution)/shard_map/ppermute | solution.py:354
  29.9 10.1 %copy-start.2 = (s32[3,8192]{1,0:T(4,128)S(1)}, s32[3,8192]{1,0:T(4,128)}, u32[]{:S(2)}) copy-start(s32[3,8192]{1,0:T(4,128)} %numbers_ref.1) | copy-start | bytes 294916
  29.9 10.1 %copy-start.9 = (f32[3]{0:T(128)S(1)}, f32[3]{0:T(128)}, u32[]{:S(2)}) copy-start(f32[3]{0:T(128)} %cell_ref.1) | copy-start | bytes 40
  31.1 4.0 %collective-permute-start.9 = (f32[80,128]{1,0:T(8,128)S(1)}, f32[80,128]{1,0:T(8,128)S(1)}, u32[]{:S(2)}, u32[]{:S(2)}) collective-permute-start(f32[80,128]{1,0:T(8,128)S(1)} %add.15), channel_id=1, source_target_pairs={{0,8},{4,12},{8,0},{12,4},{16,24},{20,28},{24,16},{28,20},{1,9},{5... | collective-permute-start | bytes 122888 | tf_op jit(solution)/shard_map/ppermute | solution.py:354
  35.1 4.0 %collective-permute-start.10 = (f32[80,128]{1,0:T(8,128)S(1)}, f32[80,128]{1,0:T(8,128)S(1)}, u32[]{:S(2)}, u32[]{:S(2)}) collective-permute-start(f32[80,128]{1,0:T(8,128)S(1)} %add.16), channel_id=1, source_target_pairs={{0,16},{4,20},{8,24},{12,28},{16,0},{20,4},{24,8},{28,12},{1,17},{... | collective-permute-start | bytes 122888 | tf_op jit(solution)/shard_map/ppermute | solution.py:354
  39.1 4.0 %collective-permute-start.11 = (f32[80,128]{1,0:T(8,128)S(1)}, f32[80,128]{1,0:T(8,128)S(1)}, u32[]{:S(2)}, u32[]{:S(2)}) collective-permute-start(f32[80,128]{1,0:T(8,128)S(1)} %add.17), channel_id=1, source_target_pairs={{0,1},{1,0},{2,3},{3,2},{4,5},{5,4},{6,7},{7,6},{8,9},{9,8},{10,11... | collective-permute-start | bytes 122888 | tf_op jit(solution)/shard_map/ppermute | solution.py:354
  43.2 4.9 %collective-permute-start.12 = (f32[80,128]{1,0:T(8,128)S(1)}, f32[80,128]{1,0:T(8,128)S(1)}, u32[]{:S(2)}, u32[]{:S(2)}) collective-permute-start(f32[80,128]{1,0:T(8,128)S(1)} %add.18), channel_id=1, source_target_pairs={{0,2},{1,3},{2,0},{3,1},{4,6},{5,7},{6,4},{7,5},{8,10},{9,11},{10,... | collective-permute-start | bytes 122888 | tf_op jit(solution)/shard_map/ppermute | solution.py:354
  48.1 1.2 %collective-permute-start.13 = (f32[80,128]{1,0:T(8,128)S(1)}, f32[80,128]{1,0:T(8,128)S(1)}, u32[]{:S(2)}, u32[]{:S(2)}) collective-permute-start(f32[80,128]{1,0:T(8,128)S(1)} %add.19.half_ref), channel_id=1, source_target_pairs={{0,4},{4,0},{8,12},{12,8},{16,20},{20,16},{24,28},{28,24},{1,5},{5... | collective-permute-start | bytes 122888 | tf_op jit(solution)/shard_map/ppermute | solution.py:354

commit v6 on v5

--- a/solution.py
+++ b/solution.py
@@ -90,20 +90,20 @@
     lax.fori_loop(0, edges_ref.shape[0] // rows, one_tile, 0)
 
 
-def far_edge_kernel(senders_ref, radial_ref, index_ref, hidden_ref, edges_ref, pick_ref, pa, pb):
+def pick_kernel(index_ref, hidden_ref, pick_ref, pa, pb):
     wide_kernel(hidden_ref, index_ref, pa, pb)
     ghosts = index_ref.shape[1]
     for i, block in enumerate(block_order("narrow")):
         pick_ref[:, i * ghosts : (i + 1) * ghosts] = pick_matrix(
-            index_ref, block, senders_ref.shape[1]
+            index_ref, block, hidden_ref.shape[1]
         )
-    edge_tiles(senders_ref, radial_ref, edges_ref, 0, "wide")
-
-
-def near_edge_kernel(
-    senders_ref, radial_ref, self_ref, message_ref, edges_ref, self_rows_ref, message_rows_ref
+
+
+def edge_kernel(
+    senders_ref, radial_ref, self_ref, message_ref, near_ref, far_ref, self_rows_ref, message_rows_ref
 ):
-    edge_tiles(senders_ref, radial_ref, edges_ref, senders_ref.shape[1], "narrow")
+    edge_tiles(senders_ref, radial_ref, near_ref, senders_ref.shape[1], "narrow")
+    edge_tiles(senders_ref, radial_ref, far_ref, 0, "wide")
     for layer in range(self_ref.shape[0]):
         self_rows_ref[layer] = jnp.transpose(self_ref[layer].astype(f32)).astype(bf16)
         message = jnp.transpose(message_ref[layer].astype(f32)).astype(bf16)
@@ -350,19 +350,32 @@
     return one, two
 
 
-def flipped(block, axis, step):
-    return lax.ppermute(block, axis, [(i, i ^ step) for i in range(lax.axis_size(axis))])
+def flipped(block, wide_step, narrow_step):
+    wide, narrow = lax.axis_size("wide"), lax.axis_size("narrow")
+    pairs = [
+        (w * narrow + z, (w ^ wide_step) * narrow + (z ^ narrow_step))
+        for w in range(wide)
+        for z in range(narrow)
+    ]
+    return lax.ppermute(block, ("wide", "narrow"), pairs)
 
 
 def summed(send, keep, beside):
-    block = keep + flipped(send, "wide", 1)
-    for axis, step in (("wide", 2), ("narrow", 1)):
-        while step < lax.axis_size(axis):
-            if axis == "narrow" and 2 * step >= lax.axis_size(axis):
-                block, beside = lax.optimization_barrier((block, beside))
-            block = block + flipped(block, axis, step)
-            step *= 2
-    return block, flipped(block, "wide", 1), beside
+    wide_steps = [2**i for i in range(1, (lax.axis_size("wide") - 1).bit_length())]
+    narrow_steps = [2**i for i in range((lax.axis_size("narrow") - 1).bit_length())]
+    count = max(len(wide_steps), len(narrow_steps))
+    block = keep + flipped(send, 1, 0)
+    for i in range(count):
+        if i == count - 1:
+            block, beside = lax.optimization_barrier((block, beside))
+        wide_step = wide_steps[i] if i < len(wide_steps) else 0
+        narrow_step = narrow_steps[i] if i < len(narrow_steps) else 0
+        if wide_step and narrow_step:
+            one, two, three = [flipped(block, *steps) for steps in [(0, narrow_step), (wide_step, narrow_step), (wide_step, 0)]]
+            block = block + ((one + two) + three)
+        else:
+            block = block + flipped(block, wide_step, narrow_step)
+    return block, flipped(block, 1, 0), beside
 
 
 def per_device(
@@ -400,21 +413,16 @@
         cost=busy,
     )
     g2, g3 = matched(p2, p3, "narrow")
-    far_edges, picks, p0, p1 = call(
-        far_edge_kernel,
-        [((2 * ghosts, atoms), bf16), ((atoms, 2 * ghosts), bf16)] + picked_outs,
-        senders,
-        radial,
-        send_index,
-        hidden,
-        cost=busy,
+    picks, p0, p1 = call(
+        pick_kernel, [((atoms, 2 * ghosts), bf16)] + picked_outs, send_index, hidden, cost=busy
     )
     g0, g1 = matched(p0, p1, "wide")
     layers = self_weight.shape[0]
-    near_edges, self_rows, message_rows = call(
-        near_edge_kernel,
+    near_edges, far_edges, self_rows, message_rows = call(
+        edge_kernel,
         [
             ((rows - 2 * ghosts, atoms), bf16),
+            ((2 * ghosts, atoms), bf16),
             ((layers, width, width), bf16),
             ((layers, width, 2 * width), bf16),
         ],

time: 50.4 us -> 48.1 us (0.954)
  waiting for transfers between devices: 20.2 us -> 15.2 us
  starting transfers between devices: 15.7 us -> 18.4 us
    ppermute x6 -> x8, waiting for transfers between devices: 10.5 us -> 5.98 us  [flipped(): return lax.ppermute(block, ('wide', 'narrow'), pairs)]
    ppermute x6 -> x8, starting transfers between devices: 5.94 us -> 8.08 us  [flipped(): return lax.ppermute(block, ('wide', 'narrow'), pairs)]
    ppermute x4, waiting for transfers between devices: 5.71 us -> 4.7 us  [matched(): lax.ppermute(first, axis, [(i, (i + ways[i % 2]) % count) for i in range(...]
    ppermute x4, waiting for transfers between devices: 3.98 us -> 4.5 us  [matched(): lax.ppermute(second, axis, [(i, (i - ways[i % 2]) % count) for i in range...]
    ppermute x4, starting transfers between devices: 8.9 us -> 9.41 us  [matched(): lax.ppermute(first, axis, [(i, (i + ways[i % 2]) % count) for i in range(...]
  transfers between devices with their start and end apart: 14 -> 16, of which waited for: 10 -> 8; matrix products, arithmetic and copies ran while one was open for 0% -> 0% of each run, Pallas kernels for 18% -> 19%
where the time goes in v6:
time: 48.1 us; the launch traced here: 47.9 us
  starting transfers between devices  18.4 us (38%)
  waiting for transfers between devices  15.2 us (32%)
  Pallas kernels  11.9 us (25%)
  between operations  1.52 us (3%)
  local copies, waits for them, and re-layouts  0.92 us (2%)
    pallas_call x14, Pallas kernels, call(): pl.pallas_call(kernel, out_shape=[jax.ShapeDtypeStruct(shape, dtype) for...  11.9 us
    ppermute x4, starting transfers between devices, matched(): lax.ppermute(first, axis, [(i, (i + ways[i % 2]) % count) for i in range(...  9.41 us
    ppermute x8, starting transfers between devices, flipped(): return lax.ppermute(block, ('wide', 'narrow'), pairs)  8.08 us
    ppermute x8, waiting for transfers between devices, flipped(): return lax.ppermute(block, ('wide', 'narrow'), pairs)  5.98 us
    ppermute x4, waiting for transfers between devices, matched(): lax.ppermute(first, axis, [(i, (i + ways[i % 2]) % count) for i in range(...  4.7 us
    ppermute x4, waiting for transfers between devices, matched(): lax.ppermute(second, axis, [(i, (i - ways[i % 2]) % count) for i in range...  4.5 us
  transfers between devices with their start and end apart: 16, of which 8 were waited for; matrix products, arithmetic and copies ran while one was open for 0% of the time, Pallas kernels for 19%

profile of v6, /device:TPU:0, one launch (start us, length us, event | category | flops | bytes accessed | tf_op | source)
XLA Modules:
  0.0 47.9 jit_solution(3445834440932649584)
XLA Ops:
  0.7 0.9 %copy-done.1 = bf16[512,128]{1,0:T(8,128)(2,1)S(1)} copy-done((bf16[512,128]{1,0:T(8,128)(2,1)S(1)}, bf16[512,128]{1,0:T(8,128)(2,1)}, u32[]{:S(2)}) %copy-start.1) | copy-done | bytes 131096
  1.5 0.4 shard_map.131
  1.9 5.1 %collective-permute-start = (f32[128,384]{1,0:T(8,128)S(1)}, f32[128,384]{1,0:T(8,128)S(1)}, u32[]{:S(2)}, u32[]{:S(2)}) collective-permute-start(f32[128,384]{1,0:T(8,128)S(1)} %get-tuple-element.39), channel_id=1, source_target_pairs={{0,3},{1,2},{2,1},{3,0},{4,7},{5,6},{6,5},{7,4},{8,11},{9,10},{10,... | collective-permute-start | bytes 589832 | tf_op jit(solution)/shard_map/ppermute | solution.py:348
  7.1 0.4 shard_map.135
  7.5 1.7 %collective-permute-start.2 = (f32[128,384]{1,0:T(8,128)S(1)}, f32[128,384]{1,0:T(8,128)S(1)}, u32[]{:S(2)}, u32[]{:S(2)}) collective-permute-start(f32[128,384]{1,0:T(8,128)S(1)} %get-tuple-element.41), channel_id=1, source_target_pairs={{0,28},{4,8},{8,4},{12,16},{16,12},{20,24},{24,20},{28,0},{1,29},{... | collective-permute-start | bytes 589832 | tf_op jit(solution)/shard_map/ppermute | solution.py:348
  9.2 4.1 %shard_map.132 = (bf16[1280,512]{1,0:T(8,128)(2,1)S(1)}, bf16[768,512]{1,0:T(8,128)(2,1)S(1)}, bf16[2,128,128]{2,1,0:T(8,128)(2,1)S(1)}, bf16[2,128,256]{2,1,0:T(8,128)(2,1)S(1)}) custom-call(s32[16,512]{1,0:T(8,128)S(1)} %copy-done.5, f32[16,512]{1,0:T(8,128)S(1)} %copy-done.6, bf16[2,128,128]{2,1,0:T(8,128)(2,1)S(1)} %copy-done.3, ...), custom_call_target="tpu_custom_call" | custom-call | flops 1000000000 | bytes 20971520 | tf_op jit(solution)/shard_map/pallas_call | solution.py:334
  13.3 0.2 shard_map.133
  13.6 2.7 %collective-permute-done.1.g3 = f32[128,384]{1,0:T(8,128)S(1)} collective-permute-done((f32[128,384]{1,0:T(8,128)S(1)}, f32[128,384]{1,0:T(8,128)S(1)}, u32[]{:S(2)}, u32[]{:S(2)}) %collective-permute-start.1) | collective-permute-done | bytes 196640 | tf_op jit(solution)/shard_map/ppermute | solution.py:349
  16.3 0.3 shard_map.134.gathered_ref
  16.6 0.7 %shard_map.136 = (bf16[128,512]{1,0:T(8,128)(2,1)S(1)}, f32[128,384]{1,0:T(8,128)S(1)}, f32[128,384]{1,0:T(8,128)S(1)}) custom-call(bf16[128,512]{1,0:T(8,128)(2,1)S(1)} %get-tuple-element.34.hidden_ref, f32[128,512]{1,0:T(8,128)S(1)} %get-tuple-element.37.own_ref, f32[128,512]{1,0:T(8,128)S(1)} %shard_map.134.gathered_ref, ...), custom_call_target="tpu_custom_call" | custom-call | flops 1000000000 | bytes 20971520 | tf_op jit(solution)/shard_map/pallas_call | solution.py:334
  17.3 1.8 %collective-permute-start.4 = (f32[128,384]{1,0:T(8,128)S(1)}, f32[128,384]{1,0:T(8,128)S(1)}, u32[]{:S(2)}, u32[]{:S(2)}) collective-permute-start(f32[128,384]{1,0:T(8,128)S(1)} %get-tuple-element.49), channel_id=1, source_target_pairs={{0,3},{1,2},{2,1},{3,0},{4,7},{5,6},{6,5},{7,4},{8,11},{9,10},{10,... | collective-permute-start | bytes 589832 | tf_op jit(solution)/shard_map/ppermute | solution.py:348
  19.1 0.6 %shard_map.139 = (bf16[2,136,512]{2,1,0:T(8,128)(2,1)S(1)}, f32[24,512]{1,0:T(8,128)S(1)}, f32[128,384]{1,0:T(8,128)S(1)}, f32[128,384]{1,0:T(8,128)S(1)}) custom-call(f32[3,512]{1,0:T(4,128)S(1)} %copy-done.7, bf16[128,512]{1,0:T(8,128)(2,1)S(1)} %get-tuple-element.46.hidden_ref, s32[4,384]{1,0:T(4,128)S(1)} %copy-done.8), custom_call_target="tpu_custom_call" | custom-call | flops 1000000000 | bytes 20971520 | tf_op jit(solution)/shard_map/pallas_call | solution.py:334
  19.7 0.8 %collective-permute-start.6 = (f32[128,384]{1,0:T(8,128)S(1)}, f32[128,384]{1,0:T(8,128)S(1)}, u32[]{:S(2)}, u32[]{:S(2)}) collective-permute-start(f32[128,384]{1,0:T(8,128)S(1)} %get-tuple-element.51), channel_id=1, source_target_pairs={{0,28},{4,8},{8,4},{12,16},{16,12},{20,24},{24,20},{28,0},{1,29},{... | collective-permute-start | bytes 589832 | tf_op jit(solution)/shard_map/ppermute | solution.py:348
  20.5 0.8 %collective-permute-start.7 = (f32[128,384]{1,0:T(8,128)S(1)}, f32[128,384]{1,0:T(8,128)S(1)}, u32[]{:S(2)}, u32[]{:S(2)}) collective-permute-start(f32[128,384]{1,0:T(8,128)S(1)} %get-tuple-element.52), channel_id=1, source_target_pairs={{0,4},{4,0},{8,12},{12,8},{16,20},{20,16},{24,28},{28,24},{1,5},{5... | collective-permute-start | bytes 589832 | tf_op jit(solution)/shard_map/ppermute | solution.py:349
  22.0 0.3 shard_map.137
  22.2 4.7 %collective-permute-done.4.g2 = f32[128,384]{1,0:T(8,128)S(1)} collective-permute-done((f32[128,384]{1,0:T(8,128)S(1)}, f32[128,384]{1,0:T(8,128)S(1)}, u32[]{:S(2)}, u32[]{:S(2)}) %collective-permute-start.4) | collective-permute-done | bytes 196640 | tf_op jit(solution)/shard_map/ppermute | solution.py:348
  26.9 1.8 %collective-permute-done.5.g3 = f32[128,384]{1,0:T(8,128)S(1)} collective-permute-done((f32[128,384]{1,0:T(8,128)S(1)}, f32[128,384]{1,0:T(8,128)S(1)}, u32[]{:S(2)}, u32[]{:S(2)}) %collective-permute-start.5) | collective-permute-done | bytes 196640 | tf_op jit(solution)/shard_map/ppermute | solution.py:349
  28.8 0.3 shard_map.138.gathered_ref
  29.1 0.8 %shard_map.140 = (f32[80,128]{1,0:T(8,128)S(1)}, f32[72,512]{1,0:T(8,128)S(1)}) custom-call(bf16[128,512]{1,0:T(8,128)(2,1)S(1)} %get-tuple-element.46.hidden_ref, f32[128,512]{1,0:T(8,128)S(1)} %get-tuple-element.47.own_ref, f32[128,512]{1,0:T(8,128)S(1)} %shard_map.138.gathered_ref, f32[128,384]{1,0:T(8,128)S(1)} %collective-permute-done.6.g0, ...), custom_call_target="tpu_custom_call" | custom-call | tf_op jit(solution)/shard_map/pallas_call | solution.py:334
  30.1 1.0 %collective-permute-done.8 = f32[80,128]{1,0:T(8,128)S(1)} collective-permute-done((f32[80,128]{1,0:T(8,128)S(1)}, f32[80,128]{1,0:T(8,128)S(1)}, u32[]{:S(2)}, u32[]{:S(2)}) %collective-permute-start.8) | collective-permute-done | bytes 40992 | tf_op jit(solution)/shard_map/ppermute | solution.py:360
  31.1 1.2 %collective-permute-start.10 = (f32[80,128]{1,0:T(8,128)S(1)}, f32[80,128]{1,0:T(8,128)S(1)}, u32[]{:S(2)}, u32[]{:S(2)}) collective-permute-start(f32[80,128]{1,0:T(8,128)S(1)} %add.21), channel_id=1, source_target_pairs={{0,9},{1,8},{2,11},{3,10},{4,13},{5,12},{6,15},{7,14},{8,1},{9,0},... | collective-permute-start | bytes 122888 | tf_op jit(solution)/shard_map/ppermute | solution.py:360
  32.3 0.9 %collective-permute-start.11 = (f32[80,128]{1,0:T(8,128)S(1)}, f32[80,128]{1,0:T(8,128)S(1)}, u32[]{:S(2)}, u32[]{:S(2)}) collective-permute-start(f32[80,128]{1,0:T(8,128)S(1)} %add.21), channel_id=1, source_target_pairs={{0,8},{1,9},{2,10},{3,11},{4,12},{5,13},{6,14},{7,15},{8,0},{9,1},... | collective-permute-start | bytes 122888 | tf_op jit(solution)/shard_map/ppermute | solution.py:360
  33.2 1.4 %collective-permute-start.9 = (f32[80,128]{1,0:T(8,128)S(1)}, f32[80,128]{1,0:T(8,128)S(1)}, u32[]{:S(2)}, u32[]{:S(2)}) collective-permute-start(f32[80,128]{1,0:T(8,128)S(1)} %add.21), channel_id=1, source_target_pairs={{0,1},{1,0},{2,3},{3,2},{4,5},{5,4},{6,7},{7,6},{8,9},{9,8},{10,11... | collective-permute-start | bytes 122888 | tf_op jit(solution)/shard_map/ppermute | solution.py:360
  34.6 2.8 %shard_map.142 = (f32[72,136]{1,0:T(8,128)S(1)}, f32[8,512]{1,0:T(8,128)S(1)}, f32[3,512]{1,0:T(4,128)}) custom-call(f32[3]{0:T(128)S(1)} %copy-done.9, s32[3,8192]{1,0:T(4,128)S(1)} %copy-done.2, f32[72,512]{1,0:T(8,128)S(1)} %get-tuple-element.55.lattice_ref, f32[24,512]{1,0:T(8,128)S(1)} %get-tuple-element.54.third_ref, s32[1,1]{1,0:T(1,128)} %bitcast.4.count_ref), custom_call_target="tpu_custom_call" | custom-call | flops 1000000000 | bytes 20971520 | tf_op jit(solution)/shard_map/pallas_call | solution.py:334
  37.4 2.1 %collective-permute-start.12 = (f32[80,128]{1,0:T(8,128)S(1)}, f32[80,128]{1,0:T(8,128)S(1)}, u32[]{:S(2)}, u32[]{:S(2)}) collective-permute-start(f32[80,128]{1,0:T(8,128)S(1)} %add_add_fusion.1), channel_id=1, source_target_pairs={{0,2},{1,3},{2,0},{3,1},{4,6},{5,7},{6,4},{7,5},{8,10},{9,11},{10,... | collective-permute-start | bytes 122888 | tf_op jit(solution)/shard_map/ppermute | solution.py:360
  39.5 1.7 %collective-permute-start.13 = (f32[80,128]{1,0:T(8,128)S(1)}, f32[80,128]{1,0:T(8,128)S(1)}, u32[]{:S(2)}, u32[]{:S(2)}) collective-permute-start(f32[80,128]{1,0:T(8,128)S(1)} %add_add_fusion.1), channel_id=1, source_target_pairs={{0,18},{1,19},{2,16},{3,17},{4,22},{5,23},{6,20},{7,21},{8,26},{9,... | collective-permute-start | bytes 122888 | tf_op jit(solution)/shard_map/ppermute | solution.py:360
  41.2 0.7 %collective-permute-start.14 = (f32[80,128]{1,0:T(8,128)S(1)}, f32[80,128]{1,0:T(8,128)S(1)}, u32[]{:S(2)}, u32[]{:S(2)}) collective-permute-start(f32[80,128]{1,0:T(8,128)S(1)} %add_add_fusion.1), channel_id=1, source_target_pairs={{0,16},{1,17},{2,18},{3,19},{4,20},{5,21},{6,22},{7,23},{8,24},{9,... | collective-permute-start | bytes 122888 | tf_op jit(solution)/shard_map/ppermute | solution.py:360
  41.9 0.5 %collective-permute-done.12 = f32[80,128]{1,0:T(8,128)S(1)} collective-permute-done((f32[80,128]{1,0:T(8,128)S(1)}, f32[80,128]{1,0:T(8,128)S(1)}, u32[]{:S(2)}, u32[]{:S(2)}) %collective-permute-start.12) | collective-permute-done | bytes 40992 | tf_op jit(solution)/shard_map/ppermute | solution.py:360
  42.4 3.0 %collective-permute-done.13 = f32[80,128]{1,0:T(8,128)S(1)} collective-permute-done((f32[80,128]{1,0:T(8,128)S(1)}, f32[80,128]{1,0:T(8,128)S(1)}, u32[]{:S(2)}, u32[]{:S(2)}) %collective-permute-start.13) | collective-permute-done | bytes 40992 | tf_op jit(solution)/shard_map/ppermute | solution.py:360
  45.4 0.2 collective-permute-done.14
  45.7 1.2 %collective-permute-done.15.other_ref = f32[80,128]{1,0:T(8,128)S(1)} collective-permute-done((f32[80,128]{1,0:T(8,128)S(1)}, f32[80,128]{1,0:T(8,128)S(1)}, u32[]{:S(2)}, u32[]{:S(2)}) %collective-permute-start.15) | collective-permute-done | bytes 40992 | tf_op jit(solution)/shard_map/ppermute | solution.py:360
  47.0 1.0 %shard_map.143 = (f32[3,512]{1,0:T(4,128)}, f32[1,1]{1,0:T(1,128)}) custom-call(f32[80,128]{1,0:T(8,128)S(1)} %add_add_fusion.half_ref, f32[80,128]{1,0:T(8,128)S(1)} %collective-permute-done.15.other_ref, f32[72,512]{1,0:T(8,128)S(1)} %get-tuple-element.55.lattice_ref, bf16[2,136,512]{2,1,0:T(8,128)(2,1)S(1)} %get-tuple-element.53.phase_ref, ...), custom_call_target="tpu_custom_call" | custom-call | tf_op jit(solution)/shard_map/pallas_call | solution.py:334
  (37 shorter events, 0.5 us)
Async XLA Ops:
  0.6 0.9 %copy-start.1 = (bf16[512,128]{1,0:T(8,128)(2,1)S(1)}, bf16[512,128]{1,0:T(8,128)(2,1)}, u32[]{:S(2)}) copy-start(bf16[512,128]{1,0:T(8,128)(2,1)} %features_ref.1) | copy-start | bytes 393220
  0.6 0.9 %copy-start.8 = (s32[4,384]{1,0:T(4,128)S(1)}, s32[4,384]{1,0:T(4,128)}, u32[]{:S(2)}) copy-start(s32[4,384]{1,0:T(4,128)} %index_ref.5) | copy-start | bytes 18436
  1.9 11.6 %collective-permute-start = (f32[128,384]{1,0:T(8,128)S(1)}, f32[128,384]{1,0:T(8,128)S(1)}, u32[]{:S(2)}, u32[]{:S(2)}) collective-permute-start(f32[128,384]{1,0:T(8,128)S(1)} %get-tuple-element.39), channel_id=1, source_target_pairs={{0,3},{1,2},{2,1},{3,0},{4,7},{5,6},{6,5},{7,4},{8,11},{9,10},{10,... | collective-permute-start | bytes 589832 | tf_op jit(solution)/shard_map/ppermute | solution.py:348
  7.0 9.2 %collective-permute-start.1 = (f32[128,384]{1,0:T(8,128)S(1)}, f32[128,384]{1,0:T(8,128)S(1)}, u32[]{:S(2)}, u32[]{:S(2)}) collective-permute-start(f32[128,384]{1,0:T(8,128)S(1)} %get-tuple-element.40), channel_id=1, source_target_pairs={{0,1},{1,0},{2,3},{3,2},{4,5},{5,4},{6,7},{7,6},{8,9},{9,8},{10,11... | collective-permute-start | bytes 589832 | tf_op jit(solution)/shard_map/ppermute | solution.py:349
  7.0 2.1 %copy-start.3 = (bf16[2,128,128]{2,1,0:T(8,128)(2,1)S(1)}, bf16[2,128,128]{2,1,0:T(8,128)(2,1)}, u32[]{:S(2)}) copy-start(bf16[2,128,128]{2,1,0:T(8,128)(2,1)} %self_ref.1) | copy-start | bytes 196612
  7.0 2.1 %copy-start.4 = (bf16[2,128,128]{2,1,0:T(8,128)(2,1)S(1)}, bf16[2,128,128]{2,1,0:T(8,128)(2,1)}, u32[]{:S(2)}) copy-start(bf16[2,128,128]{2,1,0:T(8,128)(2,1)} %message_ref.1) | copy-start | bytes 196612
  7.1 2.1 %copy-start.5 = (s32[16,512]{1,0:T(8,128)S(1)}, s32[16,512]{1,0:T(8,128)}, u32[]{:S(2)}) copy-start(s32[16,512]{1,0:T(8,128)} %senders_ref.1) | copy-start | bytes 98308
  7.1 2.1 %copy-start.6 = (f32[16,512]{1,0:T(8,128)S(1)}, f32[16,512]{1,0:T(8,128)}, u32[]{:S(2)}) copy-start(f32[16,512]{1,0:T(8,128)} %radial_ref.1) | copy-start | bytes 98308
  7.5 9.1 %collective-permute-start.2 = (f32[128,384]{1,0:T(8,128)S(1)}, f32[128,384]{1,0:T(8,128)S(1)}, u32[]{:S(2)}, u32[]{:S(2)}) collective-permute-start(f32[128,384]{1,0:T(8,128)S(1)} %get-tuple-element.41), channel_id=1, source_target_pairs={{0,28},{4,8},{8,4},{12,16},{16,12},{20,24},{24,20},{28,0},{1,29},{... | collective-permute-start | bytes 589832 | tf_op jit(solution)/shard_map/ppermute | solution.py:348
  9.2 7.4 %collective-permute-start.3 = (f32[128,384]{1,0:T(8,128)S(1)}, f32[128,384]{1,0:T(8,128)S(1)}, u32[]{:S(2)}, u32[]{:S(2)}) collective-permute-start(f32[128,384]{1,0:T(8,128)S(1)} %get-tuple-element.42), channel_id=1, source_target_pairs={{0,4},{4,0},{8,12},{12,8},{16,20},{20,16},{24,28},{28,24},{1,5},{5... | collective-permute-start | bytes 589832 | tf_op jit(solution)/shard_map/ppermute | solution.py:349
  16.6 2.5 %copy-start.7 = (f32[3,512]{1,0:T(4,128)S(1)}, f32[3,512]{1,0:T(4,128)}, u32[]{:S(2)}) copy-start(f32[3,512]{1,0:T(4,128)} %fractions_ref.1) | copy-start | bytes 18436
  17.3 9.7 %collective-permute-start.4 = (f32[128,384]{1,0:T(8,128)S(1)}, f32[128,384]{1,0:T(8,128)S(1)}, u32[]{:S(2)}, u32[]{:S(2)}) collective-permute-start(f32[128,384]{1,0:T(8,128)S(1)} %get-tuple-element.49), channel_id=1, source_target_pairs={{0,3},{1,2},{2,1},{3,0},{4,7},{5,6},{6,5},{7,4},{8,11},{9,10},{10,... | collective-permute-start | bytes 589832 | tf_op jit(solution)/shard_map/ppermute | solution.py:348
  19.1 9.7 %collective-permute-start.5 = (f32[128,384]{1,0:T(8,128)S(1)}, f32[128,384]{1,0:T(8,128)S(1)}, u32[]{:S(2)}, u32[]{:S(2)}) collective-permute-start(f32[128,384]{1,0:T(8,128)S(1)} %get-tuple-element.50), channel_id=1, source_target_pairs={{0,1},{1,0},{2,3},{3,2},{4,5},{5,4},{6,7},{7,6},{8,9},{9,8},{10,11... | collective-permute-start | bytes 589832 | tf_op jit(solution)/shard_map/ppermute | solution.py:349
  19.7 9.4 %collective-permute-start.6 = (f32[128,384]{1,0:T(8,128)S(1)}, f32[128,384]{1,0:T(8,128)S(1)}, u32[]{:S(2)}, u32[]{:S(2)}) collective-permute-start(f32[128,384]{1,0:T(8,128)S(1)} %get-tuple-element.51), channel_id=1, source_target_pairs={{0,28},{4,8},{8,4},{12,16},{16,12},{20,24},{24,20},{28,0},{1,29},{... | collective-permute-start | bytes 589832 | tf_op jit(solution)/shard_map/ppermute | solution.py:348
  20.5 8.5 %collective-permute-start.7 = (f32[128,384]{1,0:T(8,128)S(1)}, f32[128,384]{1,0:T(8,128)S(1)}, u32[]{:S(2)}, u32[]{:S(2)}) collective-permute-start(f32[128,384]{1,0:T(8,128)S(1)} %get-tuple-element.52), channel_id=1, source_target_pairs={{0,4},{4,0},{8,12},{12,8},{16,20},{20,16},{24,28},{28,24},{1,5},{5... | collective-permute-start | bytes 589832 | tf_op jit(solution)/shard_map/ppermute | solution.py:349
  22.2 6.8 %copy-start = (bf16[128,4]{0,1:T(4,128)(2,1)S(1)}, bf16[128,4]{0,1:T(4,128)(2,1)}, u32[]{:S(2)}) copy-start(bf16[128,4]{0,1:T(4,128)(2,1)} %param.20) | copy-start | bytes 3076
  29.8 1.3 %collective-permute-start.8 = (f32[80,128]{1,0:T(8,128)S(1)}, f32[80,128]{1,0:T(8,128)S(1)}, u32[]{:S(2)}, u32[]{:S(2)}) collective-permute-start(f32[80,128]{1,0:T(8,128)S(1)} %get-tuple-element.56), channel_id=1, source_target_pairs={{0,4},{1,5},{2,6},{3,7},{4,0},{5,1},{6,2},{7,3},{8,12},{9,13},{10,... | collective-permute-start | bytes 122888 | tf_op jit(solution)/shard_map/ppermute | solution.py:360
  29.9 4.7 %copy-start.2 = (s32[3,8192]{1,0:T(4,128)S(1)}, s32[3,8192]{1,0:T(4,128)}, u32[]{:S(2)}) copy-start(s32[3,8192]{1,0:T(4,128)} %numbers_ref.1) | copy-start | bytes 294916
  29.9 4.7 %copy-start.9 = (f32[3]{0:T(128)S(1)}, f32[3]{0:T(128)}, u32[]{:S(2)}) copy-start(f32[3]{0:T(128)} %cell_ref.1) | copy-start | bytes 40
  31.1 6.3 %collective-permute-start.10 = (f32[80,128]{1,0:T(8,128)S(1)}, f32[80,128]{1,0:T(8,128)S(1)}, u32[]{:S(2)}, u32[]{:S(2)}) collective-permute-start(f32[80,128]{1,0:T(8,128)S(1)} %add.21), channel_id=1, source_target_pairs={{0,9},{1,8},{2,11},{3,10},{4,13},{5,12},{6,15},{7,14},{8,1},{9,0},... | collective-permute-start | bytes 122888 | tf_op jit(solution)/shard_map/ppermute | solution.py:360
  32.3 5.1 %collective-permute-start.11 = (f32[80,128]{1,0:T(8,128)S(1)}, f32[80,128]{1,0:T(8,128)S(1)}, u32[]{:S(2)}, u32[]{:S(2)}) collective-permute-start(f32[80,128]{1,0:T(8,128)S(1)} %add.21), channel_id=1, source_target_pairs={{0,8},{1,9},{2,10},{3,11},{4,12},{5,13},{6,14},{7,15},{8,0},{9,1},... | collective-permute-start | bytes 122888 | tf_op jit(solution)/shard_map/ppermute | solution.py:360
  33.2 4.2 %collective-permute-start.9 = (f32[80,128]{1,0:T(8,128)S(1)}, f32[80,128]{1,0:T(8,128)S(1)}, u32[]{:S(2)}, u32[]{:S(2)}) collective-permute-start(f32[80,128]{1,0:T(8,128)S(1)} %add.21), channel_id=1, source_target_pairs={{0,1},{1,0},{2,3},{3,2},{4,5},{5,4},{6,7},{7,6},{8,9},{9,8},{10,11... | collective-permute-start | bytes 122888 | tf_op jit(solution)/shard_map/ppermute | solution.py:360
  37.4 5.0 %collective-permute-start.12 = (f32[80,128]{1,0:T(8,128)S(1)}, f32[80,128]{1,0:T(8,128)S(1)}, u32[]{:S(2)}, u32[]{:S(2)}) collective-permute-start(f32[80,128]{1,0:T(8,128)S(1)} %add_add_fusion.1), channel_id=1, source_target_pairs={{0,2},{1,3},{2,0},{3,1},{4,6},{5,7},{6,4},{7,5},{8,10},{9,11},{10,... | collective-permute-start | bytes 122888 | tf_op jit(solution)/shard_map/ppermute | solution.py:360
  39.5 5.9 %collective-permute-start.13 = (f32[80,128]{1,0:T(8,128)S(1)}, f32[80,128]{1,0:T(8,128)S(1)}, u32[]{:S(2)}, u32[]{:S(2)}) collective-permute-start(f32[80,128]{1,0:T(8,128)S(1)} %add_add_fusion.1), channel_id=1, source_target_pairs={{0,18},{1,19},{2,16},{3,17},{4,22},{5,23},{6,20},{7,21},{8,26},{9,... | collective-permute-start | bytes 122888 | tf_op jit(solution)/shard_map/ppermute | solution.py:360
  41.2 4.4 %collective-permute-start.14 = (f32[80,128]{1,0:T(8,128)S(1)}, f32[80,128]{1,0:T(8,128)S(1)}, u32[]{:S(2)}, u32[]{:S(2)}) collective-permute-start(f32[80,128]{1,0:T(8,128)S(1)} %add_add_fusion.1), channel_id=1, source_target_pairs={{0,16},{1,17},{2,18},{3,19},{4,20},{5,21},{6,22},{7,23},{8,24},{9,... | collective-permute-start | bytes 122888 | tf_op jit(solution)/shard_map/ppermute | solution.py:360
  45.7 1.3 %collective-permute-start.15 = (f32[80,128]{1,0:T(8,128)S(1)}, f32[80,128]{1,0:T(8,128)S(1)}, u32[]{:S(2)}, u32[]{:S(2)}) collective-permute-start(f32[80,128]{1,0:T(8,128)S(1)} %add_add_fusion.half_ref), channel_id=1, source_target_pairs={{0,4},{1,5},{2,6},{3,7},{4,0},{5,1},{6,2},{7,3},{8,12},{9,13},{10,... | collective-permute-start | bytes 122888 | tf_op jit(solution)/shard_map/ppermute | solution.py:360

commit v7 on v6

--- a/solution.py
+++ b/solution.py
@@ -31,7 +31,7 @@
 
 
 def block_order(axis):
-    odd = parity(axis)
+    odd = parity(axis) if axis == "wide" else 1 - parity(axis)
     first = 0 if axis == "wide" else 2
     return first + odd, first + 1 - odd
 
@@ -344,7 +344,7 @@
 
 def matched(first, second, axis):
     count = lax.axis_size(axis)
-    ways = (-1, 1)
+    ways = (-1, 1) if axis == "wide" else (1, -1)
     one = lax.ppermute(first, axis, [(i, (i + ways[i % 2]) % count) for i in range(count)])
     two = lax.ppermute(second, axis, [(i, (i - ways[i % 2]) % count) for i in range(count)])
     return one, two
@@ -366,12 +366,16 @@
     count = max(len(wide_steps), len(narrow_steps))
     block = keep + flipped(send, 1, 0)
     for i in range(count):
-        if i == count - 1:
+        last = i == count - 1
+        if last:
             block, beside = lax.optimization_barrier((block, beside))
         wide_step = wide_steps[i] if i < len(wide_steps) else 0
         narrow_step = narrow_steps[i] if i < len(narrow_steps) else 0
         if wide_step and narrow_step:
-            one, two, three = [flipped(block, *steps) for steps in [(0, narrow_step), (wide_step, narrow_step), (wide_step, 0)]]
+            steps = [(0, narrow_step), (wide_step, narrow_step), (wide_step, 0)]
+            if last:
+                steps = [steps[1], steps[0], steps[2]]
+            one, two, three = [flipped(block, *step) for step in steps]
             block = block + ((one + two) + three)
         else:
             block = block + flipped(block, wide_step, narrow_step)

time: 48.1 us -> 47.4 us (0.985)
  waiting for transfers between devices: 15.2 us -> 12.7 us
  starting transfers between devices: 18.4 us -> 20.3 us
    ppermute x4, starting transfers between devices: 0.88 us -> 6.98 us  [matched(): lax.ppermute(second, axis, [(i, (i - ways[i % 2]) % count) for i in range...]
    ppermute x4, starting transfers between devices: 9.41 us -> 5.19 us  [matched(): lax.ppermute(first, axis, [(i, (i + ways[i % 2]) % count) for i in range(...]
    ppermute x4, waiting for transfers between devices: 4.5 us -> 2.45 us  [matched(): lax.ppermute(second, axis, [(i, (i - ways[i % 2]) % count) for i in range...]
    ppermute x8, waiting for transfers between devices: 5.98 us -> 5 us  [flipped(): return lax.ppermute(block, ('wide', 'narrow'), pairs)]
    ppermute x4, waiting for transfers between devices: 4.7 us -> 5.22 us  [matched(): lax.ppermute(first, axis, [(i, (i + ways[i % 2]) % count) for i in range(...]
where the time goes in v7:
time: 47.4 us; the launch traced here: 47.2 us
  starting transfers between devices  20.3 us (43%)
  waiting for transfers between devices  12.7 us (27%)
  Pallas kernels  11.9 us (25%)
  between operations  1.48 us (3%)
  local copies, waits for them, and re-layouts  0.92 us (2%)
    pallas_call x14, Pallas kernels, call(): pl.pallas_call(kernel, out_shape=[jax.ShapeDtypeStruct(shape, dtype) for...  11.9 us
    ppermute x8, starting transfers between devices, flipped(): return lax.ppermute(block, ('wide', 'narrow'), pairs)  8.08 us
    ppermute x4, starting transfers between devices, matched(): lax.ppermute(second, axis, [(i, (i - ways[i % 2]) % count) for i in range...  6.98 us
    ppermute x4, waiting for transfers between devices, matched(): lax.ppermute(first, axis, [(i, (i + ways[i % 2]) % count) for i in range(...  5.22 us
    ppermute x4, starting transfers between devices, matched(): lax.ppermute(first, axis, [(i, (i + ways[i % 2]) % count) for i in range(...  5.19 us
    ppermute x8, waiting for transfers between devices, flipped(): return lax.ppermute(block, ('wide', 'narrow'), pairs)  5 us
    ppermute x4, waiting for transfers between devices, matched(): lax.ppermute(second, axis, [(i, (i - ways[i % 2]) % count) for i in range...  2.45 us
  transfers between devices with their start and end apart: 16, of which 8 were waited for; matrix products, arithmetic and copies ran while one was open for 0% of the time, Pallas kernels for 19%

profile of v7, /device:TPU:0, one launch (start us, length us, event | category | flops | bytes accessed | tf_op | source)
XLA Modules:
  0.0 47.2 jit_solution(5112152906874247720)
XLA Ops:
  0.7 0.9 %copy-done.1 = bf16[512,128]{1,0:T(8,128)(2,1)S(1)} copy-done((bf16[512,128]{1,0:T(8,128)(2,1)S(1)}, bf16[512,128]{1,0:T(8,128)(2,1)}, u32[]{:S(2)}) %copy-start.1) | copy-done | bytes 131096
  1.5 0.4 shard_map.131
  1.9 3.1 %collective-permute-start = (f32[128,384]{1,0:T(8,128)S(1)}, f32[128,384]{1,0:T(8,128)S(1)}, u32[]{:S(2)}, u32[]{:S(2)}) collective-permute-start(f32[128,384]{1,0:T(8,128)S(1)} %get-tuple-element.39), channel_id=1, source_target_pairs={{0,1},{1,0},{2,3},{3,2},{4,5},{5,4},{6,7},{7,6},{8,9},{9,8},{10,11... | collective-permute-start | bytes 589832 | tf_op jit(solution)/shard_map/ppermute | solution.py:348
  5.0 2.5 %collective-permute-start.1 = (f32[128,384]{1,0:T(8,128)S(1)}, f32[128,384]{1,0:T(8,128)S(1)}, u32[]{:S(2)}, u32[]{:S(2)}) collective-permute-start(f32[128,384]{1,0:T(8,128)S(1)} %get-tuple-element.40), channel_id=1, source_target_pairs={{0,3},{1,2},{2,1},{3,0},{4,7},{5,6},{6,5},{7,4},{8,11},{9,10},{10,... | collective-permute-start | bytes 589832 | tf_op jit(solution)/shard_map/ppermute | solution.py:349
  7.5 0.4 shard_map.135
  7.9 1.4 %collective-permute-start.2 = (f32[128,384]{1,0:T(8,128)S(1)}, f32[128,384]{1,0:T(8,128)S(1)}, u32[]{:S(2)}, u32[]{:S(2)}) collective-permute-start(f32[128,384]{1,0:T(8,128)S(1)} %get-tuple-element.41), channel_id=1, source_target_pairs={{0,28},{4,8},{8,4},{12,16},{16,12},{20,24},{24,20},{28,0},{1,29},{... | collective-permute-start | bytes 589832 | tf_op jit(solution)/shard_map/ppermute | solution.py:348
  9.3 0.3 collective-permute-start.3
  9.6 4.1 %shard_map.132 = (bf16[1280,512]{1,0:T(8,128)(2,1)S(1)}, bf16[768,512]{1,0:T(8,128)(2,1)S(1)}, bf16[2,128,128]{2,1,0:T(8,128)(2,1)S(1)}, bf16[2,128,256]{2,1,0:T(8,128)(2,1)S(1)}) custom-call(s32[16,512]{1,0:T(8,128)S(1)} %copy-done.5, f32[16,512]{1,0:T(8,128)S(1)} %copy-done.6, bf16[2,128,128]{2,1,0:T(8,128)(2,1)S(1)} %copy-done.3, ...), custom_call_target="tpu_custom_call" | custom-call | flops 1000000000 | bytes 20971520 | tf_op jit(solution)/shard_map/pallas_call | solution.py:334
  14.0 2.4 %collective-permute-done.1.g3 = f32[128,384]{1,0:T(8,128)S(1)} collective-permute-done((f32[128,384]{1,0:T(8,128)S(1)}, f32[128,384]{1,0:T(8,128)S(1)}, u32[]{:S(2)}, u32[]{:S(2)}) %collective-permute-start.1) | collective-permute-done | bytes 196640 | tf_op jit(solution)/shard_map/ppermute | solution.py:349
  16.4 0.3 shard_map.134.gathered_ref
  16.7 0.7 %shard_map.136 = (bf16[128,512]{1,0:T(8,128)(2,1)S(1)}, f32[128,384]{1,0:T(8,128)S(1)}, f32[128,384]{1,0:T(8,128)S(1)}) custom-call(bf16[128,512]{1,0:T(8,128)(2,1)S(1)} %get-tuple-element.34.hidden_ref, f32[128,512]{1,0:T(8,128)S(1)} %get-tuple-element.37.own_ref, f32[128,512]{1,0:T(8,128)S(1)} %shard_map.134.gathered_ref, ...), custom_call_target="tpu_custom_call" | custom-call | flops 1000000000 | bytes 20971520 | tf_op jit(solution)/shard_map/pallas_call | solution.py:334
  17.4 0.6 %collective-permute-start.4 = (f32[128,384]{1,0:T(8,128)S(1)}, f32[128,384]{1,0:T(8,128)S(1)}, u32[]{:S(2)}, u32[]{:S(2)}) collective-permute-start(f32[128,384]{1,0:T(8,128)S(1)} %get-tuple-element.49), channel_id=1, source_target_pairs={{0,1},{1,0},{2,3},{3,2},{4,5},{5,4},{6,7},{7,6},{8,9},{9,8},{10,11... | collective-permute-start | bytes 589832 | tf_op jit(solution)/shard_map/ppermute | solution.py:348
  18.1 2.6 %collective-permute-start.5 = (f32[128,384]{1,0:T(8,128)S(1)}, f32[128,384]{1,0:T(8,128)S(1)}, u32[]{:S(2)}, u32[]{:S(2)}) collective-permute-start(f32[128,384]{1,0:T(8,128)S(1)} %get-tuple-element.50), channel_id=1, source_target_pairs={{0,3},{1,2},{2,1},{3,0},{4,7},{5,6},{6,5},{7,4},{8,11},{9,10},{10,... | collective-permute-start | bytes 589832 | tf_op jit(solution)/shard_map/ppermute | solution.py:349
  20.7 0.6 %shard_map.139 = (bf16[2,136,512]{2,1,0:T(8,128)(2,1)S(1)}, f32[24,512]{1,0:T(8,128)S(1)}, f32[128,384]{1,0:T(8,128)S(1)}, f32[128,384]{1,0:T(8,128)S(1)}) custom-call(f32[3,512]{1,0:T(4,128)S(1)} %copy-done.7, bf16[128,512]{1,0:T(8,128)(2,1)S(1)} %get-tuple-element.46.hidden_ref, s32[4,384]{1,0:T(4,128)S(1)} %copy-done.8), custom_call_target="tpu_custom_call" | custom-call | flops 1000000000 | bytes 20971520 | tf_op jit(solution)/shard_map/pallas_call | solution.py:334
  21.4 1.6 %collective-permute-start.7 = (f32[128,384]{1,0:T(8,128)S(1)}, f32[128,384]{1,0:T(8,128)S(1)}, u32[]{:S(2)}, u32[]{:S(2)}) collective-permute-start(f32[128,384]{1,0:T(8,128)S(1)} %get-tuple-element.52), channel_id=1, source_target_pairs={{0,4},{4,0},{8,12},{12,8},{16,20},{20,16},{24,28},{28,24},{1,5},{5... | collective-permute-start | bytes 589832 | tf_op jit(solution)/shard_map/ppermute | solution.py:349
  23.9 3.6 %collective-permute-done.4.g2 = f32[128,384]{1,0:T(8,128)S(1)} collective-permute-done((f32[128,384]{1,0:T(8,128)S(1)}, f32[128,384]{1,0:T(8,128)S(1)}, u32[]{:S(2)}, u32[]{:S(2)}) %collective-permute-start.4) | collective-permute-done | bytes 196640 | tf_op jit(solution)/shard_map/ppermute | solution.py:348
  27.4 0.3 shard_map.138.gathered_ref
  27.7 1.7 %collective-permute-done.6.g0 = f32[128,384]{1,0:T(8,128)S(1)} collective-permute-done((f32[128,384]{1,0:T(8,128)S(1)}, f32[128,384]{1,0:T(8,128)S(1)}, u32[]{:S(2)}, u32[]{:S(2)}) %collective-permute-start.6) | collective-permute-done | bytes 196640 | tf_op jit(solution)/shard_map/ppermute | solution.py:348
  29.4 0.8 %shard_map.140 = (f32[80,128]{1,0:T(8,128)S(1)}, f32[72,512]{1,0:T(8,128)S(1)}) custom-call(bf16[128,512]{1,0:T(8,128)(2,1)S(1)} %get-tuple-element.46.hidden_ref, f32[128,512]{1,0:T(8,128)S(1)} %get-tuple-element.47.own_ref, f32[128,512]{1,0:T(8,128)S(1)} %shard_map.138.gathered_ref, f32[128,384]{1,0:T(8,128)S(1)} %collective-permute-done.6.g0, ...), custom_call_target="tpu_custom_call" | custom-call | tf_op jit(solution)/shard_map/pallas_call | solution.py:334
  30.4 1.0 %collective-permute-done.8 = f32[80,128]{1,0:T(8,128)S(1)} collective-permute-done((f32[80,128]{1,0:T(8,128)S(1)}, f32[80,128]{1,0:T(8,128)S(1)}, u32[]{:S(2)}, u32[]{:S(2)}) %collective-permute-start.8) | collective-permute-done | bytes 40992 | tf_op jit(solution)/shard_map/ppermute | solution.py:360
  31.4 1.0 %collective-permute-start.10 = (f32[80,128]{1,0:T(8,128)S(1)}, f32[80,128]{1,0:T(8,128)S(1)}, u32[]{:S(2)}, u32[]{:S(2)}) collective-permute-start(f32[80,128]{1,0:T(8,128)S(1)} %add.21), channel_id=1, source_target_pairs={{0,9},{1,8},{2,11},{3,10},{4,13},{5,12},{6,15},{7,14},{8,1},{9,0},... | collective-permute-start | bytes 122888 | tf_op jit(solution)/shard_map/ppermute | solution.py:360
  32.5 0.5 %collective-permute-start.11 = (f32[80,128]{1,0:T(8,128)S(1)}, f32[80,128]{1,0:T(8,128)S(1)}, u32[]{:S(2)}, u32[]{:S(2)}) collective-permute-start(f32[80,128]{1,0:T(8,128)S(1)} %add.21), channel_id=1, source_target_pairs={{0,8},{1,9},{2,10},{3,11},{4,12},{5,13},{6,14},{7,15},{8,0},{9,1},... | collective-permute-start | bytes 122888 | tf_op jit(solution)/shard_map/ppermute | solution.py:360
  33.0 1.9 %collective-permute-start.9 = (f32[80,128]{1,0:T(8,128)S(1)}, f32[80,128]{1,0:T(8,128)S(1)}, u32[]{:S(2)}, u32[]{:S(2)}) collective-permute-start(f32[80,128]{1,0:T(8,128)S(1)} %add.21), channel_id=1, source_target_pairs={{0,1},{1,0},{2,3},{3,2},{4,5},{5,4},{6,7},{7,6},{8,9},{9,8},{10,11... | collective-permute-start | bytes 122888 | tf_op jit(solution)/shard_map/ppermute | solution.py:360
  34.9 2.8 %shard_map.142 = (f32[72,136]{1,0:T(8,128)S(1)}, f32[8,512]{1,0:T(8,128)S(1)}, f32[3,512]{1,0:T(4,128)}) custom-call(f32[3]{0:T(128)S(1)} %copy-done.9, s32[3,8192]{1,0:T(4,128)S(1)} %copy-done.2, f32[72,512]{1,0:T(8,128)S(1)} %get-tuple-element.55.lattice_ref, f32[24,512]{1,0:T(8,128)S(1)} %get-tuple-element.54.third_ref, s32[1,1]{1,0:T(1,128)} %bitcast.4.count_ref), custom_call_target="tpu_custom_call" | custom-call | flops 1000000000 | bytes 20971520 | tf_op jit(solution)/shard_map/pallas_call | solution.py:334
  37.7 1.3 %collective-permute-start.12 = (f32[80,128]{1,0:T(8,128)S(1)}, f32[80,128]{1,0:T(8,128)S(1)}, u32[]{:S(2)}, u32[]{:S(2)}) collective-permute-start(f32[80,128]{1,0:T(8,128)S(1)} %add_add_fusion.1), channel_id=1, source_target_pairs={{0,18},{1,19},{2,16},{3,17},{4,22},{5,23},{6,20},{7,21},{8,26},{9,... | collective-permute-start | bytes 122888 | tf_op jit(solution)/shard_map/ppermute | solution.py:360
  39.0 2.0 %collective-permute-start.13 = (f32[80,128]{1,0:T(8,128)S(1)}, f32[80,128]{1,0:T(8,128)S(1)}, u32[]{:S(2)}, u32[]{:S(2)}) collective-permute-start(f32[80,128]{1,0:T(8,128)S(1)} %add_add_fusion.1), channel_id=1, source_target_pairs={{0,2},{1,3},{2,0},{3,1},{4,6},{5,7},{6,4},{7,5},{8,10},{9,11},{10,... | collective-permute-start | bytes 122888 | tf_op jit(solution)/shard_map/ppermute | solution.py:360
  41.0 1.2 %collective-permute-start.14 = (f32[80,128]{1,0:T(8,128)S(1)}, f32[80,128]{1,0:T(8,128)S(1)}, u32[]{:S(2)}, u32[]{:S(2)}) collective-permute-start(f32[80,128]{1,0:T(8,128)S(1)} %add_add_fusion.1), channel_id=1, source_target_pairs={{0,16},{1,17},{2,18},{3,19},{4,20},{5,21},{6,22},{7,23},{8,24},{9,... | collective-permute-start | bytes 122888 | tf_op jit(solution)/shard_map/ppermute | solution.py:360
  42.2 1.4 %collective-permute-done.12 = f32[80,128]{1,0:T(8,128)S(1)} collective-permute-done((f32[80,128]{1,0:T(8,128)S(1)}, f32[80,128]{1,0:T(8,128)S(1)}, u32[]{:S(2)}, u32[]{:S(2)}) %collective-permute-start.12) | collective-permute-done | bytes 40992 | tf_op jit(solution)/shard_map/ppermute | solution.py:360
  43.6 0.3 collective-permute-done.13
  43.9 1.0 %collective-permute-done.14 = f32[80,128]{1,0:T(8,128)S(1)} collective-permute-done((f32[80,128]{1,0:T(8,128)S(1)}, f32[80,128]{1,0:T(8,128)S(1)}, u32[]{:S(2)}, u32[]{:S(2)}) %collective-permute-start.14) | collective-permute-done | bytes 40992 | tf_op jit(solution)/shard_map/ppermute | solution.py:360
  45.1 1.2 %collective-permute-done.15.other_ref = f32[80,128]{1,0:T(8,128)S(1)} collective-permute-done((f32[80,128]{1,0:T(8,128)S(1)}, f32[80,128]{1,0:T(8,128)S(1)}, u32[]{:S(2)}, u32[]{:S(2)}) %collective-permute-start.15) | collective-permute-done | bytes 40992 | tf_op jit(solution)/shard_map/ppermute | solution.py:360
  46.3 1.0 %shard_map.143 = (f32[3,512]{1,0:T(4,128)}, f32[1,1]{1,0:T(1,128)}) custom-call(f32[80,128]{1,0:T(8,128)S(1)} %add_add_fusion.half_ref, f32[80,128]{1,0:T(8,128)S(1)} %collective-permute-done.15.other_ref, f32[72,512]{1,0:T(8,128)S(1)} %get-tuple-element.55.lattice_ref, bf16[2,136,512]{2,1,0:T(8,128)(2,1)S(1)} %get-tuple-element.53.phase_ref, ...), custom_call_target="tpu_custom_call" | custom-call | tf_op jit(solution)/shard_map/pallas_call | solution.py:334
  (37 shorter events, 1.0 us)
Async XLA Ops:
  0.6 0.9 %copy-start.1 = (bf16[512,128]{1,0:T(8,128)(2,1)S(1)}, bf16[512,128]{1,0:T(8,128)(2,1)}, u32[]{:S(2)}) copy-start(bf16[512,128]{1,0:T(8,128)(2,1)} %features_ref.1) | copy-start | bytes 393220
  0.6 0.9 %copy-start.8 = (s32[4,384]{1,0:T(4,128)S(1)}, s32[4,384]{1,0:T(4,128)}, u32[]{:S(2)}) copy-start(s32[4,384]{1,0:T(4,128)} %index_ref.5) | copy-start | bytes 18436
  1.9 12.1 %collective-permute-start = (f32[128,384]{1,0:T(8,128)S(1)}, f32[128,384]{1,0:T(8,128)S(1)}, u32[]{:S(2)}, u32[]{:S(2)}) collective-permute-start(f32[128,384]{1,0:T(8,128)S(1)} %get-tuple-element.39), channel_id=1, source_target_pairs={{0,1},{1,0},{2,3},{3,2},{4,5},{5,4},{6,7},{7,6},{8,9},{9,8},{10,11... | collective-permute-start | bytes 589832 | tf_op jit(solution)/shard_map/ppermute | solution.py:348
  5.0 11.4 %collective-permute-start.1 = (f32[128,384]{1,0:T(8,128)S(1)}, f32[128,384]{1,0:T(8,128)S(1)}, u32[]{:S(2)}, u32[]{:S(2)}) collective-permute-start(f32[128,384]{1,0:T(8,128)S(1)} %get-tuple-element.40), channel_id=1, source_target_pairs={{0,3},{1,2},{2,1},{3,0},{4,7},{5,6},{6,5},{7,4},{8,11},{9,10},{10,... | collective-permute-start | bytes 589832 | tf_op jit(solution)/shard_map/ppermute | solution.py:349
  7.5 2.1 %copy-start.3 = (bf16[2,128,128]{2,1,0:T(8,128)(2,1)S(1)}, bf16[2,128,128]{2,1,0:T(8,128)(2,1)}, u32[]{:S(2)}) copy-start(bf16[2,128,128]{2,1,0:T(8,128)(2,1)} %self_ref.1) | copy-start | bytes 196612
  7.5 2.1 %copy-start.4 = (bf16[2,128,128]{2,1,0:T(8,128)(2,1)S(1)}, bf16[2,128,128]{2,1,0:T(8,128)(2,1)}, u32[]{:S(2)}) copy-start(bf16[2,128,128]{2,1,0:T(8,128)(2,1)} %message_ref.1) | copy-start | bytes 196612
  7.5 2.1 %copy-start.5 = (s32[16,512]{1,0:T(8,128)S(1)}, s32[16,512]{1,0:T(8,128)}, u32[]{:S(2)}) copy-start(s32[16,512]{1,0:T(8,128)} %senders_ref.1) | copy-start | bytes 98308
  7.5 2.1 %copy-start.6 = (f32[16,512]{1,0:T(8,128)S(1)}, f32[16,512]{1,0:T(8,128)}, u32[]{:S(2)}) copy-start(f32[16,512]{1,0:T(8,128)} %radial_ref.1) | copy-start | bytes 98308
  7.9 8.8 %collective-permute-start.2 = (f32[128,384]{1,0:T(8,128)S(1)}, f32[128,384]{1,0:T(8,128)S(1)}, u32[]{:S(2)}, u32[]{:S(2)}) collective-permute-start(f32[128,384]{1,0:T(8,128)S(1)} %get-tuple-element.41), channel_id=1, source_target_pairs={{0,28},{4,8},{8,4},{12,16},{16,12},{20,24},{24,20},{28,0},{1,29},{... | collective-permute-start | bytes 589832 | tf_op jit(solution)/shard_map/ppermute | solution.py:348
  9.3 7.4 %collective-permute-start.3 = (f32[128,384]{1,0:T(8,128)S(1)}, f32[128,384]{1,0:T(8,128)S(1)}, u32[]{:S(2)}, u32[]{:S(2)}) collective-permute-start(f32[128,384]{1,0:T(8,128)S(1)} %get-tuple-element.42), channel_id=1, source_target_pairs={{0,4},{4,0},{8,12},{12,8},{16,20},{20,16},{24,28},{28,24},{1,5},{5... | collective-permute-start | bytes 589832 | tf_op jit(solution)/shard_map/ppermute | solution.py:349
  16.7 4.0 %copy-start.7 = (f32[3,512]{1,0:T(4,128)S(1)}, f32[3,512]{1,0:T(4,128)}, u32[]{:S(2)}) copy-start(f32[3,512]{1,0:T(4,128)} %fractions_ref.1) | copy-start | bytes 18436
  17.4 10.0 %collective-permute-start.4 = (f32[128,384]{1,0:T(8,128)S(1)}, f32[128,384]{1,0:T(8,128)S(1)}, u32[]{:S(2)}, u32[]{:S(2)}) collective-permute-start(f32[128,384]{1,0:T(8,128)S(1)} %get-tuple-element.49), channel_id=1, source_target_pairs={{0,1},{1,0},{2,3},{3,2},{4,5},{5,4},{6,7},{7,6},{8,9},{9,8},{10,11... | collective-permute-start | bytes 589832 | tf_op jit(solution)/shard_map/ppermute | solution.py:348
  18.1 9.3 %collective-permute-start.5 = (f32[128,384]{1,0:T(8,128)S(1)}, f32[128,384]{1,0:T(8,128)S(1)}, u32[]{:S(2)}, u32[]{:S(2)}) collective-permute-start(f32[128,384]{1,0:T(8,128)S(1)} %get-tuple-element.50), channel_id=1, source_target_pairs={{0,3},{1,2},{2,1},{3,0},{4,7},{5,6},{6,5},{7,4},{8,11},{9,10},{10,... | collective-permute-start | bytes 589832 | tf_op jit(solution)/shard_map/ppermute | solution.py:349
  21.3 8.1 %collective-permute-start.6 = (f32[128,384]{1,0:T(8,128)S(1)}, f32[128,384]{1,0:T(8,128)S(1)}, u32[]{:S(2)}, u32[]{:S(2)}) collective-permute-start(f32[128,384]{1,0:T(8,128)S(1)} %get-tuple-element.51), channel_id=1, source_target_pairs={{0,28},{4,8},{8,4},{12,16},{16,12},{20,24},{24,20},{28,0},{1,29},{... | collective-permute-start | bytes 589832 | tf_op jit(solution)/shard_map/ppermute | solution.py:348
  21.4 8.0 %collective-permute-start.7 = (f32[128,384]{1,0:T(8,128)S(1)}, f32[128,384]{1,0:T(8,128)S(1)}, u32[]{:S(2)}, u32[]{:S(2)}) collective-permute-start(f32[128,384]{1,0:T(8,128)S(1)} %get-tuple-element.52), channel_id=1, source_target_pairs={{0,4},{4,0},{8,12},{12,8},{16,20},{20,16},{24,28},{28,24},{1,5},{5... | collective-permute-start | bytes 589832 | tf_op jit(solution)/shard_map/ppermute | solution.py:349
  23.9 5.5 %copy-start = (bf16[128,4]{0,1:T(4,128)(2,1)S(1)}, bf16[128,4]{0,1:T(4,128)(2,1)}, u32[]{:S(2)}) copy-start(bf16[128,4]{0,1:T(4,128)(2,1)} %param.20) | copy-start | bytes 3076
  30.1 1.3 %collective-permute-start.8 = (f32[80,128]{1,0:T(8,128)S(1)}, f32[80,128]{1,0:T(8,128)S(1)}, u32[]{:S(2)}, u32[]{:S(2)}) collective-permute-start(f32[80,128]{1,0:T(8,128)S(1)} %get-tuple-element.56), channel_id=1, source_target_pairs={{0,4},{1,5},{2,6},{3,7},{4,0},{5,1},{6,2},{7,3},{8,12},{9,13},{10,... | collective-permute-start | bytes 122888 | tf_op jit(solution)/shard_map/ppermute | solution.py:360
  30.2 4.7 %copy-start.2 = (s32[3,8192]{1,0:T(4,128)S(1)}, s32[3,8192]{1,0:T(4,128)}, u32[]{:S(2)}) copy-start(s32[3,8192]{1,0:T(4,128)} %numbers_ref.1) | copy-start | bytes 294916
  30.2 4.7 %copy-start.9 = (f32[3]{0:T(128)S(1)}, f32[3]{0:T(128)}, u32[]{:S(2)}) copy-start(f32[3]{0:T(128)} %cell_ref.1) | copy-start | bytes 40
  31.4 6.3 %collective-permute-start.10 = (f32[80,128]{1,0:T(8,128)S(1)}, f32[80,128]{1,0:T(8,128)S(1)}, u32[]{:S(2)}, u32[]{:S(2)}) collective-permute-start(f32[80,128]{1,0:T(8,128)S(1)} %add.21), channel_id=1, source_target_pairs={{0,9},{1,8},{2,11},{3,10},{4,13},{5,12},{6,15},{7,14},{8,1},{9,0},... | collective-permute-start | bytes 122888 | tf_op jit(solution)/shard_map/ppermute | solution.py:360
  32.5 5.2 %collective-permute-start.11 = (f32[80,128]{1,0:T(8,128)S(1)}, f32[80,128]{1,0:T(8,128)S(1)}, u32[]{:S(2)}, u32[]{:S(2)}) collective-permute-start(f32[80,128]{1,0:T(8,128)S(1)} %add.21), channel_id=1, source_target_pairs={{0,8},{1,9},{2,10},{3,11},{4,12},{5,13},{6,14},{7,15},{8,0},{9,1},... | collective-permute-start | bytes 122888 | tf_op jit(solution)/shard_map/ppermute | solution.py:360
  33.0 4.7 %collective-permute-start.9 = (f32[80,128]{1,0:T(8,128)S(1)}, f32[80,128]{1,0:T(8,128)S(1)}, u32[]{:S(2)}, u32[]{:S(2)}) collective-permute-start(f32[80,128]{1,0:T(8,128)S(1)} %add.21), channel_id=1, source_target_pairs={{0,1},{1,0},{2,3},{3,2},{4,5},{5,4},{6,7},{7,6},{8,9},{9,8},{10,11... | collective-permute-start | bytes 122888 | tf_op jit(solution)/shard_map/ppermute | solution.py:360
  37.7 5.9 %collective-permute-start.12 = (f32[80,128]{1,0:T(8,128)S(1)}, f32[80,128]{1,0:T(8,128)S(1)}, u32[]{:S(2)}, u32[]{:S(2)}) collective-permute-start(f32[80,128]{1,0:T(8,128)S(1)} %add_add_fusion.1), channel_id=1, source_target_pairs={{0,18},{1,19},{2,16},{3,17},{4,22},{5,23},{6,20},{7,21},{8,26},{9,... | collective-permute-start | bytes 122888 | tf_op jit(solution)/shard_map/ppermute | solution.py:360
  39.0 4.9 %collective-permute-start.13 = (f32[80,128]{1,0:T(8,128)S(1)}, f32[80,128]{1,0:T(8,128)S(1)}, u32[]{:S(2)}, u32[]{:S(2)}) collective-permute-start(f32[80,128]{1,0:T(8,128)S(1)} %add_add_fusion.1), channel_id=1, source_target_pairs={{0,2},{1,3},{2,0},{3,1},{4,6},{5,7},{6,4},{7,5},{8,10},{9,11},{10,... | collective-permute-start | bytes 122888 | tf_op jit(solution)/shard_map/ppermute | solution.py:360
  41.0 4.0 %collective-permute-start.14 = (f32[80,128]{1,0:T(8,128)S(1)}, f32[80,128]{1,0:T(8,128)S(1)}, u32[]{:S(2)}, u32[]{:S(2)}) collective-permute-start(f32[80,128]{1,0:T(8,128)S(1)} %add_add_fusion.1), channel_id=1, source_target_pairs={{0,16},{1,17},{2,18},{3,19},{4,20},{5,21},{6,22},{7,23},{8,24},{9,... | collective-permute-start | bytes 122888 | tf_op jit(solution)/shard_map/ppermute | solution.py:360
  45.0 1.3 %collective-permute-start.15 = (f32[80,128]{1,0:T(8,128)S(1)}, f32[80,128]{1,0:T(8,128)S(1)}, u32[]{:S(2)}, u32[]{:S(2)}) collective-permute-start(f32[80,128]{1,0:T(8,128)S(1)} %add_add_fusion.half_ref), channel_id=1, source_target_pairs={{0,4},{1,5},{2,6},{3,7},{4,0},{5,1},{6,2},{7,3},{8,12},{9,13},{10,... | collective-permute-start | bytes 122888 | tf_op jit(solution)/shard_map/ppermute | solution.py:360

commit v8 on v7

--- a/solution.py
+++ b/solution.py
@@ -361,24 +361,21 @@
 
 
 def summed(send, keep, beside):
-    wide_steps = [2**i for i in range(1, (lax.axis_size("wide") - 1).bit_length())]
-    narrow_steps = [2**i for i in range((lax.axis_size("narrow") - 1).bit_length())]
-    count = max(len(wide_steps), len(narrow_steps))
+    stages = []
+    for axis, step in (("wide", 2), ("narrow", 1)):
+        while step < lax.axis_size(axis):
+            if 2 * step < lax.axis_size(axis):
+                stage = (2 * step, 3 * step, step) if axis == "wide" else (3 * step, 2 * step, step)
+            else:
+                stage = (step,)
+            stages.append([(bits, 0) if axis == "wide" else (0, bits) for bits in stage])
+            step *= 4
     block = keep + flipped(send, 1, 0)
-    for i in range(count):
-        last = i == count - 1
-        if last:
+    for i, stage in enumerate(stages):
+        if i == len(stages) - 1:
             block, beside = lax.optimization_barrier((block, beside))
-        wide_step = wide_steps[i] if i < len(wide_steps) else 0
-        narrow_step = narrow_steps[i] if i < len(narrow_steps) else 0
-        if wide_step and narrow_step:
-            steps = [(0, narrow_step), (wide_step, narrow_step), (wide_step, 0)]
-            if last:
-                steps = [steps[1], steps[0], steps[2]]
-            one, two, three = [flipped(block, *step) for step in steps]
-            block = block + ((one + two) + three)
-        else:
-            block = block + flipped(block, wide_step, narrow_step)
+        received = [flipped(block, *steps) for steps in stage]
+        block = block + functools.reduce(jnp.add, received)
     return block, flipped(block, 1, 0), beside
 
 

time: 47.4 us -> 47 us (level)
  transfers between devices with their start and end apart: 16 -> 16, of which waited for: 8 -> 7; matrix products, arithmetic and copies ran while one was open for 0% -> 0% of each run, Pallas kernels for 19% -> 19%
where the time goes in v8:
time: 47 us; the launch traced here: 46.9 us
  starting transfers between devices  20.3 us (43%)
  waiting for transfers between devices  12.3 us (26%)
  Pallas kernels  11.9 us (25%)
  between operations  1.48 us (3%)
  local copies, waits for them, and re-layouts  0.92 us (2%)
    pallas_call x14, Pallas kernels, call(): pl.pallas_call(kernel, out_shape=[jax.ShapeDtypeStruct(shape, dtype) for...  11.9 us
    ppermute x8, starting transfers between devices, flipped(): return lax.ppermute(block, ('wide', 'narrow'), pairs)  8.08 us
    ppermute x4, starting transfers between devices, matched(): lax.ppermute(second, axis, [(i, (i - ways[i % 2]) % count) for i in range...  6.98 us
    ppermute x4, waiting for transfers between devices, matched(): lax.ppermute(first, axis, [(i, (i + ways[i % 2]) % count) for i in range(...  5.22 us
    ppermute x4, starting transfers between devices, matched(): lax.ppermute(first, axis, [(i, (i + ways[i % 2]) % count) for i in range(...  5.19 us
    ppermute x8, waiting for transfers between devices, flipped(): return lax.ppermute(block, ('wide', 'narrow'), pairs)  4.63 us
    ppermute x4, waiting for transfers between devices, matched(): lax.ppermute(second, axis, [(i, (i - ways[i % 2]) % count) for i in range...  2.45 us
  transfers between devices with their start and end apart: 16, of which 7 were waited for; matrix products, arithmetic and copies ran while one was open for 0% of the time, Pallas kernels for 19%

profile of v8, /device:TPU:0, one launch (start us, length us, event | category | flops | bytes accessed | tf_op | source)
XLA Modules:
  0.0 46.9 jit_solution(11803035394516759507)
XLA Ops:
  0.7 0.9 %copy-done.1 = bf16[512,128]{1,0:T(8,128)(2,1)S(1)} copy-done((bf16[512,128]{1,0:T(8,128)(2,1)S(1)}, bf16[512,128]{1,0:T(8,128)(2,1)}, u32[]{:S(2)}) %copy-start.1) | copy-done | bytes 131096
  1.5 0.4 shard_map.131
  1.9 3.1 %collective-permute-start = (f32[128,384]{1,0:T(8,128)S(1)}, f32[128,384]{1,0:T(8,128)S(1)}, u32[]{:S(2)}, u32[]{:S(2)}) collective-permute-start(f32[128,384]{1,0:T(8,128)S(1)} %get-tuple-element.39), channel_id=1, source_target_pairs={{0,1},{1,0},{2,3},{3,2},{4,5},{5,4},{6,7},{7,6},{8,9},{9,8},{10,11... | collective-permute-start | bytes 589832 | tf_op jit(solution)/shard_map/ppermute | solution.py:348
  5.0 2.5 %collective-permute-start.1 = (f32[128,384]{1,0:T(8,128)S(1)}, f32[128,384]{1,0:T(8,128)S(1)}, u32[]{:S(2)}, u32[]{:S(2)}) collective-permute-start(f32[128,384]{1,0:T(8,128)S(1)} %get-tuple-element.40), channel_id=1, source_target_pairs={{0,3},{1,2},{2,1},{3,0},{4,7},{5,6},{6,5},{7,4},{8,11},{9,10},{10,... | collective-permute-start | bytes 589832 | tf_op jit(solution)/shard_map/ppermute | solution.py:349
  7.5 0.4 shard_map.135
  7.9 1.4 %collective-permute-start.2 = (f32[128,384]{1,0:T(8,128)S(1)}, f32[128,384]{1,0:T(8,128)S(1)}, u32[]{:S(2)}, u32[]{:S(2)}) collective-permute-start(f32[128,384]{1,0:T(8,128)S(1)} %get-tuple-element.41), channel_id=1, source_target_pairs={{0,28},{4,8},{8,4},{12,16},{16,12},{20,24},{24,20},{28,0},{1,29},{... | collective-permute-start | bytes 589832 | tf_op jit(solution)/shard_map/ppermute | solution.py:348
  9.3 0.3 collective-permute-start.3
  9.6 4.1 %shard_map.132 = (bf16[1280,512]{1,0:T(8,128)(2,1)S(1)}, bf16[768,512]{1,0:T(8,128)(2,1)S(1)}, bf16[2,128,128]{2,1,0:T(8,128)(2,1)S(1)}, bf16[2,128,256]{2,1,0:T(8,128)(2,1)S(1)}) custom-call(s32[16,512]{1,0:T(8,128)S(1)} %copy-done.5, f32[16,512]{1,0:T(8,128)S(1)} %copy-done.6, bf16[2,128,128]{2,1,0:T(8,128)(2,1)S(1)} %copy-done.3, ...), custom_call_target="tpu_custom_call" | custom-call | flops 1000000000 | bytes 20971520 | tf_op jit(solution)/shard_map/pallas_call | solution.py:334
  13.7 0.3 shard_map.133
  14.0 2.4 %collective-permute-done.1.g3 = f32[128,384]{1,0:T(8,128)S(1)} collective-permute-done((f32[128,384]{1,0:T(8,128)S(1)}, f32[128,384]{1,0:T(8,128)S(1)}, u32[]{:S(2)}, u32[]{:S(2)}) %collective-permute-start.1) | collective-permute-done | bytes 196640 | tf_op jit(solution)/shard_map/ppermute | solution.py:349
  16.4 0.3 shard_map.134.gathered_ref
  16.7 0.7 %shard_map.136 = (bf16[128,512]{1,0:T(8,128)(2,1)S(1)}, f32[128,384]{1,0:T(8,128)S(1)}, f32[128,384]{1,0:T(8,128)S(1)}) custom-call(bf16[128,512]{1,0:T(8,128)(2,1)S(1)} %get-tuple-element.34.hidden_ref, f32[128,512]{1,0:T(8,128)S(1)} %get-tuple-element.37.own_ref, f32[128,512]{1,0:T(8,128)S(1)} %shard_map.134.gathered_ref, ...), custom_call_target="tpu_custom_call" | custom-call | flops 1000000000 | bytes 20971520 | tf_op jit(solution)/shard_map/pallas_call | solution.py:334
  17.4 0.6 %collective-permute-start.4 = (f32[128,384]{1,0:T(8,128)S(1)}, f32[128,384]{1,0:T(8,128)S(1)}, u32[]{:S(2)}, u32[]{:S(2)}) collective-permute-start(f32[128,384]{1,0:T(8,128)S(1)} %get-tuple-element.49), channel_id=1, source_target_pairs={{0,1},{1,0},{2,3},{3,2},{4,5},{5,4},{6,7},{7,6},{8,9},{9,8},{10,11... | collective-permute-start | bytes 589832 | tf_op jit(solution)/shard_map/ppermute | solution.py:348
  18.1 2.6 %collective-permute-start.5 = (f32[128,384]{1,0:T(8,128)S(1)}, f32[128,384]{1,0:T(8,128)S(1)}, u32[]{:S(2)}, u32[]{:S(2)}) collective-permute-start(f32[128,384]{1,0:T(8,128)S(1)} %get-tuple-element.50), channel_id=1, source_target_pairs={{0,3},{1,2},{2,1},{3,0},{4,7},{5,6},{6,5},{7,4},{8,11},{9,10},{10,... | collective-permute-start | bytes 589832 | tf_op jit(solution)/shard_map/ppermute | solution.py:349
  20.7 0.6 %shard_map.139 = (bf16[2,136,512]{2,1,0:T(8,128)(2,1)S(1)}, f32[24,512]{1,0:T(8,128)S(1)}, f32[128,384]{1,0:T(8,128)S(1)}, f32[128,384]{1,0:T(8,128)S(1)}) custom-call(f32[3,512]{1,0:T(4,128)S(1)} %copy-done.7, bf16[128,512]{1,0:T(8,128)(2,1)S(1)} %get-tuple-element.46.hidden_ref, s32[4,384]{1,0:T(4,128)S(1)} %copy-done.8), custom_call_target="tpu_custom_call" | custom-call | flops 1000000000 | bytes 20971520 | tf_op jit(solution)/shard_map/pallas_call | solution.py:334
  21.4 1.6 %collective-permute-start.7 = (f32[128,384]{1,0:T(8,128)S(1)}, f32[128,384]{1,0:T(8,128)S(1)}, u32[]{:S(2)}, u32[]{:S(2)}) collective-permute-start(f32[128,384]{1,0:T(8,128)S(1)} %get-tuple-element.52), channel_id=1, source_target_pairs={{0,4},{4,0},{8,12},{12,8},{16,20},{20,16},{24,28},{28,24},{1,5},{5... | collective-permute-start | bytes 589832 | tf_op jit(solution)/shard_map/ppermute | solution.py:349
  23.9 3.6 %collective-permute-done.4.g2 = f32[128,384]{1,0:T(8,128)S(1)} collective-permute-done((f32[128,384]{1,0:T(8,128)S(1)}, f32[128,384]{1,0:T(8,128)S(1)}, u32[]{:S(2)}, u32[]{:S(2)}) %collective-permute-start.4) | collective-permute-done | bytes 196640 | tf_op jit(solution)/shard_map/ppermute | solution.py:348
  27.4 0.3 shard_map.138.gathered_ref
  27.7 1.7 %collective-permute-done.6.g0 = f32[128,384]{1,0:T(8,128)S(1)} collective-permute-done((f32[128,384]{1,0:T(8,128)S(1)}, f32[128,384]{1,0:T(8,128)S(1)}, u32[]{:S(2)}, u32[]{:S(2)}) %collective-permute-start.6) | collective-permute-done | bytes 196640 | tf_op jit(solution)/shard_map/ppermute | solution.py:348
  29.4 0.8 %shard_map.140 = (f32[80,128]{1,0:T(8,128)S(1)}, f32[72,512]{1,0:T(8,128)S(1)}) custom-call(bf16[128,512]{1,0:T(8,128)(2,1)S(1)} %get-tuple-element.46.hidden_ref, f32[128,512]{1,0:T(8,128)S(1)} %get-tuple-element.47.own_ref, f32[128,512]{1,0:T(8,128)S(1)} %shard_map.138.gathered_ref, f32[128,384]{1,0:T(8,128)S(1)} %collective-permute-done.6.g0, ...), custom_call_target="tpu_custom_call" | custom-call | tf_op jit(solution)/shard_map/pallas_call | solution.py:334
  30.4 1.0 %collective-permute-done.8 = f32[80,128]{1,0:T(8,128)S(1)} collective-permute-done((f32[80,128]{1,0:T(8,128)S(1)}, f32[80,128]{1,0:T(8,128)S(1)}, u32[]{:S(2)}, u32[]{:S(2)}) %collective-permute-start.8) | collective-permute-done | bytes 40992 | tf_op jit(solution)/shard_map/ppermute | solution.py:360
  31.4 0.8 %collective-permute-start.10 = (f32[80,128]{1,0:T(8,128)S(1)}, f32[80,128]{1,0:T(8,128)S(1)}, u32[]{:S(2)}, u32[]{:S(2)}) collective-permute-start(f32[80,128]{1,0:T(8,128)S(1)} %add.21), channel_id=1, source_target_pairs={{0,24},{1,25},{2,26},{3,27},{4,28},{5,29},{6,30},{7,31},{8,16},{9,... | collective-permute-start | bytes 122888 | tf_op jit(solution)/shard_map/ppermute | solution.py:360
  32.3 1.3 %collective-permute-start.11 = (f32[80,128]{1,0:T(8,128)S(1)}, f32[80,128]{1,0:T(8,128)S(1)}, u32[]{:S(2)}, u32[]{:S(2)}) collective-permute-start(f32[80,128]{1,0:T(8,128)S(1)} %add.21), channel_id=1, source_target_pairs={{0,8},{1,9},{2,10},{3,11},{4,12},{5,13},{6,14},{7,15},{8,0},{9,1},... | collective-permute-start | bytes 122888 | tf_op jit(solution)/shard_map/ppermute | solution.py:360
  33.6 1.3 %collective-permute-start.9 = (f32[80,128]{1,0:T(8,128)S(1)}, f32[80,128]{1,0:T(8,128)S(1)}, u32[]{:S(2)}, u32[]{:S(2)}) collective-permute-start(f32[80,128]{1,0:T(8,128)S(1)} %add.21), channel_id=1, source_target_pairs={{0,16},{1,17},{2,18},{3,19},{4,20},{5,21},{6,22},{7,23},{8,24},{9,... | collective-permute-start | bytes 122888 | tf_op jit(solution)/shard_map/ppermute | solution.py:360
  34.9 2.8 %shard_map.142 = (f32[72,136]{1,0:T(8,128)S(1)}, f32[8,512]{1,0:T(8,128)S(1)}, f32[3,512]{1,0:T(4,128)}) custom-call(f32[3]{0:T(128)S(1)} %copy-done.9, s32[3,8192]{1,0:T(4,128)S(1)} %copy-done.2, f32[72,512]{1,0:T(8,128)S(1)} %get-tuple-element.55.lattice_ref, f32[24,512]{1,0:T(8,128)S(1)} %get-tuple-element.54.third_ref, s32[1,1]{1,0:T(1,128)} %bitcast.4.count_ref), custom_call_target="tpu_custom_call" | custom-call | flops 1000000000 | bytes 20971520 | tf_op jit(solution)/shard_map/pallas_call | solution.py:334
  37.7 1.3 %collective-permute-start.12 = (f32[80,128]{1,0:T(8,128)S(1)}, f32[80,128]{1,0:T(8,128)S(1)}, u32[]{:S(2)}, u32[]{:S(2)}) collective-permute-start(f32[80,128]{1,0:T(8,128)S(1)} %add_add_fusion.1), channel_id=1, source_target_pairs={{0,3},{1,2},{2,1},{3,0},{4,7},{5,6},{6,5},{7,4},{8,11},{9,10},{10,... | collective-permute-start | bytes 122888 | tf_op jit(solution)/shard_map/ppermute | solution.py:360
  39.0 1.1 %collective-permute-start.13 = (f32[80,128]{1,0:T(8,128)S(1)}, f32[80,128]{1,0:T(8,128)S(1)}, u32[]{:S(2)}, u32[]{:S(2)}) collective-permute-start(f32[80,128]{1,0:T(8,128)S(1)} %add_add_fusion.1), channel_id=1, source_target_pairs={{0,2},{1,3},{2,0},{3,1},{4,6},{5,7},{6,4},{7,5},{8,10},{9,11},{10,... | collective-permute-start | bytes 122888 | tf_op jit(solution)/shard_map/ppermute | solution.py:360
  40.1 2.1 %collective-permute-start.14 = (f32[80,128]{1,0:T(8,128)S(1)}, f32[80,128]{1,0:T(8,128)S(1)}, u32[]{:S(2)}, u32[]{:S(2)}) collective-permute-start(f32[80,128]{1,0:T(8,128)S(1)} %add_add_fusion.1), channel_id=1, source_target_pairs={{0,1},{1,0},{2,3},{3,2},{4,5},{5,4},{6,7},{7,6},{8,9},{9,8},{10,11... | collective-permute-start | bytes 122888 | tf_op jit(solution)/shard_map/ppermute | solution.py:360
  42.2 1.5 %collective-permute-done.12 = f32[80,128]{1,0:T(8,128)S(1)} collective-permute-done((f32[80,128]{1,0:T(8,128)S(1)}, f32[80,128]{1,0:T(8,128)S(1)}, u32[]{:S(2)}, u32[]{:S(2)}) %collective-permute-start.12) | collective-permute-done | bytes 40992 | tf_op jit(solution)/shard_map/ppermute | solution.py:360
  43.7 0.9 %collective-permute-done.13 = f32[80,128]{1,0:T(8,128)S(1)} collective-permute-done((f32[80,128]{1,0:T(8,128)S(1)}, f32[80,128]{1,0:T(8,128)S(1)}, u32[]{:S(2)}, u32[]{:S(2)}) %collective-permute-start.13) | collective-permute-done | bytes 40992 | tf_op jit(solution)/shard_map/ppermute | solution.py:360
  44.7 1.2 %collective-permute-done.15.other_ref = f32[80,128]{1,0:T(8,128)S(1)} collective-permute-done((f32[80,128]{1,0:T(8,128)S(1)}, f32[80,128]{1,0:T(8,128)S(1)}, u32[]{:S(2)}, u32[]{:S(2)}) %collective-permute-start.15) | collective-permute-done | bytes 40992 | tf_op jit(solution)/shard_map/ppermute | solution.py:360
  45.9 1.0 %shard_map.143 = (f32[3,512]{1,0:T(4,128)}, f32[1,1]{1,0:T(1,128)}) custom-call(f32[80,128]{1,0:T(8,128)S(1)} %add_add_fusion.half_ref, f32[80,128]{1,0:T(8,128)S(1)} %collective-permute-done.15.other_ref, f32[72,512]{1,0:T(8,128)S(1)} %get-tuple-element.55.lattice_ref, bf16[2,136,512]{2,1,0:T(8,128)(2,1)S(1)} %get-tuple-element.53.phase_ref, ...), custom_call_target="tpu_custom_call" | custom-call | tf_op jit(solution)/shard_map/pallas_call | solution.py:334
  (37 shorter events, 0.8 us)
Async XLA Ops:
  0.6 0.9 %copy-start.1 = (bf16[512,128]{1,0:T(8,128)(2,1)S(1)}, bf16[512,128]{1,0:T(8,128)(2,1)}, u32[]{:S(2)}) copy-start(bf16[512,128]{1,0:T(8,128)(2,1)} %features_ref.1) | copy-start | bytes 393220
  0.6 0.9 %copy-start.8 = (s32[4,384]{1,0:T(4,128)S(1)}, s32[4,384]{1,0:T(4,128)}, u32[]{:S(2)}) copy-start(s32[4,384]{1,0:T(4,128)} %index_ref.5) | copy-start | bytes 18436
  1.9 12.1 %collective-permute-start = (f32[128,384]{1,0:T(8,128)S(1)}, f32[128,384]{1,0:T(8,128)S(1)}, u32[]{:S(2)}, u32[]{:S(2)}) collective-permute-start(f32[128,384]{1,0:T(8,128)S(1)} %get-tuple-element.39), channel_id=1, source_target_pairs={{0,1},{1,0},{2,3},{3,2},{4,5},{5,4},{6,7},{7,6},{8,9},{9,8},{10,11... | collective-permute-start | bytes 589832 | tf_op jit(solution)/shard_map/ppermute | solution.py:348
  5.0 11.4 %collective-permute-start.1 = (f32[128,384]{1,0:T(8,128)S(1)}, f32[128,384]{1,0:T(8,128)S(1)}, u32[]{:S(2)}, u32[]{:S(2)}) collective-permute-start(f32[128,384]{1,0:T(8,128)S(1)} %get-tuple-element.40), channel_id=1, source_target_pairs={{0,3},{1,2},{2,1},{3,0},{4,7},{5,6},{6,5},{7,4},{8,11},{9,10},{10,... | collective-permute-start | bytes 589832 | tf_op jit(solution)/shard_map/ppermute | solution.py:349
  7.5 2.1 %copy-start.3 = (bf16[2,128,128]{2,1,0:T(8,128)(2,1)S(1)}, bf16[2,128,128]{2,1,0:T(8,128)(2,1)}, u32[]{:S(2)}) copy-start(bf16[2,128,128]{2,1,0:T(8,128)(2,1)} %self_ref.1) | copy-start | bytes 196612
  7.5 2.1 %copy-start.4 = (bf16[2,128,128]{2,1,0:T(8,128)(2,1)S(1)}, bf16[2,128,128]{2,1,0:T(8,128)(2,1)}, u32[]{:S(2)}) copy-start(bf16[2,128,128]{2,1,0:T(8,128)(2,1)} %message_ref.1) | copy-start | bytes 196612
  7.5 2.1 %copy-start.5 = (s32[16,512]{1,0:T(8,128)S(1)}, s32[16,512]{1,0:T(8,128)}, u32[]{:S(2)}) copy-start(s32[16,512]{1,0:T(8,128)} %senders_ref.1) | copy-start | bytes 98308
  7.5 2.1 %copy-start.6 = (f32[16,512]{1,0:T(8,128)S(1)}, f32[16,512]{1,0:T(8,128)}, u32[]{:S(2)}) copy-start(f32[16,512]{1,0:T(8,128)} %radial_ref.1) | copy-start | bytes 98308
  7.9 8.8 %collective-permute-start.2 = (f32[128,384]{1,0:T(8,128)S(1)}, f32[128,384]{1,0:T(8,128)S(1)}, u32[]{:S(2)}, u32[]{:S(2)}) collective-permute-start(f32[128,384]{1,0:T(8,128)S(1)} %get-tuple-element.41), channel_id=1, source_target_pairs={{0,28},{4,8},{8,4},{12,16},{16,12},{20,24},{24,20},{28,0},{1,29},{... | collective-permute-start | bytes 589832 | tf_op jit(solution)/shard_map/ppermute | solution.py:348
  9.3 7.4 %collective-permute-start.3 = (f32[128,384]{1,0:T(8,128)S(1)}, f32[128,384]{1,0:T(8,128)S(1)}, u32[]{:S(2)}, u32[]{:S(2)}) collective-permute-start(f32[128,384]{1,0:T(8,128)S(1)} %get-tuple-element.42), channel_id=1, source_target_pairs={{0,4},{4,0},{8,12},{12,8},{16,20},{20,16},{24,28},{28,24},{1,5},{5... | collective-permute-start | bytes 589832 | tf_op jit(solution)/shard_map/ppermute | solution.py:349
  16.7 4.0 %copy-start.7 = (f32[3,512]{1,0:T(4,128)S(1)}, f32[3,512]{1,0:T(4,128)}, u32[]{:S(2)}) copy-start(f32[3,512]{1,0:T(4,128)} %fractions_ref.1) | copy-start | bytes 18436
  17.4 10.0 %collective-permute-start.4 = (f32[128,384]{1,0:T(8,128)S(1)}, f32[128,384]{1,0:T(8,128)S(1)}, u32[]{:S(2)}, u32[]{:S(2)}) collective-permute-start(f32[128,384]{1,0:T(8,128)S(1)} %get-tuple-element.49), channel_id=1, source_target_pairs={{0,1},{1,0},{2,3},{3,2},{4,5},{5,4},{6,7},{7,6},{8,9},{9,8},{10,11... | collective-permute-start | bytes 589832 | tf_op jit(solution)/shard_map/ppermute | solution.py:348
  18.1 9.3 %collective-permute-start.5 = (f32[128,384]{1,0:T(8,128)S(1)}, f32[128,384]{1,0:T(8,128)S(1)}, u32[]{:S(2)}, u32[]{:S(2)}) collective-permute-start(f32[128,384]{1,0:T(8,128)S(1)} %get-tuple-element.50), channel_id=1, source_target_pairs={{0,3},{1,2},{2,1},{3,0},{4,7},{5,6},{6,5},{7,4},{8,11},{9,10},{10,... | collective-permute-start | bytes 589832 | tf_op jit(solution)/shard_map/ppermute | solution.py:349
  21.3 8.1 %collective-permute-start.6 = (f32[128,384]{1,0:T(8,128)S(1)}, f32[128,384]{1,0:T(8,128)S(1)}, u32[]{:S(2)}, u32[]{:S(2)}) collective-permute-start(f32[128,384]{1,0:T(8,128)S(1)} %get-tuple-element.51), channel_id=1, source_target_pairs={{0,28},{4,8},{8,4},{12,16},{16,12},{20,24},{24,20},{28,0},{1,29},{... | collective-permute-start | bytes 589832 | tf_op jit(solution)/shard_map/ppermute | solution.py:348
  21.4 8.0 %collective-permute-start.7 = (f32[128,384]{1,0:T(8,128)S(1)}, f32[128,384]{1,0:T(8,128)S(1)}, u32[]{:S(2)}, u32[]{:S(2)}) collective-permute-start(f32[128,384]{1,0:T(8,128)S(1)} %get-tuple-element.52), channel_id=1, source_target_pairs={{0,4},{4,0},{8,12},{12,8},{16,20},{20,16},{24,28},{28,24},{1,5},{5... | collective-permute-start | bytes 589832 | tf_op jit(solution)/shard_map/ppermute | solution.py:349
  23.9 5.5 %copy-start = (bf16[128,4]{0,1:T(4,128)(2,1)S(1)}, bf16[128,4]{0,1:T(4,128)(2,1)}, u32[]{:S(2)}) copy-start(bf16[128,4]{0,1:T(4,128)(2,1)} %param.20) | copy-start | bytes 3076
  30.1 1.3 %collective-permute-start.8 = (f32[80,128]{1,0:T(8,128)S(1)}, f32[80,128]{1,0:T(8,128)S(1)}, u32[]{:S(2)}, u32[]{:S(2)}) collective-permute-start(f32[80,128]{1,0:T(8,128)S(1)} %get-tuple-element.56), channel_id=1, source_target_pairs={{0,4},{1,5},{2,6},{3,7},{4,0},{5,1},{6,2},{7,3},{8,12},{9,13},{10,... | collective-permute-start | bytes 122888 | tf_op jit(solution)/shard_map/ppermute | solution.py:360
  30.2 4.7 %copy-start.2 = (s32[3,8192]{1,0:T(4,128)S(1)}, s32[3,8192]{1,0:T(4,128)}, u32[]{:S(2)}) copy-start(s32[3,8192]{1,0:T(4,128)} %numbers_ref.1) | copy-start | bytes 294916
  30.2 4.7 %copy-start.9 = (f32[3]{0:T(128)S(1)}, f32[3]{0:T(128)}, u32[]{:S(2)}) copy-start(f32[3]{0:T(128)} %cell_ref.1) | copy-start | bytes 40
  31.4 6.3 %collective-permute-start.10 = (f32[80,128]{1,0:T(8,128)S(1)}, f32[80,128]{1,0:T(8,128)S(1)}, u32[]{:S(2)}, u32[]{:S(2)}) collective-permute-start(f32[80,128]{1,0:T(8,128)S(1)} %add.21), channel_id=1, source_target_pairs={{0,24},{1,25},{2,26},{3,27},{4,28},{5,29},{6,30},{7,31},{8,16},{9,... | collective-permute-start | bytes 122888 | tf_op jit(solution)/shard_map/ppermute | solution.py:360
  32.3 5.5 %collective-permute-start.11 = (f32[80,128]{1,0:T(8,128)S(1)}, f32[80,128]{1,0:T(8,128)S(1)}, u32[]{:S(2)}, u32[]{:S(2)}) collective-permute-start(f32[80,128]{1,0:T(8,128)S(1)} %add.21), channel_id=1, source_target_pairs={{0,8},{1,9},{2,10},{3,11},{4,12},{5,13},{6,14},{7,15},{8,0},{9,1},... | collective-permute-start | bytes 122888 | tf_op jit(solution)/shard_map/ppermute | solution.py:360
  33.6 4.1 %collective-permute-start.9 = (f32[80,128]{1,0:T(8,128)S(1)}, f32[80,128]{1,0:T(8,128)S(1)}, u32[]{:S(2)}, u32[]{:S(2)}) collective-permute-start(f32[80,128]{1,0:T(8,128)S(1)} %add.21), channel_id=1, source_target_pairs={{0,16},{1,17},{2,18},{3,19},{4,20},{5,21},{6,22},{7,23},{8,24},{9,... | collective-permute-start | bytes 122888 | tf_op jit(solution)/shard_map/ppermute | solution.py:360
  37.7 6.0 %collective-permute-start.12 = (f32[80,128]{1,0:T(8,128)S(1)}, f32[80,128]{1,0:T(8,128)S(1)}, u32[]{:S(2)}, u32[]{:S(2)}) collective-permute-start(f32[80,128]{1,0:T(8,128)S(1)} %add_add_fusion.1), channel_id=1, source_target_pairs={{0,3},{1,2},{2,1},{3,0},{4,7},{5,6},{6,5},{7,4},{8,11},{9,10},{10,... | collective-permute-start | bytes 122888 | tf_op jit(solution)/shard_map/ppermute | solution.py:360
  39.0 5.6 %collective-permute-start.13 = (f32[80,128]{1,0:T(8,128)S(1)}, f32[80,128]{1,0:T(8,128)S(1)}, u32[]{:S(2)}, u32[]{:S(2)}) collective-permute-start(f32[80,128]{1,0:T(8,128)S(1)} %add_add_fusion.1), channel_id=1, source_target_pairs={{0,2},{1,3},{2,0},{3,1},{4,6},{5,7},{6,4},{7,5},{8,10},{9,11},{10,... | collective-permute-start | bytes 122888 | tf_op jit(solution)/shard_map/ppermute | solution.py:360
  40.1 4.5 %collective-permute-start.14 = (f32[80,128]{1,0:T(8,128)S(1)}, f32[80,128]{1,0:T(8,128)S(1)}, u32[]{:S(2)}, u32[]{:S(2)}) collective-permute-start(f32[80,128]{1,0:T(8,128)S(1)} %add_add_fusion.1), channel_id=1, source_target_pairs={{0,1},{1,0},{2,3},{3,2},{4,5},{5,4},{6,7},{7,6},{8,9},{9,8},{10,11... | collective-permute-start | bytes 122888 | tf_op jit(solution)/shard_map/ppermute | solution.py:360
  44.6 1.3 %collective-permute-start.15 = (f32[80,128]{1,0:T(8,128)S(1)}, f32[80,128]{1,0:T(8,128)S(1)}, u32[]{:S(2)}, u32[]{:S(2)}) collective-permute-start(f32[80,128]{1,0:T(8,128)S(1)} %add_add_fusion.half_ref), channel_id=1, source_target_pairs={{0,4},{1,5},{2,6},{3,7},{4,0},{5,1},{6,2},{7,3},{8,12},{9,13},{10,... | collective-permute-start | bytes 122888 | tf_op jit(solution)/shard_map/ppermute | solution.py:360

commit v9 on v8

--- a/solution.py
+++ b/solution.py
@@ -90,18 +90,23 @@
     lax.fori_loop(0, edges_ref.shape[0] // rows, one_tile, 0)
 
 
-def pick_kernel(index_ref, hidden_ref, pick_ref, pa, pb):
-    wide_kernel(hidden_ref, index_ref, pa, pb)
+def edge_kernel(
+    senders_ref,
+    radial_ref,
+    self_ref,
+    message_ref,
+    index_ref,
+    near_ref,
+    far_ref,
+    self_rows_ref,
+    message_rows_ref,
+    pick_ref,
+):
     ghosts = index_ref.shape[1]
     for i, block in enumerate(block_order("narrow")):
         pick_ref[:, i * ghosts : (i + 1) * ghosts] = pick_matrix(
-            index_ref, block, hidden_ref.shape[1]
+            index_ref, block, senders_ref.shape[1]
         )
-
-
-def edge_kernel(
-    senders_ref, radial_ref, self_ref, message_ref, near_ref, far_ref, self_rows_ref, message_rows_ref
-):
     edge_tiles(senders_ref, radial_ref, near_ref, senders_ref.shape[1], "narrow")
     edge_tiles(senders_ref, radial_ref, far_ref, 0, "wide")
     for layer in range(self_ref.shape[0]):
@@ -193,8 +198,7 @@
     return jnp.exp(-0.5 * smearing * smearing * squared) / squared
 
 
-def phase_kernel(fractions_ref, hidden_ref, index_ref, phase_ref, third_ref, p0, p1):
-    wide_kernel(hidden_ref, index_ref, p0, p1)
+def phase_kernel(fractions_ref, after_ref, phase_ref, third_ref):
     atoms = fractions_ref.shape[1]
     orders = lax.broadcasted_iota(jnp.int32, (8, atoms), 0).astype(f32) + 1.0
     cosines, sines = [], []
@@ -414,23 +418,23 @@
         cost=busy,
     )
     g2, g3 = matched(p2, p3, "narrow")
-    picks, p0, p1 = call(
-        pick_kernel, [((atoms, 2 * ghosts), bf16)] + picked_outs, send_index, hidden, cost=busy
-    )
+    p0, p1 = call(wide_kernel, picked_outs, hidden, send_index, cost=busy)
     g0, g1 = matched(p0, p1, "wide")
     layers = self_weight.shape[0]
-    near_edges, far_edges, self_rows, message_rows = call(
+    near_edges, far_edges, self_rows, message_rows, picks = call(
         edge_kernel,
         [
             ((rows - 2 * ghosts, atoms), bf16),
             ((2 * ghosts, atoms), bf16),
             ((layers, width, width), bf16),
             ((layers, width, 2 * width), bf16),
+            ((atoms, 2 * ghosts), bf16),
         ],
         senders,
         radial,
         self_weight,
         message_weight,
+        send_index,
         cost=busy,
     )
     for layer in range(layers):
@@ -454,15 +458,15 @@
             cost=busy,
         )
         g2, g3 = matched(p2, p3, "narrow")
-        phases, third, p0, p1 = call(
-            phase_kernel,
-            [((2, grid_rows, atoms), bf16), ((24, atoms), f32)] + picked_outs,
-            fractions,
-            hidden,
-            send_index,
-            cost=busy,
-        )
+        p0, p1 = call(wide_kernel, picked_outs, hidden, send_index, cost=busy)
         g0, g1 = matched(p0, p1, "wide")
+    phases, third = call(
+        phase_kernel,
+        [((2, grid_rows, atoms), bf16), ((24, atoms), f32)],
+        fractions,
+        hidden,
+        cost=busy,
+    )
     send, lattice = call(
         functools.partial(last_kernel, layers - 1),
         [((half_rows, 128), f32), ((72, atoms), f32)],

time: 47 us -> 47.1 us (level)
  waiting for transfers between devices: 12.3 us -> 11.6 us
    ppermute x4, waiting for transfers between devices: 5.22 us -> 4.49 us  [matched(): lax.ppermute(first, axis, [(i, (i + ways[i % 2]) % count) for i in range(...]
    pallas_call x14 -> x15, Pallas kernels: 11.9 us -> 12 us  [call(): pl.pallas_call(kernel, out_shape=[jax.ShapeDtypeStruct(shape, dtype) for...]
  transfers between devices with their start and end apart: 16 -> 16, of which waited for: 7 -> 8; matrix products, arithmetic and copies ran while one was open for 0% -> 0% of each run, Pallas kernels for 19% -> 20%
where the time goes in v9:
time: 47.1 us; the launch traced here: 46.8 us
  starting transfers between devices  20.3 us (43%)
  Pallas kernels  12 us (25%)
  waiting for transfers between devices  11.6 us (25%)
  between operations  1.49 us (3%)
  local copies, waits for them, and re-layouts  1.36 us (3%)
    pallas_call x15, Pallas kernels, call(): pl.pallas_call(kernel, out_shape=[jax.ShapeDtypeStruct(shape, dtype) for...  12 us
    ppermute x8, starting transfers between devices, flipped(): return lax.ppermute(block, ('wide', 'narrow'), pairs)  8.08 us
    ppermute x4, starting transfers between devices, matched(): lax.ppermute(second, axis, [(i, (i - ways[i % 2]) % count) for i in range...  7 us
    ppermute x4, starting transfers between devices, matched(): lax.ppermute(first, axis, [(i, (i + ways[i % 2]) % count) for i in range(...  5.2 us
    ppermute x8, waiting for transfers between devices, flipped(): return lax.ppermute(block, ('wide', 'narrow'), pairs)  4.77 us
    ppermute x4, waiting for transfers between devices, matched(): lax.ppermute(first, axis, [(i, (i + ways[i % 2]) % count) for i in range(...  4.49 us
    ppermute x4, waiting for transfers between devices, matched(): lax.ppermute(second, axis, [(i, (i - ways[i % 2]) % count) for i in range...  2.33 us
    unnamed x20, local copies, waits for them, and re-layouts  1.36 us
  transfers between devices with their start and end apart: 16, of which 8 were waited for; matrix products, arithmetic and copies ran while one was open for 0% of the time, Pallas kernels for 20%

profile of v9, /device:TPU:0, one launch (start us, length us, event | category | flops | bytes accessed | tf_op | source)
XLA Modules:
  0.0 46.8 jit_solution(4260093758409243923)
XLA Ops:
  0.7 0.7 %copy-done.8 = s32[4,384]{1,0:T(4,128)S(1)} copy-done((s32[4,384]{1,0:T(4,128)S(1)}, s32[4,384]{1,0:T(4,128)}, u32[]{:S(2)}) %copy-start.8) | copy-done | bytes 6168
  1.6 0.4 shard_map.131
  1.9 3.1 %collective-permute-start = (f32[128,384]{1,0:T(8,128)S(1)}, f32[128,384]{1,0:T(8,128)S(1)}, u32[]{:S(2)}, u32[]{:S(2)}) collective-permute-start(f32[128,384]{1,0:T(8,128)S(1)} %get-tuple-element.39), channel_id=1, source_target_pairs={{0,1},{1,0},{2,3},{3,2},{4,5},{5,4},{6,7},{7,6},{8,9},{9,8},{10,11... | collective-permute-start | bytes 589832 | tf_op jit(solution)/shard_map/ppermute | solution.py:352
  5.0 2.5 %collective-permute-start.1 = (f32[128,384]{1,0:T(8,128)S(1)}, f32[128,384]{1,0:T(8,128)S(1)}, u32[]{:S(2)}, u32[]{:S(2)}) collective-permute-start(f32[128,384]{1,0:T(8,128)S(1)} %get-tuple-element.40), channel_id=1, source_target_pairs={{0,3},{1,2},{2,1},{3,0},{4,7},{5,6},{6,5},{7,4},{8,11},{9,10},{10,... | collective-permute-start | bytes 589832 | tf_op jit(solution)/shard_map/ppermute | solution.py:353
  7.5 0.3 shard_map.135
  7.8 1.4 %collective-permute-start.2 = (f32[128,384]{1,0:T(8,128)S(1)}, f32[128,384]{1,0:T(8,128)S(1)}, u32[]{:S(2)}, u32[]{:S(2)}) collective-permute-start(f32[128,384]{1,0:T(8,128)S(1)} %get-tuple-element.41), channel_id=1, source_target_pairs={{0,28},{4,8},{8,4},{12,16},{16,12},{20,24},{24,20},{28,0},{1,29},{... | collective-permute-start | bytes 589832 | tf_op jit(solution)/shard_map/ppermute | solution.py:352
  9.2 0.3 collective-permute-start.3
  9.6 4.3 %shard_map.132 = (bf16[1280,512]{1,0:T(8,128)(2,1)S(1)}, bf16[768,512]{1,0:T(8,128)(2,1)S(1)}, bf16[2,128,128]{2,1,0:T(8,128)(2,1)S(1)}, bf16[2,128,256]{2,1,0:T(8,128)(2,1)S(1)}, bf16[512,768]{1,0:T(8,128)(2,1)S(1)}) custom-call(s32[16,512]{1,0:T(8,128)S(1)} %copy-done.5, f32[16,512]{1,0:T(8,128)S(1)} %copy-done.6, bf16[2,128,128]{2,1,0:T(8,128)(2,1)S(1)} %copy-done.3, ...), custom_call_target="tpu_custom_call" | custom-call | flops 1000000000 | bytes 20971520 | tf_op jit(solution)/shard_map/pallas_call | solution.py:338
  14.1 2.3 %collective-permute-done.1.g3 = f32[128,384]{1,0:T(8,128)S(1)} collective-permute-done((f32[128,384]{1,0:T(8,128)S(1)}, f32[128,384]{1,0:T(8,128)S(1)}, u32[]{:S(2)}, u32[]{:S(2)}) %collective-permute-start.1) | collective-permute-done | bytes 196640 | tf_op jit(solution)/shard_map/ppermute | solution.py:353
  16.4 0.3 shard_map.134.gathered_ref
  16.7 0.7 %shard_map.136 = (bf16[128,512]{1,0:T(8,128)(2,1)S(1)}, f32[128,384]{1,0:T(8,128)S(1)}, f32[128,384]{1,0:T(8,128)S(1)}) custom-call(bf16[128,512]{1,0:T(8,128)(2,1)S(1)} %get-tuple-element.34.hidden_ref, f32[128,512]{1,0:T(8,128)S(1)} %get-tuple-element.37.own_ref, f32[128,512]{1,0:T(8,128)S(1)} %shard_map.134.gathered_ref, ...), custom_call_target="tpu_custom_call" | custom-call | flops 1000000000 | bytes 20971520 | tf_op jit(solution)/shard_map/pallas_call | solution.py:338
  17.4 0.6 %collective-permute-start.4 = (f32[128,384]{1,0:T(8,128)S(1)}, f32[128,384]{1,0:T(8,128)S(1)}, u32[]{:S(2)}, u32[]{:S(2)}) collective-permute-start(f32[128,384]{1,0:T(8,128)S(1)} %get-tuple-element.49), channel_id=1, source_target_pairs={{0,1},{1,0},{2,3},{3,2},{4,5},{5,4},{6,7},{7,6},{8,9},{9,8},{10,11... | collective-permute-start | bytes 589832 | tf_op jit(solution)/shard_map/ppermute | solution.py:352
  18.1 2.6 %collective-permute-start.5 = (f32[128,384]{1,0:T(8,128)S(1)}, f32[128,384]{1,0:T(8,128)S(1)}, u32[]{:S(2)}, u32[]{:S(2)}) collective-permute-start(f32[128,384]{1,0:T(8,128)S(1)} %get-tuple-element.50), channel_id=1, source_target_pairs={{0,3},{1,2},{2,1},{3,0},{4,7},{5,6},{6,5},{7,4},{8,11},{9,10},{10,... | collective-permute-start | bytes 589832 | tf_op jit(solution)/shard_map/ppermute | solution.py:353
  20.7 0.3 shard_map.139
  21.1 1.6 %collective-permute-start.7 = (f32[128,384]{1,0:T(8,128)S(1)}, f32[128,384]{1,0:T(8,128)S(1)}, u32[]{:S(2)}, u32[]{:S(2)}) collective-permute-start(f32[128,384]{1,0:T(8,128)S(1)} %get-tuple-element.52), channel_id=1, source_target_pairs={{0,4},{4,0},{8,12},{12,8},{16,20},{20,16},{24,28},{28,24},{1,5},{5... | collective-permute-start | bytes 589832 | tf_op jit(solution)/shard_map/ppermute | solution.py:353
  23.7 0.4 copy-done.7
  24.4 3.1 %collective-permute-done.4.g2 = f32[128,384]{1,0:T(8,128)S(1)} collective-permute-done((f32[128,384]{1,0:T(8,128)S(1)}, f32[128,384]{1,0:T(8,128)S(1)}, u32[]{:S(2)}, u32[]{:S(2)}) %collective-permute-start.4) | collective-permute-done | bytes 196640 | tf_op jit(solution)/shard_map/ppermute | solution.py:352
  27.4 0.3 shard_map.138.gathered_ref
  27.7 1.4 %collective-permute-done.6.g0 = f32[128,384]{1,0:T(8,128)S(1)} collective-permute-done((f32[128,384]{1,0:T(8,128)S(1)}, f32[128,384]{1,0:T(8,128)S(1)}, u32[]{:S(2)}, u32[]{:S(2)}) %collective-permute-start.6) | collective-permute-done | bytes 196640 | tf_op jit(solution)/shard_map/ppermute | solution.py:352
  29.1 0.8 %shard_map.141 = (f32[80,128]{1,0:T(8,128)S(1)}, f32[72,512]{1,0:T(8,128)S(1)}) custom-call(bf16[128,512]{1,0:T(8,128)(2,1)S(1)} %get-tuple-element.46.hidden_ref.after_ref, f32[128,512]{1,0:T(8,128)S(1)} %get-tuple-element.47.own_ref, f32[128,512]{1,0:T(8,128)S(1)} %shard_map.138.gathered_ref, f32[128,384]{1,0:T(8,128)S(1)} %collective-permute-done.6.g0, ...), custom_call_target="tpu_custom_call" | custom-call | tf_op jit(solution)/shard_map/pallas_call | solution.py:338
  30.2 1.0 %collective-permute-done.8 = f32[80,128]{1,0:T(8,128)S(1)} collective-permute-done((f32[80,128]{1,0:T(8,128)S(1)}, f32[80,128]{1,0:T(8,128)S(1)}, u32[]{:S(2)}, u32[]{:S(2)}) %collective-permute-start.8) | collective-permute-done | bytes 40992 | tf_op jit(solution)/shard_map/ppermute | solution.py:364
  31.2 1.1 %collective-permute-start.10 = (f32[80,128]{1,0:T(8,128)S(1)}, f32[80,128]{1,0:T(8,128)S(1)}, u32[]{:S(2)}, u32[]{:S(2)}) collective-permute-start(f32[80,128]{1,0:T(8,128)S(1)} %add.21), channel_id=1, source_target_pairs={{0,24},{1,25},{2,26},{3,27},{4,28},{5,29},{6,30},{7,31},{8,16},{9,... | collective-permute-start | bytes 122888 | tf_op jit(solution)/shard_map/ppermute | solution.py:364
  32.3 1.1 %collective-permute-start.11 = (f32[80,128]{1,0:T(8,128)S(1)}, f32[80,128]{1,0:T(8,128)S(1)}, u32[]{:S(2)}, u32[]{:S(2)}) collective-permute-start(f32[80,128]{1,0:T(8,128)S(1)} %add.21), channel_id=1, source_target_pairs={{0,8},{1,9},{2,10},{3,11},{4,12},{5,13},{6,14},{7,15},{8,0},{9,1},... | collective-permute-start | bytes 122888 | tf_op jit(solution)/shard_map/ppermute | solution.py:364
  33.4 1.3 %collective-permute-start.9 = (f32[80,128]{1,0:T(8,128)S(1)}, f32[80,128]{1,0:T(8,128)S(1)}, u32[]{:S(2)}, u32[]{:S(2)}) collective-permute-start(f32[80,128]{1,0:T(8,128)S(1)} %add.21), channel_id=1, source_target_pairs={{0,16},{1,17},{2,18},{3,19},{4,20},{5,21},{6,22},{7,23},{8,24},{9,... | collective-permute-start | bytes 122888 | tf_op jit(solution)/shard_map/ppermute | solution.py:364
  34.7 2.8 %shard_map.143 = (f32[72,136]{1,0:T(8,128)S(1)}, f32[8,512]{1,0:T(8,128)S(1)}, f32[3,512]{1,0:T(4,128)}) custom-call(f32[3]{0:T(128)S(1)} %copy-done.9, s32[3,8192]{1,0:T(4,128)S(1)} %copy-done.2, f32[72,512]{1,0:T(8,128)S(1)} %get-tuple-element.55.lattice_ref, f32[24,512]{1,0:T(8,128)S(1)} %get-tuple-element.54.third_ref, s32[1,1]{1,0:T(1,128)} %bitcast.4.count_ref), custom_call_target="tpu_custom_call" | custom-call | flops 1000000000 | bytes 20971520 | tf_op jit(solution)/shard_map/pallas_call | solution.py:338
  37.5 1.5 %collective-permute-start.12 = (f32[80,128]{1,0:T(8,128)S(1)}, f32[80,128]{1,0:T(8,128)S(1)}, u32[]{:S(2)}, u32[]{:S(2)}) collective-permute-start(f32[80,128]{1,0:T(8,128)S(1)} %add_add_fusion.1), channel_id=1, source_target_pairs={{0,3},{1,2},{2,1},{3,0},{4,7},{5,6},{6,5},{7,4},{8,11},{9,10},{10,... | collective-permute-start | bytes 122888 | tf_op jit(solution)/shard_map/ppermute | solution.py:364
  39.0 1.1 %collective-permute-start.13 = (f32[80,128]{1,0:T(8,128)S(1)}, f32[80,128]{1,0:T(8,128)S(1)}, u32[]{:S(2)}, u32[]{:S(2)}) collective-permute-start(f32[80,128]{1,0:T(8,128)S(1)} %add_add_fusion.1), channel_id=1, source_target_pairs={{0,2},{1,3},{2,0},{3,1},{4,6},{5,7},{6,4},{7,5},{8,10},{9,11},{10,... | collective-permute-start | bytes 122888 | tf_op jit(solution)/shard_map/ppermute | solution.py:364
  40.1 1.9 %collective-permute-start.14 = (f32[80,128]{1,0:T(8,128)S(1)}, f32[80,128]{1,0:T(8,128)S(1)}, u32[]{:S(2)}, u32[]{:S(2)}) collective-permute-start(f32[80,128]{1,0:T(8,128)S(1)} %add_add_fusion.1), channel_id=1, source_target_pairs={{0,1},{1,0},{2,3},{3,2},{4,5},{5,4},{6,7},{7,6},{8,9},{9,8},{10,11... | collective-permute-start | bytes 122888 | tf_op jit(solution)/shard_map/ppermute | solution.py:364
  42.0 1.5 %collective-permute-done.12 = f32[80,128]{1,0:T(8,128)S(1)} collective-permute-done((f32[80,128]{1,0:T(8,128)S(1)}, f32[80,128]{1,0:T(8,128)S(1)}, u32[]{:S(2)}, u32[]{:S(2)}) %collective-permute-start.12) | collective-permute-done | bytes 40992 | tf_op jit(solution)/shard_map/ppermute | solution.py:364
  43.5 0.9 %collective-permute-done.13 = f32[80,128]{1,0:T(8,128)S(1)} collective-permute-done((f32[80,128]{1,0:T(8,128)S(1)}, f32[80,128]{1,0:T(8,128)S(1)}, u32[]{:S(2)}, u32[]{:S(2)}) %collective-permute-start.13) | collective-permute-done | bytes 40992 | tf_op jit(solution)/shard_map/ppermute | solution.py:364
  44.6 1.2 %collective-permute-done.15.other_ref = f32[80,128]{1,0:T(8,128)S(1)} collective-permute-done((f32[80,128]{1,0:T(8,128)S(1)}, f32[80,128]{1,0:T(8,128)S(1)}, u32[]{:S(2)}, u32[]{:S(2)}) %collective-permute-start.15) | collective-permute-done | bytes 40992 | tf_op jit(solution)/shard_map/ppermute | solution.py:364
  45.8 1.0 %shard_map.144 = (f32[3,512]{1,0:T(4,128)}, f32[1,1]{1,0:T(1,128)}) custom-call(f32[80,128]{1,0:T(8,128)S(1)} %add_add_fusion.half_ref, f32[80,128]{1,0:T(8,128)S(1)} %collective-permute-done.15.other_ref, f32[72,512]{1,0:T(8,128)S(1)} %get-tuple-element.55.lattice_ref, bf16[2,136,512]{2,1,0:T(8,128)(2,1)S(1)} %get-tuple-element.53.phase_ref, ...), custom_call_target="tpu_custom_call" | custom-call | tf_op jit(solution)/shard_map/pallas_call | solution.py:338
  (38 shorter events, 1.6 us)
Async XLA Ops:
  0.6 0.7 %copy-start.8 = (s32[4,384]{1,0:T(4,128)S(1)}, s32[4,384]{1,0:T(4,128)}, u32[]{:S(2)}) copy-start(s32[4,384]{1,0:T(4,128)} %index_ref.7) | copy-start | bytes 18436
  0.6 0.9 %copy-start.1 = (bf16[512,128]{1,0:T(8,128)(2,1)S(1)}, bf16[512,128]{1,0:T(8,128)(2,1)}, u32[]{:S(2)}) copy-start(bf16[512,128]{1,0:T(8,128)(2,1)} %features_ref.1) | copy-start | bytes 393220
  1.9 12.2 %collective-permute-start = (f32[128,384]{1,0:T(8,128)S(1)}, f32[128,384]{1,0:T(8,128)S(1)}, u32[]{:S(2)}, u32[]{:S(2)}) collective-permute-start(f32[128,384]{1,0:T(8,128)S(1)} %get-tuple-element.39), channel_id=1, source_target_pairs={{0,1},{1,0},{2,3},{3,2},{4,5},{5,4},{6,7},{7,6},{8,9},{9,8},{10,11... | collective-permute-start | bytes 589832 | tf_op jit(solution)/shard_map/ppermute | solution.py:352
  5.0 11.4 %collective-permute-start.1 = (f32[128,384]{1,0:T(8,128)S(1)}, f32[128,384]{1,0:T(8,128)S(1)}, u32[]{:S(2)}, u32[]{:S(2)}) collective-permute-start(f32[128,384]{1,0:T(8,128)S(1)} %get-tuple-element.40), channel_id=1, source_target_pairs={{0,3},{1,2},{2,1},{3,0},{4,7},{5,6},{6,5},{7,4},{8,11},{9,10},{10,... | collective-permute-start | bytes 589832 | tf_op jit(solution)/shard_map/ppermute | solution.py:353
  7.5 2.1 %copy-start.3 = (bf16[2,128,128]{2,1,0:T(8,128)(2,1)S(1)}, bf16[2,128,128]{2,1,0:T(8,128)(2,1)}, u32[]{:S(2)}) copy-start(bf16[2,128,128]{2,1,0:T(8,128)(2,1)} %self_ref.1) | copy-start | bytes 196612
  7.5 2.1 %copy-start.4 = (bf16[2,128,128]{2,1,0:T(8,128)(2,1)S(1)}, bf16[2,128,128]{2,1,0:T(8,128)(2,1)}, u32[]{:S(2)}) copy-start(bf16[2,128,128]{2,1,0:T(8,128)(2,1)} %message_ref.1) | copy-start | bytes 196612
  7.5 2.1 %copy-start.5 = (s32[16,512]{1,0:T(8,128)S(1)}, s32[16,512]{1,0:T(8,128)}, u32[]{:S(2)}) copy-start(s32[16,512]{1,0:T(8,128)} %senders_ref.1) | copy-start | bytes 98308
  7.5 2.1 %copy-start.6 = (f32[16,512]{1,0:T(8,128)S(1)}, f32[16,512]{1,0:T(8,128)}, u32[]{:S(2)}) copy-start(f32[16,512]{1,0:T(8,128)} %radial_ref.1) | copy-start | bytes 98308
  7.8 8.9 %collective-permute-start.2 = (f32[128,384]{1,0:T(8,128)S(1)}, f32[128,384]{1,0:T(8,128)S(1)}, u32[]{:S(2)}, u32[]{:S(2)}) collective-permute-start(f32[128,384]{1,0:T(8,128)S(1)} %get-tuple-element.41), channel_id=1, source_target_pairs={{0,28},{4,8},{8,4},{12,16},{16,12},{20,24},{24,20},{28,0},{1,29},{... | collective-permute-start | bytes 589832 | tf_op jit(solution)/shard_map/ppermute | solution.py:352
  9.2 7.5 %collective-permute-start.3 = (f32[128,384]{1,0:T(8,128)S(1)}, f32[128,384]{1,0:T(8,128)S(1)}, u32[]{:S(2)}, u32[]{:S(2)}) collective-permute-start(f32[128,384]{1,0:T(8,128)S(1)} %get-tuple-element.42), channel_id=1, source_target_pairs={{0,4},{4,0},{8,12},{12,8},{16,20},{20,16},{24,28},{28,24},{1,5},{5... | collective-permute-start | bytes 589832 | tf_op jit(solution)/shard_map/ppermute | solution.py:353
  17.4 10.0 %collective-permute-start.4 = (f32[128,384]{1,0:T(8,128)S(1)}, f32[128,384]{1,0:T(8,128)S(1)}, u32[]{:S(2)}, u32[]{:S(2)}) collective-permute-start(f32[128,384]{1,0:T(8,128)S(1)} %get-tuple-element.49), channel_id=1, source_target_pairs={{0,1},{1,0},{2,3},{3,2},{4,5},{5,4},{6,7},{7,6},{8,9},{9,8},{10,11... | collective-permute-start | bytes 589832 | tf_op jit(solution)/shard_map/ppermute | solution.py:352
  18.1 9.4 %collective-permute-start.5 = (f32[128,384]{1,0:T(8,128)S(1)}, f32[128,384]{1,0:T(8,128)S(1)}, u32[]{:S(2)}, u32[]{:S(2)}) collective-permute-start(f32[128,384]{1,0:T(8,128)S(1)} %get-tuple-element.50), channel_id=1, source_target_pairs={{0,3},{1,2},{2,1},{3,0},{4,7},{5,6},{6,5},{7,4},{8,11},{9,10},{10,... | collective-permute-start | bytes 589832 | tf_op jit(solution)/shard_map/ppermute | solution.py:353
  21.1 8.1 %collective-permute-start.6 = (f32[128,384]{1,0:T(8,128)S(1)}, f32[128,384]{1,0:T(8,128)S(1)}, u32[]{:S(2)}, u32[]{:S(2)}) collective-permute-start(f32[128,384]{1,0:T(8,128)S(1)} %get-tuple-element.51), channel_id=1, source_target_pairs={{0,28},{4,8},{8,4},{12,16},{16,12},{20,24},{24,20},{28,0},{1,29},{... | collective-permute-start | bytes 589832 | tf_op jit(solution)/shard_map/ppermute | solution.py:352
  21.1 8.0 %collective-permute-start.7 = (f32[128,384]{1,0:T(8,128)S(1)}, f32[128,384]{1,0:T(8,128)S(1)}, u32[]{:S(2)}, u32[]{:S(2)}) collective-permute-start(f32[128,384]{1,0:T(8,128)S(1)} %get-tuple-element.52), channel_id=1, source_target_pairs={{0,4},{4,0},{8,12},{12,8},{16,20},{20,16},{24,28},{28,24},{1,5},{5... | collective-permute-start | bytes 589832 | tf_op jit(solution)/shard_map/ppermute | solution.py:353
  23.4 0.7 %copy-start.7 = (f32[3,512]{1,0:T(4,128)S(1)}, f32[3,512]{1,0:T(4,128)}, u32[]{:S(2)}) copy-start(f32[3,512]{1,0:T(4,128)} %fractions_ref.1) | copy-start | bytes 18436
  24.4 4.8 %copy-start = (bf16[128,4]{0,1:T(4,128)(2,1)S(1)}, bf16[128,4]{0,1:T(4,128)(2,1)}, u32[]{:S(2)}) copy-start(bf16[128,4]{0,1:T(4,128)(2,1)} %param.20) | copy-start | bytes 3076
  29.9 1.3 %collective-permute-start.8 = (f32[80,128]{1,0:T(8,128)S(1)}, f32[80,128]{1,0:T(8,128)S(1)}, u32[]{:S(2)}, u32[]{:S(2)}) collective-permute-start(f32[80,128]{1,0:T(8,128)S(1)} %get-tuple-element.56), channel_id=1, source_target_pairs={{0,4},{1,5},{2,6},{3,7},{4,0},{5,1},{6,2},{7,3},{8,12},{9,13},{10,... | collective-permute-start | bytes 122888 | tf_op jit(solution)/shard_map/ppermute | solution.py:364
  30.0 4.7 %copy-start.2 = (s32[3,8192]{1,0:T(4,128)S(1)}, s32[3,8192]{1,0:T(4,128)}, u32[]{:S(2)}) copy-start(s32[3,8192]{1,0:T(4,128)} %numbers_ref.1) | copy-start | bytes 294916
  30.0 4.7 %copy-start.9 = (f32[3]{0:T(128)S(1)}, f32[3]{0:T(128)}, u32[]{:S(2)}) copy-start(f32[3]{0:T(128)} %cell_ref.1) | copy-start | bytes 40
  31.2 6.3 %collective-permute-start.10 = (f32[80,128]{1,0:T(8,128)S(1)}, f32[80,128]{1,0:T(8,128)S(1)}, u32[]{:S(2)}, u32[]{:S(2)}) collective-permute-start(f32[80,128]{1,0:T(8,128)S(1)} %add.21), channel_id=1, source_target_pairs={{0,24},{1,25},{2,26},{3,27},{4,28},{5,29},{6,30},{7,31},{8,16},{9,... | collective-permute-start | bytes 122888 | tf_op jit(solution)/shard_map/ppermute | solution.py:364
  32.3 5.2 %collective-permute-start.11 = (f32[80,128]{1,0:T(8,128)S(1)}, f32[80,128]{1,0:T(8,128)S(1)}, u32[]{:S(2)}, u32[]{:S(2)}) collective-permute-start(f32[80,128]{1,0:T(8,128)S(1)} %add.21), channel_id=1, source_target_pairs={{0,8},{1,9},{2,10},{3,11},{4,12},{5,13},{6,14},{7,15},{8,0},{9,1},... | collective-permute-start | bytes 122888 | tf_op jit(solution)/shard_map/ppermute | solution.py:364
  33.4 4.1 %collective-permute-start.9 = (f32[80,128]{1,0:T(8,128)S(1)}, f32[80,128]{1,0:T(8,128)S(1)}, u32[]{:S(2)}, u32[]{:S(2)}) collective-permute-start(f32[80,128]{1,0:T(8,128)S(1)} %add.21), channel_id=1, source_target_pairs={{0,16},{1,17},{2,18},{3,19},{4,20},{5,21},{6,22},{7,23},{8,24},{9,... | collective-permute-start | bytes 122888 | tf_op jit(solution)/shard_map/ppermute | solution.py:364
  37.5 6.0 %collective-permute-start.12 = (f32[80,128]{1,0:T(8,128)S(1)}, f32[80,128]{1,0:T(8,128)S(1)}, u32[]{:S(2)}, u32[]{:S(2)}) collective-permute-start(f32[80,128]{1,0:T(8,128)S(1)} %add_add_fusion.1), channel_id=1, source_target_pairs={{0,3},{1,2},{2,1},{3,0},{4,7},{5,6},{6,5},{7,4},{8,11},{9,10},{10,... | collective-permute-start | bytes 122888 | tf_op jit(solution)/shard_map/ppermute | solution.py:364
  39.0 5.4 %collective-permute-start.13 = (f32[80,128]{1,0:T(8,128)S(1)}, f32[80,128]{1,0:T(8,128)S(1)}, u32[]{:S(2)}, u32[]{:S(2)}) collective-permute-start(f32[80,128]{1,0:T(8,128)S(1)} %add_add_fusion.1), channel_id=1, source_target_pairs={{0,2},{1,3},{2,0},{3,1},{4,6},{5,7},{6,4},{7,5},{8,10},{9,11},{10,... | collective-permute-start | bytes 122888 | tf_op jit(solution)/shard_map/ppermute | solution.py:364
  40.1 4.4 %collective-permute-start.14 = (f32[80,128]{1,0:T(8,128)S(1)}, f32[80,128]{1,0:T(8,128)S(1)}, u32[]{:S(2)}, u32[]{:S(2)}) collective-permute-start(f32[80,128]{1,0:T(8,128)S(1)} %add_add_fusion.1), channel_id=1, source_target_pairs={{0,1},{1,0},{2,3},{3,2},{4,5},{5,4},{6,7},{7,6},{8,9},{9,8},{10,11... | collective-permute-start | bytes 122888 | tf_op jit(solution)/shard_map/ppermute | solution.py:364
  44.5 1.3 %collective-permute-start.15 = (f32[80,128]{1,0:T(8,128)S(1)}, f32[80,128]{1,0:T(8,128)S(1)}, u32[]{:S(2)}, u32[]{:S(2)}) collective-permute-start(f32[80,128]{1,0:T(8,128)S(1)} %add_add_fusion.half_ref), channel_id=1, source_target_pairs={{0,4},{1,5},{2,6},{3,7},{4,0},{5,1},{6,2},{7,3},{8,12},{9,13},{10,... | collective-permute-start | bytes 122888 | tf_op jit(solution)/shard_map/ppermute | solution.py:364

commit v10 on v9

--- a/solution.py
+++ b/solution.py
@@ -168,6 +168,7 @@
     count_ref,
     phase_ref,
     third_ref,
+    after_ref,
     send_ref,
     lattice_ref,
 ):
@@ -231,19 +232,15 @@
     scale,
     cell_ref,
     numbers_ref,
-    lattice_ref,
-    third_ref,
     count_ref,
+    after_ref,
     weight_ref,
     factor_ref,
-    born_ref,
     acc,
 ):
-    alive = lax.broadcasted_iota(jnp.int32, (1, lattice_ref.shape[1]), 1) < count_ref[...]
+    alive = lax.broadcasted_iota(jnp.int32, (1, factor_ref.shape[1]), 1) < count_ref[...]
     for axis in range(3):
         factor_ref[axis : axis + 1, :] = jnp.where(alive, -(two_pi * scale / cell_ref[axis]), 0.0)
-    total = jnp.sum(lattice_ref[64:68, :], axis=0, keepdims=True)
-    born_ref[...] = total * third_ref[16:19, :]
     acc[...] = jnp.zeros_like(acc)
     width = math.gcd(numbers_ref.shape[1], 1024)
     plane_ids = lax.broadcasted_iota(jnp.int32, (grid_rows, width), 0)
@@ -274,6 +271,12 @@
         weight_ref[8 * c : 8 * c + 8, :] = up
         weight_ref[32 + 8 * c : 40 + 8 * c, :] = down
     weight_ref[64:72, :] = flat
+
+
+def born_kernel(lattice_ref, third_ref, born_ref, done_ref):
+    total = jnp.sum(lattice_ref[64:68, :], axis=0, keepdims=True)
+    born_ref[...] = total * third_ref[16:19, :]
+    done_ref[...] = jnp.zeros(done_ref.shape, f32)
 
 
 def force_kernel(
@@ -467,6 +470,17 @@
         hidden,
         cost=busy,
     )
+    weights, factor = call(
+        functools.partial(weight_kernel, scale),
+        [((72, grid_rows), f32), ((8, atoms), f32)],
+        cell_lengths,
+        wave_numbers,
+        counts,
+        hidden,
+        smem=(0,),
+        scratch=[pltpu.VMEM((32, grid_rows), f32)],
+        cost=busy,
+    )
     send, lattice = call(
         functools.partial(last_kernel, layers - 1),
         [((half_rows, 128), f32), ((72, atoms), f32)],
@@ -481,21 +495,13 @@
         counts,
         phases,
         third,
-    )
-    weights, factor, born_charges = call(
-        functools.partial(weight_kernel, scale),
-        [((72, grid_rows), f32), ((8, atoms), f32), ((3, atoms), f32)],
-        cell_lengths,
-        wave_numbers,
-        lattice,
-        third,
-        counts,
-        smem=(0,),
-        scratch=[pltpu.VMEM((32, grid_rows), f32)],
-        cost=busy,
+        factor,
+    )
+    born_charges, done = call(
+        born_kernel, [((3, atoms), f32), ((8, 128), f32)], lattice, third, cost=busy
     )
     (keep,) = call(keep_kernel, [((half_rows, 128), f32)], lattice, phases, cost=busy)
-    half, other, (weights, factor) = summed(send, keep, (weights, factor))
+    half, other, done = summed(send, keep, done)
     forces, energy = call(
         functools.partial(force_kernel, scale),
         [((3, atoms), f32), ((1, 1), f32)],

time: 47.1 us -> 47 us (level)
  waiting for transfers between devices: 11.6 us -> 11.1 us
    ppermute x8, waiting for transfers between devices: 4.77 us -> 6.95 us  [flipped(): return lax.ppermute(block, ('wide', 'narrow'), pairs)]
    ppermute x4, waiting for transfers between devices: 4.49 us -> 2.51 us  [matched(): lax.ppermute(first, axis, [(i, (i + ways[i % 2]) % count) for i in range(...]
    ppermute x4, waiting for transfers between devices: 2.33 us -> 1.65 us  [matched(): lax.ppermute(second, axis, [(i, (i - ways[i % 2]) % count) for i in range...]
    pallas_call x15 -> x16, Pallas kernels: 12 us -> 12.3 us  [call(): pl.pallas_call(kernel, out_shape=[jax.ShapeDtypeStruct(shape, dtype) for...]
  transfers between devices with their start and end apart: 16 -> 16, of which waited for: 8 -> 10; matrix products, arithmetic and copies ran while one was open for 0% -> 0% of each run, Pallas kernels for 20% -> 20%
where the time goes in v10:
time: 47 us; the launch traced here: 46.8 us
  starting transfers between devices  20.3 us (43%)
  Pallas kernels  12.3 us (26%)
  waiting for transfers between devices  11.1 us (24%)
  local copies, waits for them, and re-layouts  1.55 us (3%)
  between operations  1.53 us (3%)
    pallas_call x16, Pallas kernels, call(): pl.pallas_call(kernel, out_shape=[jax.ShapeDtypeStruct(shape, dtype) for...  12.3 us
    ppermute x8, starting transfers between devices, flipped(): return lax.ppermute(block, ('wide', 'narrow'), pairs)  8.08 us
    ppermute x4, starting transfers between devices, matched(): lax.ppermute(second, axis, [(i, (i - ways[i % 2]) % count) for i in range...  6.99 us
    ppermute x8, waiting for transfers between devices, flipped(): return lax.ppermute(block, ('wide', 'narrow'), pairs)  6.95 us
    ppermute x4, starting transfers between devices, matched(): lax.ppermute(first, axis, [(i, (i + ways[i % 2]) % count) for i in range(...  5.2 us
    ppermute x4, waiting for transfers between devices, matched(): lax.ppermute(first, axis, [(i, (i + ways[i % 2]) % count) for i in range(...  2.51 us
    ppermute x4, waiting for transfers between devices, matched(): lax.ppermute(second, axis, [(i, (i - ways[i % 2]) % count) for i in range...  1.65 us
    unnamed x20, local copies, waits for them, and re-layouts  1.55 us
  transfers between devices with their start and end apart: 16, of which 10 were waited for; matrix products, arithmetic and copies ran while one was open for 0% of the time, Pallas kernels for 20%

profile of v10, /device:TPU:0, one launch (start us, length us, event | category | flops | bytes accessed | tf_op | source)
XLA Modules:
  0.0 46.8 jit_solution(16245487621659142605)
XLA Ops:
  0.7 0.7 %copy-done.8 = s32[4,384]{1,0:T(4,128)S(1)} copy-done((s32[4,384]{1,0:T(4,128)S(1)}, s32[4,384]{1,0:T(4,128)}, u32[]{:S(2)}) %copy-start.8) | copy-done | bytes 6168
  1.6 0.4 shard_map.131
  1.9 3.1 %collective-permute-start = (f32[128,384]{1,0:T(8,128)S(1)}, f32[128,384]{1,0:T(8,128)S(1)}, u32[]{:S(2)}, u32[]{:S(2)}) collective-permute-start(f32[128,384]{1,0:T(8,128)S(1)} %get-tuple-element.36), channel_id=1, source_target_pairs={{0,1},{1,0},{2,3},{3,2},{4,5},{5,4},{6,7},{7,6},{8,9},{9,8},{10,11... | collective-permute-start | bytes 589832 | tf_op jit(solution)/shard_map/ppermute | solution.py:355
  5.0 2.5 %collective-permute-start.1 = (f32[128,384]{1,0:T(8,128)S(1)}, f32[128,384]{1,0:T(8,128)S(1)}, u32[]{:S(2)}, u32[]{:S(2)}) collective-permute-start(f32[128,384]{1,0:T(8,128)S(1)} %get-tuple-element.37), channel_id=1, source_target_pairs={{0,3},{1,2},{2,1},{3,0},{4,7},{5,6},{6,5},{7,4},{8,11},{9,10},{10,... | collective-permute-start | bytes 589832 | tf_op jit(solution)/shard_map/ppermute | solution.py:356
  7.5 0.3 shard_map.135
  7.8 1.4 %collective-permute-start.2 = (f32[128,384]{1,0:T(8,128)S(1)}, f32[128,384]{1,0:T(8,128)S(1)}, u32[]{:S(2)}, u32[]{:S(2)}) collective-permute-start(f32[128,384]{1,0:T(8,128)S(1)} %get-tuple-element.38), channel_id=1, source_target_pairs={{0,28},{4,8},{8,4},{12,16},{16,12},{20,24},{24,20},{28,0},{1,29},{... | collective-permute-start | bytes 589832 | tf_op jit(solution)/shard_map/ppermute | solution.py:355
  10.2 4.3 %shard_map.132 = (bf16[1280,512]{1,0:T(8,128)(2,1)S(1)}, bf16[768,512]{1,0:T(8,128)(2,1)S(1)}, bf16[2,128,128]{2,1,0:T(8,128)(2,1)S(1)}, bf16[2,128,256]{2,1,0:T(8,128)(2,1)S(1)}, bf16[512,768]{1,0:T(8,128)(2,1)S(1)}) custom-call(s32[16,512]{1,0:T(8,128)S(1)} %copy-done.5, f32[16,512]{1,0:T(8,128)S(1)} %copy-done.6, bf16[2,128,128]{2,1,0:T(8,128)(2,1)S(1)} %copy-done.3, ...), custom_call_target="tpu_custom_call" | custom-call | flops 1000000000 | bytes 20971520 | tf_op jit(solution)/shard_map/pallas_call | solution.py:341
  14.8 1.6 %collective-permute-done.1.g3 = f32[128,384]{1,0:T(8,128)S(1)} collective-permute-done((f32[128,384]{1,0:T(8,128)S(1)}, f32[128,384]{1,0:T(8,128)S(1)}, u32[]{:S(2)}, u32[]{:S(2)}) %collective-permute-start.1) | collective-permute-done | bytes 196640 | tf_op jit(solution)/shard_map/ppermute | solution.py:356
  16.7 0.7 %shard_map.136 = (bf16[128,512]{1,0:T(8,128)(2,1)S(1)}, f32[128,384]{1,0:T(8,128)S(1)}, f32[128,384]{1,0:T(8,128)S(1)}) custom-call(bf16[128,512]{1,0:T(8,128)(2,1)S(1)} %get-tuple-element.31.hidden_ref, f32[128,512]{1,0:T(8,128)S(1)} %get-tuple-element.34.own_ref, f32[128,512]{1,0:T(8,128)S(1)} %shard_map.134.gathered_ref, ...), custom_call_target="tpu_custom_call" | custom-call | flops 1000000000 | bytes 20971520 | tf_op jit(solution)/shard_map/pallas_call | solution.py:341
  17.4 0.6 %collective-permute-start.4 = (f32[128,384]{1,0:T(8,128)S(1)}, f32[128,384]{1,0:T(8,128)S(1)}, u32[]{:S(2)}, u32[]{:S(2)}) collective-permute-start(f32[128,384]{1,0:T(8,128)S(1)} %get-tuple-element.46), channel_id=1, source_target_pairs={{0,1},{1,0},{2,3},{3,2},{4,5},{5,4},{6,7},{7,6},{8,9},{9,8},{10,11... | collective-permute-start | bytes 589832 | tf_op jit(solution)/shard_map/ppermute | solution.py:355
  18.1 2.6 %collective-permute-start.5 = (f32[128,384]{1,0:T(8,128)S(1)}, f32[128,384]{1,0:T(8,128)S(1)}, u32[]{:S(2)}, u32[]{:S(2)}) collective-permute-start(f32[128,384]{1,0:T(8,128)S(1)} %get-tuple-element.47), channel_id=1, source_target_pairs={{0,3},{1,2},{2,1},{3,0},{4,7},{5,6},{6,5},{7,4},{8,11},{9,10},{10,... | collective-permute-start | bytes 589832 | tf_op jit(solution)/shard_map/ppermute | solution.py:356
  20.7 0.3 shard_map.139
  21.2 1.6 %collective-permute-start.7 = (f32[128,384]{1,0:T(8,128)S(1)}, f32[128,384]{1,0:T(8,128)S(1)}, u32[]{:S(2)}, u32[]{:S(2)}) collective-permute-start(f32[128,384]{1,0:T(8,128)S(1)} %get-tuple-element.49), channel_id=1, source_target_pairs={{0,4},{4,0},{8,12},{12,8},{16,20},{20,16},{24,28},{28,24},{1,5},{5... | collective-permute-start | bytes 589832 | tf_op jit(solution)/shard_map/ppermute | solution.py:356
  23.3 0.6 %copy-done.2 = s32[3,8192]{1,0:T(4,128)S(1)} copy-done((s32[3,8192]{1,0:T(4,128)S(1)}, s32[3,8192]{1,0:T(4,128)}, u32[]{:S(2)}) %copy-start.2) | copy-done | bytes 98328
  23.9 2.4 %shard_map.141 = (f32[72,136]{1,0:T(8,128)S(1)}, f32[8,512]{1,0:T(8,128)S(1)}) custom-call(f32[3]{0:T(128)S(1)} %copy-done.9, s32[3,8192]{1,0:T(4,128)S(1)} %copy-done.2, s32[1,1]{1,0:T(1,128)} %bitcast.3.count_ref, bf16[128,512]{1,0:T(8,128)(2,1)S(1)} %get-tuple-element.43.hidden_ref.after_ref), custom_call_target="tpu_custom_call" | custom-call | flops 1000000000 | bytes 20971520 | tf_op jit(solution)/shard_map/pallas_call | solution.py:341
  26.3 1.1 %collective-permute-done.4.g2 = f32[128,384]{1,0:T(8,128)S(1)} collective-permute-done((f32[128,384]{1,0:T(8,128)S(1)}, f32[128,384]{1,0:T(8,128)S(1)}, u32[]{:S(2)}, u32[]{:S(2)}) %collective-permute-start.4) | collective-permute-done | bytes 196640 | tf_op jit(solution)/shard_map/ppermute | solution.py:355
  27.7 1.4 %collective-permute-done.6.g0 = f32[128,384]{1,0:T(8,128)S(1)} collective-permute-done((f32[128,384]{1,0:T(8,128)S(1)}, f32[128,384]{1,0:T(8,128)S(1)}, u32[]{:S(2)}, u32[]{:S(2)}) %collective-permute-start.6) | collective-permute-done | bytes 196640 | tf_op jit(solution)/shard_map/ppermute | solution.py:355
  29.1 0.8 %shard_map.142 = (f32[80,128]{1,0:T(8,128)S(1)}, f32[72,512]{1,0:T(8,128)S(1)}) custom-call(bf16[128,512]{1,0:T(8,128)(2,1)S(1)} %get-tuple-element.43.hidden_ref.after_ref, f32[128,512]{1,0:T(8,128)S(1)} %get-tuple-element.44.own_ref, f32[128,512]{1,0:T(8,128)S(1)} %shard_map.138.gathered_ref, f32[128,384]{1,0:T(8,128)S(1)} %collective-permute-done.6.g0, ...), custom_call_target="tpu_custom_call" | custom-call | tf_op jit(solution)/shard_map/pallas_call | solution.py:341
  30.2 1.0 %collective-permute-done.8 = f32[80,128]{1,0:T(8,128)S(1)} collective-permute-done((f32[80,128]{1,0:T(8,128)S(1)}, f32[80,128]{1,0:T(8,128)S(1)}, u32[]{:S(2)}, u32[]{:S(2)}) %collective-permute-start.8) | collective-permute-done | bytes 40992 | tf_op jit(solution)/shard_map/ppermute | solution.py:367
  31.2 1.1 %collective-permute-start.10 = (f32[80,128]{1,0:T(8,128)S(1)}, f32[80,128]{1,0:T(8,128)S(1)}, u32[]{:S(2)}, u32[]{:S(2)}) collective-permute-start(f32[80,128]{1,0:T(8,128)S(1)} %add.21), channel_id=1, source_target_pairs={{0,24},{1,25},{2,26},{3,27},{4,28},{5,29},{6,30},{7,31},{8,16},{9,... | collective-permute-start | bytes 122888 | tf_op jit(solution)/shard_map/ppermute | solution.py:367
  32.3 1.1 %collective-permute-start.11 = (f32[80,128]{1,0:T(8,128)S(1)}, f32[80,128]{1,0:T(8,128)S(1)}, u32[]{:S(2)}, u32[]{:S(2)}) collective-permute-start(f32[80,128]{1,0:T(8,128)S(1)} %add.21), channel_id=1, source_target_pairs={{0,8},{1,9},{2,10},{3,11},{4,12},{5,13},{6,14},{7,15},{8,0},{9,1},... | collective-permute-start | bytes 122888 | tf_op jit(solution)/shard_map/ppermute | solution.py:367
  33.4 1.3 %collective-permute-start.9 = (f32[80,128]{1,0:T(8,128)S(1)}, f32[80,128]{1,0:T(8,128)S(1)}, u32[]{:S(2)}, u32[]{:S(2)}) collective-permute-start(f32[80,128]{1,0:T(8,128)S(1)} %add.21), channel_id=1, source_target_pairs={{0,16},{1,17},{2,18},{3,19},{4,20},{5,21},{6,22},{7,23},{8,24},{9,... | collective-permute-start | bytes 122888 | tf_op jit(solution)/shard_map/ppermute | solution.py:367
  34.7 1.5 %collective-permute-done.10 = f32[80,128]{1,0:T(8,128)S(1)} collective-permute-done((f32[80,128]{1,0:T(8,128)S(1)}, f32[80,128]{1,0:T(8,128)S(1)}, u32[]{:S(2)}, u32[]{:S(2)}) %collective-permute-start.10) | collective-permute-done | bytes 40992 | tf_op jit(solution)/shard_map/ppermute | solution.py:367
  36.3 1.1 %collective-permute-done.9 = f32[80,128]{1,0:T(8,128)S(1)} collective-permute-done((f32[80,128]{1,0:T(8,128)S(1)}, f32[80,128]{1,0:T(8,128)S(1)}, u32[]{:S(2)}, u32[]{:S(2)}) %collective-permute-start.9) | collective-permute-done | bytes 40992 | tf_op jit(solution)/shard_map/ppermute | solution.py:367
  37.4 1.6 %collective-permute-start.12 = (f32[80,128]{1,0:T(8,128)S(1)}, f32[80,128]{1,0:T(8,128)S(1)}, u32[]{:S(2)}, u32[]{:S(2)}) collective-permute-start(f32[80,128]{1,0:T(8,128)S(1)} %add_add_fusion.1), channel_id=1, source_target_pairs={{0,3},{1,2},{2,1},{3,0},{4,7},{5,6},{6,5},{7,4},{8,11},{9,10},{10,... | collective-permute-start | bytes 122888 | tf_op jit(solution)/shard_map/ppermute | solution.py:367
  39.0 1.1 %collective-permute-start.13 = (f32[80,128]{1,0:T(8,128)S(1)}, f32[80,128]{1,0:T(8,128)S(1)}, u32[]{:S(2)}, u32[]{:S(2)}) collective-permute-start(f32[80,128]{1,0:T(8,128)S(1)} %add_add_fusion.1), channel_id=1, source_target_pairs={{0,2},{1,3},{2,0},{3,1},{4,6},{5,7},{6,4},{7,5},{8,10},{9,11},{10,... | collective-permute-start | bytes 122888 | tf_op jit(solution)/shard_map/ppermute | solution.py:367
  40.1 1.8 %collective-permute-start.14 = (f32[80,128]{1,0:T(8,128)S(1)}, f32[80,128]{1,0:T(8,128)S(1)}, u32[]{:S(2)}, u32[]{:S(2)}) collective-permute-start(f32[80,128]{1,0:T(8,128)S(1)} %add_add_fusion.1), channel_id=1, source_target_pairs={{0,1},{1,0},{2,3},{3,2},{4,5},{5,4},{6,7},{7,6},{8,9},{9,8},{10,11... | collective-permute-start | bytes 122888 | tf_op jit(solution)/shard_map/ppermute | solution.py:367
  41.8 1.4 %collective-permute-done.12 = f32[80,128]{1,0:T(8,128)S(1)} collective-permute-done((f32[80,128]{1,0:T(8,128)S(1)}, f32[80,128]{1,0:T(8,128)S(1)}, u32[]{:S(2)}, u32[]{:S(2)}) %collective-permute-start.12) | collective-permute-done | bytes 40992 | tf_op jit(solution)/shard_map/ppermute | solution.py:367
  43.3 0.9 %collective-permute-done.13 = f32[80,128]{1,0:T(8,128)S(1)} collective-permute-done((f32[80,128]{1,0:T(8,128)S(1)}, f32[80,128]{1,0:T(8,128)S(1)}, u32[]{:S(2)}, u32[]{:S(2)}) %collective-permute-start.13) | collective-permute-done | bytes 40992 | tf_op jit(solution)/shard_map/ppermute | solution.py:367
  44.6 0.6 %shard_map.145 = (f32[3,512]{1,0:T(4,128)}, f32[8,128]{1,0:T(8,128)}) custom-call(f32[72,512]{1,0:T(8,128)S(1)} %get-tuple-element.53.lattice_ref, f32[24,512]{1,0:T(8,128)S(1)} %get-tuple-element.51.third_ref), custom_call_target="tpu_custom_call" | custom-call | flops 1000000000 | bytes 20971520 | tf_op jit(solution)/shard_map/pallas_call | solution.py:341
  45.2 0.6 %collective-permute-done.15.other_ref = f32[80,128]{1,0:T(8,128)S(1)} collective-permute-done((f32[80,128]{1,0:T(8,128)S(1)}, f32[80,128]{1,0:T(8,128)S(1)}, u32[]{:S(2)}, u32[]{:S(2)}) %collective-permute-start.15) | collective-permute-done | bytes 40992 | tf_op jit(solution)/shard_map/ppermute | solution.py:367
  45.8 1.0 %shard_map.144 = (f32[3,512]{1,0:T(4,128)}, f32[1,1]{1,0:T(1,128)}) custom-call(f32[80,128]{1,0:T(8,128)S(1)} %add_add_fusion.half_ref, f32[80,128]{1,0:T(8,128)S(1)} %collective-permute-done.15.other_ref, f32[72,512]{1,0:T(8,128)S(1)} %get-tuple-element.53.lattice_ref, bf16[2,136,512]{2,1,0:T(8,128)(2,1)S(1)} %get-tuple-element.50.phase_ref, ...), custom_call_target="tpu_custom_call" | custom-call | tf_op jit(solution)/shard_map/pallas_call | solution.py:341
  (39 shorter events, 2.7 us)
Async XLA Ops:
  0.6 0.7 %copy-start.8 = (s32[4,384]{1,0:T(4,128)S(1)}, s32[4,384]{1,0:T(4,128)}, u32[]{:S(2)}) copy-start(s32[4,384]{1,0:T(4,128)} %index_ref.7) | copy-start | bytes 18436
  0.6 0.9 %copy-start.1 = (bf16[512,128]{1,0:T(8,128)(2,1)S(1)}, bf16[512,128]{1,0:T(8,128)(2,1)}, u32[]{:S(2)}) copy-start(bf16[512,128]{1,0:T(8,128)(2,1)} %features_ref.1) | copy-start | bytes 393220
  1.9 12.8 %collective-permute-start = (f32[128,384]{1,0:T(8,128)S(1)}, f32[128,384]{1,0:T(8,128)S(1)}, u32[]{:S(2)}, u32[]{:S(2)}) collective-permute-start(f32[128,384]{1,0:T(8,128)S(1)} %get-tuple-element.36), channel_id=1, source_target_pairs={{0,1},{1,0},{2,3},{3,2},{4,5},{5,4},{6,7},{7,6},{8,9},{9,8},{10,11... | collective-permute-start | bytes 589832 | tf_op jit(solution)/shard_map/ppermute | solution.py:355
  5.0 11.4 %collective-permute-start.1 = (f32[128,384]{1,0:T(8,128)S(1)}, f32[128,384]{1,0:T(8,128)S(1)}, u32[]{:S(2)}, u32[]{:S(2)}) collective-permute-start(f32[128,384]{1,0:T(8,128)S(1)} %get-tuple-element.37), channel_id=1, source_target_pairs={{0,3},{1,2},{2,1},{3,0},{4,7},{5,6},{6,5},{7,4},{8,11},{9,10},{10,... | collective-permute-start | bytes 589832 | tf_op jit(solution)/shard_map/ppermute | solution.py:356
  7.5 2.7 %copy-start.3 = (bf16[2,128,128]{2,1,0:T(8,128)(2,1)S(1)}, bf16[2,128,128]{2,1,0:T(8,128)(2,1)}, u32[]{:S(2)}) copy-start(bf16[2,128,128]{2,1,0:T(8,128)(2,1)} %self_ref.1) | copy-start | bytes 196612
  7.5 2.7 %copy-start.4 = (bf16[2,128,128]{2,1,0:T(8,128)(2,1)S(1)}, bf16[2,128,128]{2,1,0:T(8,128)(2,1)}, u32[]{:S(2)}) copy-start(bf16[2,128,128]{2,1,0:T(8,128)(2,1)} %message_ref.1) | copy-start | bytes 196612
  7.5 2.7 %copy-start.5 = (s32[16,512]{1,0:T(8,128)S(1)}, s32[16,512]{1,0:T(8,128)}, u32[]{:S(2)}) copy-start(s32[16,512]{1,0:T(8,128)} %senders_ref.1) | copy-start | bytes 98308
  7.5 2.7 %copy-start.6 = (f32[16,512]{1,0:T(8,128)S(1)}, f32[16,512]{1,0:T(8,128)}, u32[]{:S(2)}) copy-start(f32[16,512]{1,0:T(8,128)} %radial_ref.1) | copy-start | bytes 98308
  7.8 8.9 %collective-permute-start.2 = (f32[128,384]{1,0:T(8,128)S(1)}, f32[128,384]{1,0:T(8,128)S(1)}, u32[]{:S(2)}, u32[]{:S(2)}) collective-permute-start(f32[128,384]{1,0:T(8,128)S(1)} %get-tuple-element.38), channel_id=1, source_target_pairs={{0,28},{4,8},{8,4},{12,16},{16,12},{20,24},{24,20},{28,0},{1,29},{... | collective-permute-start | bytes 589832 | tf_op jit(solution)/shard_map/ppermute | solution.py:355
  9.2 7.5 %collective-permute-start.3 = (f32[128,384]{1,0:T(8,128)S(1)}, f32[128,384]{1,0:T(8,128)S(1)}, u32[]{:S(2)}, u32[]{:S(2)}) collective-permute-start(f32[128,384]{1,0:T(8,128)S(1)} %get-tuple-element.39), channel_id=1, source_target_pairs={{0,4},{4,0},{8,12},{12,8},{16,20},{20,16},{24,28},{28,24},{1,5},{5... | collective-permute-start | bytes 589832 | tf_op jit(solution)/shard_map/ppermute | solution.py:356
  17.4 10.0 %collective-permute-start.4 = (f32[128,384]{1,0:T(8,128)S(1)}, f32[128,384]{1,0:T(8,128)S(1)}, u32[]{:S(2)}, u32[]{:S(2)}) collective-permute-start(f32[128,384]{1,0:T(8,128)S(1)} %get-tuple-element.46), channel_id=1, source_target_pairs={{0,1},{1,0},{2,3},{3,2},{4,5},{5,4},{6,7},{7,6},{8,9},{9,8},{10,11... | collective-permute-start | bytes 589832 | tf_op jit(solution)/shard_map/ppermute | solution.py:355
  18.1 9.4 %collective-permute-start.5 = (f32[128,384]{1,0:T(8,128)S(1)}, f32[128,384]{1,0:T(8,128)S(1)}, u32[]{:S(2)}, u32[]{:S(2)}) collective-permute-start(f32[128,384]{1,0:T(8,128)S(1)} %get-tuple-element.47), channel_id=1, source_target_pairs={{0,3},{1,2},{2,1},{3,0},{4,7},{5,6},{6,5},{7,4},{8,11},{9,10},{10,... | collective-permute-start | bytes 589832 | tf_op jit(solution)/shard_map/ppermute | solution.py:356
  21.1 8.1 %collective-permute-start.6 = (f32[128,384]{1,0:T(8,128)S(1)}, f32[128,384]{1,0:T(8,128)S(1)}, u32[]{:S(2)}, u32[]{:S(2)}) collective-permute-start(f32[128,384]{1,0:T(8,128)S(1)} %get-tuple-element.48), channel_id=1, source_target_pairs={{0,28},{4,8},{8,4},{12,16},{16,12},{20,24},{24,20},{28,0},{1,29},{... | collective-permute-start | bytes 589832 | tf_op jit(solution)/shard_map/ppermute | solution.py:355
  21.1 1.9 %copy-start.7 = (f32[3,512]{1,0:T(4,128)S(1)}, f32[3,512]{1,0:T(4,128)}, u32[]{:S(2)}) copy-start(f32[3,512]{1,0:T(4,128)} %fractions_ref.1) | copy-start | bytes 18436
  21.2 8.0 %collective-permute-start.7 = (f32[128,384]{1,0:T(8,128)S(1)}, f32[128,384]{1,0:T(8,128)S(1)}, u32[]{:S(2)}, u32[]{:S(2)}) collective-permute-start(f32[128,384]{1,0:T(8,128)S(1)} %get-tuple-element.49), channel_id=1, source_target_pairs={{0,4},{4,0},{8,12},{12,8},{16,20},{20,16},{24,28},{28,24},{1,5},{5... | collective-permute-start | bytes 589832 | tf_op jit(solution)/shard_map/ppermute | solution.py:356
  23.0 0.9 %copy-start.2 = (s32[3,8192]{1,0:T(4,128)S(1)}, s32[3,8192]{1,0:T(4,128)}, u32[]{:S(2)}) copy-start(s32[3,8192]{1,0:T(4,128)} %numbers_ref.1) | copy-start | bytes 294916
  23.0 0.9 %copy-start.9 = (f32[3]{0:T(128)S(1)}, f32[3]{0:T(128)}, u32[]{:S(2)}) copy-start(f32[3]{0:T(128)} %cell_ref.1) | copy-start | bytes 40
  26.3 2.8 %copy-start = (bf16[128,4]{0,1:T(4,128)(2,1)S(1)}, bf16[128,4]{0,1:T(4,128)(2,1)}, u32[]{:S(2)}) copy-start(bf16[128,4]{0,1:T(4,128)(2,1)} %param.20) | copy-start | bytes 3076
  29.9 1.3 %collective-permute-start.8 = (f32[80,128]{1,0:T(8,128)S(1)}, f32[80,128]{1,0:T(8,128)S(1)}, u32[]{:S(2)}, u32[]{:S(2)}) collective-permute-start(f32[80,128]{1,0:T(8,128)S(1)} %get-tuple-element.54), channel_id=1, source_target_pairs={{0,4},{1,5},{2,6},{3,7},{4,0},{5,1},{6,2},{7,3},{8,12},{9,13},{10,... | collective-permute-start | bytes 122888 | tf_op jit(solution)/shard_map/ppermute | solution.py:367
  31.2 5.0 %collective-permute-start.10 = (f32[80,128]{1,0:T(8,128)S(1)}, f32[80,128]{1,0:T(8,128)S(1)}, u32[]{:S(2)}, u32[]{:S(2)}) collective-permute-start(f32[80,128]{1,0:T(8,128)S(1)} %add.21), channel_id=1, source_target_pairs={{0,24},{1,25},{2,26},{3,27},{4,28},{5,29},{6,30},{7,31},{8,16},{9,... | collective-permute-start | bytes 122888 | tf_op jit(solution)/shard_map/ppermute | solution.py:367
  32.3 4.0 %collective-permute-start.11 = (f32[80,128]{1,0:T(8,128)S(1)}, f32[80,128]{1,0:T(8,128)S(1)}, u32[]{:S(2)}, u32[]{:S(2)}) collective-permute-start(f32[80,128]{1,0:T(8,128)S(1)} %add.21), channel_id=1, source_target_pairs={{0,8},{1,9},{2,10},{3,11},{4,12},{5,13},{6,14},{7,15},{8,0},{9,1},... | collective-permute-start | bytes 122888 | tf_op jit(solution)/shard_map/ppermute | solution.py:367
  33.4 4.0 %collective-permute-start.9 = (f32[80,128]{1,0:T(8,128)S(1)}, f32[80,128]{1,0:T(8,128)S(1)}, u32[]{:S(2)}, u32[]{:S(2)}) collective-permute-start(f32[80,128]{1,0:T(8,128)S(1)} %add.21), channel_id=1, source_target_pairs={{0,16},{1,17},{2,18},{3,19},{4,20},{5,21},{6,22},{7,23},{8,24},{9,... | collective-permute-start | bytes 122888 | tf_op jit(solution)/shard_map/ppermute | solution.py:367
  37.4 5.9 %collective-permute-start.12 = (f32[80,128]{1,0:T(8,128)S(1)}, f32[80,128]{1,0:T(8,128)S(1)}, u32[]{:S(2)}, u32[]{:S(2)}) collective-permute-start(f32[80,128]{1,0:T(8,128)S(1)} %add_add_fusion.1), channel_id=1, source_target_pairs={{0,3},{1,2},{2,1},{3,0},{4,7},{5,6},{6,5},{7,4},{8,11},{9,10},{10,... | collective-permute-start | bytes 122888 | tf_op jit(solution)/shard_map/ppermute | solution.py:367
  39.0 5.2 %collective-permute-start.13 = (f32[80,128]{1,0:T(8,128)S(1)}, f32[80,128]{1,0:T(8,128)S(1)}, u32[]{:S(2)}, u32[]{:S(2)}) collective-permute-start(f32[80,128]{1,0:T(8,128)S(1)} %add_add_fusion.1), channel_id=1, source_target_pairs={{0,2},{1,3},{2,0},{3,1},{4,6},{5,7},{6,4},{7,5},{8,10},{9,11},{10,... | collective-permute-start | bytes 122888 | tf_op jit(solution)/shard_map/ppermute | solution.py:367
  40.1 4.4 %collective-permute-start.14 = (f32[80,128]{1,0:T(8,128)S(1)}, f32[80,128]{1,0:T(8,128)S(1)}, u32[]{:S(2)}, u32[]{:S(2)}) collective-permute-start(f32[80,128]{1,0:T(8,128)S(1)} %add_add_fusion.1), channel_id=1, source_target_pairs={{0,1},{1,0},{2,3},{3,2},{4,5},{5,4},{6,7},{7,6},{8,9},{9,8},{10,11... | collective-permute-start | bytes 122888 | tf_op jit(solution)/shard_map/ppermute | solution.py:367
  44.5 1.3 %collective-permute-start.15 = (f32[80,128]{1,0:T(8,128)S(1)}, f32[80,128]{1,0:T(8,128)S(1)}, u32[]{:S(2)}, u32[]{:S(2)}) collective-permute-start(f32[80,128]{1,0:T(8,128)S(1)} %add_add_fusion.half_ref), channel_id=1, source_target_pairs={{0,4},{1,5},{2,6},{3,7},{4,0},{5,1},{6,2},{7,3},{8,12},{9,13},{10,... | collective-permute-start | bytes 122888 | tf_op jit(solution)/shard_map/ppermute | solution.py:367
